TPU v7x, 32 devices: a whole 2x2x4 slice. The times are simulated.
32 devices in a mesh: dp: 16 (over z, x, core), worker: 2 (over y).
Axes of the slice: x: 2, y: 2, z: 4, core: 2. Of those that a mesh axis runs over, the one named last changes fastest.
Arguments:
- acts: bfloat16 [16384, 4096], P('dp', 'worker'), may hold values from -6 to 6
- cotan: bfloat16 [16384, 4096], P('dp', 'worker'), may hold values from -0.15625 to 0.15625
- block_ids: int32 [32], P('dp'), may hold values from 0 to 7
- basis_in: bfloat16 [8, 512, 512], P('worker'), may hold values from -0.25 to 0.25
- basis_out: bfloat16 [8, 512, 512], replicated, may hold values from -0.25 to 0.25
- act_factor: float32 [8, 512, 512], P('worker'), may hold values from -0.0009375 to 1, as said below
- grad_factor: float32 [8, 512, 512], P('worker'), may hold values from -0.0009375 to 1, as said below
Outputs:
- precond: bfloat16 [4096, 4096], P('dp', 'worker')
- act_new: float32 [8, 512, 512], P('worker')
- grad_new: float32 [8, 512, 512], P('worker')
Inputs may be any that keep to these rules, and one draw needn't show every extreme that they name: `act_factor`: each block is symmetric, and each diagonal entry exceeds the sum of magnitudes of the other entries of its row. `grad_factor`: each block is symmetric, and each diagonal entry exceeds the sum of magnitudes of the other entries of its row.
All inputs are finite; a program needn't handle non-finite values.
Results may differ from a plain program's by a relative error of at most 0.025.
Values may be sent and summed in bfloat16 or wider, within the bound.
No kernel may reach another device: no remote copies, remote signals or barrier semaphores. Data moves between devices by JAX's collectives and lax.ppermute only.
A program may use at most 128 MiB of HBM per device.

v0:
```python
import jax
import jax.numpy as jnp
from jax import lax
from jax.sharding import PartitionSpec as P

BLK = 128


DECAY_RATE = 0.75
DAMPING = 0.03


def per_device(acts, cotan, block_ids, basis_in, basis_out, act_factor, grad_factor):
    highest = lax.Precision.HIGHEST
    n_replicas = lax.axis_size("dp")
    pool_rows, width = acts.shape
    local_blocks, block_size, _ = basis_in.shape
    model_width = basis_out.shape[0] * block_size
    samples = block_ids.shape[0] * BLK * n_replicas
    tokens = pool_rows * n_replicas
    act_pick = jnp.take(acts.reshape(pool_rows // BLK, BLK, width), block_ids, axis=0).reshape(
        -1, local_blocks, block_size
    )
    cot_pick = jnp.take(cotan.reshape(pool_rows // BLK, BLK, width), block_ids, axis=0).reshape(
        -1, local_blocks, block_size
    )
    act_term = (
        jnp.einsum("rbi,rbj->bij", act_pick, act_pick, preferred_element_type=jnp.float32) / samples
    )
    cot_term = jnp.einsum(
        "rbi,rbj->bij", cot_pick, cot_pick, preferred_element_type=jnp.float32
    ) * (tokens / samples)
    act_total, cot_total = (
        lax.psum(act_term.astype(jnp.bfloat16), "dp").astype(jnp.float32),
        lax.psum(cot_term.astype(jnp.bfloat16), "dp").astype(jnp.float32),
    )
    act_new = DECAY_RATE * act_factor + (1.0 - DECAY_RATE) * act_total
    grad_new = DECAY_RATE * grad_factor + (1.0 - DECAY_RATE) * cot_total
    basis_act = basis_in.astype(jnp.float32)
    eig_in = jnp.sum(
        basis_act * jnp.einsum("bij,bjk->bik", act_new, basis_act, precision=highest), axis=1
    )
    local_out = lax.dynamic_slice_in_dim(
        basis_out, lax.axis_index("worker") * local_blocks, local_blocks, 0
    ).astype(jnp.float32)
    eig_local = jnp.sum(
        local_out * jnp.einsum("bij,bjk->bik", grad_new, local_out, precision=highest), axis=1
    )
    eig_out = lax.all_gather(eig_local, "worker", axis=0, tiled=True)
    partial_grad = jnp.einsum(
        "pk,pw->kw",
        lax.all_gather(cotan, "worker", axis=1, tiled=True),
        acts,
        preferred_element_type=jnp.float32,
    )
    rows_dev = model_width // n_replicas
    my_start = lax.axis_index("dp") * rows_dev
    block = my_start // block_size
    block_start = block * block_size
    offset = my_start - block_start
    basis_block = lax.dynamic_slice_in_dim(basis_out, block, 1, 0)[0]
    eig_block = lax.dynamic_slice_in_dim(eig_out, block, 1, 0)[0]
    basis_rows = lax.dynamic_slice_in_dim(basis_block, offset, rows_dev, 0)
    summed = lax.psum(partial_grad.astype(jnp.bfloat16), "dp").astype(jnp.float32)
    block_rows = lax.dynamic_slice_in_dim(summed, block_start, block_size, 0).astype(jnp.bfloat16)
    right_side = jnp.einsum(
        "rbj,bjk->rbk",
        block_rows.reshape(block_size, local_blocks, block_size),
        basis_in,
        preferred_element_type=jnp.float32,
    ).astype(jnp.bfloat16)
    inner_term = jnp.einsum(
        "ra,rbk->abk", basis_block, right_side, preferred_element_type=jnp.float32
    )
    scaled = (inner_term / (eig_block[:, None, None] * eig_in[None, :, :] + DAMPING)).astype(
        jnp.bfloat16
    )
    upper_term = jnp.einsum(
        "ra,abk->rbk", basis_rows, scaled, preferred_element_type=jnp.float32
    ).astype(jnp.bfloat16)
    precond = jnp.einsum("rbk,bjk->rbj", upper_term, basis_in, preferred_element_type=jnp.float32)
    return (precond.reshape(rows_dev, width).astype(jnp.bfloat16), act_new, grad_new)


def solution(mesh):
    return jax.shard_map(
        per_device,
        mesh=mesh,
        in_specs=(
            P("dp", "worker"),
            P("dp", "worker"),
            P("dp"),
            P("worker", None, None),
            P(),
            P("worker", None, None),
            P("worker", None, None),
        ),
        out_specs=(P("dp", "worker"), P("worker", None, None), P("worker", None, None)),
        check_vma=False,
    )
```

profile of v0, /device:TPU:12, one launch (start us, length us, event | category | flops | bytes accessed | tf_op | source)
XLA Modules:
  0.0 541.7 jit_solution(6546250592506006912)
XLA Ops:
  7.2 0.0 copy-start.5
  7.2 0.0 all-gather.3.cloned.1.call-start
  7.2 0.7 all-gather.3.cloned.1.call-update
  7.9 0.0 all-reduce.3.cloned.1.call-start
  8.0 0.0 copy-done.5
  8.0 2.8 gather_fusion
  10.8 2.8 gather_fusion.1
  13.6 1.2 broadcast_select_fusion.1
  14.9 1.8 reshape.63
  16.7 0.8 reshape.62
  17.5 2.1 multiply_convert_fusion
  19.6 2.1 multiply_convert_fusion.1
  21.8 92.0 %all-gather.3.cloned.1.call-done = bf16[1024,4096]{1,0:T(8,128)(2,1)} async-done(((bf16[1024,2048]{1,0:T(8,128)(2,1)}), bf16[1024,4096]{1,0:T(8,128)(2,1)}) %all-gather.3.cloned.1.call-update) | async-done | bytes 8388624 | tf_op jit(solution)/shard_map/all_gather | solution.py:52
  113.8 24.6 %convolution_convert_fusion = bf16[4096,2048]{1,0:T(8,128)(2,1)} fusion(bf16[1024,4096]{1,0:T(8,128)(2,1)} %all-gather.3.cloned.1.call-done, bf16[1024,2048]{1,0:T(8,128)(2,1)} %param.9), kind=kOutput, calls=%fused_computation.2 | convolution fusion | flops 17188257792 | bytes 29360128 | tf_op jit(solution)/shard_map/pk,pw->kw/dot_general | solution.py:50
  138.4 0.0 all-reduce.3.cloned.1.call-update
  138.5 364.7 %all-reduce.3.cloned.1.call-done = (bf16[4,512,512]{2,1,0:T(8,128)(2,1)}, bf16[4,512,512]{2,1,0:T(8,128)(2,1)}, bf16[4096,2048]{1,0:T(8,128)(2,1)}) async-done(((bf16[4,512,512]{2,1,0:T(8,128)(2,1)}, bf16[4,512,512]{2,1,0:T(8,128)(2,1)}, bf16[4096,2048]{1,0:T(8,128)(2,1)}), (bf16[4,512,512]{2,1,0:T(8,128)(2,1)}, bf16[4,512,512]{2,1,0:T(8,128)(2,1)}, ...) | async-done | bytes 20971536 | tf_op jit(solution)/shard_map/psum | solution.py:34
  503.1 3.7 multiply_add_fusion.1
  506.8 0.4 copy-done.1
  507.2 3.7 multiply_reduce_fusion.1
  510.9 0.0 copy-done
  510.9 4.4 all-gather
  515.3 0.0 copy-done.3
  515.3 0.0 copy-start.4
  515.3 3.1 multiply_add_fusion
  518.4 0.0 copy-start.2
  518.4 3.8 multiply_reduce_fusion
  522.2 1.8 convert_convert_fusion
  524.1 2.6 fusion
  526.7 3.9 fusion.12
  530.6 2.3 fusion.15
  532.9 0.5 copy.26
  533.5 1.4 copy.27
  (10 shorter events, 0.0 us)
Async XLA Ops:
  7.2 0.8 copy-start.5
  7.2 106.6 %all-gather.3.cloned.1.call-start = ((), (), s32[]{:S(2)}) async-start(), calls=%async_computation | async-start | bytes 12582912 | tf_op jit(solution)/shard_map/all_gather | solution.py:52
  7.9 495.2 %all-reduce.3.cloned.1.call-start = ((), (), s32[]{:S(2)}) async-start(), calls=%async_computation.1 | async-start | bytes 41943040 | tf_op jit(solution)/shard_map/psum | solution.py:34
  503.1 4.0 copy-start.1
  507.2 3.8 copy-start
  507.2 8.1 %copy-start.3 = (bf16[4,512,512]{2,1,0:T(8,128)(2,1)S(1)}, bf16[4,512,512]{2,1,0:T(8,128)(2,1)}, u32[]{:S(2)}) copy-start(bf16[4,512,512]{2,1,0:T(8,128)(2,1)} %get-tuple-element.10) | copy-start | bytes 6291460
  515.3 3.1 copy-start.4
  518.4 5.7 %copy-start.2 = (f32[4,512,512]{2,1,0:T(8,128)}, f32[4,512,512]{2,1,0:T(8,128)S(1)}, u32[]{:S(2)}) copy-start(f32[4,512,512]{2,1,0:T(8,128)S(1)} %multiply_add_fusion) | copy-start | bytes 12582916
Sparse Core Ops, SparseCore 0:
  9.6 104.1 all-gather.2
  138.5 364.5 all-reduce.2
where the time goes:
time: 544 us; the launch traced here: 542 us
  waiting for transfers between devices  457 us (84%)
  matrix products  45.3 us (8%)
  between operations  14.3 us (3%)
  local copies, waits for them, and re-layouts  10.6 us (2%)
  other arithmetic  9.79 us (2%)
    psum x1, waiting for transfers between devices, per_device(): lax.psum(act_term.astype(jnp.bfloat16), 'dp').astype(jnp.float32)  365 us
    all_gather x1, waiting for transfers between devices, per_device(): lax.all_gather(cotan, 'worker', axis=1, tiled=True)  92 us
    dot_general x1, matrix products, per_device(): jnp.einsum('pk,pw->kw', lax.all_gather(cotan, 'worker', axis=1, tiled=Tru...  24.6 us
  transfers between devices with their start and end apart: 2, of which 2 were waited for; matrix products, arithmetic and copies ran while one was open for 3% of the time, Pallas kernels for 0%

commit v1 on v0

v1 whole, which is shorter than its diff:
```python
import jax
import jax.numpy as jnp
from jax import lax
from jax.experimental import pallas as pl
from jax.experimental.pallas import tpu as pltpu
from jax.sharding import PartitionSpec as P

BLK = 128
QUARTER = 128
VMEM = 56 * 2**20
COL_CHUNKS = 2
DEPTH = 2


DECAY_RATE = 0.75
DAMPING = 0.03

BF16 = jnp.bfloat16
F32 = jnp.float32


def pack_upper(full):
    q = QUARTER
    first = full[:, :q, :]
    second = jnp.concatenate([full[:, q : 2 * q, q:], full[:, 3 * q :, 3 * q :]], axis=2)
    third = full[:, 2 * q : 3 * q, 2 * q :]
    third = jnp.concatenate([third[:, : q // 2], third[:, q // 2 :]], axis=2)
    return jnp.concatenate([first, second, third], axis=1)


def unpack_upper(packed):
    q = QUARTER
    tiles = {}
    for j in range(4):
        tiles[0, j] = packed[:q, j * q : (j + 1) * q]
    for j in range(1, 4):
        tiles[1, j] = packed[q : 2 * q, (j - 1) * q : j * q]
    tiles[3, 3] = packed[q : 2 * q, 3 * q :]
    third = jnp.concatenate([packed[2 * q :, : 2 * q], packed[2 * q :, 2 * q :]], axis=0)
    tiles[2, 2], tiles[2, 3] = third[:, :q], third[:, q:]
    return [[tiles[i, j] if j >= i else tiles[j, i].T for j in range(4)] for i in range(4)]


def factor_kernel(start_ref, *refs):
    del start_ref
    for packed, factor, basis, new, eig in zip(refs[0:2], refs[2:4], refs[4:6], refs[6:8], refs[8:10]):
        rows = unpack_upper(packed[0].astype(F32))
        q = QUARTER
        for i in range(4):
            for j in range(4):
                at = (0, pl.ds(i * q, q), pl.ds(j * q, q))
                new[at] = DECAY_RATE * factor[at] + (1.0 - DECAY_RATE) * rows[i][j]
        vectors = basis[0]
        rest = new[0]
        product = 0.0
        for _ in range(3):
            part = rest.astype(BF16)
            rest = rest - part.astype(F32)
            product = product + jnp.dot(part, vectors, preferred_element_type=F32)
        eig[0] = jnp.sum(vectors.astype(F32) * product, axis=0, keepdims=True)


def update_factors(packed, factors, basis_in, basis_out, first_block):
    blocks, size, _ = basis_in.shape
    packed_rows = packed[0].shape[1]

    def local(b, start):
        return (b, 0, 0)

    square = pl.BlockSpec((1, size, size), local)
    narrow = pl.BlockSpec((1, packed_rows, size), local)
    line = pl.BlockSpec((1, 1, size), local)
    return pl.pallas_call(
        factor_kernel,
        grid_spec=pltpu.PrefetchScalarGridSpec(
            num_scalar_prefetch=1,
            grid=(blocks,),
            in_specs=[narrow, narrow, square, square, square]
            + [pl.BlockSpec((1, size, size), lambda b, start: (start[0] + b, 0, 0))],
            out_specs=[square, square, line, line],
        ),
        out_shape=[jax.ShapeDtypeStruct((blocks, size, size), F32)] * 2
        + [jax.ShapeDtypeStruct((blocks, 1, size), F32)] * 2,
        compiler_params=pltpu.CompilerParams(vmem_limit_bytes=VMEM),
        cost_estimate=pl.CostEstimate(
            flops=blocks * 12 * size**3, bytes_accessed=blocks * 19 * size**2, transcendentals=0
        ),
    )(first_block, *packed, *factors, basis_in, basis_out)


def tail_kernel(place_ref, *refs):
    parts, (basis, outer, eig_in, eig_out, out, whole) = refs[:-6], refs[-6:]
    sharers = len(parts)
    rows = parts[0].shape[0]
    me = place_ref[1]
    for step, part in enumerate(parts):
        spot = lax.rem(me - step + sharers, sharers)
        whole[pl.ds(pl.multiple_of(spot * rows, rows), rows), :] = part[...]
    right = jnp.dot(whole[...], basis[0], preferred_element_type=F32).astype(BF16)
    inner = lax.dot_general(outer[0], right, (((0,), (0,)), ((), ())), preferred_element_type=F32)
    scaled = (inner / (eig_out[...] * eig_in[0] + DAMPING)).astype(BF16)
    mine = outer[0, pl.ds(pl.multiple_of(me * rows, rows), rows), :]
    upper = jnp.dot(mine, scaled, preferred_element_type=F32).astype(BF16)
    out[...] = lax.dot_general(
        upper, basis[0], (((1,), (1,)), ((), ())), preferred_element_type=F32
    ).astype(BF16)


def tail(place, parts, basis_in, basis_out, eig_in, eig_out):
    blocks, size, _ = basis_in.shape
    rows, width = parts[0].shape
    strip = pl.BlockSpec((rows, size), lambda b, place: (0, b))
    return pl.pallas_call(
        tail_kernel,
        grid_spec=pltpu.PrefetchScalarGridSpec(
            num_scalar_prefetch=1,
            grid=(blocks,),
            in_specs=[strip] * len(parts)
            + [
                pl.BlockSpec((1, size, size), lambda b, place: (b, 0, 0)),
                pl.BlockSpec((1, size, size), lambda b, place: (place[0], 0, 0)),
                pl.BlockSpec((1, 1, size), lambda b, place: (b, 0, 0)),
                pl.BlockSpec((size, 1), lambda b, place: (0, 0)),
            ],
            out_specs=strip,
            scratch_shapes=[pltpu.VMEM((size, size), BF16)],
        ),
        out_shape=jax.ShapeDtypeStruct((rows, width), BF16),
        compiler_params=pltpu.CompilerParams(vmem_limit_bytes=VMEM),
        cost_estimate=pl.CostEstimate(
            flops=blocks * 6 * size**3, bytes_accessed=4 * blocks * size**2, transcendentals=0
        ),
    )(place, *parts, basis_in, basis_out, eig_in, eig_out)


def product_kernel(*refs):
    left, right, outs, turned = refs[:2], refs[2:4], refs[4:-1], refs[-1]
    step = pl.program_id(0)
    tokens = left[0].shape[0]

    @pl.when(step == 0)
    def _():
        for i in range(2):
            turned[:, i * tokens : (i + 1) * tokens] = left[i][...].T

    total = jnp.dot(turned[:, :tokens], right[0][...], preferred_element_type=F32)
    total = total + jnp.dot(turned[:, tokens:], right[1][...], preferred_element_type=F32)
    each = pl.num_programs(0) // len(outs)
    for n, out in enumerate(outs):

        @pl.when(step // each == n)
        def _(out=out):
            out[...] = total.astype(BF16)


def products(pieces, rows, chunks):
    tokens, width = rows[0].shape
    n_rows = pieces[0].shape[1]
    tile = 512
    each = width // chunks // tile
    whole = pl.BlockSpec((tokens, n_rows), lambda i: (0, 0))
    strip = pl.BlockSpec((tokens, tile), lambda i: (0, i))
    return pl.pallas_call(
        product_kernel,
        grid=(width // tile,),
        in_specs=[whole, whole, strip, strip],
        out_specs=[
            pl.BlockSpec((n_rows, tile), lambda i, n=n: (0, jnp.clip(i - n * each, 0, each - 1)))
            for n in range(chunks)
        ],
        out_shape=[jax.ShapeDtypeStruct((n_rows, width // chunks), BF16)] * chunks,
        scratch_shapes=[pltpu.VMEM((n_rows, 2 * tokens), BF16)],
        compiler_params=pltpu.CompilerParams(vmem_limit_bytes=VMEM),
        cost_estimate=pl.CostEstimate(
            flops=4 * tokens * n_rows * width, bytes_accessed=4 * tokens * width, transcendentals=0
        ),
    )(*pieces, *rows)


def per_device(acts, cotan, block_ids, basis_in, basis_out, act_factor, grad_factor):
    n_dp = lax.axis_size("dp")
    n_worker = lax.axis_size("worker")
    d = lax.axis_index("dp")
    w = lax.axis_index("worker")
    core, x = d % 2, (d // 2) % 2
    n_z = n_dp // 4
    pool_rows, width = acts.shape
    local_blocks, block_size, _ = basis_in.shape
    model_width = basis_out.shape[0] * block_size
    samples = block_ids.shape[0] * BLK * n_dp
    tokens = pool_rows * n_dp
    rows_dev = model_width // n_dp
    z_per_worker = n_z // n_worker
    cols = width // COL_CHUNKS if width >= 1024 else width
    both = ("dp", "worker")

    def swap_core(v):
        return lax.ppermute(v, "dp", [(i, i ^ 1) for i in range(n_dp)])

    def swap_x(v):
        return lax.ppermute(v, "dp", [(i, i ^ 2) for i in range(n_dp)])

    def from_worker(v, step, flip):
        return lax.ppermute(
            v,
            both,
            [
                ((i ^ flip) * n_worker + (j + step) % n_worker, i * n_worker + j)
                for i in range(n_dp)
                for j in range(n_worker)
            ],
        )

    def place(owner, j):
        return owner * z_per_worker + (j if owner < n_worker // 2 else z_per_worker - 1 - j)

    z = d // 4
    starts = list(range(0, width, cols))
    shards = [(step, j) for j in range(z_per_worker) for step in range(n_worker)]

    def hops_of(step, j):
        ends = [place((i + step) % n_worker, j) for i in range(n_worker)]
        hops = []
        for hop in range(1, n_z):
            moves = []
            for i in range(n_worker):
                if hop <= ends[i]:
                    moves.append((i, hop - 1, hop))
                if hop <= n_z - 1 - ends[i]:
                    moves.append((i, n_z - hop, n_z - hop - 1))
            if moves:
                hops.append(moves)
        return hops

    def hop(v, moves):
        return lax.ppermute(
            v,
            both,
            [((a * 4 + r) * n_worker + i, (b * 4 + r) * n_worker + i) for i, a, b in moves for r in range(4)],
        )

    def piece(rows, j, at, flip):
        part = jnp.where(w < n_worker // 2, j, z_per_worker - 1 - j)
        x_to = x if at else 1 - x
        core_to = 1 - core if flip else core
        return lax.dynamic_slice_in_dim(rows, ((part * 2 + x_to) * 2 + core_to) * rows_dev, rows_dev, 1)

    def pick(v):
        return jnp.take(v.reshape(pool_rows // BLK, BLK, width), block_ids, axis=0).reshape(-1, width)

    y_items = [(step, j, at, flip) for step, j in shards if step for at in range(2) for flip in range(2)]
    y_stage = {item: max(0, at - 1) for at, item in enumerate(y_items)}
    x_items = [(step, j, n) for step, j in shards for n in range(len(starts))]
    x_stage, z_stage, mine_stage, other_stage, busy = {}, {}, {}, {}, set()
    clock = 0
    for step, j, n in x_items:
        ready = y_stage[step, j, 0, 1] + DEPTH if step else 0
        clock = max(clock, ready) + 1
        x_stage[step, j, n] = clock
        if n == 0:
            other_stage[step, j] = clock - 1
            mine_stage[step, j] = max(clock + 1, y_stage[step, j, 1, 1] + DEPTH if step else 0)
    for step, j, n in x_items:
        clock = max(x_stage[step, j, n] + DEPTH, mine_stage[step, j] + 1)
        for at, moves in enumerate(hops_of(step, j)):
            while any((clock, move) in busy for move in moves):
                clock += 1
            busy.update((clock, move) for move in moves)
            z_stage[step, j, n, at] = clock
            clock += DEPTH
    last = max(z_stage.values()) + DEPTH - 1

    groups = [[i * 4 + r for i in range(n_z)] for r in range(4)]
    is_act = core == 0
    env = {"acts": acts, "cotan": cotan}
    pending = {}

    def want(stage):
        keys = {(item[1], item[2], item[3]) for item, when in y_stage.items() if when == stage}
        for j in range(z_per_worker):
            if stage == min(j, 1):
                keys |= {(j, at, flip) for at in range(2) for flip in range(2)}
        return sorted(keys)

    for j, at, flip in want(0):
        env["p", j, at, flip] = piece(cotan, j, at, flip)
    for n in range(len(starts)):
        env["sum", n] = jnp.zeros((rows_dev, cols), BF16)
    env["act_pick"], env["cot_pick"] = pick(acts), pick(cotan)
    reduced = gathered = None
    for stage in range(last + 1):
        keys = sorted(env, key=str)
        env = dict(zip(keys, lax.optimization_barrier(tuple(env[k] for k in keys))))
        soon, late = {}, {}
        if stage == 0:
            soon["acts_sib"] = swap_core(env["acts"])
            soon["theirs"] = swap_core(jnp.where(is_act, env["cot_pick"], env["act_pick"]))
            soon["ours"] = jnp.where(is_act, env.pop("act_pick"), env.pop("cot_pick"))
        for item, when in y_stage.items():
            if when == stage:
                step, j, at, flip = item
                late["c", step, j, at, flip] = from_worker(env["p", j, at, flip], step, flip)
        for step, j, n in x_items:
            if x_stage[step, j, n] == stage:
                late["got", step, j, n] = swap_x(env.pop(("out", step, j, n)))
        for (step, j, n, at), when in z_stage.items():
            if when == stage:
                late["hop", step, j, n] = hop(env["acc", step, j, n], hops_of(step, j)[at])
        for j in range(z_per_worker):
            if stage == min(j, 1):
                for at in range(2):
                    soon["c", 0, j, at, 0] = env["p", j, at, 0]
                    soon["c", 0, j, at, 1] = swap_core(env["p", j, at, 1])
        for key in want(stage + 1):
            if ("p", *key) not in env:
                soon[("p", *key)] = piece(env["cotan"], *key)

        ready = {**env, **soon} if stage == 0 else env
        rows = (ready["acts"], ready["acts_sib"])
        for step, j in shards:
            for at, when, name in ((0, other_stage, "out"), (1, mine_stage, "mine")):
                if when[step, j] == stage:
                    pair = [ready["c", step, j, at, flip] for flip in range(2)]
                    for n, out in enumerate(products(pair, rows, len(starts))):
                        soon[name, step, j, n] = out

        if stage == 1:
            sample = jnp.concatenate([env.pop("ours"), env.pop("theirs")], axis=0)
            sample = sample.reshape(-1, local_blocks, block_size)
            scale = jnp.where(is_act, 1.0 / samples, tokens / samples)
            term = jnp.einsum("rbi,rbj->bij", sample, sample, preferred_element_type=F32) * scale
            packed = pack_upper(term.astype(BF16)).reshape(2, -1, block_size)
            soon["half"] = lax.dynamic_index_in_dim(packed, x, 0, keepdims=False)
            soon["away"] = lax.dynamic_index_in_dim(packed, 1 - x, 0, keepdims=False)
        if stage == 2:
            late["back"] = swap_x(env.pop("away"))
        if stage == 4:
            half = (env.pop("half").astype(F32) + env.pop("back").astype(F32)).astype(BF16)
            reduced = lax.psum_scatter(half, "dp", axis_index_groups=groups, tiled=True)
        if stage == 6:
            soon["reduced"] = reduced
        if stage == 7:
            gathered = lax.all_gather(env.pop("reduced"), "dp", axis_index_groups=groups, tiled=True)
        if stage == last - 4:
            soon["half"] = gathered
        if stage == last - 3:
            late["back"] = swap_x(env["half"])
        if stage == last - 1:
            half, back = env.pop("half"), env.pop("back")
            packed = jnp.where(x == 0, jnp.stack([half, back]), jnp.stack([back, half]))
            packed = packed.reshape(local_blocks, -1, block_size)
            packed_sib = swap_core(packed)
            soon["packed_act"] = jnp.where(is_act, packed, packed_sib)
            soon["packed_cot"] = jnp.where(is_act, packed_sib, packed)
        if stage == last:
            act_new, grad_new, eig_in, eig_local = update_factors(
                (env.pop("packed_act"), env.pop("packed_cot")),
                (act_factor, grad_factor),
                basis_in,
                basis_out,
                jnp.reshape(w * local_blocks, (1,)),
            )

        env.update(soon)
        env.update(pending)
        pending = late
        for step, j, n in x_items:
            mine, got, acc = ("mine", step, j, n), ("got", step, j, n), ("acc", step, j, n)
            if mine in env and got in env:
                env[acc] = (env.pop(mine).astype(F32) + env.pop(got).astype(F32)).astype(BF16)
            if ("hop", step, j, n) in env:
                total = (env[acc].astype(F32) + env.pop(("hop", step, j, n)).astype(F32)).astype(BF16)
                env[acc] = total
                if stage == z_stage[step, j, n, len(hops_of(step, j)) - 1] + DEPTH - 1:
                    ends = jnp.array([place((i + step) % n_worker, j) for i in range(n_worker)], jnp.int32)
                    env["sum", n] = jnp.where(ends[w] == z, env.pop(acc), env["sum", n])
    summed = jnp.concatenate([env["sum", n] for n in range(len(starts))], axis=1)

    my_start = d * rows_dev
    block = my_start // block_size
    eig_block = jnp.zeros((block_size,), F32)
    for step in range(n_worker):
        held = eig_local if step == 0 else from_worker(eig_local, step, 0)
        row = lax.dynamic_index_in_dim(held, block % local_blocks, 0, keepdims=False)[0]
        owner = (w + step) % n_worker
        eig_block = jnp.where(owner == block // local_blocks, row, eig_block)

    sharers = block_size // rows_dev
    parts = [summed]
    for step in range(1, sharers):
        pairs = [(i, i // sharers * sharers + (i + step) % sharers) for i in range(n_dp)]
        parts.append(lax.ppermute(summed, "dp", pairs))
    spot = jnp.stack([block, d % sharers]).astype(jnp.int32)
    precond = tail(spot, parts, basis_in, basis_out, eig_in, eig_block[:, None])
    return precond, act_new, grad_new


def solution(mesh):
    return jax.shard_map(
        per_device,
        mesh=mesh,
        in_specs=(
            P("dp", "worker"),
            P("dp", "worker"),
            P("dp"),
            P("worker", None, None),
            P(),
            P("worker", None, None),
            P("worker", None, None),
        ),
        out_specs=(P("dp", "worker"), P("worker", None, None), P("worker", None, None)),
        check_vma=False,
    )
```

time: 544 us -> 277 us (0.51)
  waiting for transfers between devices: 457 us -> 65.9 us
  Pallas kernels: 0 us -> 75.5 us
  starting transfers between devices: 0.08 us -> 53 us
  matrix products: 45.3 us -> 1.28 us
  blocking collectives: 4.36 us -> 21.5 us
  other arithmetic: 9.79 us -> 24.1 us
  local copies, waits for them, and re-layouts: 10.6 us -> 17.1 us
    psum x1 -> x0, waiting for transfers between devices: 365 us -> none  [per_device(): lax.psum(act_term.astype(jnp.bfloat16), 'dp').astype(jnp.float32)]
    all_gather x1 -> x0, waiting for transfers between devices: 92 us -> none  [per_device(): lax.all_gather(cotan, 'worker', axis=1, tiled=True)]
    pallas_call x0 -> x10, Pallas kernels: none -> 75.5 us  [the longest x8 56.6 us: products(): pl.pallas_call(product_kernel, grid=(width // tile,), in_specs=[whole, wh...]
    ppermute x0 -> x47, waiting for transfers between devices: none -> 65.8 us  [the longest x20 35.5 us: hop(): lax.ppermute(v, both, [((a * 4 + r) * n_worker + i, (b * 4 + r) * n_worke...]
    ppermute x0 -> x47, starting transfers between devices: none -> 53 us  [the longest x20 36.5 us: hop(): lax.ppermute(v, both, [((a * 4 + r) * n_worker + i, (b * 4 + r) * n_worke...]
    dot_general x8 -> x1, matrix products: 45.3 us -> 1.28 us  [per_device(): jnp.einsum('rbi,rbj->bij', sample, sample, preferred_element_type=F32)]
    all_gather x1, blocking collectives: 4.36 us -> 21.5 us  [per_device(): lax.all_gather(env.pop('reduced'), 'dp', axis_index_groups=groups, tiled=...]
    convert_element_type x1 -> x21, other arithmetic: 1.83 us -> 12.5 us  [the longest x8 7.12 us: per_device(): (env.pop(mine).astype(F32) + env.pop(got).astype(F32)).astype(BF16)]
  transfers between devices with their start and end apart: 2 -> 48, of which waited for: 2 -> 18; matrix products, arithmetic and copies ran while one was open for 3% -> 11% of each run, Pallas kernels for 0% -> 25%
where the time goes in v1:
time: 277 us; the launch traced here: 275 us
  Pallas kernels  75.5 us (27%)
  waiting for transfers between devices  65.9 us (24%)
  starting transfers between devices  53 us (19%)
  other arithmetic  24.1 us (9%)
  blocking collectives  21.5 us (8%)
  local copies, waits for them, and re-layouts  17.1 us (6%)
  between operations  17.1 us (6%)
    pallas_call x8, Pallas kernels, products(): pl.pallas_call(product_kernel, grid=(width // tile,), in_specs=[whole, wh...  56.6 us
    ppermute x20, starting transfers between devices, hop(): lax.ppermute(v, both, [((a * 4 + r) * n_worker + i, (b * 4 + r) * n_worke...  36.5 us
    ppermute x20, waiting for transfers between devices, hop(): lax.ppermute(v, both, [((a * 4 + r) * n_worker + i, (b * 4 + r) * n_worke...  35.5 us
    all_gather x1, blocking collectives, per_device(): lax.all_gather(env.pop('reduced'), 'dp', axis_index_groups=groups, tiled=...  21.5 us
    ppermute x9, waiting for transfers between devices, from_worker(): lax.ppermute(v, both, [((i ^ flip) * n_worker + (j + step) % n_worker, i...  19.5 us
    ppermute x10, starting transfers between devices, swap_x(): return lax.ppermute(v, 'dp', [(i, i ^ 2) for i in range(n_dp)])  11.4 us
    pallas_call x1, Pallas kernels, update_factors(): pl.pallas_call(factor_kernel, grid_spec=pltpu.PrefetchScalarGridSpec(num_...  10.8 us
    ppermute x10, waiting for transfers between devices, swap_x(): return lax.ppermute(v, 'dp', [(i, i ^ 2) for i in range(n_dp)])  10.7 us
  transfers between devices with their start and end apart: 48, of which 18 were waited for; matrix products, arithmetic and copies ran while one was open for 11% of the time, Pallas kernels for 25%

profile of v1, /device:TPU:12, one launch (start us, length us, event | category | flops | bytes accessed | tf_op | source)
XLA Modules:
  0.0 275.3 jit_solution(9389456882010896569)
XLA Ops:
  8.6 2.8 %gather_fusion = bf16[2,128,2048]{2,1,0:T(8,128)(2,1)S(1)} fusion(bf16[8,128,2048]{2,1,0:T(8,128)(2,1)} %bitcast.2, s32[1024]{0:T(1024)S(1)} %pad_clamp_fusion), kind=kCustom, calls=%fused_computation.clone | custom fusion | bytes 2097160 | tf_op jit(solution)/shard_map/jit(_take)/gather | solution.py:249
  11.4 2.8 %gather_fusion.1 = bf16[2,128,2048]{2,1,0:T(8,128)(2,1)S(1)} fusion(bf16[8,128,2048]{2,1,0:T(8,128)(2,1)} %bitcast.23, s32[1024]{0:T(1024)S(1)} %pad_clamp_fusion), kind=kCustom, calls=%fused_computation.1.clone | custom fusion | bytes 2097160 | tf_op jit(solution)/shard_map/jit(_take)/gather | solution.py:249
  24.5 2.8 %constant_dynamic-slice_fusion.2 = (bf16[1024,256]{1,0:T(8,128)(2,1)}, bf16[1024,256]{1,0:T(8,128)(2,1)}, bf16[1024,256]{1,0:T(8,128)(2,1)}, bf16[1024,256]{1,0:T(8,128)(2,1)S(1)}) fusion(bf16[1024,2048]{1,0:T(8,128)(2,1)} %param.18, s32[]{:T(128)S(6)} %select_n.242, s32[]{:T(128)S(6)} %select_n.241, s32[]{:T(128)S(6)} %select_n.240, s32[]{:T(128)S(6)} %select_n.239), kind=kLoop, calls=%fused_computation.57 | loop fusion | bytes 4194320 | tf_op jit(solution)/shard_map/dynamic_slice | solution.py:246
  28.8 7.1 %shard_map.166 = (bf16[256,1024]{1,0:T(8,128)(2,1)}, bf16[256,1024]{1,0:T(8,128)(2,1)}) custom-call(bf16[1024,256]{1,0:T(8,128)(2,1)} %get-tuple-element.198.refs_0_, bf16[1024,256]{1,0:T(8,128)(2,1)} %collective-permute-done.refs_1_, bf16[1024,2048]{1,0:T(8,128)(2,1)} %refs_2_.9, bf16[1024,2048]{1,0:T(8,128)(2,1)} %collective-permute-done.2.refs_3_), custom_call_target="tpu_custom_call" | custom-call | flops 2147483648 | bytes 8388608 | tf_op jit(solution)/shard_map/pallas_call | solution.py:163
  40.4 6.7 %collective-permute-done.6.refs_0_ = bf16[1024,256]{1,0:T(8,128)(2,1)S(1)} collective-permute-done((bf16[1024,256]{1,0:T(8,128)(2,1)S(1)}, bf16[1024,256]{1,0:T(8,128)(2,1)S(1)}, u32[]{:S(2)}, u32[]{:S(2)}) %collective-permute-start.6) | collective-permute-done | bytes 524320 | tf_op jit(solution)/shard_map/ppermute | solution.py:204
  49.8 7.1 %shard_map.168 = (bf16[256,1024]{1,0:T(8,128)(2,1)}, bf16[256,1024]{1,0:T(8,128)(2,1)}) custom-call(bf16[1024,256]{1,0:T(8,128)(2,1)} %copy-done.12, bf16[1024,256]{1,0:T(8,128)(2,1)} %collective-permute-done.7.refs_1_, bf16[1024,2048]{1,0:T(8,128)(2,1)} %refs_2_.9, bf16[1024,2048]{1,0:T(8,128)(2,1)} %collective-permute-done.2.refs_3_), custom_call_target="tpu_custom_call" | custom-call | flops 2147483648 | bytes 8388608 | tf_op jit(solution)/shard_map/pallas_call | solution.py:163
  57.0 7.0 %shard_map.167 = (bf16[256,1024]{1,0:T(8,128)(2,1)}, bf16[256,1024]{1,0:T(8,128)(2,1)}) custom-call(bf16[1024,256]{1,0:T(8,128)(2,1)} %get-tuple-element.225.refs_0_, bf16[1024,256]{1,0:T(8,128)(2,1)} %copy-done.6, bf16[1024,2048]{1,0:T(8,128)(2,1)} %refs_2_.9, bf16[1024,2048]{1,0:T(8,128)(2,1)} %collective-permute-done.2.refs_3_), custom_call_target="tpu_custom_call" | custom-call | flops 2147483648 | bytes 8388608 | tf_op jit(solution)/shard_map/pallas_call | solution.py:163
  70.7 8.3 %collective-permute-done.12 = bf16[640,512]{1,0:T(8,128)(2,1)S(1)} collective-permute-done((bf16[640,512]{1,0:T(8,128)(2,1)S(1)}, bf16[640,512]{1,0:T(8,128)(2,1)S(1)}, u32[]{:S(2)}, u32[]{:S(2)}) %collective-permute-start.12) | collective-permute-done | bytes 655392 | tf_op jit(solution)/shard_map/ppermute | solution.py:201
  80.0 1.6 collective-permute-start.17
  82.9 7.2 %shard_map.170 = (bf16[256,1024]{1,0:T(8,128)(2,1)}, bf16[256,1024]{1,0:T(8,128)(2,1)}) custom-call(bf16[1024,256]{1,0:T(8,128)(2,1)} %copy-done.4, bf16[1024,256]{1,0:T(8,128)(2,1)} %copy-done.8, bf16[1024,2048]{1,0:T(8,128)(2,1)} %refs_2_.9, bf16[1024,2048]{1,0:T(8,128)(2,1)} %collective-permute-done.2.refs_3_), custom_call_target="tpu_custom_call" | custom-call | flops 2147483648 | bytes 8388608 | tf_op jit(solution)/shard_map/pallas_call | solution.py:163
  90.0 7.1 %shard_map.169 = (bf16[256,1024]{1,0:T(8,128)(2,1)}, bf16[256,1024]{1,0:T(8,128)(2,1)}) custom-call(bf16[1024,256]{1,0:T(8,128)(2,1)} %copy-done.11, bf16[1024,256]{1,0:T(8,128)(2,1)} %copy-done.13, bf16[1024,2048]{1,0:T(8,128)(2,1)} %refs_2_.9, bf16[1024,2048]{1,0:T(8,128)(2,1)} %collective-permute-done.2.refs_3_), custom_call_target="tpu_custom_call" | custom-call | flops 2147483648 | bytes 8388608 | tf_op jit(solution)/shard_map/pallas_call | solution.py:163
  100.6 3.5 %collective-permute-start.19 = (bf16[256,1024]{1,0:T(8,128)(2,1)S(1)}, bf16[256,1024]{1,0:T(8,128)(2,1)S(1)}, u32[]{:S(2)}, u32[]{:S(2)}) collective-permute-start(bf16[256,1024]{1,0:T(8,128)(2,1)S(1)} %add_convert_fusion.26), channel_id=1, source_target_pairs={{16,8},{18,10},{20,12},{22,14},{9,17},{11,19},{13,21},{15,23}} | collective-permute-start | bytes 1572872 | tf_op jit(solution)/shard_map/ppermute | solution.py:236
  105.5 5.3 %collective-permute-done.18.refs_1_ = bf16[1024,256]{1,0:T(8,128)(2,1)S(1)} collective-permute-done((bf16[1024,256]{1,0:T(8,128)(2,1)}, bf16[1024,256]{1,0:T(8,128)(2,1)S(1)}, u32[]{:S(2)}, u32[]{:S(2)}) %collective-permute-start.18) | collective-permute-done | bytes 524320 | tf_op jit(solution)/shard_map/ppermute | solution.py:204
  112.2 7.1 %shard_map.172 = (bf16[256,1024]{1,0:T(8,128)(2,1)}, bf16[256,1024]{1,0:T(8,128)(2,1)}) custom-call(bf16[1024,256]{1,0:T(8,128)(2,1)} %copy-done.10, bf16[1024,256]{1,0:T(8,128)(2,1)} %copy-done.15, bf16[1024,2048]{1,0:T(8,128)(2,1)} %refs_2_.9, bf16[1024,2048]{1,0:T(8,128)(2,1)} %collective-permute-done.2.refs_3_), custom_call_target="tpu_custom_call" | custom-call | flops 2147483648 | bytes 8388608 | tf_op jit(solution)/shard_map/pallas_call | solution.py:163
  119.3 7.1 %shard_map.171 = (bf16[256,1024]{1,0:T(8,128)(2,1)}, bf16[256,1024]{1,0:T(8,128)(2,1)}) custom-call(bf16[1024,256]{1,0:T(8,128)(2,1)} %get-tuple-element.304.refs_0_, bf16[1024,256]{1,0:T(8,128)(2,1)} %copy-done.7, bf16[1024,2048]{1,0:T(8,128)(2,1)} %refs_2_.9, bf16[1024,2048]{1,0:T(8,128)(2,1)} %collective-permute-done.2.refs_3_), custom_call_target="tpu_custom_call" | custom-call | flops 2147483648 | bytes 8388608 | tf_op jit(solution)/shard_map/pallas_call | solution.py:163
  127.2 4.4 %collective-permute-start.23 = (bf16[256,1024]{1,0:T(8,128)(2,1)S(1)}, bf16[256,1024]{1,0:T(8,128)(2,1)}, u32[]{:S(2)}, u32[]{:S(2)}) collective-permute-start(bf16[256,1024]{1,0:T(8,128)(2,1)S(1)} %add_convert_fusion.24), channel_id=1, source_target_pairs={{16,8},{18,10},{20,12},{22,14},{9,17},{11,19},{13,21},{15,23}} | collective-permute-start | bytes 1572872 | tf_op jit(solution)/shard_map/ppermute | solution.py:236
  136.4 1.8 collective-permute-done.24
  142.7 4.0 %collective-permute-done.26.refs_1_ = bf16[1024,256]{1,0:T(8,128)(2,1)} collective-permute-done((bf16[1024,256]{1,0:T(8,128)(2,1)}, bf16[1024,256]{1,0:T(8,128)(2,1)}, u32[]{:S(2)}, u32[]{:S(2)}) %collective-permute-start.26) | collective-permute-done | bytes 524320 | tf_op jit(solution)/shard_map/ppermute | solution.py:204
  146.7 1.6 collective-permute-start.29
  148.9 7.0 %shard_map.173 = (bf16[256,1024]{1,0:T(8,128)(2,1)}, bf16[256,1024]{1,0:T(8,128)(2,1)}) custom-call(bf16[1024,256]{1,0:T(8,128)(2,1)} %copy-done.9, bf16[1024,256]{1,0:T(8,128)(2,1)} %collective-permute-done.26.refs_1_, bf16[1024,2048]{1,0:T(8,128)(2,1)} %refs_2_.9, bf16[1024,2048]{1,0:T(8,128)(2,1)} %collective-permute-done.2.refs_3_), custom_call_target="tpu_custom_call" | custom-call | flops 2147483648 | bytes 8388608 | tf_op jit(solution)/shard_map/pallas_call | solution.py:163
  156.0 21.5 %all_gather.3 = bf16[640,512]{1,0:T(8,128)(2,1)S(1)} all-gather(bf16[160,512]{1,0:T(8,128)(2,1)S(1)} %copy-done.18), channel_id=1, replica_groups={{0,8,16,24},{2,10,18,26},{4,12,20,28},{6,14,22,30},{1,9,17,25},{3,11,19..., dimensions={0}, use_global_device_ids=true | all-gather | bytes 819200 | tf_op jit(solution)/shard_map/all_gather | solution.py:343
  181.9 4.6 %collective-permute-start.36 = (bf16[256,1024]{1,0:T(8,128)(2,1)S(1)}, bf16[256,1024]{1,0:T(8,128)(2,1)S(1)}, u32[]{:S(2)}, u32[]{:S(2)}) collective-permute-start(bf16[256,1024]{1,0:T(8,128)(2,1)S(1)} %add_convert_fusion.16), channel_id=1, source_target_pairs={{16,8},{18,10},{20,12},{22,14},{9,17},{11,19},{13,21},{15,23}} | collective-permute-start | bytes 1572872 | tf_op jit(solution)/shard_map/ppermute | solution.py:236
  189.9 6.9 %collective-permute-done.31 = bf16[256,1024]{1,0:T(8,128)(2,1)S(1)} collective-permute-done((bf16[256,1024]{1,0:T(8,128)(2,1)S(1)}, bf16[256,1024]{1,0:T(8,128)(2,1)S(1)}, u32[]{:S(2)}, u32[]{:S(2)}) %collective-permute-start.31) | collective-permute-done | bytes 524320 | tf_op jit(solution)/shard_map/ppermute | solution.py:236
  197.0 4.7 %collective-permute-start.39 = (bf16[256,1024]{1,0:T(8,128)(2,1)S(1)}, bf16[256,1024]{1,0:T(8,128)(2,1)S(1)}, u32[]{:S(2)}, u32[]{:S(2)}) collective-permute-start(bf16[256,1024]{1,0:T(8,128)(2,1)S(1)} %add_convert_fusion.12), channel_id=1, source_target_pairs={{16,8},{18,10},{20,12},{22,14},{9,17},{11,19},{13,21},{15,23}} | collective-permute-start | bytes 1572872 | tf_op jit(solution)/shard_map/ppermute | solution.py:236
  206.1 2.0 collective-permute-done.35
  208.3 5.9 %collective-permute-done.38 = bf16[256,1024]{1,0:T(8,128)(2,1)S(1)} collective-permute-done((bf16[256,1024]{1,0:T(8,128)(2,1)S(1)}, bf16[256,1024]{1,0:T(8,128)(2,1)S(1)}, u32[]{:S(2)}, u32[]{:S(2)}) %collective-permute-start.38) | collective-permute-done | bytes 524320 | tf_op jit(solution)/shard_map/ppermute | solution.py:236
  219.4 12.6 %collective-permute-done.42 = bf16[256,1024]{1,0:T(8,128)(2,1)} collective-permute-done((bf16[256,1024]{1,0:T(8,128)(2,1)S(1)}, bf16[256,1024]{1,0:T(8,128)(2,1)}, u32[]{:S(2)}, u32[]{:S(2)}) %collective-permute-start.42) | collective-permute-done | bytes 524320 | tf_op jit(solution)/shard_map/ppermute | solution.py:236
  233.4 3.0 %broadcast_select_fusion = (bf16[4,320,512]{2,1,0:T(8,128)(2,1)}, bf16[4,320,512]{2,1,0:T(8,128)(2,1)}) fusion(bf16[4,320,512]{2,1,0:T(8,128)(2,1)} %collective-permute-done.43, bf16[4,320,512]{2,1,0:T(8,128)(2,1)S(1)} %bitcast.26, pred[]{:T(512)S(6)} %eq.44), kind=kLoop, calls=%fused_computation.7 | loop fusion | flops 1310720 | bytes 5242881 | tf_op jit(solution)/shard_map/jit(_where)/select_n | solution.py:354
  236.3 6.4 %collective-permute-done.44 = bf16[256,1024]{1,0:T(8,128)(2,1)S(1)} collective-permute-done((bf16[256,1024]{1,0:T(8,128)(2,1)S(1)}, bf16[256,1024]{1,0:T(8,128)(2,1)S(1)}, u32[]{:S(2)}, u32[]{:S(2)}) %collective-permute-start.44) | collective-permute-done | bytes 524320 | tf_op jit(solution)/shard_map/ppermute | solution.py:236
  243.2 10.8 %shard_map.174 = (f32[4,512,512]{2,1,0:T(8,128)}, f32[4,512,512]{2,1,0:T(8,128)}, f32[4,1,512]{2,1,0:T(1,128)}, f32[4,1,512]{2,1,0:T(1,128)}) custom-call(s32[1]{0:T(128)} %bitcast.16.start_ref, bf16[4,320,512]{2,1,0:T(8,128)(2,1)} %get-tuple-element.386.refs_0_, bf16[4,320,512]{2,1,0:T(8,128)(2,1)} %get-tuple-element.387.refs_1_, f32[4,512,512]{2,1,0:T(8,128)} %refs_2_.10, ...), custom_call_target="tpu_custom_call" | custom-call | flops 6442450944 | bytes 19922944 | tf_op jit(solution)/shard_map/pallas_call | solution.py:73
  254.8 3.2 %collective-permute-done.46 = f32[4,1,512]{2,1,0:T(1,128)S(1)} collective-permute-done((f32[4,1,512]{2,1,0:T(1,128)}, f32[4,1,512]{2,1,0:T(1,128)S(1)}, u32[]{:S(2)}, u32[]{:S(2)}) %collective-permute-start.46) | collective-permute-done | bytes 8224 | tf_op jit(solution)/shard_map/ppermute | solution.py:204
  260.5 8.0 %shard_map.175 = bf16[256,2048]{1,0:T(8,128)(2,1)} custom-call(s32[2]{0:T(128)} %pad_add_fusion.place_ref, bf16[256,2048]{1,0:T(8,128)(2,1)} %copy-done.5, bf16[256,2048]{1,0:T(8,128)(2,1)} %copy-done.19, bf16[4,512,512]{2,1,0:T(8,128)(2,1)} %refs_2_.11, bf16[8,512,512]{2,1,0:T(8,128)(2,1)} %refs_3_.3, f32[4,1,512]{2,1,0:T(1,128)} %get-tuple-element.388.refs_4_, ...), custom_call_target="tpu_custom_call" | custom-call | flops 3221225472 | bytes 4194304 | tf_op jit(solution)/shard_map/pallas_call | solution.py:113
  (184 shorter events, 66.5 us)
Async XLA Ops:
  7.2 126.0 %reduce-scatter.2.cloned.1.call-start = ((), (), s32[]{:S(2)}) async-start(), calls=%async_computation.1 | async-start | bytes 819200 | tf_op jit(solution)/shard_map/reduce_scatter | solution.py:339
  21.5 26.2 %collective-permute-start.7 = (bf16[1024,256]{1,0:T(8,128)(2,1)}, bf16[1024,256]{1,0:T(8,128)(2,1)}, u32[]{:S(2)}, u32[]{:S(2)}) collective-permute-start(bf16[1024,256]{1,0:T(8,128)(2,1)} %get-tuple-element.199), channel_id=1, source_target_pairs={{3,0},{2,1},{1,2},{0,3},{7,4},{6,5},{5,6},{4,7},{11,8},{10,9},{9,1... | collective-permute-start | bytes 1572872 | tf_op jit(solution)/shard_map/ppermute | solution.py:204
  27.3 19.9 %collective-permute-start.6 = (bf16[1024,256]{1,0:T(8,128)(2,1)S(1)}, bf16[1024,256]{1,0:T(8,128)(2,1)S(1)}, u32[]{:S(2)}, u32[]{:S(2)}) collective-permute-start(bf16[1024,256]{1,0:T(8,128)(2,1)S(1)} %copy-done.3), channel_id=1, source_target_pairs={{1,0},{0,1},{3,2},{2,3},{5,4},{4,5},{7,6},{6,7},{9,8},{8,9},{11,10... | collective-permute-start | bytes 1572872 | tf_op jit(solution)/shard_map/ppermute | solution.py:204
  38.7 25.3 %collective-permute-start.8 = (bf16[256,1024]{1,0:T(8,128)(2,1)}, bf16[256,1024]{1,0:T(8,128)(2,1)S(1)}, u32[]{:S(2)}, u32[]{:S(2)}) collective-permute-start(bf16[256,1024]{1,0:T(8,128)(2,1)} %get-tuple-element.230), channel_id=1, source_target_pairs={{0,4},{2,6},{4,0},{6,2},{8,12},{10,14},{12,8},{14,10},{16,20},{18,... | collective-permute-start | bytes 1572872 | tf_op jit(solution)/shard_map/ppermute | solution.py:201
  47.2 18.1 %collective-permute-start.9 = (bf16[1024,256]{1,0:T(8,128)(2,1)S(1)}, bf16[1024,256]{1,0:T(8,128)(2,1)S(1)}, u32[]{:S(2)}, u32[]{:S(2)}) collective-permute-start(bf16[1024,256]{1,0:T(8,128)(2,1)S(1)} %copy-done.2), channel_id=1, source_target_pairs={{1,0},{0,1},{3,2},{2,3},{5,4},{4,5},{7,6},{6,7},{9,8},{8,9},{11,10... | collective-permute-start | bytes 1572872 | tf_op jit(solution)/shard_map/ppermute | solution.py:204
  47.7 20.4 %collective-permute-start.10 = (bf16[256,1024]{1,0:T(8,128)(2,1)S(1)}, bf16[256,1024]{1,0:T(8,128)(2,1)S(1)}, u32[]{:S(2)}, u32[]{:S(2)}) collective-permute-start(bf16[256,1024]{1,0:T(8,128)(2,1)S(1)} %copy-done.21), channel_id=1, source_target_pairs={{0,4},{2,6},{4,0},{6,2},{8,12},{10,14},{12,8},{14,10},{16,20},{18,... | collective-permute-start | bytes 1572872 | tf_op jit(solution)/shard_map/ppermute | solution.py:201
  49.3 29.7 %collective-permute-start.12 = (bf16[640,512]{1,0:T(8,128)(2,1)S(1)}, bf16[640,512]{1,0:T(8,128)(2,1)S(1)}, u32[]{:S(2)}, u32[]{:S(2)}) collective-permute-start(bf16[640,512]{1,0:T(8,128)(2,1)S(1)} %get-tuple-element.265), channel_id=1, source_target_pairs={{0,4},{2,6},{4,0},{6,2},{8,12},{10,14},{12,8},{14,10},{16,20},{18,... | collective-permute-start | bytes 1966088 | tf_op jit(solution)/shard_map/ppermute | solution.py:201
  49.8 20.8 %collective-permute-start.11 = (bf16[1024,256]{1,0:T(8,128)(2,1)}, bf16[1024,256]{1,0:T(8,128)(2,1)S(1)}, u32[]{:S(2)}, u32[]{:S(2)}) collective-permute-start(bf16[1024,256]{1,0:T(8,128)(2,1)} %get-tuple-element.240), channel_id=1, source_target_pairs={{3,0},{2,1},{1,2},{0,3},{7,4},{6,5},{5,6},{4,7},{11,8},{10,9},{9,1... | collective-permute-start | bytes 1572872 | tf_op jit(solution)/shard_map/ppermute | solution.py:204
  65.3 31.8 %collective-permute-start.14 = (bf16[256,1024]{1,0:T(8,128)(2,1)}, bf16[256,1024]{1,0:T(8,128)(2,1)}, u32[]{:S(2)}, u32[]{:S(2)}) collective-permute-start(bf16[256,1024]{1,0:T(8,128)(2,1)} %get-tuple-element.274), channel_id=1, source_target_pairs={{0,4},{2,6},{4,0},{6,2},{8,12},{10,14},{12,8},{14,10},{16,20},{18,... | collective-permute-start | bytes 1572872 | tf_op jit(solution)/shard_map/ppermute | solution.py:201
  66.8 31.8 %collective-permute-start.13 = (bf16[256,1024]{1,0:T(8,128)(2,1)S(1)}, bf16[256,1024]{1,0:T(8,128)(2,1)S(1)}, u32[]{:S(2)}, u32[]{:S(2)}) collective-permute-start(bf16[256,1024]{1,0:T(8,128)(2,1)S(1)} %add_convert_fusion.28), channel_id=1, source_target_pairs={{24,16},{26,18},{28,20},{30,22},{1,9},{3,11},{5,13},{7,15}} | collective-permute-start | bytes 1572872 | tf_op jit(solution)/shard_map/ppermute | solution.py:236
  68.1 30.7 %collective-permute-start.15 = (bf16[1024,256]{1,0:T(8,128)(2,1)S(1)}, bf16[1024,256]{1,0:T(8,128)(2,1)S(1)}, u32[]{:S(2)}, u32[]{:S(2)}) collective-permute-start(bf16[1024,256]{1,0:T(8,128)(2,1)S(1)} %get-tuple-element.275.refs_0_), channel_id=1, source_target_pairs={{1,0},{0,1},{3,2},{2,3},{5,4},{4,5},{7,6},{6,7},{9,8},{8,9},{11,10... | collective-permute-start | bytes 1572872 | tf_op jit(solution)/shard_map/ppermute | solution.py:204
  80.0 20.6 %collective-permute-start.17 = (bf16[256,1024]{1,0:T(8,128)(2,1)}, bf16[256,1024]{1,0:T(8,128)(2,1)S(1)}, u32[]{:S(2)}, u32[]{:S(2)}) collective-permute-start(bf16[256,1024]{1,0:T(8,128)(2,1)} %get-tuple-element.291), channel_id=1, source_target_pairs={{0,4},{2,6},{4,0},{6,2},{8,12},{10,14},{12,8},{14,10},{16,20},{18,... | collective-permute-start | bytes 1572872 | tf_op jit(solution)/shard_map/ppermute | solution.py:201
  81.6 23.7 %collective-permute-start.16 = (bf16[256,1024]{1,0:T(8,128)(2,1)S(1)}, bf16[256,1024]{1,0:T(8,128)(2,1)S(1)}, u32[]{:S(2)}, u32[]{:S(2)}) collective-permute-start(bf16[256,1024]{1,0:T(8,128)(2,1)S(1)} %add_convert_fusion.27), channel_id=1, source_target_pairs={{24,16},{26,18},{28,20},{30,22},{1,9},{3,11},{5,13},{7,15}} | collective-permute-start | bytes 1572872 | tf_op jit(solution)/shard_map/ppermute | solution.py:236
  98.9 27.5 %collective-permute-start.21 = (bf16[256,1024]{1,0:T(8,128)(2,1)S(1)}, bf16[256,1024]{1,0:T(8,128)(2,1)S(1)}, u32[]{:S(2)}, u32[]{:S(2)}) collective-permute-start(bf16[256,1024]{1,0:T(8,128)(2,1)S(1)} %add_convert_fusion.25), channel_id=1, source_target_pairs={{0,8},{2,10},{4,12},{6,14},{25,17},{27,19},{29,21},{31,23}} | collective-permute-start | bytes 1572872 | tf_op jit(solution)/shard_map/ppermute | solution.py:236
  99.6 27.6 %collective-permute-start.20 = (bf16[256,1024]{1,0:T(8,128)(2,1)S(1)}, bf16[256,1024]{1,0:T(8,128)(2,1)S(1)}, u32[]{:S(2)}, u32[]{:S(2)}) collective-permute-start(bf16[256,1024]{1,0:T(8,128)(2,1)S(1)} %copy-done.22), channel_id=1, source_target_pairs={{0,4},{2,6},{4,0},{6,2},{8,12},{10,14},{12,8},{14,10},{16,20},{18,... | collective-permute-start | bytes 1572872 | tf_op jit(solution)/shard_map/ppermute | solution.py:201
  100.6 32.3 %collective-permute-start.19 = (bf16[256,1024]{1,0:T(8,128)(2,1)S(1)}, bf16[256,1024]{1,0:T(8,128)(2,1)S(1)}, u32[]{:S(2)}, u32[]{:S(2)}) collective-permute-start(bf16[256,1024]{1,0:T(8,128)(2,1)S(1)} %add_convert_fusion.26), channel_id=1, source_target_pairs={{16,8},{18,10},{20,12},{22,14},{9,17},{11,19},{13,21},{15,23}} | collective-permute-start | bytes 1572872 | tf_op jit(solution)/shard_map/ppermute | solution.py:236
  105.3 27.8 %collective-permute-start.22 = (bf16[1024,256]{1,0:T(8,128)(2,1)}, bf16[1024,256]{1,0:T(8,128)(2,1)S(1)}, u32[]{:S(2)}, u32[]{:S(2)}) collective-permute-start(bf16[1024,256]{1,0:T(8,128)(2,1)} %get-tuple-element.304.refs_0_), channel_id=1, source_target_pairs={{1,0},{0,1},{3,2},{2,3},{5,4},{4,5},{7,6},{6,7},{9,8},{8,9},{11,10... | collective-permute-start | bytes 1572872 | tf_op jit(solution)/shard_map/ppermute | solution.py:204
  110.8 23.1 %collective-permute-start.25 = (bf16[256,1024]{1,0:T(8,128)(2,1)S(1)}, bf16[256,1024]{1,0:T(8,128)(2,1)}, u32[]{:S(2)}, u32[]{:S(2)}) collective-permute-start(bf16[256,1024]{1,0:T(8,128)(2,1)S(1)} %add_convert_fusion.23), channel_id=1, source_target_pairs={{0,8},{2,10},{4,12},{6,14},{25,17},{27,19},{29,21},{31,23}} | collective-permute-start | bytes 1572872 | tf_op jit(solution)/shard_map/ppermute | solution.py:236
  133.2 44.3 %collective-permute-start.30 = (bf16[256,1024]{1,0:T(8,128)(2,1)S(1)}, bf16[256,1024]{1,0:T(8,128)(2,1)S(1)}, u32[]{:S(2)}, u32[]{:S(2)}) collective-permute-start(bf16[256,1024]{1,0:T(8,128)(2,1)S(1)} %add_convert_fusion.22), channel_id=1, source_target_pairs={{8,0},{10,2},{12,4},{14,6},{17,25},{19,27},{21,29},{23,31}} | collective-permute-start | bytes 1572872 | tf_op jit(solution)/shard_map/ppermute | solution.py:236
  133.9 46.2 %collective-permute-start.28 = (bf16[256,1024]{1,0:T(8,128)(2,1)S(1)}, bf16[256,1024]{1,0:T(8,128)(2,1)S(1)}, u32[]{:S(2)}, u32[]{:S(2)}) collective-permute-start(bf16[256,1024]{1,0:T(8,128)(2,1)S(1)} %add_convert_fusion.20), channel_id=1, source_target_pairs={{8,16},{10,18},{12,20},{14,22},{17,9},{19,11},{21,13},{23,15}} | collective-permute-start | bytes 1572872 | tf_op jit(solution)/shard_map/ppermute | solution.py:236
  138.2 43.5 %collective-permute-start.27 = (bf16[256,1024]{1,0:T(8,128)(2,1)S(1)}, bf16[256,1024]{1,0:T(8,128)(2,1)S(1)}, u32[]{:S(2)}, u32[]{:S(2)}) collective-permute-start(bf16[256,1024]{1,0:T(8,128)(2,1)S(1)} %add_convert_fusion.21), channel_id=1, source_target_pairs={{0,8},{2,10},{4,12},{6,14},{24,16},{26,18},{28,20},{30,22},{1,9},{... | collective-permute-start | bytes 1572872 | tf_op jit(solution)/shard_map/ppermute | solution.py:236
  146.7 31.9 %collective-permute-start.29 = (bf16[256,1024]{1,0:T(8,128)(2,1)}, bf16[256,1024]{1,0:T(8,128)(2,1)S(1)}, u32[]{:S(2)}, u32[]{:S(2)}) collective-permute-start(bf16[256,1024]{1,0:T(8,128)(2,1)} %get-tuple-element.345), channel_id=1, source_target_pairs={{0,4},{2,6},{4,0},{6,2},{8,12},{10,14},{12,8},{14,10},{16,20},{18,... | collective-permute-start | bytes 1572872 | tf_op jit(solution)/shard_map/ppermute | solution.py:201
  148.2 38.2 %collective-permute-start.34 = (bf16[256,1024]{1,0:T(8,128)(2,1)S(1)}, bf16[256,1024]{1,0:T(8,128)(2,1)S(1)}, u32[]{:S(2)}, u32[]{:S(2)}) collective-permute-start(bf16[256,1024]{1,0:T(8,128)(2,1)S(1)} %add_convert_fusion.19), channel_id=1, source_target_pairs={{8,0},{10,2},{12,4},{14,6},{17,25},{19,27},{21,29},{23,31}} | collective-permute-start | bytes 1572872 | tf_op jit(solution)/shard_map/ppermute | solution.py:236
  180.1 16.7 %collective-permute-start.31 = (bf16[256,1024]{1,0:T(8,128)(2,1)S(1)}, bf16[256,1024]{1,0:T(8,128)(2,1)S(1)}, u32[]{:S(2)}, u32[]{:S(2)}) collective-permute-start(bf16[256,1024]{1,0:T(8,128)(2,1)S(1)} %add_convert_fusion.18), channel_id=1, source_target_pairs={{0,8},{2,10},{4,12},{6,14},{24,16},{26,18},{28,20},{30,22},{1,9},{... | collective-permute-start | bytes 1572872 | tf_op jit(solution)/shard_map/ppermute | solution.py:236
  181.9 21.2 %collective-permute-start.36 = (bf16[256,1024]{1,0:T(8,128)(2,1)S(1)}, bf16[256,1024]{1,0:T(8,128)(2,1)S(1)}, u32[]{:S(2)}, u32[]{:S(2)}) collective-permute-start(bf16[256,1024]{1,0:T(8,128)(2,1)S(1)} %add_convert_fusion.16), channel_id=1, source_target_pairs={{16,8},{18,10},{20,12},{22,14},{9,17},{11,19},{13,21},{15,23}} | collective-permute-start | bytes 1572872 | tf_op jit(solution)/shard_map/ppermute | solution.py:236
  186.5 17.9 %collective-permute-start.37 = (bf16[256,1024]{1,0:T(8,128)(2,1)S(1)}, bf16[256,1024]{1,0:T(8,128)(2,1)S(1)}, u32[]{:S(2)}, u32[]{:S(2)}) collective-permute-start(bf16[256,1024]{1,0:T(8,128)(2,1)S(1)} %add_convert_fusion.15), channel_id=1, source_target_pairs={{16,24},{18,26},{20,28},{22,30},{9,1},{11,3},{13,5},{15,7}} | collective-permute-start | bytes 1572872 | tf_op jit(solution)/shard_map/ppermute | solution.py:236
  188.1 20.0 %collective-permute-start.35 = (bf16[256,1024]{1,0:T(8,128)(2,1)S(1)}, bf16[256,1024]{1,0:T(8,128)(2,1)S(1)}, u32[]{:S(2)}, u32[]{:S(2)}) collective-permute-start(bf16[256,1024]{1,0:T(8,128)(2,1)S(1)} %add_convert_fusion.14), channel_id=1, source_target_pairs={{0,8},{2,10},{4,12},{6,14},{24,16},{26,18},{28,20},{30,22},{1,9},{... | collective-permute-start | bytes 1572872 | tf_op jit(solution)/shard_map/ppermute | solution.py:236
  197.0 17.3 %collective-permute-start.39 = (bf16[256,1024]{1,0:T(8,128)(2,1)S(1)}, bf16[256,1024]{1,0:T(8,128)(2,1)S(1)}, u32[]{:S(2)}, u32[]{:S(2)}) collective-permute-start(bf16[256,1024]{1,0:T(8,128)(2,1)S(1)} %add_convert_fusion.12), channel_id=1, source_target_pairs={{16,8},{18,10},{20,12},{22,14},{9,17},{11,19},{13,21},{15,23}} | collective-permute-start | bytes 1572872 | tf_op jit(solution)/shard_map/ppermute | solution.py:236
  215.2 18.1 %collective-permute-start.43 = (bf16[4,320,512]{2,1,0:T(8,128)(2,1)S(1)}, bf16[4,320,512]{2,1,0:T(8,128)(2,1)}, u32[]{:S(2)}, u32[]{:S(2)}) collective-permute-start(bf16[4,320,512]{2,1,0:T(8,128)(2,1)S(1)} %bitcast.25), channel_id=1, source_target_pairs={{0,2},{2,0},{4,6},{6,4},{8,10},{10,8},{12,14},{14,12},{16,18},{18,... | collective-permute-start | bytes 3932168 | tf_op jit(solution)/shard_map/ppermute | solution.py:198
  215.3 16.7 %collective-permute-start.42 = (bf16[256,1024]{1,0:T(8,128)(2,1)S(1)}, bf16[256,1024]{1,0:T(8,128)(2,1)}, u32[]{:S(2)}, u32[]{:S(2)}) collective-permute-start(bf16[256,1024]{1,0:T(8,128)(2,1)S(1)} %add_convert_fusion.8), channel_id=1, source_target_pairs={{8,16},{10,18},{12,20},{14,22},{17,9},{19,11},{21,13},{23,15}} | collective-permute-start | bytes 1572872 | tf_op jit(solution)/shard_map/ppermute | solution.py:236
  217.9 24.9 %collective-permute-start.44 = (bf16[256,1024]{1,0:T(8,128)(2,1)S(1)}, bf16[256,1024]{1,0:T(8,128)(2,1)S(1)}, u32[]{:S(2)}, u32[]{:S(2)}) collective-permute-start(bf16[256,1024]{1,0:T(8,128)(2,1)S(1)} %add_convert_fusion.5), channel_id=1, source_target_pairs={{8,16},{10,18},{12,20},{14,22},{17,9},{19,11},{21,13},{23,15}} | collective-permute-start | bytes 1572872 | tf_op jit(solution)/shard_map/ppermute | solution.py:236
  243.1 16.4 %collective-permute-start.45 = (bf16[256,2048]{1,0:T(8,128)(2,1)S(1)}, bf16[256,2048]{1,0:T(8,128)(2,1)S(1)}, u32[]{:S(2)}, u32[]{:S(2)}) collective-permute-start(bf16[256,2048]{1,0:T(8,128)(2,1)S(1)} %pad_maximum_fusion.1.refs_0_), channel_id=1, source_target_pairs={{0,2},{2,0},{4,6},{6,4},{8,10},{10,8},{12,14},{14,12},{16,18},{18,... | collective-permute-start | bytes 3145736 | tf_op jit(solution)/shard_map/ppermute | solution.py:392
  (42 other events, 419.8 us)
Sparse Core Ops, SparseCore 0:
  80.1 26.2 reduce-scatter.1

commit v2 on v1

v2 whole, which is shorter than its diff:
```python
import functools

import jax
import jax.numpy as jnp
from jax import lax
from jax.experimental import pallas as pl
from jax.experimental.pallas import tpu as pltpu
from jax.sharding import PartitionSpec as P

BLK = 128
QUARTER = 128
VMEM = 56 * 2**20
COL_CHUNKS = 2
DEPTH = 2


DECAY_RATE = 0.75
DAMPING = 0.03

BF16 = jnp.bfloat16
F32 = jnp.float32


def pick_kernel(n_picks, which_ref, acts, cotan, ours, theirs):
    is_act = which_ref[n_picks] == 0
    ours[...] = jnp.where(is_act, acts[...], cotan[...])
    theirs[...] = jnp.where(is_act, cotan[...], acts[...])


def pick(acts, cotan, block_ids, core):
    n_picks, width = block_ids.shape[0], acts.shape[1]
    chosen = pl.BlockSpec((BLK, width), lambda i, which: (which[i], 0))
    out = pl.BlockSpec((BLK, width), lambda i, which: (i, 0))
    return pl.pallas_call(
        functools.partial(pick_kernel, n_picks),
        grid_spec=pltpu.PrefetchScalarGridSpec(
            num_scalar_prefetch=1, grid=(n_picks,), in_specs=[chosen] * 2, out_specs=[out] * 2
        ),
        out_shape=[jax.ShapeDtypeStruct((n_picks * BLK, width), BF16)] * 2,
        compiler_params=pltpu.CompilerParams(vmem_limit_bytes=VMEM),
        cost_estimate=pl.CostEstimate(
            flops=0, bytes_accessed=8 * n_picks * BLK * width, transcendentals=0
        ),
    )(jnp.concatenate([block_ids, jnp.reshape(core, (1,))]).astype(jnp.int32), acts, cotan)


def pack_upper(full):
    q = QUARTER
    second = jnp.concatenate([full[q : 2 * q, q:], full[3 * q :, 3 * q :]], axis=1)
    third = full[2 * q : 3 * q, 2 * q :]
    third = jnp.concatenate([third[: q // 2], third[q // 2 :]], axis=1)
    return jnp.concatenate([full[:q], second, third], axis=0)


def term_kernel(scales, place_ref, ours, theirs, keep, away):
    total = 0.0
    for rows in (ours[...], theirs[...]):
        total = total + lax.dot_general(
            rows, rows, (((0,), (0,)), ((), ())), preferred_element_type=F32
        )
    scale = jnp.where(place_ref[0] == 0, scales[0], scales[1]).astype(F32)
    packed = pack_upper(total * scale)
    half = packed.shape[0] // 2
    low = place_ref[1] == 0
    keep[0] = jnp.where(low, packed[:half], packed[half:]).astype(BF16)
    away[0] = jnp.where(low, packed[half:], packed[:half]).astype(BF16)


def terms(place, ours, theirs, size, scales):
    rows, width = ours.shape
    blocks, half = width // size, 5 * QUARTER // 4
    strip = pl.BlockSpec((rows, size), lambda b, place: (0, b))
    out = pl.BlockSpec((1, half, size), lambda b, place: (b, 0, 0))
    return pl.pallas_call(
        functools.partial(term_kernel, scales),
        grid_spec=pltpu.PrefetchScalarGridSpec(
            num_scalar_prefetch=1, grid=(blocks,), in_specs=[strip] * 2, out_specs=[out] * 2
        ),
        out_shape=[jax.ShapeDtypeStruct((blocks, half, size), BF16)] * 2,
        compiler_params=pltpu.CompilerParams(vmem_limit_bytes=VMEM),
        cost_estimate=pl.CostEstimate(
            flops=4 * rows * width * size, bytes_accessed=8 * rows * width, transcendentals=0
        ),
    )(place, ours, theirs)


def unpack_upper(packed):
    q = QUARTER
    tiles = {}
    for j in range(4):
        tiles[0, j] = packed[:q, j * q : (j + 1) * q]
    for j in range(1, 4):
        tiles[1, j] = packed[q : 2 * q, (j - 1) * q : j * q]
    tiles[3, 3] = packed[q : 2 * q, 3 * q :]
    third = jnp.concatenate([packed[2 * q :, : 2 * q], packed[2 * q :, 2 * q :]], axis=0)
    tiles[2, 2], tiles[2, 3] = third[:, :q], third[:, q:]
    return [[tiles[i, j] if j >= i else tiles[j, i].T for j in range(4)] for i in range(4)]


def factor_kernel(place_ref, keep, back, keep_sib, back_sib, *refs):
    low = place_ref[2] == 0
    for kind, (factor, basis, new, eig) in enumerate(zip(refs[0:2], refs[2:4], refs[4:6], refs[6:8])):
        here = place_ref[1] == kind
        kept = jnp.where(here, keep[0], keep_sib[0])
        came = jnp.where(here, back[0], back_sib[0])
        halves = [jnp.where(low, kept, came), jnp.where(low, came, kept)]
        rows = unpack_upper(jnp.concatenate(halves, axis=0).astype(F32))
        q = QUARTER
        for i in range(4):
            for j in range(4):
                at = (0, pl.ds(i * q, q), pl.ds(j * q, q))
                new[at] = DECAY_RATE * factor[at] + (1.0 - DECAY_RATE) * rows[i][j]
        vectors = basis[0]
        rest = new[0]
        product = 0.0
        for _ in range(3):
            part = rest.astype(BF16)
            rest = rest - part.astype(F32)
            product = product + jnp.dot(part, vectors, preferred_element_type=F32)
        eig[0] = jnp.sum(vectors.astype(F32) * product, axis=0, keepdims=True)


def update_factors(place, halves, factors, basis_in, basis_out):
    blocks, size, _ = basis_in.shape

    def local(b, place):
        return (b, 0, 0)

    square = pl.BlockSpec((1, size, size), local)
    narrow = pl.BlockSpec((1, halves[0].shape[1], size), local)
    line = pl.BlockSpec((1, 1, size), local)
    return pl.pallas_call(
        factor_kernel,
        grid_spec=pltpu.PrefetchScalarGridSpec(
            num_scalar_prefetch=1,
            grid=(blocks,),
            in_specs=[narrow] * 4
            + [square] * 3
            + [pl.BlockSpec((1, size, size), lambda b, place: (place[0] + b, 0, 0))],
            out_specs=[square, square, line, line],
        ),
        out_shape=[jax.ShapeDtypeStruct((blocks, size, size), F32)] * 2
        + [jax.ShapeDtypeStruct((blocks, 1, size), F32)] * 2,
        compiler_params=pltpu.CompilerParams(vmem_limit_bytes=VMEM),
        cost_estimate=pl.CostEstimate(
            flops=blocks * 12 * size**3, bytes_accessed=blocks * 19 * size**2, transcendentals=0
        ),
    )(place, *halves, *factors, basis_in, basis_out)


def tail_kernel(n_parts, place_ref, *refs):
    parts, (basis, outer, eig_in, eig_out) = refs[:n_parts], refs[n_parts : n_parts + 4]
    out, whole = refs[-2:]
    sharers = len(parts)
    rows = parts[0].shape[0]
    me = place_ref[1]
    for step, part in enumerate(parts):
        spot = lax.rem(me - step + sharers, sharers)
        whole[pl.ds(pl.multiple_of(spot * rows, rows), rows), :] = part[...]
    right = jnp.dot(whole[...], basis[0], preferred_element_type=F32).astype(BF16)
    inner = lax.dot_general(outer[0], right, (((0,), (0,)), ((), ())), preferred_element_type=F32)
    scaled = (inner / (eig_out[...] * eig_in[0] + DAMPING)).astype(BF16)
    mine = outer[0, pl.ds(pl.multiple_of(me * rows, rows), rows), :]
    upper = jnp.dot(mine, scaled, preferred_element_type=F32).astype(BF16)
    out[...] = lax.dot_general(
        upper, basis[0], (((1,), (1,)), ((), ())), preferred_element_type=F32
    ).astype(BF16)


def tail(place, parts, basis_in, basis_out, eig_in, eig_out, chunk, filled):
    blocks, size, _ = basis_in.shape
    rows, cols = parts[0].shape
    each = cols // size
    strip = pl.BlockSpec((rows, size), lambda b, place: (0, b))
    in_specs = [strip] * len(parts) + [
        pl.BlockSpec((1, size, size), lambda b, place: (chunk * each + b, 0, 0)),
        pl.BlockSpec((1, size, size), lambda b, place: (place[0], 0, 0)),
        pl.BlockSpec((1, 1, size), lambda b, place: (chunk * each + b, 0, 0)),
        pl.BlockSpec((size, 1), lambda b, place: (0, 0)),
    ]
    args = [place, *parts, basis_in, basis_out, eig_in, eig_out]
    aliases = {}
    if filled is not None:
        in_specs.append(pl.BlockSpec(memory_space=pl.ANY))
        aliases = {len(args): 0}
        args.append(filled)
    return pl.pallas_call(
        functools.partial(tail_kernel, len(parts)),
        grid_spec=pltpu.PrefetchScalarGridSpec(
            num_scalar_prefetch=1,
            grid=(each,),
            in_specs=in_specs,
            out_specs=pl.BlockSpec((rows, size), lambda b, place: (0, chunk * each + b)),
            scratch_shapes=[pltpu.VMEM((size, size), BF16)],
        ),
        out_shape=jax.ShapeDtypeStruct((rows, blocks * size), BF16),
        input_output_aliases=aliases,
        compiler_params=pltpu.CompilerParams(vmem_limit_bytes=VMEM),
        cost_estimate=pl.CostEstimate(
            flops=each * 6 * size**3, bytes_accessed=4 * each * size**2, transcendentals=0
        ),
    )(*args)


def turn_kernel(which_ref, block, *outs):
    del which_ref
    for n, out in enumerate(outs):

        @pl.when(pl.program_id(0) == n)
        def _(out=out):
            out[...] = block[...].T


def turned(rows, which, n_rows):
    tokens, _ = rows.shape
    return pl.pallas_call(
        turn_kernel,
        grid_spec=pltpu.PrefetchScalarGridSpec(
            num_scalar_prefetch=1,
            grid=(len(which),),
            in_specs=[pl.BlockSpec((tokens, n_rows), lambda i, which: (0, which[i]))],
            out_specs=[pl.BlockSpec((n_rows, tokens), lambda i, which: (0, 0))] * len(which),
        ),
        out_shape=[jax.ShapeDtypeStruct((n_rows, tokens), BF16)] * len(which),
        compiler_params=pltpu.CompilerParams(vmem_limit_bytes=VMEM),
        cost_estimate=pl.CostEstimate(
            flops=0, bytes_accessed=4 * len(which) * tokens * n_rows, transcendentals=0
        ),
    )(jnp.stack(which).astype(jnp.int32), rows)


def product_kernel(n_pairs, *refs):
    pieces, right, outs, left = refs[: 2 * n_pairs], refs[2 * n_pairs : 2 * n_pairs + 2], refs[2 * n_pairs + 2 : -1], refs[-1]
    step = pl.program_id(0)
    rows, tokens = pieces[0].shape

    @pl.when(step == 0)
    def _():
        for n, piece in enumerate(pieces):
            left[n // 2 * rows : (n // 2 + 1) * rows, n % 2 * tokens : (n % 2 + 1) * tokens] = piece[...]

    total = jnp.dot(left[:, :tokens], right[0][...], preferred_element_type=F32)
    total = total + jnp.dot(left[:, tokens:], right[1][...], preferred_element_type=F32)
    chunks = len(outs) // n_pairs
    each = pl.num_programs(0) // chunks
    for n in range(chunks):

        @pl.when(step // each == n)
        def _(n=n):
            for m in range(n_pairs):
                outs[m * chunks + n][...] = total[m * rows : (m + 1) * rows].astype(BF16)


def products(pairs, rows, chunks):
    tokens, width = rows[0].shape
    n_rows = pairs[0][0].shape[0]
    tile = 512
    each = width // chunks // tile
    whole = pl.BlockSpec((n_rows, tokens), lambda i: (0, 0))
    strip = pl.BlockSpec((tokens, tile), lambda i: (0, i))
    outs = pl.pallas_call(
        functools.partial(product_kernel, len(pairs)),
        grid=(width // tile,),
        in_specs=[whole] * (2 * len(pairs)) + [strip] * 2,
        out_specs=[
            pl.BlockSpec((n_rows, tile), lambda i, n=n: (0, jnp.clip(i - n * each, 0, each - 1)))
            for _ in pairs
            for n in range(chunks)
        ],
        out_shape=[jax.ShapeDtypeStruct((n_rows, width // chunks), BF16)] * (chunks * len(pairs)),
        scratch_shapes=[pltpu.VMEM((len(pairs) * n_rows, 2 * tokens), BF16)],
        compiler_params=pltpu.CompilerParams(vmem_limit_bytes=VMEM),
        cost_estimate=pl.CostEstimate(
            flops=4 * len(pairs) * tokens * n_rows * width,
            bytes_accessed=4 * tokens * width,
            transcendentals=0,
        ),
    )(*[piece for pair in pairs for piece in pair], *rows)
    return [outs[m * chunks : (m + 1) * chunks] for m in range(len(pairs))]


def per_device(acts, cotan, block_ids, basis_in, basis_out, act_factor, grad_factor):
    n_dp = lax.axis_size("dp")
    n_worker = lax.axis_size("worker")
    d = lax.axis_index("dp")
    w = lax.axis_index("worker")
    core, x = d % 2, (d // 2) % 2
    n_z = n_dp // 4
    pool_rows, width = acts.shape
    local_blocks, block_size, _ = basis_in.shape
    model_width = basis_out.shape[0] * block_size
    samples = block_ids.shape[0] * BLK * n_dp
    tokens = pool_rows * n_dp
    rows_dev = model_width // n_dp
    z_per_worker = n_z // n_worker
    cols = width // COL_CHUNKS if width >= 1024 else width
    both = ("dp", "worker")

    def swap_core(v):
        return lax.ppermute(v, "dp", [(i, i ^ 1) for i in range(n_dp)])

    def swap_x(v):
        return lax.ppermute(v, "dp", [(i, i ^ 2) for i in range(n_dp)])

    def from_worker(v, step, flip):
        return lax.ppermute(
            v,
            both,
            [
                ((i ^ flip) * n_worker + (j + step) % n_worker, i * n_worker + j)
                for i in range(n_dp)
                for j in range(n_worker)
            ],
        )

    def place(owner, j):
        return owner * z_per_worker + (j if owner < n_worker // 2 else z_per_worker - 1 - j)

    z = d // 4
    starts = list(range(0, width, cols))
    shards = [(step, j) for j in range(z_per_worker) for step in range(n_worker)]

    def hops_of(step, j):
        hops = []
        size = 1
        while size < n_z:
            moves = []
            for i in range(n_worker):
                end = place((i + step) % n_worker, j)
                for low in range(0, n_z, 2 * size):
                    heads = [min(max(end, at), at + size - 1) for at in (low, low + size)]
                    to = min(max(end, low), low + 2 * size - 1)
                    moves.append((i, sum(heads) - to, to))
            hops.append(moves)
            size *= 2
        return hops

    def links(moves):
        found = set()
        for i, a, b in moves:
            ahead = 1 if b > a else -1
            found.update((i, at, at + ahead) for at in range(a, b, ahead))
        return found

    def swap_z(v, far):
        return lax.ppermute(v, "dp", [(i, (i + 4 * far) % n_dp) for i in range(n_dp)])

    def hop(v, moves):
        return lax.ppermute(
            v,
            both,
            [((a * 4 + r) * n_worker + i, (b * 4 + r) * n_worker + i) for i, a, b in moves for r in range(4)],
        )

    def piece(j, at, flip):
        part = jnp.where(w < n_worker // 2, j, z_per_worker - 1 - j)
        x_to = x if at else 1 - x
        core_to = 1 - core if flip else core
        return (part * 2 + x_to) * 2 + core_to

    y_items = [(step, j, at, flip) for step, j in shards if step for at in range(2) for flip in range(2)]
    y_stage = {item: max(0, at - 1) for at, item in enumerate(y_items)}
    x_items = [(step, j, n) for step, j in shards for n in range(len(starts))]
    x_stage, z_stage, product_stage, busy = {}, {}, {}, set()
    clock = 0
    for step, j, n in x_items:
        ready = y_stage[step, j, 0, 1] + DEPTH if step else 0
        clock = max(clock, ready) + 1
        x_stage[step, j, n] = clock
        if n == 0:
            product_stage[step, j, 0] = clock - 1
            product_stage[step, j, 1] = max(clock + 1, y_stage[step, j, 1, 1] + DEPTH if step else 2)
            if step == 0 and j > 0:
                product_stage[step, j, 0] = product_stage[step, j, 1] = 3
    for step, j, n in x_items:
        clock = max(x_stage[step, j, n] + DEPTH, product_stage[step, j, 1] + 1)
        for at, moves in enumerate(hops_of(step, j)):
            while any((clock, link) in busy for link in links(moves)):
                clock += 1
            busy.update((clock, link) for link in links(moves))
            z_stage[step, j, n, at] = clock
            clock += DEPTH
    last = max(z_stage.values()) + DEPTH - 1

    my_start = d * rows_dev
    block = my_start // block_size
    flags = jnp.stack([w * local_blocks, core, x]).astype(jnp.int32)
    env = {"acts": acts, "cotan": cotan}
    pending = {}
    first = [(0, 0, 1), (0, 0, 0)]
    others = [(j, at, flip) for j in range(z_per_worker) for at in range(2) for flip in range(2)]
    others = [key for key in others if key not in first]
    done = {}
    for stage in range(last + 1):
        if stage:
            keys = sorted(env, key=str)
            env = dict(zip(keys, lax.optimization_barrier(tuple(env[k] for k in keys))))
        soon, late = {}, {}
        if stage == 0:
            soon["acts_sib"] = swap_core(acts)
            for key, part in zip(first, turned(cotan, [piece(*key) for key in first], rows_dev)):
                env["p", *key] = part
            for key, part in zip(others, turned(cotan, [piece(*key) for key in others], rows_dev)):
                soon["p", *key] = part
            ours, theirs = pick(acts, cotan, block_ids, core)
            scales = (1.0 / samples, tokens / samples)
            soon["keep"], away = terms(flags[1:], ours, swap_core(theirs), block_size, scales)
            late["back"] = swap_x(away)
            for j, at, _ in [key for key in first + others if key[2] == 1]:
                when = soon if (j, at) == (0, 0) else late
                got = {**env, **soon}
                when["c", 0, j, at, 0] = got["p", j, at, 0]
                when["c", 0, j, at, 1] = swap_core(got["p", j, at, 1])
        for item, when in y_stage.items():
            if when == stage:
                step, j, at, flip = item
                late["c", step, j, at, flip] = from_worker(env["p", j, at, flip], step, flip)
        for step, j, n in x_items:
            if x_stage[step, j, n] == stage:
                late["got", step, j, n] = swap_x(env.pop(("out", step, j, n)))
        for (step, j, n, at), when in z_stage.items():
            if when == stage:
                late["hop", step, j, n] = hop(env["acc", step, j, n], hops_of(step, j)[at])

        ready = {**env, **soon} if stage == 0 else env
        due = [key for key, when in product_stage.items() if when == stage]
        if due:
            pairs = [[ready["c", step, j, at, flip] for flip in range(2)] for step, j, at in due]
            found = products(pairs, (ready["acts"], ready["acts_sib"]), len(starts))
            for (step, j, at), outs in zip(due, found):
                for n, out in enumerate(outs):
                    soon["mine" if at else "out", step, j, n] = out

        if stage == 2:
            half = (env.pop("keep") + env.pop("back")).reshape(n_z, -1, block_size)
            soon["quarter"] = lax.dynamic_index_in_dim(half, z, 0, keepdims=False)
            for far in range(1, n_z):
                away = lax.dynamic_index_in_dim(half, (z + far) % n_z, 0, keepdims=False)
                late["quarter", far] = swap_z(away, far)
        if stage == 4:
            total = env.pop("quarter").astype(F32)
            for far in range(1, n_z):
                total = total + env.pop(("quarter", far)).astype(F32)
            soon["whole", 0] = total.astype(BF16)
        if stage == 5:
            for far in range(1, n_z):
                late["whole", far] = swap_z(env["whole", 0], far)
        if stage == 7:
            half = jnp.zeros((n_z, *env["whole", 0].shape), BF16)
            for far in range(n_z):
                half = lax.dynamic_update_index_in_dim(half, env.pop(("whole", far)), (z - far) % n_z, 0)
            soon["keep"] = half.reshape(local_blocks, -1, block_size)
        if stage == 8:
            late["back"] = swap_x(env["keep"])
            late["keep_sib"] = swap_core(env["keep"])
        if stage == 10:
            late["back_sib"] = swap_core(env["back"])
        if stage == max(12, last - 1):
            act_new, grad_new, eig_in, eig_local = update_factors(
                flags,
                [env.pop(key) for key in ("keep", "back", "keep_sib", "back_sib")],
                (act_factor, grad_factor),
                basis_in,
                basis_out,
            )

        env.update(soon)
        env.update(pending)
        pending = late
        for step, j, n in x_items:
            mine, got, acc = ("mine", step, j, n), ("got", step, j, n), ("acc", step, j, n)
            if mine in env and got in env:
                env[acc] = env.pop(mine) + env.pop(got)
            if ("hop", step, j, n) in env:
                env[acc] = env[acc] + env.pop(("hop", step, j, n))
        for n in range(len(starts)):
            final = [z_stage[step, j, n, len(hops_of(step, j)) - 1] for step, j in shards]
            if stage == max(final) + DEPTH - 1:
                total = None
                for step, j in shards:
                    ends = jnp.array([place((i + step) % n_worker, j) for i in range(n_worker)], jnp.int32)
                    acc = env.pop(("acc", step, j, n))
                    total = acc if total is None else jnp.where(ends[w] == z, acc, total)
                done[n] = total

    eig_block = jnp.zeros((block_size,), F32)
    for step in range(n_worker):
        held = eig_local if step == 0 else from_worker(eig_local, step, 0)
        row = lax.dynamic_index_in_dim(held, block % local_blocks, 0, keepdims=False)[0]
        owner = (w + step) % n_worker
        eig_block = jnp.where(owner == block // local_blocks, row, eig_block)

    sharers = block_size // rows_dev
    spot = jnp.stack([block, d % sharers]).astype(jnp.int32)
    precond = None
    for n in range(len(starts)):
        parts = [done[n]]
        for step in range(1, sharers):
            pairs = [(i, i // sharers * sharers + (i + step) % sharers) for i in range(n_dp)]
            parts.append(lax.ppermute(parts[0], "dp", pairs))
        precond = tail(spot, parts, basis_in, basis_out, eig_in, eig_block[:, None], n, precond)
    return precond, act_new, grad_new


def solution(mesh):
    return jax.shard_map(
        per_device,
        mesh=mesh,
        in_specs=(
            P("dp", "worker"),
            P("dp", "worker"),
            P("dp"),
            P("worker", None, None),
            P(),
            P("worker", None, None),
            P("worker", None, None),
        ),
        out_specs=(P("dp", "worker"), P("worker", None, None), P("worker", None, None)),
        check_vma=False,
    )
```

time: 277 us -> 270 us (0.975)
  starting transfers between devices: 53 us -> 78.3 us
  blocking collectives: 21.5 us -> 0 us
  between operations: 17.1 us -> 3.38 us
  Pallas kernels: 75.5 us -> 85.9 us
  local copies, waits for them, and re-layouts: 17.1 us -> 7.27 us
  waiting for transfers between devices: 65.9 us -> 69.1 us
    all_gather x1 -> x0, blocking collectives: 21.5 us -> none  [per_device(): lax.all_gather(env.pop('reduced'), 'dp', axis_index_groups=groups, tiled=...]
    ppermute x1 -> x8, starting transfers between devices: 0.07 us -> 18.8 us  [the longest x6 18.6 us: swap_z(): lax.ppermute(v, 'dp', [(i, (i + 4 * far) % n_dp) for i in range(n_dp)])]
    add x0 -> x23, other arithmetic: none -> 18.5 us  [the longest x14 11.5 us: per_device(): env[acc] = env[acc] + env.pop(('hop', step, j, n))]
    convert_element_type x21 -> x1, other arithmetic: 12.5 us -> 0.08 us  [per_device(): soon['whole', 0] = total.astype(BF16)]
    ppermute x20 -> x16, waiting for transfers between devices: 35.5 us -> 25.2 us  [hop(): lax.ppermute(v, both, [((a * 4 + r) * n_worker + i, (b * 4 + r) * n_worke...]
    pallas_call x9 -> x12, Pallas kernels: 64.6 us -> 74.3 us  [the longest x6 45.4 us: products(): pl.pallas_call(functools.partial(product_kernel, len(pairs)), grid=(width...]
    ppermute x9, starting transfers between devices: 3.66 us -> 12.7 us  [from_worker(): lax.ppermute(v, both, [((i ^ flip) * n_worker + (j + step) % n_worker, i...]
    ppermute x1 -> x8, waiting for transfers between devices: 0.01 us -> 7.05 us  [the longest x6 7.05 us: swap_z(): lax.ppermute(v, 'dp', [(i, (i + 4 * far) % n_dp) for i in range(n_dp)])]
  transfers between devices with their start and end apart: 48 -> 51, of which waited for: 18 -> 17; matrix products, arithmetic and copies ran while one was open for 11% -> 11% of each run, Pallas kernels for 25% -> 30%
where the time goes in v2:
time: 270 us; the launch traced here: 269 us
  Pallas kernels  85.9 us (32%)
  starting transfers between devices  78.3 us (29%)
  waiting for transfers between devices  69.1 us (26%)
  other arithmetic  24.8 us (9%)
  local copies, waits for them, and re-layouts  7.27 us (3%)
  between operations  3.38 us (1%)
    pallas_call x6, Pallas kernels, products(): pl.pallas_call(functools.partial(product_kernel, len(pairs)), grid=(width...  45.4 us
    ppermute x16, starting transfers between devices, hop(): lax.ppermute(v, both, [((a * 4 + r) * n_worker + i, (b * 4 + r) * n_worke...  35.2 us
    ppermute x9, waiting for transfers between devices, from_worker(): lax.ppermute(v, both, [((i ^ flip) * n_worker + (j + step) % n_worker, i...  26.3 us
    ppermute x16, waiting for transfers between devices, hop(): lax.ppermute(v, both, [((a * 4 + r) * n_worker + i, (b * 4 + r) * n_worke...  25.2 us
    ppermute x6, starting transfers between devices, swap_z(): lax.ppermute(v, 'dp', [(i, (i + 4 * far) % n_dp) for i in range(n_dp)])  18.6 us
    ppermute x9, starting transfers between devices, from_worker(): lax.ppermute(v, both, [((i ^ flip) * n_worker + (j + step) % n_worker, i...  12.7 us
    pallas_call x1, Pallas kernels, update_factors(): pl.pallas_call(factor_kernel, grid_spec=pltpu.PrefetchScalarGridSpec(num_...  11.5 us
    add x14, other arithmetic, per_device(): env[acc] = env[acc] + env.pop(('hop', step, j, n))  11.5 us
  transfers between devices with their start and end apart: 51, of which 17 were waited for; matrix products, arithmetic and copies ran while one was open for 11% of the time, Pallas kernels for 30%

profile of v2, /device:TPU:12, one launch (start us, length us, event | category | flops | bytes accessed | tf_op | source)
XLA Modules:
  0.0 268.7 jit_solution(16392396247203283327)
XLA Ops:
  2.0 3.3 %shard_map.151 = (bf16[256,2048]{1,0:T(8,128)(2,1)}, bf16[256,2048]{1,0:T(8,128)(2,1)}) custom-call(s32[3]{0:T(128)} %get-tuple-element.399.which_ref, bf16[1024,2048]{1,0:T(8,128)(2,1)} %refs_2_.7, bf16[1024,2048]{1,0:T(8,128)(2,1)} %cotan.1), custom_call_target="tpu_custom_call" | custom-call | bytes 4194304 | tf_op jit(solution)/shard_map/pallas_call | solution.py:34
  6.4 3.2 %shard_map.149 = (bf16[256,1024]{1,0:T(8,128)(2,1)}, bf16[256,1024]{1,0:T(8,128)(2,1)}) custom-call(s32[2]{0:T(128)} %pad_add_fusion.1.which_ref, bf16[1024,2048]{1,0:T(8,128)(2,1)} %cotan.1), custom_call_target="tpu_custom_call" | custom-call | bytes 2097152 | tf_op jit(solution)/shard_map/pallas_call | solution.py:216
  10.3 6.5 %shard_map.148 = (bf16[256,1024]{1,0:T(8,128)(2,1)}, bf16[256,1024]{1,0:T(8,128)(2,1)}, bf16[256,1024]{1,0:T(8,128)(2,1)}, bf16[256,1024]{1,0:T(8,128)(2,1)}, bf...) custom-call(s32[6]{0:T(128)} %stack.60.which_ref, bf16[1024,2048]{1,0:T(8,128)(2,1)} %cotan.1), custom_call_target="tpu_custom_call" | custom-call | bytes 6291456 | tf_op jit(solution)/shard_map/pallas_call | solution.py:216
  18.9 5.1 %shard_map.152 = (bf16[4,160,512]{2,1,0:T(8,128)(2,1)}, bf16[4,160,512]{2,1,0:T(8,128)(2,1)}) custom-call(s32[2]{0:T(128)} %pad_add_fusion.2.place_ref, bf16[256,2048]{1,0:T(8,128)(2,1)} %get-tuple-element.209.ours, bf16[256,2048]{1,0:T(8,128)(2,1)} %copy-done.22), custom_call_target="tpu_custom_call" | custom-call | flops 1073741824 | bytes 4194304 | tf_op jit(solution)/shard_map/pallas_call | solution.py:74
  27.6 6.9 %shard_map.150 = (bf16[256,1024]{1,0:T(8,128)(2,1)}, bf16[256,1024]{1,0:T(8,128)(2,1)}) custom-call(bf16[256,1024]{1,0:T(8,128)(2,1)} %get-tuple-element.205.refs_0_, bf16[256,1024]{1,0:T(8,128)(2,1)} %copy-done.10, bf16[1024,2048]{1,0:T(8,128)(2,1)} %refs_2_.7, bf16[1024,2048]{1,0:T(8,128)(2,1)} %collective-permute-done.6.refs_3_.refs_5_), custom_call_target="tpu_custom_call" | custom-call | flops 2147483648 | bytes 8388608 | tf_op jit(solution)/shard_map/pallas_call | solution.py:261
  35.7 5.3 %collective-permute-done.3.refs_2_ = bf16[256,1024]{1,0:T(8,128)(2,1)} collective-permute-done((bf16[256,1024]{1,0:T(8,128)(2,1)S(1)}, bf16[256,1024]{1,0:T(8,128)(2,1)}, u32[]{:S(2)}, u32[]{:S(2)}) %collective-permute-start.3) | collective-permute-done | bytes 524320 | tf_op jit(solution)/shard_map/ppermute | solution.py:306
  41.0 9.5 %collective-permute-done.4.refs_3_ = bf16[256,1024]{1,0:T(8,128)(2,1)} collective-permute-done((bf16[256,1024]{1,0:T(8,128)(2,1)S(1)}, bf16[256,1024]{1,0:T(8,128)(2,1)}, u32[]{:S(2)}, u32[]{:S(2)}) %collective-permute-start.4) | collective-permute-done | bytes 524320 | tf_op jit(solution)/shard_map/ppermute | solution.py:306
  53.8 9.1 %shard_map.153 = (bf16[256,1024]{1,0:T(8,128)(2,1)}, bf16[256,1024]{1,0:T(8,128)(2,1)}, bf16[256,1024]{1,0:T(8,128)(2,1)}, bf16[256,1024]{1,0:T(8,128)(2,1)}) custom-call(bf16[256,1024]{1,0:T(8,128)(2,1)} %get-tuple-element.223.refs_0_, bf16[256,1024]{1,0:T(8,128)(2,1)} %copy-done.30, bf16[256,1024]{1,0:T(8,128)(2,1)} %collective-permute-done.3.refs_2_, ...), custom_call_target="tpu_custom_call" | custom-call | flops 4294967296 | bytes 8388608 | tf_op jit(solution)/shard_map/pallas_call | solution.py:261
  69.6 6.6 %collective-permute-done.11 = bf16[256,1024]{1,0:T(8,128)(2,1)S(1)} collective-permute-done((bf16[256,1024]{1,0:T(8,128)(2,1)}, bf16[256,1024]{1,0:T(8,128)(2,1)S(1)}, u32[]{:S(2)}, u32[]{:S(2)}) %collective-permute-start.11) | collective-permute-done | bytes 524320 | tf_op jit(solution)/shard_map/ppermute | solution.py:303
  76.6 9.1 %shard_map.154 = (bf16[256,1024]{1,0:T(8,128)(2,1)}, bf16[256,1024]{1,0:T(8,128)(2,1)}, bf16[256,1024]{1,0:T(8,128)(2,1)}, bf16[256,1024]{1,0:T(8,128)(2,1)}) custom-call(bf16[256,1024]{1,0:T(8,128)(2,1)} %get-tuple-element.260.refs_0_, bf16[256,1024]{1,0:T(8,128)(2,1)} %copy-done.27, bf16[256,1024]{1,0:T(8,128)(2,1)} %get-tuple-element.294.refs_2_, ...), custom_call_target="tpu_custom_call" | custom-call | flops 4294967296 | bytes 8388608 | tf_op jit(solution)/shard_map/pallas_call | solution.py:261
  87.2 6.1 %collective-permute-start.18 = (bf16[256,1024]{1,0:T(8,128)(2,1)}, bf16[256,1024]{1,0:T(8,128)(2,1)S(1)}, u32[]{:S(2)}, u32[]{:S(2)}) collective-permute-start(bf16[256,1024]{1,0:T(8,128)(2,1)} %get-tuple-element.260.refs_0_), channel_id=1, source_target_pairs={{1,0},{0,1},{3,2},{2,3},{5,4},{4,5},{7,6},{6,7},{9,8},{8,9},{11,10... | collective-permute-start | bytes 1572872 | tf_op jit(solution)/shard_map/ppermute | solution.py:306
  95.3 6.8 %shard_map.155 = (bf16[256,1024]{1,0:T(8,128)(2,1)}, bf16[256,1024]{1,0:T(8,128)(2,1)}) custom-call(bf16[256,1024]{1,0:T(8,128)(2,1)} %copy-done.13, bf16[256,1024]{1,0:T(8,128)(2,1)} %copy-done.14, bf16[1024,2048]{1,0:T(8,128)(2,1)} %refs_2_.7, bf16[1024,2048]{1,0:T(8,128)(2,1)} %collective-permute-done.6.refs_3_.refs_5_), custom_call_target="tpu_custom_call" | custom-call | flops 2147483648 | bytes 8388608 | tf_op jit(solution)/shard_map/pallas_call | solution.py:261
  106.3 2.8 %collective-permute-start.24 = (bf16[256,1024]{1,0:T(8,128)(2,1)S(1)}, bf16[256,1024]{1,0:T(8,128)(2,1)}, u32[]{:S(2)}, u32[]{:S(2)}) collective-permute-start(bf16[256,1024]{1,0:T(8,128)(2,1)S(1)} %add.250), channel_id=1, source_target_pairs={{0,8},{2,10},{4,12},{6,14},{16,24},{18,26},{20,28},{22,30},{9,1},{... | collective-permute-start | bytes 1572872 | tf_op jit(solution)/shard_map/ppermute | solution.py:349
  110.5 2.9 %collective-permute-start.22 = (bf16[256,1024]{1,0:T(8,128)(2,1)S(1)}, bf16[256,1024]{1,0:T(8,128)(2,1)}, u32[]{:S(2)}, u32[]{:S(2)}) collective-permute-start(bf16[256,1024]{1,0:T(8,128)(2,1)S(1)} %add.249), channel_id=1, source_target_pairs={{16,0},{18,2},{20,4},{22,6},{9,25},{11,27},{13,29},{15,31}} | collective-permute-start | bytes 1572872 | tf_op jit(solution)/shard_map/ppermute | solution.py:349
  114.5 11.1 %collective-permute-start.26 = (bf16[160,512]{1,0:T(8,128)(2,1)S(1)}, bf16[160,512]{1,0:T(8,128)(2,1)S(1)}, u32[]{:S(2)}, u32[]{:S(2)}) collective-permute-start(bf16[160,512]{1,0:T(8,128)(2,1)S(1)} %add_convert_fusion), channel_id=1, source_target_pairs={{0,8},{2,10},{4,12},{6,14},{8,16},{10,18},{12,20},{14,22},{16,24},... | collective-permute-start | bytes 491528 | tf_op jit(solution)/shard_map/ppermute | solution.py:346
  125.6 2.8 %collective-permute-start.25 = (bf16[256,1024]{1,0:T(8,128)(2,1)}, bf16[256,1024]{1,0:T(8,128)(2,1)S(1)}, u32[]{:S(2)}, u32[]{:S(2)}) collective-permute-start(bf16[256,1024]{1,0:T(8,128)(2,1)} %get-tuple-element.294.refs_2_), channel_id=1, source_target_pairs={{1,0},{0,1},{3,2},{2,3},{5,4},{4,5},{7,6},{6,7},{9,8},{8,9},{11,10... | collective-permute-start | bytes 1572872 | tf_op jit(solution)/shard_map/ppermute | solution.py:306
  129.5 4.2 %collective-permute-start.27 = (bf16[160,512]{1,0:T(8,128)(2,1)S(1)}, bf16[160,512]{1,0:T(8,128)(2,1)S(1)}, u32[]{:S(2)}, u32[]{:S(2)}) collective-permute-start(bf16[160,512]{1,0:T(8,128)(2,1)S(1)} %add_convert_fusion), channel_id=1, source_target_pairs={{0,16},{2,18},{4,20},{6,22},{8,24},{10,26},{12,28},{14,30},{16,0},... | collective-permute-start | bytes 491528 | tf_op jit(solution)/shard_map/ppermute | solution.py:346
  134.1 5.8 %collective-permute-done.27 = bf16[160,512]{1,0:T(8,128)(2,1)S(1)} collective-permute-done((bf16[160,512]{1,0:T(8,128)(2,1)S(1)}, bf16[160,512]{1,0:T(8,128)(2,1)S(1)}, u32[]{:S(2)}, u32[]{:S(2)}) %collective-permute-start.27) | collective-permute-done | bytes 163872 | tf_op jit(solution)/shard_map/ppermute | solution.py:346
  139.9 5.1 %collective-permute-start.31 = (bf16[256,1024]{1,0:T(8,128)(2,1)S(1)}, bf16[256,1024]{1,0:T(8,128)(2,1)}, u32[]{:S(2)}, u32[]{:S(2)}) collective-permute-start(bf16[256,1024]{1,0:T(8,128)(2,1)S(1)} %add.255), channel_id=1, source_target_pairs={{0,8},{2,10},{4,12},{6,14},{16,24},{18,26},{20,28},{22,30},{9,1},{... | collective-permute-start | bytes 1572872 | tf_op jit(solution)/shard_map/ppermute | solution.py:349
  145.1 3.2 %collective-permute-start.29 = (bf16[256,1024]{1,0:T(8,128)(2,1)S(1)}, bf16[256,1024]{1,0:T(8,128)(2,1)}, u32[]{:S(2)}, u32[]{:S(2)}) collective-permute-start(bf16[256,1024]{1,0:T(8,128)(2,1)S(1)} %add.254), channel_id=1, source_target_pairs={{16,0},{18,2},{20,4},{22,6},{9,25},{11,27},{13,29},{15,31}} | collective-permute-start | bytes 1572872 | tf_op jit(solution)/shard_map/ppermute | solution.py:349
  148.3 6.7 %shard_map.156 = (bf16[256,1024]{1,0:T(8,128)(2,1)}, bf16[256,1024]{1,0:T(8,128)(2,1)}) custom-call(bf16[256,1024]{1,0:T(8,128)(2,1)} %copy-done.7, bf16[256,1024]{1,0:T(8,128)(2,1)} %copy-done.9, bf16[1024,2048]{1,0:T(8,128)(2,1)} %refs_2_.7, bf16[1024,2048]{1,0:T(8,128)(2,1)} %collective-permute-done.6.refs_3_.refs_5_), custom_call_target="tpu_custom_call" | custom-call | flops 2147483648 | bytes 8388608 | tf_op jit(solution)/shard_map/pallas_call | solution.py:261
  167.7 5.5 %collective-permute-done.32.refs_1_ = bf16[256,1024]{1,0:T(8,128)(2,1)S(1)} collective-permute-done((bf16[256,1024]{1,0:T(8,128)(2,1)S(1)}, bf16[256,1024]{1,0:T(8,128)(2,1)S(1)}, u32[]{:S(2)}, u32[]{:S(2)}) %collective-permute-start.32) | collective-permute-done | bytes 524320 | tf_op jit(solution)/shard_map/ppermute | solution.py:306
  176.8 3.4 %collective-permute-done.33 = bf16[256,1024]{1,0:T(8,128)(2,1)S(1)} collective-permute-done((bf16[256,1024]{1,0:T(8,128)(2,1)S(1)}, bf16[256,1024]{1,0:T(8,128)(2,1)S(1)}, u32[]{:S(2)}, u32[]{:S(2)}) %collective-permute-start.33) | collective-permute-done | bytes 524320 | tf_op jit(solution)/shard_map/ppermute | solution.py:349
  181.7 6.8 %shard_map.157 = (bf16[256,1024]{1,0:T(8,128)(2,1)}, bf16[256,1024]{1,0:T(8,128)(2,1)}) custom-call(bf16[256,1024]{1,0:T(8,128)(2,1)} %copy-done.5, bf16[256,1024]{1,0:T(8,128)(2,1)} %copy-done.15, bf16[1024,2048]{1,0:T(8,128)(2,1)} %refs_2_.7, bf16[1024,2048]{1,0:T(8,128)(2,1)} %collective-permute-done.6.refs_3_.refs_5_), custom_call_target="tpu_custom_call" | custom-call | flops 2147483648 | bytes 8388608 | tf_op jit(solution)/shard_map/pallas_call | solution.py:261
  191.6 5.4 %collective-permute-start.41 = (bf16[256,1024]{1,0:T(8,128)(2,1)S(1)}, bf16[256,1024]{1,0:T(8,128)(2,1)S(1)}, u32[]{:S(2)}, u32[]{:S(2)}) collective-permute-start(bf16[256,1024]{1,0:T(8,128)(2,1)S(1)} %add.270), channel_id=1, source_target_pairs={{16,8},{18,10},{20,12},{22,14},{9,17},{11,19},{13,21},{15,23}} | collective-permute-start | bytes 1572872 | tf_op jit(solution)/shard_map/ppermute | solution.py:349
  203.0 3.2 %collective-permute-start.43 = (bf16[256,1024]{1,0:T(8,128)(2,1)S(1)}, bf16[256,1024]{1,0:T(8,128)(2,1)S(1)}, u32[]{:S(2)}, u32[]{:S(2)}) collective-permute-start(bf16[256,1024]{1,0:T(8,128)(2,1)S(1)} %add.273), channel_id=1, source_target_pairs={{16,8},{18,10},{20,12},{22,14},{9,17},{11,19},{13,21},{15,23}} | collective-permute-start | bytes 1572872 | tf_op jit(solution)/shard_map/ppermute | solution.py:349
  211.5 7.5 %collective-permute-done.44 = bf16[256,1024]{1,0:T(8,128)(2,1)S(1)} collective-permute-done((bf16[256,1024]{1,0:T(8,128)(2,1)S(1)}, bf16[256,1024]{1,0:T(8,128)(2,1)S(1)}, u32[]{:S(2)}, u32[]{:S(2)}) %collective-permute-start.44) | collective-permute-done | bytes 524320 | tf_op jit(solution)/shard_map/ppermute | solution.py:349
  227.4 10.4 %collective-permute-done.46 = bf16[256,1024]{1,0:T(8,128)(2,1)} collective-permute-done((bf16[256,1024]{1,0:T(8,128)(2,1)}, bf16[256,1024]{1,0:T(8,128)(2,1)}, u32[]{:S(2)}, u32[]{:S(2)}) %collective-permute-start.46) | collective-permute-done | bytes 524320 | tf_op jit(solution)/shard_map/ppermute | solution.py:349
  239.2 11.5 %shard_map.158 = (f32[4,512,512]{2,1,0:T(8,128)}, f32[4,512,512]{2,1,0:T(8,128)}, f32[4,1,512]{2,1,0:T(1,128)}, f32[4,1,512]{2,1,0:T(1,128)}) custom-call(s32[3]{0:T(128)} %get-tuple-element.400.place_ref, bf16[4,160,512]{2,1,0:T(8,128)(2,1)} %copy-done.2, bf16[4,160,512]{2,1,0:T(8,128)(2,1)} %collective-permute-done.39.back, ...), custom_call_target="tpu_custom_call" | custom-call | flops 6442450944 | bytes 19922944 | tf_op jit(solution)/shard_map/pallas_call | solution.py:132
  251.4 3.3 %collective-permute-done.48 = f32[4,1,512]{2,1,0:T(1,128)S(1)} collective-permute-done((f32[4,1,512]{2,1,0:T(1,128)}, f32[4,1,512]{2,1,0:T(1,128)S(1)}, u32[]{:S(2)}, u32[]{:S(2)}) %collective-permute-start.48) | collective-permute-done | bytes 8224 | tf_op jit(solution)/shard_map/ppermute | solution.py:306
  257.0 5.4 %shard_map.159.refs_6_ = bf16[256,2048]{1,0:T(8,128)(2,1)} custom-call(s32[2]{0:T(128)} %pad_add_fusion.place_ref, bf16[256,1024]{1,0:T(8,128)(2,1)} %copy-done, bf16[256,1024]{1,0:T(8,128)(2,1)} %copy-done.11, bf16[4,512,512]{2,1,0:T(8,128)(2,1)} %refs_2_.10, bf16[8,512,512]{2,1,0:T(8,128)(2,1)} %refs_3_.5, f32[4,1,512]{2,1,0:T(1,128)} %get-tuple-element.387.refs_4_, ...), custom_call_target="tpu_custom_call" | custom-call | flops 1610612736 | bytes 2097152 | tf_op jit(solution)/shard_map/pallas_call | solution.py:187
  263.2 5.4 %shard_map.160 = bf16[256,2048]{1,0:T(8,128)(2,1)} custom-call(s32[2]{0:T(128)} %pad_add_fusion.place_ref, bf16[256,1024]{1,0:T(8,128)(2,1)} %copy-done.1, bf16[256,1024]{1,0:T(8,128)(2,1)} %copy-done.12, bf16[4,512,512]{2,1,0:T(8,128)(2,1)} %refs_2_.10, bf16[8,512,512]{2,1,0:T(8,128)(2,1)} %refs_3_.5, ...), custom_call_target="tpu_custom_call", output_to_operand_aliasing={{}: (7, {})} | custom-call | flops 1610612736 | bytes 2097152 | tf_op jit(solution)/shard_map/pallas_call | solution.py:187
  (195 shorter events, 75.3 us)
Async XLA Ops:
  0.6 26.2 %collective-permute-start.6 = (bf16[1024,2048]{1,0:T(8,128)(2,1)}, bf16[1024,2048]{1,0:T(8,128)(2,1)}, u32[]{:S(2)}, u32[]{:S(2)}) collective-permute-start(bf16[1024,2048]{1,0:T(8,128)(2,1)} %refs_2_.7), channel_id=1, source_target_pairs={{0,2},{2,0},{4,6},{6,4},{8,10},{10,8},{12,14},{14,12},{16,18},{18,... | collective-permute-start | bytes 12582920 | tf_op jit(solution)/shard_map/ppermute | solution.py:300
  24.0 26.4 %collective-permute-start.8 = (bf16[4,160,512]{2,1,0:T(8,128)(2,1)}, bf16[4,160,512]{2,1,0:T(8,128)(2,1)S(1)}, u32[]{:S(2)}, u32[]{:S(2)}) collective-permute-start(bf16[4,160,512]{2,1,0:T(8,128)(2,1)} %get-tuple-element.221), channel_id=1, source_target_pairs={{0,4},{2,6},{4,0},{6,2},{8,12},{10,14},{12,8},{14,10},{16,20},{18,... | collective-permute-start | bytes 1966088 | tf_op jit(solution)/shard_map/ppermute | solution.py:303
  26.8 23.6 %collective-permute-start.4 = (bf16[256,1024]{1,0:T(8,128)(2,1)S(1)}, bf16[256,1024]{1,0:T(8,128)(2,1)}, u32[]{:S(2)}, u32[]{:S(2)}) collective-permute-start(bf16[256,1024]{1,0:T(8,128)(2,1)S(1)} %copy-done.29), channel_id=1, source_target_pairs={{3,0},{2,1},{1,2},{0,3},{7,4},{6,5},{5,6},{4,7},{11,8},{10,9},{9,1... | collective-permute-start | bytes 1572872 | tf_op jit(solution)/shard_map/ppermute | solution.py:306
  34.6 31.6 %collective-permute-start.10 = (bf16[256,1024]{1,0:T(8,128)(2,1)S(1)}, bf16[256,1024]{1,0:T(8,128)(2,1)S(1)}, u32[]{:S(2)}, u32[]{:S(2)}) collective-permute-start(bf16[256,1024]{1,0:T(8,128)(2,1)S(1)} %copy-done.26), channel_id=1, source_target_pairs={{1,0},{0,1},{3,2},{2,3},{5,4},{4,5},{7,6},{6,7},{9,8},{8,9},{11,10... | collective-permute-start | bytes 1572872 | tf_op jit(solution)/shard_map/ppermute | solution.py:306
  51.0 25.1 %collective-permute-start.11 = (bf16[256,1024]{1,0:T(8,128)(2,1)}, bf16[256,1024]{1,0:T(8,128)(2,1)S(1)}, u32[]{:S(2)}, u32[]{:S(2)}) collective-permute-start(bf16[256,1024]{1,0:T(8,128)(2,1)} %get-tuple-element.247), channel_id=1, source_target_pairs={{0,4},{2,6},{4,0},{6,2},{8,12},{10,14},{12,8},{14,10},{16,20},{18,... | collective-permute-start | bytes 1572872 | tf_op jit(solution)/shard_map/ppermute | solution.py:303
  52.5 40.8 %collective-permute-start.12 = (bf16[256,1024]{1,0:T(8,128)(2,1)S(1)}, bf16[256,1024]{1,0:T(8,128)(2,1)S(1)}, u32[]{:S(2)}, u32[]{:S(2)}) collective-permute-start(bf16[256,1024]{1,0:T(8,128)(2,1)S(1)} %copy-done.25), channel_id=1, source_target_pairs={{3,0},{2,1},{1,2},{0,3},{7,4},{6,5},{5,6},{4,7},{11,8},{10,9},{9,1... | collective-permute-start | bytes 1572872 | tf_op jit(solution)/shard_map/ppermute | solution.py:306
  66.1 29.0 %collective-permute-start.17 = (bf16[256,1024]{1,0:T(8,128)(2,1)}, bf16[256,1024]{1,0:T(8,128)(2,1)S(1)}, u32[]{:S(2)}, u32[]{:S(2)}) collective-permute-start(bf16[256,1024]{1,0:T(8,128)(2,1)} %get-tuple-element.272), channel_id=1, source_target_pairs={{0,4},{2,6},{4,0},{6,2},{8,12},{10,14},{12,8},{14,10},{16,20},{18,... | collective-permute-start | bytes 1572872 | tf_op jit(solution)/shard_map/ppermute | solution.py:303
  66.7 19.1 %collective-permute-start.13 = (bf16[160,512]{1,0:T(8,128)(2,1)S(1)}, bf16[160,512]{1,0:T(8,128)(2,1)S(1)}, u32[]{:S(2)}, u32[]{:S(2)}) collective-permute-start(bf16[160,512]{1,0:T(8,128)(2,1)S(1)} %get-tuple-element.397), channel_id=1, source_target_pairs={{0,8},{2,10},{4,12},{6,14},{8,16},{10,18},{12,20},{14,22},{16,24},... | collective-permute-start | bytes 491528 | tf_op jit(solution)/shard_map/ppermute | solution.py:346
  68.3 18.8 %collective-permute-start.14 = (bf16[160,512]{1,0:T(8,128)(2,1)S(1)}, bf16[160,512]{1,0:T(8,128)(2,1)S(1)}, u32[]{:S(2)}, u32[]{:S(2)}) collective-permute-start(bf16[160,512]{1,0:T(8,128)(2,1)S(1)} %get-tuple-element.396), channel_id=1, source_target_pairs={{0,16},{2,18},{4,20},{6,22},{8,24},{10,26},{12,28},{14,30},{16,0},... | collective-permute-start | bytes 491528 | tf_op jit(solution)/shard_map/ppermute | solution.py:346
  76.1 17.1 %collective-permute-start.15 = (bf16[160,512]{1,0:T(8,128)(2,1)S(1)}, bf16[160,512]{1,0:T(8,128)(2,1)S(1)}, u32[]{:S(2)}, u32[]{:S(2)}) collective-permute-start(bf16[160,512]{1,0:T(8,128)(2,1)S(1)} %get-tuple-element.395), channel_id=1, source_target_pairs={{0,24},{2,26},{4,28},{6,30},{8,0},{10,2},{12,4},{14,6},{16,8},{18,... | collective-permute-start | bytes 491528 | tf_op jit(solution)/shard_map/ppermute | solution.py:346
  85.9 17.6 %collective-permute-start.16 = (bf16[256,1024]{1,0:T(8,128)(2,1)S(1)}, bf16[256,1024]{1,0:T(8,128)(2,1)S(1)}, u32[]{:S(2)}, u32[]{:S(2)}) collective-permute-start(bf16[256,1024]{1,0:T(8,128)(2,1)S(1)} %add.236), channel_id=1, source_target_pairs={{8,0},{10,2},{12,4},{14,6},{24,16},{26,18},{28,20},{30,22},{1,9},{... | collective-permute-start | bytes 1572872 | tf_op jit(solution)/shard_map/ppermute | solution.py:349
  87.2 19.1 %collective-permute-start.18 = (bf16[256,1024]{1,0:T(8,128)(2,1)}, bf16[256,1024]{1,0:T(8,128)(2,1)S(1)}, u32[]{:S(2)}, u32[]{:S(2)}) collective-permute-start(bf16[256,1024]{1,0:T(8,128)(2,1)} %get-tuple-element.260.refs_0_), channel_id=1, source_target_pairs={{1,0},{0,1},{3,2},{2,3},{5,4},{4,5},{7,6},{6,7},{9,8},{8,9},{11,10... | collective-permute-start | bytes 1572872 | tf_op jit(solution)/shard_map/ppermute | solution.py:306
  93.3 17.3 %collective-permute-start.20 = (bf16[256,1024]{1,0:T(8,128)(2,1)}, bf16[256,1024]{1,0:T(8,128)(2,1)S(1)}, u32[]{:S(2)}, u32[]{:S(2)}) collective-permute-start(bf16[256,1024]{1,0:T(8,128)(2,1)} %get-tuple-element.289), channel_id=1, source_target_pairs={{0,4},{2,6},{4,0},{6,2},{8,12},{10,14},{12,8},{14,10},{16,20},{18,... | collective-permute-start | bytes 1572872 | tf_op jit(solution)/shard_map/ppermute | solution.py:303
  93.9 20.6 %collective-permute-start.19 = (bf16[256,1024]{1,0:T(8,128)(2,1)S(1)}, bf16[256,1024]{1,0:T(8,128)(2,1)S(1)}, u32[]{:S(2)}, u32[]{:S(2)}) collective-permute-start(bf16[256,1024]{1,0:T(8,128)(2,1)S(1)} %add.239), channel_id=1, source_target_pairs={{8,0},{10,2},{12,4},{14,6},{24,16},{26,18},{28,20},{30,22},{1,9},{... | collective-permute-start | bytes 1572872 | tf_op jit(solution)/shard_map/ppermute | solution.py:349
  95.2 30.4 %collective-permute-start.21 = (bf16[256,1024]{1,0:T(8,128)(2,1)S(1)}, bf16[256,1024]{1,0:T(8,128)(2,1)S(1)}, u32[]{:S(2)}, u32[]{:S(2)}) collective-permute-start(bf16[256,1024]{1,0:T(8,128)(2,1)S(1)} %copy-done.24), channel_id=1, source_target_pairs={{3,0},{2,1},{1,2},{0,3},{7,4},{6,5},{5,6},{4,7},{11,8},{10,9},{9,1... | collective-permute-start | bytes 1572872 | tf_op jit(solution)/shard_map/ppermute | solution.py:306
  106.3 38.8 %collective-permute-start.24 = (bf16[256,1024]{1,0:T(8,128)(2,1)S(1)}, bf16[256,1024]{1,0:T(8,128)(2,1)}, u32[]{:S(2)}, u32[]{:S(2)}) collective-permute-start(bf16[256,1024]{1,0:T(8,128)(2,1)S(1)} %add.250), channel_id=1, source_target_pairs={{0,8},{2,10},{4,12},{6,14},{16,24},{18,26},{20,28},{22,30},{9,1},{... | collective-permute-start | bytes 1572872 | tf_op jit(solution)/shard_map/ppermute | solution.py:349
  109.0 36.0 %collective-permute-start.23 = (bf16[256,1024]{1,0:T(8,128)(2,1)}, bf16[256,1024]{1,0:T(8,128)(2,1)}, u32[]{:S(2)}, u32[]{:S(2)}) collective-permute-start(bf16[256,1024]{1,0:T(8,128)(2,1)} %get-tuple-element.302), channel_id=1, source_target_pairs={{0,4},{2,6},{4,0},{6,2},{8,12},{10,14},{12,8},{14,10},{16,20},{18,... | collective-permute-start | bytes 1572872 | tf_op jit(solution)/shard_map/ppermute | solution.py:303
  110.5 34.6 %collective-permute-start.22 = (bf16[256,1024]{1,0:T(8,128)(2,1)S(1)}, bf16[256,1024]{1,0:T(8,128)(2,1)}, u32[]{:S(2)}, u32[]{:S(2)}) collective-permute-start(bf16[256,1024]{1,0:T(8,128)(2,1)S(1)} %add.249), channel_id=1, source_target_pairs={{16,0},{18,2},{20,4},{22,6},{9,25},{11,27},{13,29},{15,31}} | collective-permute-start | bytes 1572872 | tf_op jit(solution)/shard_map/ppermute | solution.py:349
  125.6 33.5 %collective-permute-start.25 = (bf16[256,1024]{1,0:T(8,128)(2,1)}, bf16[256,1024]{1,0:T(8,128)(2,1)S(1)}, u32[]{:S(2)}, u32[]{:S(2)}) collective-permute-start(bf16[256,1024]{1,0:T(8,128)(2,1)} %get-tuple-element.294.refs_2_), channel_id=1, source_target_pairs={{1,0},{0,1},{3,2},{2,3},{5,4},{4,5},{7,6},{6,7},{9,8},{8,9},{11,10... | collective-permute-start | bytes 1572872 | tf_op jit(solution)/shard_map/ppermute | solution.py:306
  139.9 21.1 %collective-permute-start.31 = (bf16[256,1024]{1,0:T(8,128)(2,1)S(1)}, bf16[256,1024]{1,0:T(8,128)(2,1)}, u32[]{:S(2)}, u32[]{:S(2)}) collective-permute-start(bf16[256,1024]{1,0:T(8,128)(2,1)S(1)} %add.255), channel_id=1, source_target_pairs={{0,8},{2,10},{4,12},{6,14},{16,24},{18,26},{20,28},{22,30},{9,1},{... | collective-permute-start | bytes 1572872 | tf_op jit(solution)/shard_map/ppermute | solution.py:349
  145.1 18.0 %collective-permute-start.30 = (bf16[256,1024]{1,0:T(8,128)(2,1)}, bf16[256,1024]{1,0:T(8,128)(2,1)S(1)}, u32[]{:S(2)}, u32[]{:S(2)}) collective-permute-start(bf16[256,1024]{1,0:T(8,128)(2,1)} %get-tuple-element.318), channel_id=1, source_target_pairs={{0,4},{2,6},{4,0},{6,2},{8,12},{10,14},{12,8},{14,10},{16,20},{18,... | collective-permute-start | bytes 1572872 | tf_op jit(solution)/shard_map/ppermute | solution.py:303
  145.1 21.3 %collective-permute-start.29 = (bf16[256,1024]{1,0:T(8,128)(2,1)S(1)}, bf16[256,1024]{1,0:T(8,128)(2,1)}, u32[]{:S(2)}, u32[]{:S(2)}) collective-permute-start(bf16[256,1024]{1,0:T(8,128)(2,1)S(1)} %add.254), channel_id=1, source_target_pairs={{16,0},{18,2},{20,4},{22,6},{9,25},{11,27},{13,29},{15,31}} | collective-permute-start | bytes 1572872 | tf_op jit(solution)/shard_map/ppermute | solution.py:349
  159.2 17.2 %collective-permute-start.35 = (bf16[256,1024]{1,0:T(8,128)(2,1)S(1)}, bf16[256,1024]{1,0:T(8,128)(2,1)S(1)}, u32[]{:S(2)}, u32[]{:S(2)}) collective-permute-start(bf16[256,1024]{1,0:T(8,128)(2,1)S(1)} %copy-done.31), channel_id=1, source_target_pairs={{0,4},{2,6},{4,0},{6,2},{8,12},{10,14},{12,8},{14,10},{16,20},{18,... | collective-permute-start | bytes 1572872 | tf_op jit(solution)/shard_map/ppermute | solution.py:303
  176.4 25.3 %collective-permute-start.39 = (bf16[4,160,512]{2,1,0:T(8,128)(2,1)S(1)}, bf16[4,160,512]{2,1,0:T(8,128)(2,1)}, u32[]{:S(2)}, u32[]{:S(2)}) collective-permute-start(bf16[4,160,512]{2,1,0:T(8,128)(2,1)S(1)} %bitcast_dynamic-update-slice_fusion.keep), channel_id=1, source_target_pairs={{0,4},{2,6},{4,0},{6,2},{8,12},{10,14},{12,8},{14,10},{16,20},{18,... | collective-permute-start | bytes 1966088 | tf_op jit(solution)/shard_map/ppermute | solution.py:303
  176.8 24.9 %collective-permute-start.40 = (bf16[4,160,512]{2,1,0:T(8,128)(2,1)S(1)}, bf16[4,160,512]{2,1,0:T(8,128)(2,1)}, u32[]{:S(2)}, u32[]{:S(2)}) collective-permute-start(bf16[4,160,512]{2,1,0:T(8,128)(2,1)S(1)} %bitcast_dynamic-update-slice_fusion.keep), channel_id=1, source_target_pairs={{0,2},{2,0},{4,6},{6,4},{8,10},{10,8},{12,14},{14,12},{16,18},{18,... | collective-permute-start | bytes 1966088 | tf_op jit(solution)/shard_map/ppermute | solution.py:300
  180.2 18.3 %collective-permute-start.36 = (bf16[256,1024]{1,0:T(8,128)(2,1)S(1)}, bf16[256,1024]{1,0:T(8,128)(2,1)}, u32[]{:S(2)}, u32[]{:S(2)}) collective-permute-start(bf16[256,1024]{1,0:T(8,128)(2,1)S(1)} %add.260), channel_id=1, source_target_pairs={{0,8},{2,10},{4,12},{6,14},{24,16},{26,18},{28,20},{30,22},{1,9},{... | collective-permute-start | bytes 1572872 | tf_op jit(solution)/shard_map/ppermute | solution.py:349
  190.2 18.0 %collective-permute-start.42 = (bf16[256,1024]{1,0:T(8,128)(2,1)S(1)}, bf16[256,1024]{1,0:T(8,128)(2,1)S(1)}, u32[]{:S(2)}, u32[]{:S(2)}) collective-permute-start(bf16[256,1024]{1,0:T(8,128)(2,1)S(1)} %add.272), channel_id=1, source_target_pairs={{0,8},{2,10},{4,12},{6,14},{24,16},{26,18},{28,20},{30,22},{1,9},{... | collective-permute-start | bytes 1572872 | tf_op jit(solution)/shard_map/ppermute | solution.py:349
  191.6 17.6 %collective-permute-start.41 = (bf16[256,1024]{1,0:T(8,128)(2,1)S(1)}, bf16[256,1024]{1,0:T(8,128)(2,1)S(1)}, u32[]{:S(2)}, u32[]{:S(2)}) collective-permute-start(bf16[256,1024]{1,0:T(8,128)(2,1)S(1)} %add.270), channel_id=1, source_target_pairs={{16,8},{18,10},{20,12},{22,14},{9,17},{11,19},{13,21},{15,23}} | collective-permute-start | bytes 1572872 | tf_op jit(solution)/shard_map/ppermute | solution.py:349
  201.7 19.3 %collective-permute-start.45 = (bf16[4,160,512]{2,1,0:T(8,128)(2,1)}, bf16[4,160,512]{2,1,0:T(8,128)(2,1)}, u32[]{:S(2)}, u32[]{:S(2)}) collective-permute-start(bf16[4,160,512]{2,1,0:T(8,128)(2,1)} %collective-permute-done.39.back), channel_id=1, source_target_pairs={{0,2},{2,0},{4,6},{6,4},{8,10},{10,8},{12,14},{14,12},{16,18},{18,... | collective-permute-start | bytes 1966088 | tf_op jit(solution)/shard_map/ppermute | solution.py:300
  201.7 17.4 %collective-permute-start.44 = (bf16[256,1024]{1,0:T(8,128)(2,1)S(1)}, bf16[256,1024]{1,0:T(8,128)(2,1)S(1)}, u32[]{:S(2)}, u32[]{:S(2)}) collective-permute-start(bf16[256,1024]{1,0:T(8,128)(2,1)S(1)} %add.275), channel_id=1, source_target_pairs={{0,8},{2,10},{4,12},{6,14},{24,16},{26,18},{28,20},{30,22},{1,9},{... | collective-permute-start | bytes 1572872 | tf_op jit(solution)/shard_map/ppermute | solution.py:349
  227.3 28.9 %collective-permute-start.50 = (bf16[256,1024]{1,0:T(8,128)(2,1)S(1)}, bf16[256,1024]{1,0:T(8,128)(2,1)S(1)}, u32[]{:S(2)}, u32[]{:S(2)}) collective-permute-start(bf16[256,1024]{1,0:T(8,128)(2,1)S(1)} %select_select_fusion.refs_0_), channel_id=1, source_target_pairs={{0,2},{2,0},{4,6},{6,4},{8,10},{10,8},{12,14},{14,12},{16,18},{18,... | collective-permute-start | bytes 1572872 | tf_op jit(solution)/shard_map/ppermute | solution.py:500
  239.1 23.3 %collective-permute-start.47 = (bf16[256,1024]{1,0:T(8,128)(2,1)S(1)}, bf16[256,1024]{1,0:T(8,128)(2,1)S(1)}, u32[]{:S(2)}, u32[]{:S(2)}) collective-permute-start(bf16[256,1024]{1,0:T(8,128)(2,1)S(1)} %select_select_fusion.1.refs_0_), channel_id=1, source_target_pairs={{0,2},{2,0},{4,6},{6,4},{8,10},{10,8},{12,14},{14,12},{16,18},{18,... | collective-permute-start | bytes 1572872 | tf_op jit(solution)/shard_map/ppermute | solution.py:500
  (54 other events, 757.7 us)

commit v3 on v2

v3 whole, which is shorter than its diff:
```python
import functools

import jax
import jax.numpy as jnp
from jax import lax
from jax.experimental import pallas as pl
from jax.experimental.pallas import tpu as pltpu
from jax.sharding import PartitionSpec as P

BLK = 128
QUARTER = 128
VMEM = 56 * 2**20
SLOTS = 5
COL_CHUNKS = 2


DECAY_RATE = 0.75
DAMPING = 0.03

BF16 = jnp.bfloat16
F32 = jnp.float32

SMALL = pl.CostEstimate(flops=1, bytes_accessed=1, transcendentals=0)


def pick_kernel(n_picks, which_ref, acts, cotan, ours, theirs):
    is_act = which_ref[n_picks] == 0
    ours[...] = jnp.where(is_act, acts[...], cotan[...])
    theirs[...] = jnp.where(is_act, cotan[...], acts[...])


def pick(acts, cotan, block_ids, core):
    n_picks, width = block_ids.shape[0], acts.shape[1]
    chosen = pl.BlockSpec((BLK, width), lambda i, which: (which[i], 0))
    out = pl.BlockSpec((BLK, width), lambda i, which: (i, 0))
    return pl.pallas_call(
        functools.partial(pick_kernel, n_picks),
        grid_spec=pltpu.PrefetchScalarGridSpec(
            num_scalar_prefetch=1, grid=(n_picks,), in_specs=[chosen] * 2, out_specs=[out] * 2
        ),
        out_shape=[jax.ShapeDtypeStruct((n_picks * BLK, width), BF16)] * 2,
        compiler_params=pltpu.CompilerParams(vmem_limit_bytes=VMEM),
        cost_estimate=SMALL,
    )(jnp.concatenate([block_ids, jnp.reshape(core, (1,))]).astype(jnp.int32), acts, cotan)


def pack_upper(full):
    q = QUARTER
    second = jnp.concatenate([full[q : 2 * q, q:], full[3 * q :, 3 * q :]], axis=1)
    third = full[2 * q : 3 * q, 2 * q :]
    third = jnp.concatenate([third[: q // 2], third[q // 2 :]], axis=1)
    return jnp.concatenate([full[:q], second, third], axis=0)


def term_kernel(scales, place_ref, ours, theirs, keep, away):
    total = 0.0
    for rows in (ours[...], theirs[...]):
        total = total + lax.dot_general(
            rows, rows, (((0,), (0,)), ((), ())), preferred_element_type=F32
        )
    scale = jnp.where(place_ref[0] == 0, scales[0], scales[1]).astype(F32)
    packed = pack_upper(total * scale)
    half = packed.shape[0] // 2
    low = place_ref[1] == 0
    keep[0] = jnp.where(low, packed[:half], packed[half:]).astype(BF16)
    away[0] = jnp.where(low, packed[half:], packed[:half]).astype(BF16)


def terms(place, ours, theirs, size, scales):
    rows, width = ours.shape
    blocks, half = width // size, 5 * QUARTER // 4
    strip = pl.BlockSpec((rows, size), lambda b, place: (0, b))
    out = pl.BlockSpec((1, half, size), lambda b, place: (b, 0, 0))
    return pl.pallas_call(
        functools.partial(term_kernel, scales),
        grid_spec=pltpu.PrefetchScalarGridSpec(
            num_scalar_prefetch=1, grid=(blocks,), in_specs=[strip] * 2, out_specs=[out] * 2
        ),
        out_shape=[jax.ShapeDtypeStruct((blocks, half, size), BF16)] * 2,
        compiler_params=pltpu.CompilerParams(vmem_limit_bytes=VMEM),
        cost_estimate=SMALL,
    )(place, ours, theirs)


def unpack_upper(packed):
    q = QUARTER
    tiles = {}
    for j in range(4):
        tiles[0, j] = packed[:q, j * q : (j + 1) * q]
    for j in range(1, 4):
        tiles[1, j] = packed[q : 2 * q, (j - 1) * q : j * q]
    tiles[3, 3] = packed[q : 2 * q, 3 * q :]
    third = jnp.concatenate([packed[2 * q :, : 2 * q], packed[2 * q :, 2 * q :]], axis=0)
    tiles[2, 2], tiles[2, 3] = third[:, :q], third[:, q:]
    return [[tiles[i, j] if j >= i else tiles[j, i].T for j in range(4)] for i in range(4)]


def factor_kernel(place_ref, low, high, low_sib, high_sib, *refs):
    for kind, (factor, basis, new, eig) in enumerate(zip(refs[0:2], refs[2:4], refs[4:6], refs[6:8])):
        here = place_ref[1] == kind
        halves = [jnp.where(here, low[0], low_sib[0]), jnp.where(here, high[0], high_sib[0])]
        rows = unpack_upper(jnp.concatenate(halves, axis=0).astype(F32))
        q = QUARTER
        for i in range(4):
            for j in range(4):
                at = (0, pl.ds(i * q, q), pl.ds(j * q, q))
                new[at] = DECAY_RATE * factor[at] + (1.0 - DECAY_RATE) * rows[i][j]
        vectors = basis[0]
        rest = new[0]
        product = 0.0
        for _ in range(3):
            part = rest.astype(BF16)
            rest = rest - part.astype(F32)
            product = product + jnp.dot(part, vectors, preferred_element_type=F32)
        eig[0] = jnp.sum(vectors.astype(F32) * product, axis=0, keepdims=True)


def update_factors(place, halves, factors, basis_in, basis_out):
    blocks, size, _ = basis_in.shape

    def local(b, place):
        return (b, 0, 0)

    square = pl.BlockSpec((1, size, size), local)
    narrow = pl.BlockSpec((1, halves[0].shape[1], size), local)
    line = pl.BlockSpec((1, 1, size), local)
    return pl.pallas_call(
        factor_kernel,
        grid_spec=pltpu.PrefetchScalarGridSpec(
            num_scalar_prefetch=1,
            grid=(blocks,),
            in_specs=[narrow] * 4
            + [square] * 3
            + [pl.BlockSpec((1, size, size), lambda b, place: (place[0] + b, 0, 0))],
            out_specs=[square, square, line, line],
        ),
        out_shape=[jax.ShapeDtypeStruct((blocks, size, size), F32)] * 2
        + [jax.ShapeDtypeStruct((blocks, 1, size), F32)] * 2,
        compiler_params=pltpu.CompilerParams(vmem_limit_bytes=VMEM),
        cost_estimate=SMALL,
    )(place, *halves, *factors, basis_in, basis_out)


def tail_kernel(n_parts, place_ref, *refs):
    parts, (basis, outer, eig_in, eig_out) = refs[:n_parts], refs[n_parts : n_parts + 4]
    out, whole = refs[-2:]
    sharers = len(parts)
    rows = parts[0].shape[0]
    me = place_ref[1]
    for step, part in enumerate(parts):
        spot = lax.rem(me - step + sharers, sharers)
        whole[pl.ds(pl.multiple_of(spot * rows, rows), rows), :] = part[...]
    right = jnp.dot(whole[...], basis[0], preferred_element_type=F32).astype(BF16)
    inner = lax.dot_general(outer[0], right, (((0,), (0,)), ((), ())), preferred_element_type=F32)
    column = jnp.broadcast_to(eig_out[0], (QUARTER, eig_out.shape[2])).T[:, :1]
    scaled = (inner / (column * eig_in[0] + DAMPING)).astype(BF16)
    mine = outer[0, pl.ds(pl.multiple_of(me * rows, rows), rows), :]
    upper = jnp.dot(mine, scaled, preferred_element_type=F32).astype(BF16)
    out[...] = lax.dot_general(
        upper, basis[0], (((1,), (1,)), ((), ())), preferred_element_type=F32
    ).astype(BF16)


def tail(place, parts, basis_in, basis_out, eig_in, eig_out, chunk, filled):
    blocks, size, _ = basis_in.shape
    rows, cols = parts[0].shape
    each = cols // size
    strip = pl.BlockSpec((rows, size), lambda b, place: (0, b))
    in_specs = [strip] * len(parts) + [
        pl.BlockSpec((1, size, size), lambda b, place: (chunk * each + b, 0, 0)),
        pl.BlockSpec((1, size, size), lambda b, place: (place[0], 0, 0)),
        pl.BlockSpec((1, 1, size), lambda b, place: (chunk * each + b, 0, 0)),
        pl.BlockSpec((1, 1, size), lambda b, place: (place[2], 0, 0)),
    ]
    args = [place, *parts, basis_in, basis_out, eig_in, eig_out]
    aliases = {}
    if filled is not None:
        in_specs.append(pl.BlockSpec(memory_space=pl.ANY))
        aliases = {len(args): 0}
        args.append(filled)
    return pl.pallas_call(
        functools.partial(tail_kernel, len(parts)),
        grid_spec=pltpu.PrefetchScalarGridSpec(
            num_scalar_prefetch=1,
            grid=(each,),
            in_specs=in_specs,
            out_specs=pl.BlockSpec((rows, size), lambda b, place: (0, chunk * each + b)),
            scratch_shapes=[pltpu.VMEM((size, size), BF16)],
        ),
        out_shape=jax.ShapeDtypeStruct((rows, blocks * size), BF16),
        input_output_aliases=aliases,
        compiler_params=pltpu.CompilerParams(vmem_limit_bytes=VMEM),
        cost_estimate=pl.CostEstimate(
            flops=each * 6 * size**3, bytes_accessed=4 * each * size**2, transcendentals=0
        ),
    )(*args)


def turn_kernel(which_ref, block, *outs):
    del which_ref
    step = pl.program_id(0)
    for n, out in enumerate(outs):

        @pl.when((step == n) | ((n == 4) & (step >= 2)))
        def _(out=out):
            out[...] = block[...].T


def turned(rows, which, n_rows):
    tokens, _ = rows.shape
    one = pl.BlockSpec((n_rows, tokens), lambda i, which: (0, 0))
    return pl.pallas_call(
        turn_kernel,
        grid_spec=pltpu.PrefetchScalarGridSpec(
            num_scalar_prefetch=1,
            grid=(4,),
            in_specs=[pl.BlockSpec((tokens, n_rows), lambda i, which: (0, which[i]))],
            out_specs=[one] * 4
            + [pl.BlockSpec((n_rows, tokens), lambda i, which: (jnp.clip(i - 2, 0, 1), 0))],
        ),
        out_shape=[jax.ShapeDtypeStruct((n_rows, tokens), BF16)] * 4
        + [jax.ShapeDtypeStruct((2 * n_rows, tokens), BF16)],
        compiler_params=pltpu.CompilerParams(vmem_limit_bytes=VMEM),
        cost_estimate=SMALL,
    )(jnp.stack(which).astype(jnp.int32), rows)


def product_kernel(counts, n_outs, *refs):
    n_left = sum(counts)
    halves = refs[: counts[0]], refs[counts[0] : n_left]
    right, outs, left = refs[n_left : n_left + 2], refs[n_left + 2 : -1], refs[-1]
    step = pl.program_id(0)
    tokens = right[0].shape[0]

    @pl.when(step == 0)
    def _():
        for half, pieces in enumerate(halves):
            row = 0
            for piece in pieces:
                left[row : row + piece.shape[0], half * tokens : (half + 1) * tokens] = piece[...]
                row += piece.shape[0]

    total = jnp.dot(left[:, :tokens], right[0][...], preferred_element_type=F32)
    total = total + jnp.dot(left[:, tokens:], right[1][...], preferred_element_type=F32)
    chunks = len(outs) // n_outs
    rows = left.shape[0] // n_outs
    each = pl.num_programs(0) // chunks
    for n in range(chunks):

        @pl.when(step // each == n)
        def _(n=n):
            for at in range(n_outs):
                outs[at * chunks + n][...] = total[at * rows : (at + 1) * rows].astype(BF16)


def products(halves, n_outs, rows, chunks):
    tokens, width = rows[0].shape
    n_rows = sum(piece.shape[0] for piece in halves[0])
    tile = 512
    each = width // chunks // tile
    strip = pl.BlockSpec((tokens, tile), lambda i: (0, i))
    outs = pl.pallas_call(
        functools.partial(product_kernel, [len(half) for half in halves], n_outs),
        grid=(width // tile,),
        in_specs=[pl.BlockSpec(p.shape, lambda i: (0, 0)) for half in halves for p in half] + [strip] * 2,
        out_specs=[
            pl.BlockSpec((n_rows // n_outs, tile), lambda i, n=n: (0, jnp.clip(i - n * each, 0, each - 1)))
            for _ in range(n_outs)
            for n in range(chunks)
        ],
        out_shape=[jax.ShapeDtypeStruct((n_rows // n_outs, width // chunks), BF16)] * (n_outs * chunks),
        scratch_shapes=[pltpu.VMEM((n_rows, 2 * tokens), BF16)],
        compiler_params=pltpu.CompilerParams(vmem_limit_bytes=VMEM),
        cost_estimate=SMALL,
    )(*halves[0], *halves[1], *rows)
    return [outs[m * chunks : (m + 1) * chunks] for m in range(n_outs)]


def per_device(acts, cotan, block_ids, basis_in, basis_out, act_factor, grad_factor):
    n_dp = lax.axis_size("dp")
    n_worker = lax.axis_size("worker")
    d = lax.axis_index("dp")
    w = lax.axis_index("worker")
    core, x = d % 2, (d // 2) % 2
    n_z = n_dp // 4
    pool_rows, width = acts.shape
    local_blocks, block_size, _ = basis_in.shape
    model_width = basis_out.shape[0] * block_size
    samples = block_ids.shape[0] * BLK * n_dp
    tokens = pool_rows * n_dp
    rows_dev = model_width // n_dp
    z_per_worker = n_z // n_worker
    cols = width // COL_CHUNKS if width >= 1024 else width
    both = ("dp", "worker")

    def swap_core(v):
        return lax.ppermute(v, "dp", [(i, i ^ 1) for i in range(n_dp)])

    def swap_x(v):
        return lax.ppermute(v, "dp", [(i, i ^ 2) for i in range(n_dp)])

    def from_worker(v, step, flip):
        return lax.ppermute(
            v,
            both,
            [
                ((i ^ flip) * n_worker + (j + step) % n_worker, i * n_worker + j)
                for i in range(n_dp)
                for j in range(n_worker)
            ],
        )

    def place(owner, j):
        return owner * z_per_worker + (j if owner < n_worker // 2 else z_per_worker - 1 - j)

    z = d // 4
    starts = list(range(0, width, cols))
    shards = [(0, j) for j in range(z_per_worker)]
    shards += [(step, j) for j in range(z_per_worker) for step in range(1, n_worker)]

    def hops_of(step, j):
        hops = []
        size = 1
        while size < n_z:
            moves = []
            for i in range(n_worker):
                end = place((i + step) % n_worker, j)
                for low in range(0, n_z, 2 * size):
                    heads = [min(max(end, at), at + size - 1) for at in (low, low + size)]
                    to = min(max(end, low), low + 2 * size - 1)
                    moves.append((i, sum(heads) - to, to))
            hops.append(moves)
            size *= 2
        return hops

    def links(moves):
        found = set()
        for i, a, b in moves:
            ahead = 1 if b > a else -1
            found.update((i, at, at + ahead) for at in range(a, b, ahead))
        return found

    def swap_z(v, bit):
        return lax.ppermute(v, "dp", [(i, i ^ (4 * bit)) for i in range(n_dp)])

    def hop(v, moves):
        pairs = [((a * 4 + r) * n_worker + i, (b * 4 + r) * n_worker + i) for i, a, b in moves for r in range(4)]
        return lax.ppermute(v, both, pairs)

    def piece(j, at, flip):
        part = jnp.where(w < n_worker // 2, j, z_per_worker - 1 - j)
        x_to = x if at else 1 - x
        core_to = 1 - core if flip else core
        return (part * 2 + x_to) * 2 + core_to

    chunks = range(len(starts))
    used = {}

    def hold(stage):
        used[stage] = used.get(stage, 0) + 1

    x_stage, z_stage, busy = {}, {}, set()
    y_items = [(step, j, at, flip) for step, j in shards if step for at in range(2) for flip in range(2)]
    y_stage = {item: max(0, at - 1) for at, item in enumerate(y_items)}
    for stage in y_stage.values():
        hold(stage)
    product_stage = {(0, 0, 0): 0, (0, 0, 1): 0}
    clock = 0
    for step, j in shards:
        if step == 0 and j:
            product_stage[0, j, 0] = product_stage[0, j, 1] = clock
        if step:
            here, there = y_stage[step, j, 0, 1] + 1, y_stage[step, j, 1, 1] + 1
            product_stage[step, j, 0] = there if there <= clock else max(here, clock - 1)
            product_stage[step, j, 1] = there
            clock = max(clock, product_stage[step, j, 0])
        for n in chunks:
            clock += 1
            x_stage[step, j, n] = clock
            hold(clock)
    z_bits = [2**bit for bit in range((n_z - 1).bit_length())]
    hold(1)
    scatter = [1 + at for at in range(len(z_bits))]
    across = scatter[-1] + 1
    gather = [across + 1 + at for at in range(len(z_bits))]
    between = gather[-1] + 1
    for stage in range(1, between + 1):
        hold(stage)
    fresh = between + 1
    while fresh in product_stage.values():
        fresh += 1
    hold(fresh + 1)
    for n_hop in range(len(z_bits)):
        for step, j, n in x_stage:
            ready = max(x_stage[step, j, n], product_stage[step, j, 1])
            clock = (z_stage[step, j, n, n_hop - 1] if n_hop else ready) + 1
            moves = links(hops_of(step, j)[n_hop])
            while used.get(clock, 0) >= SLOTS or any((clock, link) in busy for link in moves):
                clock += 1
            busy.update((clock, link) for link in moves)
            z_stage[step, j, n, n_hop] = clock
            hold(clock)
    last = max(*z_stage.values(), fresh + 1)

    my_start = d * rows_dev
    block = my_start // block_size
    flags = jnp.stack([w * local_blocks, core, x]).astype(jnp.int32)
    env = {"acts": acts, "cotan": cotan}
    done = {}

    def turn(rows, j):
        which = [piece(j, at, flip) for flip in range(2) for at in range(2)]
        *single, both_rows = turned(rows, which, rows_dev)
        found = {("p", j, at, flip): single[2 * flip + at] for flip in range(2) for at in range(2)}
        return {**found, ("p", j): both_rows}

    def in_order(bit, mine, theirs):
        return jnp.where(bit == 0, jnp.stack([mine, theirs]), jnp.stack([theirs, mine]))

    for stage in range(last + 1):
        if stage:
            keys = sorted(env, key=str)
            env = dict(zip(keys, lax.optimization_barrier(tuple(env[k] for k in keys))))
        joined = {}
        if stage == 0:
            joined["acts_sib"] = swap_core(acts)
            env.update(turn(cotan, 0))
            ours, theirs = pick(acts, cotan, block_ids, core)
            scales = (1.0 / samples, tokens / samples)
            keep, away = terms(flags[1:], ours, swap_core(theirs), block_size, scales)
            away = swap_x(away)
            joined["c", 0] = swap_core(env.pop(("p", 0)))
        if stage == 1:
            for j in range(1, z_per_worker):
                found = turn(env["cotan"], j)
                joined["c", j] = swap_core(found.pop(("p", j)))
                joined.update(found)
        for (step, j, at, flip), when in y_stage.items():
            if when == stage:
                joined["c", step, j, at, flip] = from_worker(env["p", j, at, flip], step, flip)
        for (step, j, n), when in x_stage.items():
            if when == stage:
                joined["got", step, j, n] = swap_x(env.pop(("out", step, j, n)))
        for (step, j, n, at), when in z_stage.items():
            if when == stage:
                joined["hop", step, j, n] = hop(env["acc", step, j, n], hops_of(step, j)[at])

        for at, when in enumerate(scatter):
            if stage == when:
                bit = z // z_bits[at] % 2
                parts = env["keep"].reshape(2, -1, block_size)
                there = lax.dynamic_index_in_dim(parts, 1 - bit, 0, keepdims=False)
                here = lax.dynamic_index_in_dim(parts, bit, 0, keepdims=False)
                joined["keep"] = here + swap_z(there, z_bits[at])
        if stage == across:
            joined["keep"] = in_order(x, env["keep"], swap_x(env["keep"]))[None]
        for at, when in enumerate(gather):
            if stage == when:
                far = z_bits[-1 - at]
                joined["keep"] = in_order(z // far % 2, env["keep"], swap_z(env["keep"], far))
                joined["keep"] = joined["keep"].reshape(-1, *env["keep"].shape[1:])
        if stage == between:
            full = jnp.swapaxes(env["keep"], 0, 1).reshape(2, local_blocks, -1, block_size)
            joined["low"], joined["high"] = full[0], full[1]
            joined["other"] = swap_core(env["keep"])
            joined.pop("keep", None)
        if stage == fresh:
            full = jnp.swapaxes(env.pop("other"), 0, 1).reshape(2, local_blocks, -1, block_size)
            act_new, grad_new, joined["eig_in"], eig_local = update_factors(
                flags,
                [env.pop("low"), env.pop("high"), full[0], full[1]],
                (act_factor, grad_factor),
                basis_in,
                basis_out,
            )
            joined["eigs"] = eig_local
            done["factors"] = act_new, grad_new
        if stage == fresh + 1:
            eigs = [env["eigs"]] + [from_worker(env["eigs"], step, 0) for step in range(1, n_worker)]
            joined["eigs"] = jnp.concatenate(eigs, axis=0)

        for step, j in shards:
            due = [at for at in range(2) if product_stage[step, j, at] == stage]
            if due:
                known = {**env, **joined} if stage == 0 else env
                if step == 0:
                    halves = [[known["p", j, at, 0] for at in range(2)], [known["c", j]]]
                else:
                    halves = [[known["c", step, j, at, flip] for at in due] for flip in range(2)]
                found = products(halves, len(due), (known["acts"], known["acts_sib"]), len(starts))
                for at, outs in zip(due, found):
                    for n in chunks:
                        joined["mine" if at else "out", step, j, n] = outs[n]
        if stage == 0:
            keep, joined["out", 0, 0, 0] = lax.optimization_barrier((keep, joined["out", 0, 0, 0]))
            joined["keep"] = keep + away
        env.update(joined)
        for step, j, n in x_stage:
            mine, got, acc = ("mine", step, j, n), ("got", step, j, n), ("acc", step, j, n)
            if mine in env and got in env:
                env[acc] = env.pop(mine) + env.pop(got)
            if ("hop", step, j, n) in env:
                env[acc] = env[acc] + env.pop(("hop", step, j, n))
        for n in chunks:
            if stage == max(z_stage[step, j, n, len(z_bits) - 1] for step, j in shards):
                total = None
                for step, j in shards:
                    ends = jnp.array([place((i + step) % n_worker, j) for i in range(n_worker)], jnp.int32)
                    acc = env.pop(("acc", step, j, n))
                    total = acc if total is None else jnp.where(ends[w] == z, acc, total)
                done[n] = total

    act_new, grad_new = done["factors"]
    eig_in, eig_out = env["eig_in"], env["eigs"]
    held = (block // local_blocks - w) % n_worker * local_blocks + block % local_blocks

    sharers = block_size // rows_dev
    spot = jnp.stack([block, d % sharers, held]).astype(jnp.int32)
    precond = None
    for n in range(len(starts)):
        parts = [done[n]]
        for step in range(1, sharers):
            pairs = [(i, i // sharers * sharers + (i + step) % sharers) for i in range(n_dp)]
            parts.append(lax.ppermute(parts[0], "dp", pairs))
        precond = tail(spot, parts, basis_in, basis_out, eig_in, eig_out, n, precond)
    return precond, act_new, grad_new


def solution(mesh):
    return jax.shard_map(
        per_device,
        mesh=mesh,
        in_specs=(
            P("dp", "worker"),
            P("dp", "worker"),
            P("dp"),
            P("worker", None, None),
            P(),
            P("worker", None, None),
            P("worker", None, None),
        ),
        out_specs=(P("dp", "worker"), P("worker", None, None), P("worker", None, None)),
        check_vma=False,
    )
```

time: 270 us -> 284 us (1.052)
  waiting for transfers between devices: 69.1 us -> 101 us
  starting transfers between devices: 78.3 us -> 61.7 us
  Pallas kernels: 85.9 us -> 82.3 us
    ppermute x22 -> x20, waiting for transfers between devices: 32.3 us -> 74.6 us  [the longest x16 48.8 us: hop(): return lax.ppermute(v, both, pairs)]
    ppermute x22 -> x20, starting transfers between devices: 53.8 us -> 37.4 us  [the longest x16 30.2 us: hop(): return lax.ppermute(v, both, pairs)]
    ppermute x9, waiting for transfers between devices: 26.3 us -> 10.5 us  [from_worker(): lax.ppermute(v, both, [((i ^ flip) * n_worker + (j + step) % n_worker, i...]
    ppermute x10, waiting for transfers between devices: 10.5 us -> 15.7 us  [swap_x(): return lax.ppermute(v, 'dp', [(i, i ^ 2) for i in range(n_dp)])]
    pallas_call x6 -> x5, Pallas kernels: 45.4 us -> 40.8 us  [products(): pl.pallas_call(functools.partial(product_kernel, [len(half) for half in h...]
  transfers between devices with their start and end apart: 51 -> 46, of which waited for: 17 -> 20; matrix products, arithmetic and copies ran while one was open for 11% -> 10% of each run, Pallas kernels for 30% -> 25%
where the time goes in v3:
time: 284 us; the launch traced here: 281 us
  waiting for transfers between devices  101 us (36%)
  Pallas kernels  82.3 us (29%)
  starting transfers between devices  61.7 us (22%)
  other arithmetic  24.6 us (9%)
  local copies, waits for them, and re-layouts  8.56 us (3%)
  between operations  3.61 us (1%)
    ppermute x16, waiting for transfers between devices, hop(): return lax.ppermute(v, both, pairs)  48.8 us
    pallas_call x5, Pallas kernels, products(): pl.pallas_call(functools.partial(product_kernel, [len(half) for half in h...  40.8 us
    ppermute x16, starting transfers between devices, hop(): return lax.ppermute(v, both, pairs)  30.2 us
    ppermute x4, waiting for transfers between devices, swap_z(): return lax.ppermute(v, 'dp', [(i, i ^ 4 * bit) for i in range(n_dp)])  25.8 us
    ppermute x10, waiting for transfers between devices, swap_x(): return lax.ppermute(v, 'dp', [(i, i ^ 2) for i in range(n_dp)])  15.7 us
    ppermute x9, starting transfers between devices, from_worker(): lax.ppermute(v, both, [((i ^ flip) * n_worker + (j + step) % n_worker, i...  13.7 us
    pallas_call x1, Pallas kernels, update_factors(): pl.pallas_call(factor_kernel, grid_spec=pltpu.PrefetchScalarGridSpec(num_...  11.6 us
    pallas_call x2, Pallas kernels, tail(): pl.pallas_call(functools.partial(tail_kernel, len(parts)), grid_spec=pltp...  10.7 us
  transfers between devices with their start and end apart: 46, of which 20 were waited for; matrix products, arithmetic and copies ran while one was open for 10% of the time, Pallas kernels for 25%

profile of v3, /device:TPU:12, one launch (start us, length us, event | category | flops | bytes accessed | tf_op | source)
XLA Modules:
  0.0 281.4 jit_solution(18395519697242386984)
XLA Ops:
  2.1 3.3 %shard_map.150 = (bf16[256,2048]{1,0:T(8,128)(2,1)}, bf16[256,2048]{1,0:T(8,128)(2,1)}) custom-call(s32[3]{0:T(128)} %get-tuple-element.365.which_ref, bf16[1024,2048]{1,0:T(8,128)(2,1)} %refs_2_.4, bf16[1024,2048]{1,0:T(8,128)(2,1)} %block.2), custom_call_target="tpu_custom_call" | custom-call | flops 1 | bytes 1 | tf_op jit(solution)/shard_map/pallas_call | solution.py:36
  6.4 5.3 %shard_map.148 = (bf16[256,1024]{1,0:T(8,128)(2,1)}, bf16[256,1024]{1,0:T(8,128)(2,1)}, bf16[256,1024]{1,0:T(8,128)(2,1)}, bf16[256,1024]{1,0:T(8,128)(2,1)}, bf16[512,1024]{1,0:T(8,128)(2,1)}) custom-call(s32[4]{0:T(128)} %get-tuple-element.363.which_ref, bf16[1024,2048]{1,0:T(8,128)(2,1)} %block.2), custom_call_target="tpu_custom_call" | custom-call | flops 1 | bytes 1 | tf_op jit(solution)/shard_map/pallas_call | solution.py:212
  13.4 5.2 %shard_map.151 = (bf16[4,160,512]{2,1,0:T(8,128)(2,1)}, bf16[4,160,512]{2,1,0:T(8,128)(2,1)}) custom-call(s32[2]{0:T(128)} %pad_add_fusion.2.place_ref, bf16[256,2048]{1,0:T(8,128)(2,1)} %get-tuple-element.187.ours, bf16[256,2048]{1,0:T(8,128)(2,1)} %copy-done.6), custom_call_target="tpu_custom_call" | custom-call | flops 1 | bytes 1 | tf_op jit(solution)/shard_map/pallas_call | solution.py:74
  22.6 9.1 %shard_map.149 = (bf16[256,1024]{1,0:T(8,128)(2,1)}, bf16[256,1024]{1,0:T(8,128)(2,1)}, bf16[256,1024]{1,0:T(8,128)(2,1)}, bf16[256,1024]{1,0:T(8,128)(2,1)}) custom-call(bf16[256,1024]{1,0:T(8,128)(2,1)} %get-tuple-element.182.refs_0_, bf16[256,1024]{1,0:T(8,128)(2,1)} %get-tuple-element.202.refs_1_, bf16[512,1024]{1,0:T(8,128)(2,1)} %copy-done.5, ...), custom_call_target="tpu_custom_call" | custom-call | flops 1 | bytes 1 | tf_op jit(solution)/shard_map/pallas_call | solution.py:262
  31.7 4.2 %collective-permute-done.5 = bf16[4,160,512]{2,1,0:T(8,128)(2,1)S(1)} collective-permute-done((bf16[4,160,512]{2,1,0:T(8,128)(2,1)}, bf16[4,160,512]{2,1,0:T(8,128)(2,1)S(1)}, u32[]{:S(2)}, u32[]{:S(2)}) %collective-permute-start.5) | collective-permute-done | bytes 655392 | tf_op jit(solution)/shard_map/ppermute | solution.py:300
  36.1 8.4 %collective-permute-done.2.refs_2_ = bf16[256,1024]{1,0:T(8,128)(2,1)S(1)} collective-permute-done((bf16[256,1024]{1,0:T(8,128)(2,1)S(1)}, bf16[256,1024]{1,0:T(8,128)(2,1)S(1)}, u32[]{:S(2)}, u32[]{:S(2)}) %collective-permute-start.2) | collective-permute-done | bytes 524320 | tf_op jit(solution)/shard_map/ppermute | solution.py:303
  44.6 5.3 %shard_map.152 = (bf16[256,1024]{1,0:T(8,128)(2,1)}, bf16[256,1024]{1,0:T(8,128)(2,1)}, bf16[256,1024]{1,0:T(8,128)(2,1)}, bf16[256,1024]{1,0:T(8,128)(2,1)}, bf16[512,1024]{1,0:T(8,128)(2,1)}) custom-call(s32[4]{0:T(128)} %get-tuple-element.364.which_ref, bf16[1024,2048]{1,0:T(8,128)(2,1)} %block.2), custom_call_target="tpu_custom_call" | custom-call | flops 1 | bytes 1 | tf_op jit(solution)/shard_map/pallas_call | solution.py:212
  52.0 8.4 %collective-permute-done.9 = bf16[320,512]{1,0:T(8,128)(2,1)S(1)} collective-permute-done((bf16[320,512]{1,0:T(8,128)(2,1)S(1)}, bf16[320,512]{1,0:T(8,128)(2,1)S(1)}, u32[]{:S(2)}, u32[]{:S(2)}) %collective-permute-start.9) | collective-permute-done | bytes 327712 | tf_op jit(solution)/shard_map/ppermute | solution.py:344
  60.4 4.7 %collective-permute-done.6 = bf16[256,1024]{1,0:T(8,128)(2,1)} collective-permute-done((bf16[256,1024]{1,0:T(8,128)(2,1)}, bf16[256,1024]{1,0:T(8,128)(2,1)}, u32[]{:S(2)}, u32[]{:S(2)}) %collective-permute-start.6) | collective-permute-done | bytes 524320 | tf_op jit(solution)/shard_map/ppermute | solution.py:300
  69.7 2.7 collective-permute-start.13
  72.3 9.1 %shard_map.153 = (bf16[256,1024]{1,0:T(8,128)(2,1)}, bf16[256,1024]{1,0:T(8,128)(2,1)}, bf16[256,1024]{1,0:T(8,128)(2,1)}, bf16[256,1024]{1,0:T(8,128)(2,1)}) custom-call(bf16[256,1024]{1,0:T(8,128)(2,1)} %get-tuple-element.240.refs_0_, bf16[256,1024]{1,0:T(8,128)(2,1)} %get-tuple-element.277.refs_1_, bf16[512,1024]{1,0:T(8,128)(2,1)} %copy-done.4, ...), custom_call_target="tpu_custom_call" | custom-call | flops 1 | bytes 1 | tf_op jit(solution)/shard_map/pallas_call | solution.py:262
  87.3 4.5 %collective-permute-start.16 = (bf16[256,1024]{1,0:T(8,128)(2,1)S(1)}, bf16[256,1024]{1,0:T(8,128)(2,1)}, u32[]{:S(2)}, u32[]{:S(2)}) collective-permute-start(bf16[256,1024]{1,0:T(8,128)(2,1)S(1)} %copy-done.10), channel_id=1, source_target_pairs={{1,0},{0,1},{3,2},{2,3},{5,4},{4,5},{7,6},{6,7},{9,8},{8,9},{11,10... | collective-permute-start | bytes 1572872 | tf_op jit(solution)/shard_map/ppermute | solution.py:303
  93.2 9.1 %shard_map.154 = (bf16[256,1024]{1,0:T(8,128)(2,1)}, bf16[256,1024]{1,0:T(8,128)(2,1)}, bf16[256,1024]{1,0:T(8,128)(2,1)}, bf16[256,1024]{1,0:T(8,128)(2,1)}) custom-call(bf16[256,1024]{1,0:T(8,128)(2,1)} %copy-done.8, bf16[256,1024]{1,0:T(8,128)(2,1)} %copy-done.13, bf16[256,1024]{1,0:T(8,128)(2,1)} %copy-done.9, bf16[256,1024]{1,0:T(8,128)(2,1)} %copy-done.18, ...), custom_call_target="tpu_custom_call" | custom-call | flops 1 | bytes 1 | tf_op jit(solution)/shard_map/pallas_call | solution.py:262
  102.3 2.5 collective-permute-done.17
  106.4 4.5 %collective-permute-start.18 = (bf16[256,1024]{1,0:T(8,128)(2,1)S(1)}, bf16[256,1024]{1,0:T(8,128)(2,1)}, u32[]{:S(2)}, u32[]{:S(2)}) collective-permute-start(bf16[256,1024]{1,0:T(8,128)(2,1)S(1)} %add.200), channel_id=1, source_target_pairs={{16,0},{18,2},{20,4},{22,6},{9,25},{11,27},{13,29},{15,31}} | collective-permute-start | bytes 1572872 | tf_op jit(solution)/shard_map/ppermute | solution.py:348
  112.8 3.0 %collective-permute-start.22 = (bf16[1,2,160,512]{3,2,0,1:T(8,128)(2,1)S(1)}, bf16[1,2,160,512]{3,2,0,1:T(8,128)(2,1)S(1)}, u32[]{:S(2)}, u32[]{:S(2)}) collective-permute-start(bf16[1,2,160,512]{3,2,0,1:T(8,128)(2,1)S(1)} %maximum_select_fusion.2), channel_id=1, source_target_pairs={{0,16},{2,18},{4,20},{6,22},{8,24},{10,26},{12,28},{14,30},{16,0},... | collective-permute-start | bytes 983048 | tf_op jit(solution)/shard_map/ppermute | solution.py:344
  115.7 17.4 %collective-permute-done.22 = bf16[1,2,160,512]{3,2,0,1:T(8,128)(2,1)S(1)} collective-permute-done((bf16[1,2,160,512]{3,2,0,1:T(8,128)(2,1)S(1)}, bf16[1,2,160,512]{3,2,0,1:T(8,128)(2,1)S(1)}, u32[]{:S(2)}, u32[]{:S(2)}) %collective-permute-start.22) | collective-permute-done | bytes 327712 | tf_op jit(solution)/shard_map/ppermute | solution.py:344
  138.1 5.2 %collective-permute-start.23 = (bf16[256,1024]{1,0:T(8,128)(2,1)S(1)}, bf16[256,1024]{1,0:T(8,128)(2,1)}, u32[]{:S(2)}, u32[]{:S(2)}) collective-permute-start(bf16[256,1024]{1,0:T(8,128)(2,1)S(1)} %add.206), channel_id=1, source_target_pairs={{16,0},{18,2},{20,4},{22,6},{9,25},{11,27},{13,29},{15,31}} | collective-permute-start | bytes 1572872 | tf_op jit(solution)/shard_map/ppermute | solution.py:348
  146.1 6.8 %shard_map.155 = (bf16[256,1024]{1,0:T(8,128)(2,1)}, bf16[256,1024]{1,0:T(8,128)(2,1)}) custom-call(bf16[256,1024]{1,0:T(8,128)(2,1)} %collective-permute-done.16.refs_0_, bf16[256,1024]{1,0:T(8,128)(2,1)} %collective-permute-done.21.refs_1_, bf16[1024,2048]{1,0:T(8,128)(2,1)} %refs_2_.4, bf16[1024,2048]{1,0:T(8,128)(2,1)} %collective-permute-done.3.refs_4_.refs_5_.refs_3_), custom_call_target="tpu_custom_call" | custom-call | flops 1 | bytes 1 | tf_op jit(solution)/shard_map/pallas_call | solution.py:262
  154.5 10.1 %collective-permute-done.24 = bf16[256,1024]{1,0:T(8,128)(2,1)} collective-permute-done((bf16[256,1024]{1,0:T(8,128)(2,1)S(1)}, bf16[256,1024]{1,0:T(8,128)(2,1)}, u32[]{:S(2)}, u32[]{:S(2)}) %collective-permute-start.24) | collective-permute-done | bytes 524320 | tf_op jit(solution)/shard_map/ppermute | solution.py:348
  168.8 4.1 %collective-permute-start.28 = (bf16[256,1024]{1,0:T(8,128)(2,1)S(1)}, bf16[256,1024]{1,0:T(8,128)(2,1)S(1)}, u32[]{:S(2)}, u32[]{:S(2)}) collective-permute-start(bf16[256,1024]{1,0:T(8,128)(2,1)S(1)} %add.209), channel_id=1, source_target_pairs={{16,8},{18,10},{20,12},{22,14},{9,17},{11,19},{13,21},{15,23}} | collective-permute-start | bytes 1572872 | tf_op jit(solution)/shard_map/ppermute | solution.py:348
  176.1 8.7 %collective-permute-done.28 = bf16[256,1024]{1,0:T(8,128)(2,1)S(1)} collective-permute-done((bf16[256,1024]{1,0:T(8,128)(2,1)S(1)}, bf16[256,1024]{1,0:T(8,128)(2,1)S(1)}, u32[]{:S(2)}, u32[]{:S(2)}) %collective-permute-start.28) | collective-permute-done | bytes 524320 | tf_op jit(solution)/shard_map/ppermute | solution.py:348
  186.3 2.1 collective-permute-done.30
  193.4 6.8 %shard_map.156 = (bf16[256,1024]{1,0:T(8,128)(2,1)}, bf16[256,1024]{1,0:T(8,128)(2,1)}) custom-call(bf16[256,1024]{1,0:T(8,128)(2,1)} %collective-permute-done.26.refs_0_, bf16[256,1024]{1,0:T(8,128)(2,1)} %copy-done.23, bf16[1024,2048]{1,0:T(8,128)(2,1)} %refs_2_.4, bf16[1024,2048]{1,0:T(8,128)(2,1)} %collective-permute-done.3.refs_4_.refs_5_.refs_3_), custom_call_target="tpu_custom_call" | custom-call | flops 1 | bytes 1 | tf_op jit(solution)/shard_map/pallas_call | solution.py:262
  204.0 2.1 collective-permute-done.35
  210.8 11.6 %shard_map.157 = (f32[4,512,512]{2,1,0:T(8,128)}, f32[4,512,512]{2,1,0:T(8,128)}, f32[4,1,512]{2,1,0:T(1,128)}, f32[4,1,512]{2,1,0:T(1,128)}) custom-call(s32[3]{0:T(128)} %get-tuple-element.366.place_ref, bf16[4,160,512]{2,1,0:T(8,128)(2,1)} %get-tuple-element.326.low, bf16[4,160,512]{2,1,0:T(8,128)(2,1)} %get-tuple-element.327.high, ...), custom_call_target="tpu_custom_call" | custom-call | flops 1 | bytes 1 | tf_op jit(solution)/shard_map/pallas_call | solution.py:127
  225.6 5.4 %collective-permute-start.41 = (f32[4,1,512]{2,1,0:T(1,128)S(1)}, f32[4,1,512]{2,1,0:T(1,128)S(1)}, u32[]{:S(2)}, u32[]{:S(2)}) collective-permute-start(f32[4,1,512]{2,1,0:T(1,128)S(1)} %copy-done.25), channel_id=1, source_target_pairs={{1,0},{0,1},{3,2},{2,3},{5,4},{4,5},{7,6},{6,7},{9,8},{8,9},{11,10... | collective-permute-start | bytes 24584 | tf_op jit(solution)/shard_map/ppermute | solution.py:303
  234.2 5.4 %collective-permute-done.40 = bf16[256,1024]{1,0:T(8,128)(2,1)S(1)} collective-permute-done((bf16[256,1024]{1,0:T(8,128)(2,1)S(1)}, bf16[256,1024]{1,0:T(8,128)(2,1)S(1)}, u32[]{:S(2)}, u32[]{:S(2)}) %collective-permute-start.40) | collective-permute-done | bytes 524320 | tf_op jit(solution)/shard_map/ppermute | solution.py:348
  247.3 11.7 %collective-permute-done.44 = bf16[256,1024]{1,0:T(8,128)(2,1)} collective-permute-done((bf16[256,1024]{1,0:T(8,128)(2,1)S(1)}, bf16[256,1024]{1,0:T(8,128)(2,1)}, u32[]{:S(2)}, u32[]{:S(2)}) %collective-permute-start.44) | collective-permute-done | bytes 524320 | tf_op jit(solution)/shard_map/ppermute | solution.py:348
  260.4 6.6 %collective-permute-done.42 = bf16[256,1024]{1,0:T(8,128)(2,1)} collective-permute-done((bf16[256,1024]{1,0:T(8,128)(2,1)}, bf16[256,1024]{1,0:T(8,128)(2,1)}, u32[]{:S(2)}, u32[]{:S(2)}) %collective-permute-start.42) | collective-permute-done | bytes 524320 | tf_op jit(solution)/shard_map/ppermute | solution.py:348
  269.9 5.4 %shard_map.158.refs_6_ = bf16[256,2048]{1,0:T(8,128)(2,1)} custom-call(s32[3]{0:T(128)} %pad_add_fusion.place_ref, bf16[256,1024]{1,0:T(8,128)(2,1)} %copy-done, bf16[256,1024]{1,0:T(8,128)(2,1)} %copy-done.14, bf16[4,512,512]{2,1,0:T(8,128)(2,1)} %refs_2_.7, bf16[8,512,512]{2,1,0:T(8,128)(2,1)} %refs_3_.8, f32[4,1,512]{2,1,0:T(1,128)} %get-tuple-element.351.refs_4_, ...), custom_call_target="tpu_custom_call" | custom-call | flops 1610612736 | bytes 2097152 | tf_op jit(solution)/shard_map/pallas_call | solution.py:181
  276.1 5.4 %shard_map.159 = bf16[256,2048]{1,0:T(8,128)(2,1)} custom-call(s32[3]{0:T(128)} %pad_add_fusion.place_ref, bf16[256,1024]{1,0:T(8,128)(2,1)} %copy-done.1, bf16[256,1024]{1,0:T(8,128)(2,1)} %copy-done.17, bf16[4,512,512]{2,1,0:T(8,128)(2,1)} %refs_2_.7, bf16[8,512,512]{2,1,0:T(8,128)(2,1)} %refs_3_.8, ...), custom_call_target="tpu_custom_call", output_to_operand_aliasing={{}: (7, {})} | custom-call | flops 1610612736 | bytes 2097152 | tf_op jit(solution)/shard_map/pallas_call | solution.py:181
  (180 shorter events, 73.9 us)
Async XLA Ops:
  0.6 21.0 %collective-permute-start.3 = (bf16[1024,2048]{1,0:T(8,128)(2,1)}, bf16[1024,2048]{1,0:T(8,128)(2,1)}, u32[]{:S(2)}, u32[]{:S(2)}) collective-permute-start(bf16[1024,2048]{1,0:T(8,128)(2,1)} %refs_2_.4), channel_id=1, source_target_pairs={{0,2},{2,0},{4,6},{6,4},{8,10},{10,8},{12,14},{14,12},{16,18},{18,... | collective-permute-start | bytes 12582920 | tf_op jit(solution)/shard_map/ppermute | solution.py:297
  18.6 17.3 %collective-permute-start.5 = (bf16[4,160,512]{2,1,0:T(8,128)(2,1)}, bf16[4,160,512]{2,1,0:T(8,128)(2,1)S(1)}, u32[]{:S(2)}, u32[]{:S(2)}) collective-permute-start(bf16[4,160,512]{2,1,0:T(8,128)(2,1)} %get-tuple-element.195), channel_id=1, source_target_pairs={{0,4},{2,6},{4,0},{6,2},{8,12},{10,14},{12,8},{14,10},{16,20},{18,... | collective-permute-start | bytes 1966088 | tf_op jit(solution)/shard_map/ppermute | solution.py:300
  20.1 16.0 %collective-permute-start.1 = (bf16[256,1024]{1,0:T(8,128)(2,1)S(1)}, bf16[256,1024]{1,0:T(8,128)(2,1)S(1)}, u32[]{:S(2)}, u32[]{:S(2)}) collective-permute-start(bf16[256,1024]{1,0:T(8,128)(2,1)S(1)} %copy-done.22), channel_id=1, source_target_pairs={{1,0},{0,1},{3,2},{2,3},{5,4},{4,5},{7,6},{6,7},{9,8},{8,9},{11,10... | collective-permute-start | bytes 1572872 | tf_op jit(solution)/shard_map/ppermute | solution.py:303
  20.6 23.9 %collective-permute-start.2 = (bf16[256,1024]{1,0:T(8,128)(2,1)S(1)}, bf16[256,1024]{1,0:T(8,128)(2,1)S(1)}, u32[]{:S(2)}, u32[]{:S(2)}) collective-permute-start(bf16[256,1024]{1,0:T(8,128)(2,1)S(1)} %copy-done.29), channel_id=1, source_target_pairs={{3,0},{2,1},{1,2},{0,3},{7,4},{6,5},{5,6},{4,7},{11,8},{10,9},{9,1... | collective-permute-start | bytes 1572872 | tf_op jit(solution)/shard_map/ppermute | solution.py:303
  49.9 16.4 %collective-permute-start.7 = (bf16[512,1024]{1,0:T(8,128)(2,1)}, bf16[512,1024]{1,0:T(8,128)(2,1)S(1)}, u32[]{:S(2)}, u32[]{:S(2)}) collective-permute-start(bf16[512,1024]{1,0:T(8,128)(2,1)} %get-tuple-element.199), channel_id=1, source_target_pairs={{0,2},{2,0},{4,6},{6,4},{8,10},{10,8},{12,14},{14,12},{16,18},{18,... | collective-permute-start | bytes 3145736 | tf_op jit(solution)/shard_map/ppermute | solution.py:297
  51.7 14.6 %collective-permute-start.8 = (bf16[256,1024]{1,0:T(8,128)(2,1)}, bf16[256,1024]{1,0:T(8,128)(2,1)S(1)}, u32[]{:S(2)}, u32[]{:S(2)}) collective-permute-start(bf16[256,1024]{1,0:T(8,128)(2,1)} %get-tuple-element.202.refs_1_), channel_id=1, source_target_pairs={{1,0},{0,1},{3,2},{2,3},{5,4},{4,5},{7,6},{6,7},{9,8},{8,9},{11,10... | collective-permute-start | bytes 1572872 | tf_op jit(solution)/shard_map/ppermute | solution.py:303
  66.4 16.5 %collective-permute-start.10 = (bf16[256,1024]{1,0:T(8,128)(2,1)S(1)}, bf16[256,1024]{1,0:T(8,128)(2,1)}, u32[]{:S(2)}, u32[]{:S(2)}) collective-permute-start(bf16[256,1024]{1,0:T(8,128)(2,1)S(1)} %add.189), channel_id=1, source_target_pairs={{8,0},{10,2},{12,4},{14,6},{24,16},{26,18},{28,20},{30,22},{1,9},{... | collective-permute-start | bytes 1572872 | tf_op jit(solution)/shard_map/ppermute | solution.py:348
  67.7 16.4 %collective-permute-start.11 = (bf16[256,1024]{1,0:T(8,128)(2,1)}, bf16[256,1024]{1,0:T(8,128)(2,1)}, u32[]{:S(2)}, u32[]{:S(2)}) collective-permute-start(bf16[256,1024]{1,0:T(8,128)(2,1)} %get-tuple-element.215), channel_id=1, source_target_pairs={{0,4},{2,6},{4,0},{6,2},{8,12},{10,14},{12,8},{14,10},{16,20},{18,... | collective-permute-start | bytes 1572872 | tf_op jit(solution)/shard_map/ppermute | solution.py:300
  68.3 17.1 %collective-permute-start.12 = (bf16[256,1024]{1,0:T(8,128)(2,1)}, bf16[256,1024]{1,0:T(8,128)(2,1)S(1)}, u32[]{:S(2)}, u32[]{:S(2)}) collective-permute-start(bf16[256,1024]{1,0:T(8,128)(2,1)} %get-tuple-element.220), channel_id=1, source_target_pairs={{3,0},{2,1},{1,2},{0,3},{7,4},{6,5},{5,6},{4,7},{11,8},{10,9},{9,1... | collective-permute-start | bytes 1572872 | tf_op jit(solution)/shard_map/ppermute | solution.py:303
  85.4 19.6 %collective-permute-start.14 = (bf16[256,1024]{1,0:T(8,128)(2,1)S(1)}, bf16[256,1024]{1,0:T(8,128)(2,1)S(1)}, u32[]{:S(2)}, u32[]{:S(2)}) collective-permute-start(bf16[256,1024]{1,0:T(8,128)(2,1)S(1)} %add.201), channel_id=1, source_target_pairs={{8,0},{10,2},{12,4},{14,6},{24,16},{26,18},{28,20},{30,22},{1,9},{... | collective-permute-start | bytes 1572872 | tf_op jit(solution)/shard_map/ppermute | solution.py:348
  86.7 18.5 %collective-permute-start.15 = (bf16[256,1024]{1,0:T(8,128)(2,1)}, bf16[256,1024]{1,0:T(8,128)(2,1)}, u32[]{:S(2)}, u32[]{:S(2)}) collective-permute-start(bf16[256,1024]{1,0:T(8,128)(2,1)} %get-tuple-element.235), channel_id=1, source_target_pairs={{0,4},{2,6},{4,0},{6,2},{8,12},{10,14},{12,8},{14,10},{16,20},{18,... | collective-permute-start | bytes 1572872 | tf_op jit(solution)/shard_map/ppermute | solution.py:300
  87.3 19.1 %collective-permute-start.16 = (bf16[256,1024]{1,0:T(8,128)(2,1)S(1)}, bf16[256,1024]{1,0:T(8,128)(2,1)}, u32[]{:S(2)}, u32[]{:S(2)}) collective-permute-start(bf16[256,1024]{1,0:T(8,128)(2,1)S(1)} %copy-done.10), channel_id=1, source_target_pairs={{1,0},{0,1},{3,2},{2,3},{5,4},{4,5},{7,6},{6,7},{9,8},{8,9},{11,10... | collective-permute-start | bytes 1572872 | tf_op jit(solution)/shard_map/ppermute | solution.py:303
  106.4 26.9 %collective-permute-start.18 = (bf16[256,1024]{1,0:T(8,128)(2,1)S(1)}, bf16[256,1024]{1,0:T(8,128)(2,1)}, u32[]{:S(2)}, u32[]{:S(2)}) collective-permute-start(bf16[256,1024]{1,0:T(8,128)(2,1)S(1)} %add.200), channel_id=1, source_target_pairs={{16,0},{18,2},{20,4},{22,6},{9,25},{11,27},{13,29},{15,31}} | collective-permute-start | bytes 1572872 | tf_op jit(solution)/shard_map/ppermute | solution.py:348
  110.9 23.7 %collective-permute-start.19 = (bf16[256,1024]{1,0:T(8,128)(2,1)S(1)}, bf16[256,1024]{1,0:T(8,128)(2,1)}, u32[]{:S(2)}, u32[]{:S(2)}) collective-permute-start(bf16[256,1024]{1,0:T(8,128)(2,1)S(1)} %add.207), channel_id=1, source_target_pairs={{0,8},{2,10},{4,12},{6,14},{24,16},{26,18},{28,20},{30,22},{1,9},{... | collective-permute-start | bytes 1572872 | tf_op jit(solution)/shard_map/ppermute | solution.py:348
  112.1 23.7 %collective-permute-start.20 = (bf16[256,1024]{1,0:T(8,128)(2,1)}, bf16[256,1024]{1,0:T(8,128)(2,1)}, u32[]{:S(2)}, u32[]{:S(2)}) collective-permute-start(bf16[256,1024]{1,0:T(8,128)(2,1)} %get-tuple-element.257), channel_id=1, source_target_pairs={{0,4},{2,6},{4,0},{6,2},{8,12},{10,14},{12,8},{14,10},{16,20},{18,... | collective-permute-start | bytes 1572872 | tf_op jit(solution)/shard_map/ppermute | solution.py:300
  112.7 24.3 %collective-permute-start.21 = (bf16[256,1024]{1,0:T(8,128)(2,1)}, bf16[256,1024]{1,0:T(8,128)(2,1)}, u32[]{:S(2)}, u32[]{:S(2)}) collective-permute-start(bf16[256,1024]{1,0:T(8,128)(2,1)} %get-tuple-element.259), channel_id=1, source_target_pairs={{3,0},{2,1},{1,2},{0,3},{7,4},{6,5},{5,6},{4,7},{11,8},{10,9},{9,1... | collective-permute-start | bytes 1572872 | tf_op jit(solution)/shard_map/ppermute | solution.py:303
  112.8 20.4 %collective-permute-start.22 = (bf16[1,2,160,512]{3,2,0,1:T(8,128)(2,1)S(1)}, bf16[1,2,160,512]{3,2,0,1:T(8,128)(2,1)S(1)}, u32[]{:S(2)}, u32[]{:S(2)}) collective-permute-start(bf16[1,2,160,512]{3,2,0,1:T(8,128)(2,1)S(1)} %maximum_select_fusion.2), channel_id=1, source_target_pairs={{0,16},{2,18},{4,20},{6,22},{8,24},{10,26},{12,28},{14,30},{16,0},... | collective-permute-start | bytes 983048 | tf_op jit(solution)/shard_map/ppermute | solution.py:344
  137.1 30.0 %collective-permute-start.27 = (bf16[2,2,160,512]{3,2,0,1:T(8,128)(2,1)S(1)}, bf16[2,2,160,512]{3,2,0,1:T(8,128)(2,1)}, u32[]{:S(2)}, u32[]{:S(2)}) collective-permute-start(bf16[2,2,160,512]{3,2,0,1:T(8,128)(2,1)S(1)} %maximum_select_fusion.1), channel_id=1, source_target_pairs={{0,8},{2,10},{4,12},{6,14},{8,0},{10,2},{12,4},{14,6},{16,24},{18,... | collective-permute-start | bytes 1966088 | tf_op jit(solution)/shard_map/ppermute | solution.py:344
  138.1 15.2 %collective-permute-start.23 = (bf16[256,1024]{1,0:T(8,128)(2,1)S(1)}, bf16[256,1024]{1,0:T(8,128)(2,1)}, u32[]{:S(2)}, u32[]{:S(2)}) collective-permute-start(bf16[256,1024]{1,0:T(8,128)(2,1)S(1)} %add.206), channel_id=1, source_target_pairs={{16,0},{18,2},{20,4},{22,6},{9,25},{11,27},{13,29},{15,31}} | collective-permute-start | bytes 1572872 | tf_op jit(solution)/shard_map/ppermute | solution.py:348
  143.3 21.3 %collective-permute-start.24 = (bf16[256,1024]{1,0:T(8,128)(2,1)S(1)}, bf16[256,1024]{1,0:T(8,128)(2,1)}, u32[]{:S(2)}, u32[]{:S(2)}) collective-permute-start(bf16[256,1024]{1,0:T(8,128)(2,1)S(1)} %add.210), channel_id=1, source_target_pairs={{0,8},{2,10},{4,12},{6,14},{24,16},{26,18},{28,20},{30,22},{1,9},{... | collective-permute-start | bytes 1572872 | tf_op jit(solution)/shard_map/ppermute | solution.py:348
  144.6 21.3 %collective-permute-start.25 = (bf16[256,1024]{1,0:T(8,128)(2,1)}, bf16[256,1024]{1,0:T(8,128)(2,1)}, u32[]{:S(2)}, u32[]{:S(2)}) collective-permute-start(bf16[256,1024]{1,0:T(8,128)(2,1)} %get-tuple-element.274), channel_id=1, source_target_pairs={{0,4},{2,6},{4,0},{6,2},{8,12},{10,14},{12,8},{14,10},{16,20},{18,... | collective-permute-start | bytes 1572872 | tf_op jit(solution)/shard_map/ppermute | solution.py:300
  145.5 23.2 %collective-permute-start.26 = (bf16[256,1024]{1,0:T(8,128)(2,1)}, bf16[256,1024]{1,0:T(8,128)(2,1)}, u32[]{:S(2)}, u32[]{:S(2)}) collective-permute-start(bf16[256,1024]{1,0:T(8,128)(2,1)} %get-tuple-element.277.refs_1_), channel_id=1, source_target_pairs={{1,0},{0,1},{3,2},{2,3},{5,4},{4,5},{7,6},{6,7},{9,8},{8,9},{11,10... | collective-permute-start | bytes 1572872 | tf_op jit(solution)/shard_map/ppermute | solution.py:303
  168.7 20.3 %collective-permute-start.32 = (bf16[4,2,160,512]{3,2,0,1:T(8,128)(2,1)S(1)}, bf16[4,2,160,512]{3,2,0,1:T(8,128)(2,1)S(1)}, u32[]{:S(2)}, u32[]{:S(2)}) collective-permute-start(bf16[4,2,160,512]{3,2,0,1:T(8,128)(2,1)S(1)} %bitcast.41), channel_id=1, source_target_pairs={{0,2},{2,0},{4,6},{6,4},{8,10},{10,8},{12,14},{14,12},{16,18},{18,... | collective-permute-start | bytes 3932168 | tf_op jit(solution)/shard_map/ppermute | solution.py:297
  168.8 15.9 %collective-permute-start.28 = (bf16[256,1024]{1,0:T(8,128)(2,1)S(1)}, bf16[256,1024]{1,0:T(8,128)(2,1)S(1)}, u32[]{:S(2)}, u32[]{:S(2)}) collective-permute-start(bf16[256,1024]{1,0:T(8,128)(2,1)S(1)} %add.209), channel_id=1, source_target_pairs={{16,8},{18,10},{20,12},{22,14},{9,17},{11,19},{13,21},{15,23}} | collective-permute-start | bytes 1572872 | tf_op jit(solution)/shard_map/ppermute | solution.py:348
  174.3 14.1 %collective-permute-start.30 = (bf16[256,1024]{1,0:T(8,128)(2,1)S(1)}, bf16[256,1024]{1,0:T(8,128)(2,1)S(1)}, u32[]{:S(2)}, u32[]{:S(2)}) collective-permute-start(bf16[256,1024]{1,0:T(8,128)(2,1)S(1)} %copy-done.27), channel_id=1, source_target_pairs={{0,4},{2,6},{4,0},{6,2},{8,12},{10,14},{12,8},{14,10},{16,20},{18,... | collective-permute-start | bytes 1572872 | tf_op jit(solution)/shard_map/ppermute | solution.py:300
  174.9 14.1 %collective-permute-start.31 = (bf16[256,1024]{1,0:T(8,128)(2,1)S(1)}, bf16[256,1024]{1,0:T(8,128)(2,1)S(1)}, u32[]{:S(2)}, u32[]{:S(2)}) collective-permute-start(bf16[256,1024]{1,0:T(8,128)(2,1)S(1)} %copy-done.26), channel_id=1, source_target_pairs={{3,0},{2,1},{1,2},{0,3},{7,4},{6,5},{5,6},{4,7},{11,8},{10,9},{9,1... | collective-permute-start | bytes 1572872 | tf_op jit(solution)/shard_map/ppermute | solution.py:303
  206.4 16.0 %collective-permute-start.36 = (bf16[256,1024]{1,0:T(8,128)(2,1)S(1)}, bf16[256,1024]{1,0:T(8,128)(2,1)S(1)}, u32[]{:S(2)}, u32[]{:S(2)}) collective-permute-start(bf16[256,1024]{1,0:T(8,128)(2,1)S(1)} %add.215), channel_id=1, source_target_pairs={{8,24},{10,26},{12,28},{14,30},{17,1},{19,3},{21,5},{23,7}} | collective-permute-start | bytes 1572872 | tf_op jit(solution)/shard_map/ppermute | solution.py:348
  207.1 15.5 %collective-permute-start.37 = (bf16[256,1024]{1,0:T(8,128)(2,1)S(1)}, bf16[256,1024]{1,0:T(8,128)(2,1)S(1)}, u32[]{:S(2)}, u32[]{:S(2)}) collective-permute-start(bf16[256,1024]{1,0:T(8,128)(2,1)S(1)} %add.219), channel_id=1, source_target_pairs={{0,8},{2,10},{4,12},{6,14},{24,16},{26,18},{28,20},{30,22},{1,9},{... | collective-permute-start | bytes 1572872 | tf_op jit(solution)/shard_map/ppermute | solution.py:348
  208.4 14.4 %collective-permute-start.38 = (bf16[256,1024]{1,0:T(8,128)(2,1)}, bf16[256,1024]{1,0:T(8,128)(2,1)S(1)}, u32[]{:S(2)}, u32[]{:S(2)}) collective-permute-start(bf16[256,1024]{1,0:T(8,128)(2,1)} %get-tuple-element.325), channel_id=1, source_target_pairs={{0,4},{2,6},{4,0},{6,2},{8,12},{10,14},{12,8},{14,10},{16,20},{18,... | collective-permute-start | bytes 1572872 | tf_op jit(solution)/shard_map/ppermute | solution.py:300
  224.3 15.4 %collective-permute-start.40 = (bf16[256,1024]{1,0:T(8,128)(2,1)S(1)}, bf16[256,1024]{1,0:T(8,128)(2,1)S(1)}, u32[]{:S(2)}, u32[]{:S(2)}) collective-permute-start(bf16[256,1024]{1,0:T(8,128)(2,1)S(1)} %add.222), channel_id=1, source_target_pairs={{0,8},{2,10},{4,12},{6,14},{24,16},{26,18},{28,20},{30,22},{1,9},{... | collective-permute-start | bytes 1572872 | tf_op jit(solution)/shard_map/ppermute | solution.py:348
  240.6 18.4 %collective-permute-start.44 = (bf16[256,1024]{1,0:T(8,128)(2,1)S(1)}, bf16[256,1024]{1,0:T(8,128)(2,1)}, u32[]{:S(2)}, u32[]{:S(2)}) collective-permute-start(bf16[256,1024]{1,0:T(8,128)(2,1)S(1)} %add.221), channel_id=1, source_target_pairs={{8,16},{10,18},{12,20},{14,22},{17,9},{19,11},{21,13},{23,15}} | collective-permute-start | bytes 1572872 | tf_op jit(solution)/shard_map/ppermute | solution.py:348
  241.9 25.1 %collective-permute-start.42 = (bf16[256,1024]{1,0:T(8,128)(2,1)}, bf16[256,1024]{1,0:T(8,128)(2,1)}, u32[]{:S(2)}, u32[]{:S(2)}) collective-permute-start(bf16[256,1024]{1,0:T(8,128)(2,1)} %add.224), channel_id=1, source_target_pairs={{8,16},{10,18},{12,20},{14,22},{17,9},{19,11},{21,13},{23,15}} | collective-permute-start | bytes 1572872 | tf_op jit(solution)/shard_map/ppermute | solution.py:348
  (47 other events, 410.6 us)

commit v4 on v3

--- a/solution.py
+++ b/solution.py
@@ -10,8 +10,7 @@
 BLK = 128
 QUARTER = 128
 VMEM = 56 * 2**20
-SLOTS = 5
-COL_CHUNKS = 2
+COL_CHUNKS = 1
 
 
 DECAY_RATE = 0.75
@@ -95,10 +94,13 @@
     return [[tiles[i, j] if j >= i else tiles[j, i].T for j in range(4)] for i in range(4)]
 
 
-def factor_kernel(place_ref, low, high, low_sib, high_sib, *refs):
+def factor_kernel(place_ref, keep, back, keep_sib, back_sib, *refs):
+    low = place_ref[2] == 0
     for kind, (factor, basis, new, eig) in enumerate(zip(refs[0:2], refs[2:4], refs[4:6], refs[6:8])):
         here = place_ref[1] == kind
-        halves = [jnp.where(here, low[0], low_sib[0]), jnp.where(here, high[0], high_sib[0])]
+        kept = jnp.where(here, keep[0], keep_sib[0])
+        came = jnp.where(here, back[0], back_sib[0])
+        halves = [jnp.where(low, kept, came), jnp.where(low, came, kept)]
         rows = unpack_upper(jnp.concatenate(halves, axis=0).astype(F32))
         q = QUARTER
         for i in range(4):
@@ -290,7 +292,7 @@
     tokens = pool_rows * n_dp
     rows_dev = model_width // n_dp
     z_per_worker = n_z // n_worker
-    cols = width // COL_CHUNKS if width >= 1024 else width
+    cols = width // COL_CHUNKS
     both = ("dp", "worker")
 
     def swap_core(v):
@@ -315,8 +317,7 @@
 
     z = d // 4
     starts = list(range(0, width, cols))
-    shards = [(0, j) for j in range(z_per_worker)]
-    shards += [(step, j) for j in range(z_per_worker) for step in range(1, n_worker)]
+    shards = [(step, j) for j in range(z_per_worker) for step in range(n_worker)]
 
     def hops_of(step, j):
         hops = []
@@ -354,53 +355,34 @@
         return (part * 2 + x_to) * 2 + core_to
 
     chunks = range(len(starts))
-    used = {}
-
-    def hold(stage):
-        used[stage] = used.get(stage, 0) + 1
-
-    x_stage, z_stage, busy = {}, {}, set()
-    y_items = [(step, j, at, flip) for step, j in shards if step for at in range(2) for flip in range(2)]
-    y_stage = {item: max(0, at - 1) for at, item in enumerate(y_items)}
-    for stage in y_stage.values():
-        hold(stage)
-    product_stage = {(0, 0, 0): 0, (0, 0, 1): 0}
-    clock = 0
+    x_stage, y_stage, z_stage, product_stage, busy = {}, {}, {}, {}, set()
+    clock = arrived = 0
     for step, j in shards:
-        if step == 0 and j:
-            product_stage[0, j, 0] = product_stage[0, j, 1] = clock
         if step:
-            here, there = y_stage[step, j, 0, 1] + 1, y_stage[step, j, 1, 1] + 1
-            product_stage[step, j, 0] = there if there <= clock else max(here, clock - 1)
-            product_stage[step, j, 1] = there
-            clock = max(clock, product_stage[step, j, 0])
+            for at in range(2):
+                for flip in range(2):
+                    y_stage[step, j, at, flip] = arrived + at
+            clock = max(clock + 1, arrived + 2)
+            product_stage[step, j, 0] = clock - 1
+            product_stage[step, j, 1] = max(clock - 1, arrived + 2)
+            arrived += 2
+        else:
+            clock += 1
+            product_stage[0, j, 0] = product_stage[0, j, 1] = clock - 1
         for n in chunks:
-            clock += 1
             x_stage[step, j, n] = clock
-            hold(clock)
     z_bits = [2**bit for bit in range((n_z - 1).bit_length())]
-    hold(1)
-    scatter = [1 + at for at in range(len(z_bits))]
-    across = scatter[-1] + 1
-    gather = [across + 1 + at for at in range(len(z_bits))]
-    between = gather[-1] + 1
-    for stage in range(1, between + 1):
-        hold(stage)
-    fresh = between + 1
-    while fresh in product_stage.values():
-        fresh += 1
-    hold(fresh + 1)
+    across = max(clock, 2) + 1
     for n_hop in range(len(z_bits)):
         for step, j, n in x_stage:
             ready = max(x_stage[step, j, n], product_stage[step, j, 1])
             clock = (z_stage[step, j, n, n_hop - 1] if n_hop else ready) + 1
             moves = links(hops_of(step, j)[n_hop])
-            while used.get(clock, 0) >= SLOTS or any((clock, link) in busy for link in moves):
+            while any((clock, link) in busy for link in moves):
                 clock += 1
             busy.update((clock, link) for link in moves)
             z_stage[step, j, n, n_hop] = clock
-            hold(clock)
-    last = max(*z_stage.values(), fresh + 1)
+    last = max(*z_stage.values(), across + 1)
 
     my_start = d * rows_dev
     block = my_start // block_size
@@ -413,9 +395,6 @@
         *single, both_rows = turned(rows, which, rows_dev)
         found = {("p", j, at, flip): single[2 * flip + at] for flip in range(2) for at in range(2)}
         return {**found, ("p", j): both_rows}
-
-    def in_order(bit, mine, theirs):
-        return jnp.where(bit == 0, jnp.stack([mine, theirs]), jnp.stack([theirs, mine]))
 
     for stage in range(last + 1):
         if stage:
@@ -445,39 +424,37 @@
             if when == stage:
                 joined["hop", step, j, n] = hop(env["acc", step, j, n], hops_of(step, j)[at])
 
-        for at, when in enumerate(scatter):
-            if stage == when:
-                bit = z // z_bits[at] % 2
-                parts = env["keep"].reshape(2, -1, block_size)
+        if stage == 1:
+            part = env["keep"].reshape(-1, block_size)
+            for far in z_bits:
+                bit = z // far % 2
+                parts = part.reshape(2, -1, block_size)
                 there = lax.dynamic_index_in_dim(parts, 1 - bit, 0, keepdims=False)
-                here = lax.dynamic_index_in_dim(parts, bit, 0, keepdims=False)
-                joined["keep"] = here + swap_z(there, z_bits[at])
+                part = lax.dynamic_index_in_dim(parts, bit, 0, keepdims=False) + swap_z(there, far)
+            joined["keep"] = part
+        if stage == 2:
+            part = env["keep"]
+            for far in reversed(z_bits):
+                other = swap_z(part, far)
+                mine_first = jnp.concatenate([part, other], axis=0)
+                part = jnp.where(z // far % 2 == 0, mine_first, jnp.concatenate([other, part], axis=0))
+            joined["keep"] = part.reshape(local_blocks, -1, block_size)
         if stage == across:
-            joined["keep"] = in_order(x, env["keep"], swap_x(env["keep"]))[None]
-        for at, when in enumerate(gather):
-            if stage == when:
-                far = z_bits[-1 - at]
-                joined["keep"] = in_order(z // far % 2, env["keep"], swap_z(env["keep"], far))
-                joined["keep"] = joined["keep"].reshape(-1, *env["keep"].shape[1:])
-        if stage == between:
-            full = jnp.swapaxes(env["keep"], 0, 1).reshape(2, local_blocks, -1, block_size)
-            joined["low"], joined["high"] = full[0], full[1]
-            joined["other"] = swap_core(env["keep"])
-            joined.pop("keep", None)
-        if stage == fresh:
-            full = jnp.swapaxes(env.pop("other"), 0, 1).reshape(2, local_blocks, -1, block_size)
-            act_new, grad_new, joined["eig_in"], eig_local = update_factors(
+            joined["back"] = swap_x(env["keep"])
+            joined["keep_sib"] = swap_core(env["keep"])
+        if stage == across + 1:
+            back = env.pop("back")
+            *done["factors"], eig_in, eig_local = update_factors(
                 flags,
-                [env.pop("low"), env.pop("high"), full[0], full[1]],
+                [env.pop("keep"), back, env.pop("keep_sib"), swap_core(back)],
                 (act_factor, grad_factor),
                 basis_in,
                 basis_out,
             )
-            joined["eigs"] = eig_local
-            done["factors"] = act_new, grad_new
-        if stage == fresh + 1:
-            eigs = [env["eigs"]] + [from_worker(env["eigs"], step, 0) for step in range(1, n_worker)]
-            joined["eigs"] = jnp.concatenate(eigs, axis=0)
+            eigs = [eig_local] + [from_worker(eig_local, step, 0) for step in range(1, n_worker)]
+            eig_out = jnp.concatenate(eigs, axis=0)
+            for key in [key for key in env if key[0] == "acc"]:
+                env[key], eig_out = lax.optimization_barrier((env[key], eig_out))
 
         for step, j in shards:
             due = [at for at in range(2) if product_stage[step, j, at] == stage]
@@ -511,7 +488,6 @@
                 done[n] = total
 
     act_new, grad_new = done["factors"]
-    eig_in, eig_out = env["eig_in"], env["eigs"]
     held = (block // local_blocks - w) % n_worker * local_blocks + block % local_blocks
 
     sharers = block_size // rows_dev

time: 284 us -> 268 us (0.944)
  waiting for transfers between devices: 101 us -> 84.5 us
  starting transfers between devices: 61.7 us -> 67.2 us
  other arithmetic: 24.6 us -> 21.1 us
    ppermute x4, waiting for transfers between devices: 25.8 us -> 3.11 us  [swap_z(): return lax.ppermute(v, 'dp', [(i, i ^ 4 * bit) for i in range(n_dp)])]
    ppermute x4, starting transfers between devices: 7.15 us -> 26 us  [swap_z(): return lax.ppermute(v, 'dp', [(i, i ^ 4 * bit) for i in range(n_dp)])]
    ppermute x16 -> x8, starting transfers between devices: 30.2 us -> 21.4 us  [hop(): return lax.ppermute(v, both, pairs)]
    add x8 -> x4, other arithmetic: 6.73 us -> 1.54 us  [per_device(): env[acc] = env.pop(mine) + env.pop(got)]
    pallas_call x5 -> x6, Pallas kernels: 40.8 us -> 44.7 us  [products(): pl.pallas_call(functools.partial(product_kernel, [len(half) for half in h...]
    ppermute x9, waiting for transfers between devices: 10.5 us -> 14 us  [from_worker(): lax.ppermute(v, both, [((i ^ flip) * n_worker + (j + step) % n_worker, i...]
    ppermute x10 -> x6, waiting for transfers between devices: 15.7 us -> 12.4 us  [swap_x(): return lax.ppermute(v, 'dp', [(i, i ^ 2) for i in range(n_dp)])]
    pallas_call x2 -> x1, Pallas kernels: 10.7 us -> 7.92 us  [tail(): pl.pallas_call(functools.partial(tail_kernel, len(parts)), grid_spec=pltp...]
  transfers between devices with their start and end apart: 46 -> 34, of which waited for: 20 -> 15; matrix products, arithmetic and copies ran while one was open for 10% -> 7% of each run, Pallas kernels for 25% -> 28%
where the time goes in v4:
time: 268 us; the launch traced here: 265 us
  waiting for transfers between devices  84.5 us (32%)
  Pallas kernels  83.3 us (31%)
  starting transfers between devices  67.2 us (25%)
  other arithmetic  21.1 us (8%)
  local copies, waits for them, and re-layouts  6.32 us (2%)
  between operations  2.74 us (1%)
    ppermute x8, waiting for transfers between devices, hop(): return lax.ppermute(v, both, pairs)  50.9 us
    pallas_call x6, Pallas kernels, products(): pl.pallas_call(functools.partial(product_kernel, [len(half) for half in h...  44.7 us
    ppermute x4, starting transfers between devices, swap_z(): return lax.ppermute(v, 'dp', [(i, i ^ 4 * bit) for i in range(n_dp)])  26 us
    ppermute x8, starting transfers between devices, hop(): return lax.ppermute(v, both, pairs)  21.4 us
    ppermute x9, waiting for transfers between devices, from_worker(): lax.ppermute(v, both, [((i ^ flip) * n_worker + (j + step) % n_worker, i...  14 us
    ppermute x6, waiting for transfers between devices, swap_x(): return lax.ppermute(v, 'dp', [(i, i ^ 2) for i in range(n_dp)])  12.4 us
    ppermute x9, starting transfers between devices, from_worker(): lax.ppermute(v, both, [((i ^ flip) * n_worker + (j + step) % n_worker, i...  11.9 us
    pallas_call x1, Pallas kernels, update_factors(): pl.pallas_call(factor_kernel, grid_spec=pltpu.PrefetchScalarGridSpec(num_...  11.5 us
  transfers between devices with their start and end apart: 34, of which 15 were waited for; matrix products, arithmetic and copies ran while one was open for 7% of the time, Pallas kernels for 28%

profile of v4, /device:TPU:12, one launch (start us, length us, event | category | flops | bytes accessed | tf_op | source)
XLA Modules:
  0.0 265.1 jit_solution(1245169040459173692)
XLA Ops:
  2.0 3.3 %shard_map.123 = (bf16[256,2048]{1,0:T(8,128)(2,1)}, bf16[256,2048]{1,0:T(8,128)(2,1)}) custom-call(s32[3]{0:T(128)} %pad_add_fusion.3.which_ref, bf16[1024,2048]{1,0:T(8,128)(2,1)} %refs_2_.5, bf16[1024,2048]{1,0:T(8,128)(2,1)} %block.2), custom_call_target="tpu_custom_call" | custom-call | flops 1 | bytes 1 | tf_op jit(solution)/shard_map/pallas_call | solution.py:35
  6.4 5.3 %shard_map.121 = (bf16[256,1024]{1,0:T(8,128)(2,1)}, bf16[256,1024]{1,0:T(8,128)(2,1)}, bf16[256,1024]{1,0:T(8,128)(2,1)}, bf16[256,1024]{1,0:T(8,128)(2,1)}, bf16[512,1024]{1,0:T(8,128)(2,1)}) custom-call(s32[4]{0:T(128)} %get-tuple-element.175.which_ref, bf16[1024,2048]{1,0:T(8,128)(2,1)} %block.2), custom_call_target="tpu_custom_call" | custom-call | flops 1 | bytes 1 | tf_op jit(solution)/shard_map/pallas_call | solution.py:214
  13.4 5.2 %shard_map.124 = (bf16[4,160,512]{2,1,0:T(8,128)(2,1)}, bf16[4,160,512]{2,1,0:T(8,128)(2,1)}) custom-call(s32[2]{0:T(128)} %pad_add_fusion.2.place_ref, bf16[256,2048]{1,0:T(8,128)(2,1)} %get-tuple-element.94.ours, bf16[256,2048]{1,0:T(8,128)(2,1)} %copy-done.8), custom_call_target="tpu_custom_call" | custom-call | flops 1 | bytes 1 | tf_op jit(solution)/shard_map/pallas_call | solution.py:73
  22.6 8.9 %shard_map.122 = (bf16[256,2048]{1,0:T(8,128)(2,1)}, bf16[256,2048]{1,0:T(8,128)(2,1)}) custom-call(bf16[256,1024]{1,0:T(8,128)(2,1)} %get-tuple-element.90.refs_0_, bf16[256,1024]{1,0:T(8,128)(2,1)} %get-tuple-element.108.refs_1_, bf16[512,1024]{1,0:T(8,128)(2,1)} %copy-done.5, bf16[1024,2048]{1,0:T(8,128)(2,1)} %refs_2_.5, ...), custom_call_target="tpu_custom_call" | custom-call | flops 1 | bytes 1 | tf_op jit(solution)/shard_map/pallas_call | solution.py:264
  31.6 4.4 %collective-permute-done.5 = bf16[4,160,512]{2,1,0:T(8,128)(2,1)S(1)} collective-permute-done((bf16[4,160,512]{2,1,0:T(8,128)(2,1)}, bf16[4,160,512]{2,1,0:T(8,128)(2,1)S(1)}, u32[]{:S(2)}, u32[]{:S(2)}) %collective-permute-start.5) | collective-permute-done | bytes 655392 | tf_op jit(solution)/shard_map/ppermute | solution.py:302
  36.1 8.7 %collective-permute-done.2.refs_1_ = bf16[256,1024]{1,0:T(8,128)(2,1)S(1)} collective-permute-done((bf16[256,1024]{1,0:T(8,128)(2,1)}, bf16[256,1024]{1,0:T(8,128)(2,1)S(1)}, u32[]{:S(2)}, u32[]{:S(2)}) %collective-permute-start.2) | collective-permute-done | bytes 524320 | tf_op jit(solution)/shard_map/ppermute | solution.py:305
  46.6 5.3 %shard_map.125 = (bf16[256,1024]{1,0:T(8,128)(2,1)}, bf16[256,1024]{1,0:T(8,128)(2,1)}, bf16[256,1024]{1,0:T(8,128)(2,1)}, bf16[256,1024]{1,0:T(8,128)(2,1)}, bf16[512,1024]{1,0:T(8,128)(2,1)}) custom-call(s32[4]{0:T(128)} %get-tuple-element.176.which_ref, bf16[1024,2048]{1,0:T(8,128)(2,1)} %block.2), custom_call_target="tpu_custom_call" | custom-call | flops 1 | bytes 1 | tf_op jit(solution)/shard_map/pallas_call | solution.py:214
  53.8 2.0 collective-permute-done.10
  55.8 2.7 collective-permute-start.11
  58.5 6.8 %shard_map.126 = bf16[256,2048]{1,0:T(8,128)(2,1)} custom-call(bf16[256,1024]{1,0:T(8,128)(2,1)} %copy-done.13, bf16[256,1024]{1,0:T(8,128)(2,1)} %copy-done.14, bf16[1024,2048]{1,0:T(8,128)(2,1)} %refs_2_.5, bf16[1024,2048]{1,0:T(8,128)(2,1)} %collective-permute-done.3.refs_4_.refs_3_), custom_call_target="tpu_custom_call" | custom-call | flops 1 | bytes 1 | tf_op jit(solution)/shard_map/pallas_call | solution.py:264
  65.3 6.3 %collective-permute-done.6 = bf16[256,2048]{1,0:T(8,128)(2,1)S(1)} collective-permute-done((bf16[256,2048]{1,0:T(8,128)(2,1)}, bf16[256,2048]{1,0:T(8,128)(2,1)S(1)}, u32[]{:S(2)}, u32[]{:S(2)}) %collective-permute-start.6) | collective-permute-done | bytes 1048608 | tf_op jit(solution)/shard_map/ppermute | solution.py:302
  72.0 5.2 %collective-permute-done.9.refs_1_ = bf16[256,1024]{1,0:T(8,128)(2,1)} collective-permute-done((bf16[256,1024]{1,0:T(8,128)(2,1)}, bf16[256,1024]{1,0:T(8,128)(2,1)}, u32[]{:S(2)}, u32[]{:S(2)}) %collective-permute-start.9) | collective-permute-done | bytes 524320 | tf_op jit(solution)/shard_map/ppermute | solution.py:305
  80.1 2.6 collective-permute-start.16
  82.7 3.6 %collective-permute-start.14 = (bf16[256,1024]{1,0:T(8,128)(2,1)}, bf16[256,1024]{1,0:T(8,128)(2,1)}, u32[]{:S(2)}, u32[]{:S(2)}) collective-permute-start(bf16[256,1024]{1,0:T(8,128)(2,1)} %get-tuple-element.124.refs_0_), channel_id=1, source_target_pairs={{1,0},{0,1},{3,2},{2,3},{5,4},{4,5},{7,6},{6,7},{9,8},{8,9},{11,10... | collective-permute-start | bytes 1572872 | tf_op jit(solution)/shard_map/ppermute | solution.py:305
  88.6 20.3 %collective-permute-start.17 = (bf16[320,512]{1,0:T(8,128)(2,1)S(1)}, bf16[320,512]{1,0:T(8,128)(2,1)}, u32[]{:S(2)}, u32[]{:S(2)}) collective-permute-start(bf16[320,512]{1,0:T(8,128)(2,1)S(1)} %maximum_select_fusion.1), channel_id=1, source_target_pairs={{0,8},{2,10},{4,12},{6,14},{8,0},{10,2},{12,4},{14,6},{16,24},{18,... | collective-permute-start | bytes 983048 | tf_op jit(solution)/shard_map/ppermute | solution.py:345
  108.9 6.7 %shard_map.127 = bf16[256,2048]{1,0:T(8,128)(2,1)} custom-call(bf16[256,1024]{1,0:T(8,128)(2,1)} %collective-permute-done.8.refs_0_, bf16[256,1024]{1,0:T(8,128)(2,1)} %collective-permute-done.9.refs_1_, bf16[1024,2048]{1,0:T(8,128)(2,1)} %refs_2_.5, bf16[1024,2048]{1,0:T(8,128)(2,1)} %collective-permute-done.3.refs_4_.refs_3_), custom_call_target="tpu_custom_call" | custom-call | flops 1 | bytes 1 | tf_op jit(solution)/shard_map/pallas_call | solution.py:264
  115.7 8.9 %shard_map.128 = (bf16[256,2048]{1,0:T(8,128)(2,1)}, bf16[256,2048]{1,0:T(8,128)(2,1)}) custom-call(bf16[256,1024]{1,0:T(8,128)(2,1)} %get-tuple-element.124.refs_0_, bf16[256,1024]{1,0:T(8,128)(2,1)} %get-tuple-element.137.refs_1_, bf16[512,1024]{1,0:T(8,128)(2,1)} %copy-done.3, bf16[1024,2048]{1,0:T(8,128)(2,1)} %refs_2_.5, ...), custom_call_target="tpu_custom_call" | custom-call | flops 1 | bytes 1 | tf_op jit(solution)/shard_map/pallas_call | solution.py:264
  128.3 6.4 %collective-permute-start.18 = (bf16[256,2048]{1,0:T(8,128)(2,1)S(1)}, bf16[256,2048]{1,0:T(8,128)(2,1)}, u32[]{:S(2)}, u32[]{:S(2)}) collective-permute-start(bf16[256,2048]{1,0:T(8,128)(2,1)S(1)} %add.165), channel_id=1, source_target_pairs={{16,0},{18,2},{20,4},{22,6},{9,25},{11,27},{13,29},{15,31}} | collective-permute-start | bytes 3145736 | tf_op jit(solution)/shard_map/ppermute | solution.py:349
  134.7 2.3 collective-permute-start.20
  138.5 6.7 %shard_map.129 = bf16[256,2048]{1,0:T(8,128)(2,1)} custom-call(bf16[256,1024]{1,0:T(8,128)(2,1)} %collective-permute-done.14.refs_0_, bf16[256,1024]{1,0:T(8,128)(2,1)} %collective-permute-done.15.refs_1_, bf16[1024,2048]{1,0:T(8,128)(2,1)} %refs_2_.5, bf16[1024,2048]{1,0:T(8,128)(2,1)} %collective-permute-done.3.refs_4_.refs_3_), custom_call_target="tpu_custom_call" | custom-call | flops 1 | bytes 1 | tf_op jit(solution)/shard_map/pallas_call | solution.py:264
  145.2 10.3 %collective-permute-done.18 = bf16[256,2048]{1,0:T(8,128)(2,1)} collective-permute-done((bf16[256,2048]{1,0:T(8,128)(2,1)S(1)}, bf16[256,2048]{1,0:T(8,128)(2,1)}, u32[]{:S(2)}, u32[]{:S(2)}) %collective-permute-start.18) | collective-permute-done | bytes 1048608 | tf_op jit(solution)/shard_map/ppermute | solution.py:349
  166.2 6.7 %shard_map.130 = bf16[256,2048]{1,0:T(8,128)(2,1)} custom-call(bf16[256,1024]{1,0:T(8,128)(2,1)} %collective-permute-done.21.refs_0_, bf16[256,1024]{1,0:T(8,128)(2,1)} %collective-permute-done.22.refs_1_, bf16[1024,2048]{1,0:T(8,128)(2,1)} %refs_2_.5, bf16[1024,2048]{1,0:T(8,128)(2,1)} %collective-permute-done.3.refs_4_.refs_3_), custom_call_target="tpu_custom_call" | custom-call | flops 1 | bytes 1 | tf_op jit(solution)/shard_map/pallas_call | solution.py:264
  172.8 16.3 %collective-permute-done.23 = bf16[256,2048]{1,0:T(8,128)(2,1)S(1)} collective-permute-done((bf16[256,2048]{1,0:T(8,128)(2,1)S(1)}, bf16[256,2048]{1,0:T(8,128)(2,1)S(1)}, u32[]{:S(2)}, u32[]{:S(2)}) %collective-permute-start.23) | collective-permute-done | bytes 1048608 | tf_op jit(solution)/shard_map/ppermute | solution.py:349
  191.6 5.9 %collective-permute-start.26 = (bf16[256,2048]{1,0:T(8,128)(2,1)S(1)}, bf16[256,2048]{1,0:T(8,128)(2,1)S(1)}, u32[]{:S(2)}, u32[]{:S(2)}) collective-permute-start(bf16[256,2048]{1,0:T(8,128)(2,1)S(1)} %add.170), channel_id=1, source_target_pairs={{16,8},{18,10},{20,12},{22,14},{9,17},{11,19},{13,21},{15,23}} | collective-permute-start | bytes 3145736 | tf_op jit(solution)/shard_map/ppermute | solution.py:349
  199.5 19.5 %collective-permute-done.26 = bf16[256,2048]{1,0:T(8,128)(2,1)S(1)} collective-permute-done((bf16[256,2048]{1,0:T(8,128)(2,1)S(1)}, bf16[256,2048]{1,0:T(8,128)(2,1)S(1)}, u32[]{:S(2)}, u32[]{:S(2)}) %collective-permute-start.26) | collective-permute-done | bytes 1048608 | tf_op jit(solution)/shard_map/ppermute | solution.py:349
  219.5 3.7 %collective-permute-done.27 = bf16[256,2048]{1,0:T(8,128)(2,1)S(1)} collective-permute-done((bf16[256,2048]{1,0:T(8,128)(2,1)S(1)}, bf16[256,2048]{1,0:T(8,128)(2,1)S(1)}, u32[]{:S(2)}, u32[]{:S(2)}) %collective-permute-start.27) | collective-permute-done | bytes 1048608 | tf_op jit(solution)/shard_map/ppermute | solution.py:349
  227.4 1.9 collective-permute-done.30.back_sib
  229.2 11.5 %shard_map.131 = (f32[4,512,512]{2,1,0:T(8,128)}, f32[4,512,512]{2,1,0:T(8,128)}, f32[4,1,512]{2,1,0:T(1,128)}, f32[4,1,512]{2,1,0:T(1,128)}) custom-call(s32[3]{0:T(128)} %pad_add_fusion.5.place_ref, bf16[4,160,512]{2,1,0:T(8,128)(2,1)} %bitcast.29, bf16[4,160,512]{2,1,0:T(8,128)(2,1)} %collective-permute-done.28.back, bf16[4,160,512]{2,1,0:T(8,128)(2,1)} %copy-done.9, ...), custom_call_target="tpu_custom_call" | custom-call | flops 1 | bytes 1 | tf_op jit(solution)/shard_map/pallas_call | solution.py:129
  240.8 4.8 %collective-permute-start.31 = (f32[4,1,512]{2,1,0:T(1,128)}, f32[4,1,512]{2,1,0:T(1,128)S(1)}, u32[]{:S(2)}, u32[]{:S(2)}) collective-permute-start(f32[4,1,512]{2,1,0:T(1,128)} %get-tuple-element.163), channel_id=1, source_target_pairs={{1,0},{0,1},{3,2},{2,3},{5,4},{4,5},{7,6},{6,7},{9,8},{8,9},{11,10... | collective-permute-start | bytes 24584 | tf_op jit(solution)/shard_map/ppermute | solution.py:305
  250.6 2.7 %select_select_fusion.refs_0_ = bf16[256,2048]{1,0:T(8,128)(2,1)} fusion(bf16[256,2048]{1,0:T(8,128)(2,1)S(1)} %add.173, bf16[256,2048]{1,0:T(8,128)(2,1)S(1)} %add.171, bf16[256,2048]{1,0:T(8,128)(2,1)S(1)} %add.167, bf16[256,2048]{1,0:T(8,128)(2,1)} %add.174, bf16[256,2048]{1,0:T(8,128)(2,1)} %collective-permute-done.32, pred[]{:T(512)S(6)} %eq.29, ...), kind=kLoop, calls=%fused_computation | loop fusion | flops 2097152 | bytes 6291459 | tf_op jit(solution)/shard_map/jit(_where)/select_n | solution.py:487
  254.0 2.2 collective-permute-done.33.refs_1_
  257.2 7.9 %shard_map.132 = bf16[256,2048]{1,0:T(8,128)(2,1)} custom-call(s32[3]{0:T(128)} %pad_add_fusion.place_ref, bf16[256,2048]{1,0:T(8,128)(2,1)} %select_select_fusion.refs_0_, bf16[256,2048]{1,0:T(8,128)(2,1)} %copy-done.15, bf16[4,512,512]{2,1,0:T(8,128)(2,1)} %refs_2_.7, bf16[8,512,512]{2,1,0:T(8,128)(2,1)} %refs_3_.6, ...), custom_call_target="tpu_custom_call" | custom-call | flops 3221225472 | bytes 4194304 | tf_op jit(solution)/shard_map/pallas_call | solution.py:183
  (114 shorter events, 47.3 us)
Async XLA Ops:
  0.6 21.0 %collective-permute-start.3 = (bf16[1024,2048]{1,0:T(8,128)(2,1)}, bf16[1024,2048]{1,0:T(8,128)(2,1)}, u32[]{:S(2)}, u32[]{:S(2)}) collective-permute-start(bf16[1024,2048]{1,0:T(8,128)(2,1)} %refs_2_.5), channel_id=1, source_target_pairs={{0,2},{2,0},{4,6},{6,4},{8,10},{10,8},{12,14},{14,12},{16,18},{18,... | collective-permute-start | bytes 12582920 | tf_op jit(solution)/shard_map/ppermute | solution.py:299
  5.3 7.2 %collective-permute-start.4 = (bf16[256,2048]{1,0:T(8,128)(2,1)}, bf16[256,2048]{1,0:T(8,128)(2,1)S(1)}, u32[]{:S(2)}, u32[]{:S(2)}) collective-permute-start(bf16[256,2048]{1,0:T(8,128)(2,1)} %get-tuple-element.95), channel_id=1, source_target_pairs={{0,2},{2,0},{4,6},{6,4},{8,10},{10,8},{12,14},{14,12},{16,18},{18,... | collective-permute-start | bytes 3145736 | tf_op jit(solution)/shard_map/ppermute | solution.py:299
  11.8 9.9 %collective-permute-start = (bf16[512,1024]{1,0:T(8,128)(2,1)}, bf16[512,1024]{1,0:T(8,128)(2,1)S(1)}, u32[]{:S(2)}, u32[]{:S(2)}) collective-permute-start(bf16[512,1024]{1,0:T(8,128)(2,1)} %get-tuple-element.89), channel_id=1, source_target_pairs={{0,2},{2,0},{4,6},{6,4},{8,10},{10,8},{12,14},{14,12},{16,18},{18,... | collective-permute-start | bytes 3145736 | tf_op jit(solution)/shard_map/ppermute | solution.py:299
  18.6 17.3 %collective-permute-start.5 = (bf16[4,160,512]{2,1,0:T(8,128)(2,1)}, bf16[4,160,512]{2,1,0:T(8,128)(2,1)S(1)}, u32[]{:S(2)}, u32[]{:S(2)}) collective-permute-start(bf16[4,160,512]{2,1,0:T(8,128)(2,1)} %get-tuple-element.101), channel_id=1, source_target_pairs={{0,4},{2,6},{4,0},{6,2},{8,12},{10,14},{12,8},{14,10},{16,20},{18,... | collective-permute-start | bytes 1966088 | tf_op jit(solution)/shard_map/ppermute | solution.py:302
  20.1 16.0 %collective-permute-start.1 = (bf16[256,1024]{1,0:T(8,128)(2,1)}, bf16[256,1024]{1,0:T(8,128)(2,1)S(1)}, u32[]{:S(2)}, u32[]{:S(2)}) collective-permute-start(bf16[256,1024]{1,0:T(8,128)(2,1)} %get-tuple-element.90.refs_0_), channel_id=1, source_target_pairs={{1,0},{0,1},{3,2},{2,3},{5,4},{4,5},{7,6},{6,7},{9,8},{8,9},{11,10... | collective-permute-start | bytes 1572872 | tf_op jit(solution)/shard_map/ppermute | solution.py:305
  20.6 24.2 %collective-permute-start.2 = (bf16[256,1024]{1,0:T(8,128)(2,1)}, bf16[256,1024]{1,0:T(8,128)(2,1)S(1)}, u32[]{:S(2)}, u32[]{:S(2)}) collective-permute-start(bf16[256,1024]{1,0:T(8,128)(2,1)} %get-tuple-element.91), channel_id=1, source_target_pairs={{3,0},{2,1},{1,2},{0,3},{7,4},{6,5},{5,6},{4,7},{11,8},{10,9},{9,1... | collective-permute-start | bytes 1572872 | tf_op jit(solution)/shard_map/ppermute | solution.py:305
  45.6 10.2 %collective-permute-start.10 = (bf16[320,512]{1,0:T(8,128)(2,1)S(1)}, bf16[320,512]{1,0:T(8,128)(2,1)S(1)}, u32[]{:S(2)}, u32[]{:S(2)}) collective-permute-start(bf16[320,512]{1,0:T(8,128)(2,1)S(1)} %dynamic-slice_bitcast_fusion), channel_id=1, source_target_pairs={{0,8},{2,10},{4,12},{6,14},{8,0},{10,2},{12,4},{14,6},{16,24},{18,... | collective-permute-start | bytes 983048 | tf_op jit(solution)/shard_map/ppermute | solution.py:345
  46.0 25.6 %collective-permute-start.6 = (bf16[256,2048]{1,0:T(8,128)(2,1)}, bf16[256,2048]{1,0:T(8,128)(2,1)S(1)}, u32[]{:S(2)}, u32[]{:S(2)}) collective-permute-start(bf16[256,2048]{1,0:T(8,128)(2,1)} %get-tuple-element.103), channel_id=1, source_target_pairs={{0,4},{2,6},{4,0},{6,2},{8,12},{10,14},{12,8},{14,10},{16,20},{18,... | collective-permute-start | bytes 3145736 | tf_op jit(solution)/shard_map/ppermute | solution.py:302
  51.9 25.3 %collective-permute-start.7 = (bf16[512,1024]{1,0:T(8,128)(2,1)}, bf16[512,1024]{1,0:T(8,128)(2,1)S(1)}, u32[]{:S(2)}, u32[]{:S(2)}) collective-permute-start(bf16[512,1024]{1,0:T(8,128)(2,1)} %get-tuple-element.105), channel_id=1, source_target_pairs={{0,2},{2,0},{4,6},{6,4},{8,10},{10,8},{12,14},{14,12},{16,18},{18,... | collective-permute-start | bytes 3145736 | tf_op jit(solution)/shard_map/ppermute | solution.py:299
  52.0 20.0 %collective-permute-start.8 = (bf16[256,1024]{1,0:T(8,128)(2,1)}, bf16[256,1024]{1,0:T(8,128)(2,1)}, u32[]{:S(2)}, u32[]{:S(2)}) collective-permute-start(bf16[256,1024]{1,0:T(8,128)(2,1)} %get-tuple-element.108.refs_1_), channel_id=1, source_target_pairs={{1,0},{0,1},{3,2},{2,3},{5,4},{4,5},{7,6},{6,7},{9,8},{8,9},{11,10... | collective-permute-start | bytes 1572872 | tf_op jit(solution)/shard_map/ppermute | solution.py:305
  52.7 24.6 %collective-permute-start.9 = (bf16[256,1024]{1,0:T(8,128)(2,1)}, bf16[256,1024]{1,0:T(8,128)(2,1)}, u32[]{:S(2)}, u32[]{:S(2)}) collective-permute-start(bf16[256,1024]{1,0:T(8,128)(2,1)} %get-tuple-element.109), channel_id=1, source_target_pairs={{3,0},{2,1},{1,2},{0,3},{7,4},{6,5},{5,6},{4,7},{11,8},{10,9},{9,1... | collective-permute-start | bytes 1572872 | tf_op jit(solution)/shard_map/ppermute | solution.py:305
  55.8 9.5 %collective-permute-start.11 = (bf16[160,512]{1,0:T(8,128)(2,1)S(1)}, bf16[160,512]{1,0:T(8,128)(2,1)S(1)}, u32[]{:S(2)}, u32[]{:S(2)}) collective-permute-start(bf16[160,512]{1,0:T(8,128)(2,1)S(1)} %dynamic-slice_bitcast_fusion.1), channel_id=1, source_target_pairs={{0,16},{2,18},{4,20},{6,22},{8,24},{10,26},{12,28},{14,30},{16,0},... | collective-permute-start | bytes 491528 | tf_op jit(solution)/shard_map/ppermute | solution.py:345
  77.3 48.7 %collective-permute-start.12 = (bf16[256,2048]{1,0:T(8,128)(2,1)S(1)}, bf16[256,2048]{1,0:T(8,128)(2,1)}, u32[]{:S(2)}, u32[]{:S(2)}) collective-permute-start(bf16[256,2048]{1,0:T(8,128)(2,1)S(1)} %add.150), channel_id=1, source_target_pairs={{8,0},{10,2},{12,4},{14,6},{24,16},{26,18},{28,20},{30,22},{1,9},{... | collective-permute-start | bytes 3145736 | tf_op jit(solution)/shard_map/ppermute | solution.py:349
  78.5 49.3 %collective-permute-start.13 = (bf16[256,2048]{1,0:T(8,128)(2,1)}, bf16[256,2048]{1,0:T(8,128)(2,1)S(1)}, u32[]{:S(2)}, u32[]{:S(2)}) collective-permute-start(bf16[256,2048]{1,0:T(8,128)(2,1)} %shard_map.126), channel_id=1, source_target_pairs={{0,4},{2,6},{4,0},{6,2},{8,12},{10,14},{12,8},{14,10},{16,20},{18,... | collective-permute-start | bytes 3145736 | tf_op jit(solution)/shard_map/ppermute | solution.py:302
  80.1 7.3 %collective-permute-start.16 = (bf16[160,512]{1,0:T(8,128)(2,1)S(1)}, bf16[160,512]{1,0:T(8,128)(2,1)}, u32[]{:S(2)}, u32[]{:S(2)}) collective-permute-start(bf16[160,512]{1,0:T(8,128)(2,1)S(1)} %bitcast_add_fusion.1), channel_id=1, source_target_pairs={{0,16},{2,18},{4,20},{6,22},{8,24},{10,26},{12,28},{14,30},{16,0},... | collective-permute-start | bytes 491528 | tf_op jit(solution)/shard_map/ppermute | solution.py:345
  82.7 45.6 %collective-permute-start.14 = (bf16[256,1024]{1,0:T(8,128)(2,1)}, bf16[256,1024]{1,0:T(8,128)(2,1)}, u32[]{:S(2)}, u32[]{:S(2)}) collective-permute-start(bf16[256,1024]{1,0:T(8,128)(2,1)} %get-tuple-element.124.refs_0_), channel_id=1, source_target_pairs={{1,0},{0,1},{3,2},{2,3},{5,4},{4,5},{7,6},{6,7},{9,8},{8,9},{11,10... | collective-permute-start | bytes 1572872 | tf_op jit(solution)/shard_map/ppermute | solution.py:305
  86.3 41.9 %collective-permute-start.15 = (bf16[256,1024]{1,0:T(8,128)(2,1)}, bf16[256,1024]{1,0:T(8,128)(2,1)}, u32[]{:S(2)}, u32[]{:S(2)}) collective-permute-start(bf16[256,1024]{1,0:T(8,128)(2,1)} %get-tuple-element.125), channel_id=1, source_target_pairs={{3,0},{2,1},{1,2},{0,3},{7,4},{6,5},{5,6},{4,7},{11,8},{10,9},{9,1... | collective-permute-start | bytes 1572872 | tf_op jit(solution)/shard_map/ppermute | solution.py:305
  88.6 35.9 %collective-permute-start.17 = (bf16[320,512]{1,0:T(8,128)(2,1)S(1)}, bf16[320,512]{1,0:T(8,128)(2,1)}, u32[]{:S(2)}, u32[]{:S(2)}) collective-permute-start(bf16[320,512]{1,0:T(8,128)(2,1)S(1)} %maximum_select_fusion.1), channel_id=1, source_target_pairs={{0,8},{2,10},{4,12},{6,14},{8,0},{10,2},{12,4},{14,6},{16,24},{18,... | collective-permute-start | bytes 983048 | tf_op jit(solution)/shard_map/ppermute | solution.py:345
  128.3 27.2 %collective-permute-start.18 = (bf16[256,2048]{1,0:T(8,128)(2,1)S(1)}, bf16[256,2048]{1,0:T(8,128)(2,1)}, u32[]{:S(2)}, u32[]{:S(2)}) collective-permute-start(bf16[256,2048]{1,0:T(8,128)(2,1)S(1)} %add.165), channel_id=1, source_target_pairs={{16,0},{18,2},{20,4},{22,6},{9,25},{11,27},{13,29},{15,31}} | collective-permute-start | bytes 3145736 | tf_op jit(solution)/shard_map/ppermute | solution.py:349
  134.7 23.1 %collective-permute-start.20 = (bf16[256,2048]{1,0:T(8,128)(2,1)S(1)}, bf16[256,2048]{1,0:T(8,128)(2,1)}, u32[]{:S(2)}, u32[]{:S(2)}) collective-permute-start(bf16[256,2048]{1,0:T(8,128)(2,1)S(1)} %add.166), channel_id=1, source_target_pairs={{0,8},{2,10},{4,12},{6,14},{16,24},{18,26},{20,28},{22,30},{9,1},{... | collective-permute-start | bytes 3145736 | tf_op jit(solution)/shard_map/ppermute | solution.py:349
  137.0 24.3 %collective-permute-start.19 = (bf16[256,2048]{1,0:T(8,128)(2,1)}, bf16[256,2048]{1,0:T(8,128)(2,1)S(1)}, u32[]{:S(2)}, u32[]{:S(2)}) collective-permute-start(bf16[256,2048]{1,0:T(8,128)(2,1)} %get-tuple-element.133), channel_id=1, source_target_pairs={{0,4},{2,6},{4,0},{6,2},{8,12},{10,14},{12,8},{14,10},{16,20},{18,... | collective-permute-start | bytes 3145736 | tf_op jit(solution)/shard_map/ppermute | solution.py:302
  138.5 23.2 %collective-permute-start.21 = (bf16[256,1024]{1,0:T(8,128)(2,1)S(1)}, bf16[256,1024]{1,0:T(8,128)(2,1)}, u32[]{:S(2)}, u32[]{:S(2)}) collective-permute-start(bf16[256,1024]{1,0:T(8,128)(2,1)S(1)} %copy-done.12), channel_id=1, source_target_pairs={{1,0},{0,1},{3,2},{2,3},{5,4},{4,5},{7,6},{6,7},{9,8},{8,9},{11,10... | collective-permute-start | bytes 1572872 | tf_op jit(solution)/shard_map/ppermute | solution.py:305
  138.5 23.2 %collective-permute-start.22 = (bf16[256,1024]{1,0:T(8,128)(2,1)}, bf16[256,1024]{1,0:T(8,128)(2,1)}, u32[]{:S(2)}, u32[]{:S(2)}) collective-permute-start(bf16[256,1024]{1,0:T(8,128)(2,1)} %get-tuple-element.138), channel_id=1, source_target_pairs={{3,0},{2,1},{1,2},{0,3},{7,4},{6,5},{5,6},{4,7},{11,8},{10,9},{9,1... | collective-permute-start | bytes 1572872 | tf_op jit(solution)/shard_map/ppermute | solution.py:305
  161.7 27.5 %collective-permute-start.23 = (bf16[256,2048]{1,0:T(8,128)(2,1)S(1)}, bf16[256,2048]{1,0:T(8,128)(2,1)S(1)}, u32[]{:S(2)}, u32[]{:S(2)}) collective-permute-start(bf16[256,2048]{1,0:T(8,128)(2,1)S(1)} %add.168), channel_id=1, source_target_pairs={{0,8},{2,10},{4,12},{6,14},{24,16},{26,18},{28,20},{30,22},{1,9},{... | collective-permute-start | bytes 3145736 | tf_op jit(solution)/shard_map/ppermute | solution.py:349
  163.0 26.6 %collective-permute-start.24 = (bf16[256,2048]{1,0:T(8,128)(2,1)S(1)}, bf16[256,2048]{1,0:T(8,128)(2,1)}, u32[]{:S(2)}, u32[]{:S(2)}) collective-permute-start(bf16[256,2048]{1,0:T(8,128)(2,1)S(1)} %add.169), channel_id=1, source_target_pairs={{8,24},{10,26},{12,28},{14,30},{17,1},{19,3},{21,5},{23,7}} | collective-permute-start | bytes 3145736 | tf_op jit(solution)/shard_map/ppermute | solution.py:349
  164.7 26.5 %collective-permute-start.25 = (bf16[256,2048]{1,0:T(8,128)(2,1)S(1)}, bf16[256,2048]{1,0:T(8,128)(2,1)S(1)}, u32[]{:S(2)}, u32[]{:S(2)}) collective-permute-start(bf16[256,2048]{1,0:T(8,128)(2,1)S(1)} %copy-done.7), channel_id=1, source_target_pairs={{0,4},{2,6},{4,0},{6,2},{8,12},{10,14},{12,8},{14,10},{16,20},{18,... | collective-permute-start | bytes 3145736 | tf_op jit(solution)/shard_map/ppermute | solution.py:302
  191.6 27.5 %collective-permute-start.26 = (bf16[256,2048]{1,0:T(8,128)(2,1)S(1)}, bf16[256,2048]{1,0:T(8,128)(2,1)S(1)}, u32[]{:S(2)}, u32[]{:S(2)}) collective-permute-start(bf16[256,2048]{1,0:T(8,128)(2,1)S(1)} %add.170), channel_id=1, source_target_pairs={{16,8},{18,10},{20,12},{22,14},{9,17},{11,19},{13,21},{15,23}} | collective-permute-start | bytes 3145736 | tf_op jit(solution)/shard_map/ppermute | solution.py:349
  197.5 25.8 %collective-permute-start.27 = (bf16[256,2048]{1,0:T(8,128)(2,1)S(1)}, bf16[256,2048]{1,0:T(8,128)(2,1)S(1)}, u32[]{:S(2)}, u32[]{:S(2)}) collective-permute-start(bf16[256,2048]{1,0:T(8,128)(2,1)S(1)} %add.172), channel_id=1, source_target_pairs={{0,8},{2,10},{4,12},{6,14},{24,16},{26,18},{28,20},{30,22},{1,9},{... | collective-permute-start | bytes 3145736 | tf_op jit(solution)/shard_map/ppermute | solution.py:349
  198.8 25.8 %collective-permute-start.28 = (bf16[4,160,512]{2,1,0:T(8,128)(2,1)S(1)}, bf16[4,160,512]{2,1,0:T(8,128)(2,1)}, u32[]{:S(2)}, u32[]{:S(2)}) collective-permute-start(bf16[4,160,512]{2,1,0:T(8,128)(2,1)S(1)} %bitcast.27), channel_id=1, source_target_pairs={{0,4},{2,6},{4,0},{6,2},{8,12},{10,14},{12,8},{14,10},{16,20},{18,... | collective-permute-start | bytes 1966088 | tf_op jit(solution)/shard_map/ppermute | solution.py:302
  199.5 25.1 %collective-permute-start.29 = (bf16[4,160,512]{2,1,0:T(8,128)(2,1)S(1)}, bf16[4,160,512]{2,1,0:T(8,128)(2,1)S(1)}, u32[]{:S(2)}, u32[]{:S(2)}) collective-permute-start(bf16[4,160,512]{2,1,0:T(8,128)(2,1)S(1)} %bitcast.28), channel_id=1, source_target_pairs={{0,2},{2,0},{4,6},{6,4},{8,10},{10,8},{12,14},{14,12},{16,18},{18,... | collective-permute-start | bytes 1966088 | tf_op jit(solution)/shard_map/ppermute | solution.py:299
  225.4 25.1 %collective-permute-start.32 = (bf16[256,2048]{1,0:T(8,128)(2,1)}, bf16[256,2048]{1,0:T(8,128)(2,1)}, u32[]{:S(2)}, u32[]{:S(2)}) collective-permute-start(bf16[256,2048]{1,0:T(8,128)(2,1)} %add.174), channel_id=1, source_target_pairs={{8,16},{10,18},{12,20},{14,22},{17,9},{19,11},{21,13},{23,15}} | collective-permute-start | bytes 3145736 | tf_op jit(solution)/shard_map/ppermute | solution.py:349
  240.8 8.2 %collective-permute-start.31 = (f32[4,1,512]{2,1,0:T(1,128)}, f32[4,1,512]{2,1,0:T(1,128)S(1)}, u32[]{:S(2)}, u32[]{:S(2)}) collective-permute-start(f32[4,1,512]{2,1,0:T(1,128)} %get-tuple-element.163), channel_id=1, source_target_pairs={{1,0},{0,1},{3,2},{2,3},{5,4},{4,5},{7,6},{6,7},{9,8},{8,9},{11,10... | collective-permute-start | bytes 24584 | tf_op jit(solution)/shard_map/ppermute | solution.py:305
  (21 other events, 314.2 us)

commit v5 on v4

--- a/solution.py
+++ b/solution.py
@@ -198,30 +198,43 @@
     )(*args)
 
 
-def turn_kernel(which_ref, block, *outs):
+def turn_kernel(which_ref, block, first, second, across):
     del which_ref
     step = pl.program_id(0)
-    for n, out in enumerate(outs):
-
-        @pl.when((step == n) | ((n == 4) & (step >= 2)))
-        def _(out=out):
-            out[...] = block[...].T
+    flipped = block[...].T
+
+    @pl.when(step < 2)
+    def _():
+        first[...] = flipped
+
+    @pl.when(step >= 2)
+    def _():
+        second[...] = flipped
+
+    @pl.when(step % 2 == 1)
+    def _():
+        across[...] = flipped
 
 
 def turned(rows, which, n_rows):
     tokens, _ = rows.shape
-    one = pl.BlockSpec((n_rows, tokens), lambda i, which: (0, 0))
+
+    def out(place):
+        return pl.BlockSpec((n_rows, tokens), lambda i, which: (place(i), 0))
+
     return pl.pallas_call(
         turn_kernel,
         grid_spec=pltpu.PrefetchScalarGridSpec(
             num_scalar_prefetch=1,
             grid=(4,),
             in_specs=[pl.BlockSpec((tokens, n_rows), lambda i, which: (0, which[i]))],
-            out_specs=[one] * 4
-            + [pl.BlockSpec((n_rows, tokens), lambda i, which: (jnp.clip(i - 2, 0, 1), 0))],
-        ),
-        out_shape=[jax.ShapeDtypeStruct((n_rows, tokens), BF16)] * 4
-        + [jax.ShapeDtypeStruct((2 * n_rows, tokens), BF16)],
+            out_specs=[
+                out(lambda i: jnp.minimum(i, 1)),
+                out(lambda i: jnp.maximum(i - 2, 0)),
+                out(lambda i: i // 2),
+            ],
+        ),
+        out_shape=[jax.ShapeDtypeStruct((2 * n_rows, tokens), BF16)] * 3,
         compiler_params=pltpu.CompilerParams(vmem_limit_bytes=VMEM),
         cost_estimate=SMALL,
     )(jnp.stack(which).astype(jnp.int32), rows)
@@ -255,25 +268,27 @@
                 outs[at * chunks + n][...] = total[at * rows : (at + 1) * rows].astype(BF16)
 
 
-def products(halves, n_outs, rows, chunks):
+def products(halves, n_outs, n_rows, rows, chunks):
     tokens, width = rows[0].shape
-    n_rows = sum(piece.shape[0] for piece in halves[0])
     tile = 512
     each = width // chunks // tile
     strip = pl.BlockSpec((tokens, tile), lambda i: (0, i))
+    first, second = ([min(p.shape[0], n_rows * n_outs // len(half)) for p in half] for half in halves)
     outs = pl.pallas_call(
         functools.partial(product_kernel, [len(half) for half in halves], n_outs),
         grid=(width // tile,),
-        in_specs=[pl.BlockSpec(p.shape, lambda i: (0, 0)) for half in halves for p in half] + [strip] * 2,
+        in_specs=[pl.BlockSpec((size, tokens), lambda i: (0, 0)) for size in first + second] + [strip] * 2,
         out_specs=[
-            pl.BlockSpec((n_rows // n_outs, tile), lambda i, n=n: (0, jnp.clip(i - n * each, 0, each - 1)))
+            pl.BlockSpec((n_rows, tile), lambda i, n=n: (0, jnp.clip(i - n * each, 0, each - 1)))
             for _ in range(n_outs)
             for n in range(chunks)
         ],
-        out_shape=[jax.ShapeDtypeStruct((n_rows // n_outs, width // chunks), BF16)] * (n_outs * chunks),
-        scratch_shapes=[pltpu.VMEM((n_rows, 2 * tokens), BF16)],
+        out_shape=[jax.ShapeDtypeStruct((n_rows, width // chunks), BF16)] * (n_outs * chunks),
+        scratch_shapes=[pltpu.VMEM((n_outs * n_rows, 2 * tokens), BF16)],
         compiler_params=pltpu.CompilerParams(vmem_limit_bytes=VMEM),
-        cost_estimate=SMALL,
+        cost_estimate=pl.CostEstimate(
+            flops=8 * n_outs * tokens * n_rows * width, bytes_accessed=4 * tokens * width, transcendentals=0
+        ),
     )(*halves[0], *halves[1], *rows)
     return [outs[m * chunks : (m + 1) * chunks] for m in range(n_outs)]
 
@@ -301,16 +316,8 @@
     def swap_x(v):
         return lax.ppermute(v, "dp", [(i, i ^ 2) for i in range(n_dp)])
 
-    def from_worker(v, step, flip):
-        return lax.ppermute(
-            v,
-            both,
-            [
-                ((i ^ flip) * n_worker + (j + step) % n_worker, i * n_worker + j)
-                for i in range(n_dp)
-                for j in range(n_worker)
-            ],
-        )
+    def from_worker(v, step):
+        return lax.ppermute(v, "worker", [((j + step) % n_worker, j) for j in range(n_worker)])
 
     def place(owner, j):
         return owner * z_per_worker + (j if owner < n_worker // 2 else z_per_worker - 1 - j)
@@ -360,8 +367,7 @@
     for step, j in shards:
         if step:
             for at in range(2):
-                for flip in range(2):
-                    y_stage[step, j, at, flip] = arrived + at
+                y_stage[step, j, at] = arrived + at
             clock = max(clock + 1, arrived + 2)
             product_stage[step, j, 0] = clock - 1
             product_stage[step, j, 1] = max(clock - 1, arrived + 2)
@@ -376,7 +382,7 @@
     for n_hop in range(len(z_bits)):
         for step, j, n in x_stage:
             ready = max(x_stage[step, j, n], product_stage[step, j, 1])
-            clock = (z_stage[step, j, n, n_hop - 1] if n_hop else ready) + 1
+            clock = (z_stage[step, j, n, n_hop - 1] if n_hop else max(ready, 2)) + 1
             moves = links(hops_of(step, j)[n_hop])
             while any((clock, link) in busy for link in moves):
                 clock += 1
@@ -391,10 +397,16 @@
     done = {}
 
     def turn(rows, j):
-        which = [piece(j, at, flip) for flip in range(2) for at in range(2)]
-        *single, both_rows = turned(rows, which, rows_dev)
-        found = {("p", j, at, flip): single[2 * flip + at] for flip in range(2) for at in range(2)}
-        return {**found, ("p", j): both_rows}
+        which = [piece(j, at, flip) for at in range(2) for flip in range(2)]
+        other, own, across = turned(rows, which, rows_dev)
+        return {("p", j, 0): other, ("p", j, 1): own, ("p", j): across}
+
+    def gathered(part, bits):
+        for far in bits:
+            other = swap_z(part, far)
+            mine_first = jnp.concatenate([part, other], axis=0)
+            part = jnp.where(z // far % 2 == 0, mine_first, jnp.concatenate([other, part], axis=0))
+        return part
 
     for stage in range(last + 1):
         if stage:
@@ -414,9 +426,12 @@
                 found = turn(env["cotan"], j)
                 joined["c", j] = swap_core(found.pop(("p", j)))
                 joined.update(found)
-        for (step, j, at, flip), when in y_stage.items():
+        arrivals = {}
+        for (step, j, at), when in y_stage.items():
             if when == stage:
-                joined["c", step, j, at, flip] = from_worker(env["p", j, at, flip], step, flip)
+                joined["r", step, j, at] = from_worker(env["p", j, at], step)
+            if when == stage - 1:
+                arrivals[step, j, at] = swap_core(env["r", step, j, at][rows_dev:])
         for (step, j, n), when in x_stage.items():
             if when == stage:
                 joined["got", step, j, n] = swap_x(env.pop(("out", step, j, n)))
@@ -431,13 +446,9 @@
                 parts = part.reshape(2, -1, block_size)
                 there = lax.dynamic_index_in_dim(parts, 1 - bit, 0, keepdims=False)
                 part = lax.dynamic_index_in_dim(parts, bit, 0, keepdims=False) + swap_z(there, far)
-            joined["keep"] = part
+            joined["keep"] = gathered(part, z_bits[-1:])
         if stage == 2:
-            part = env["keep"]
-            for far in reversed(z_bits):
-                other = swap_z(part, far)
-                mine_first = jnp.concatenate([part, other], axis=0)
-                part = jnp.where(z // far % 2 == 0, mine_first, jnp.concatenate([other, part], axis=0))
+            part = gathered(env["keep"], reversed(z_bits[:-1]))
             joined["keep"] = part.reshape(local_blocks, -1, block_size)
         if stage == across:
             joined["back"] = swap_x(env["keep"])
@@ -451,20 +462,22 @@
                 basis_in,
                 basis_out,
             )
-            eigs = [eig_local] + [from_worker(eig_local, step, 0) for step in range(1, n_worker)]
+            eigs = [eig_local] + [from_worker(eig_local, step) for step in range(1, n_worker)]
             eig_out = jnp.concatenate(eigs, axis=0)
             for key in [key for key in env if key[0] == "acc"]:
                 env[key], eig_out = lax.optimization_barrier((env[key], eig_out))
 
+        for (step, j, at), rows in arrivals.items():
+            joined["s", step, j, at] = rows
         for step, j in shards:
             due = [at for at in range(2) if product_stage[step, j, at] == stage]
             if due:
-                known = {**env, **joined} if stage == 0 else env
+                known = {**env, **joined} if stage == 0 else {**env, **{("s", *k): v for k, v in arrivals.items()}}
                 if step == 0:
-                    halves = [[known["p", j, at, 0] for at in range(2)], [known["c", j]]]
+                    halves = [[known["p", j, at] for at in range(2)], [known["c", j]]]
                 else:
-                    halves = [[known["c", step, j, at, flip] for at in due] for flip in range(2)]
-                found = products(halves, len(due), (known["acts"], known["acts_sib"]), len(starts))
+                    halves = [[known[name, step, j, at] for at in due] for name in ("r", "s")]
+                found = products(halves, len(due), rows_dev, (known["acts"], known["acts_sib"]), len(starts))
                 for at, outs in zip(due, found):
                     for n in chunks:
                         joined["mine" if at else "out", step, j, n] = outs[n]

time: 268 us -> 235 us (0.88)
  starting transfers between devices: 67.2 us -> 42.7 us
  waiting for transfers between devices: 84.5 us -> 73.6 us
  local copies, waits for them, and re-layouts: 6.32 us -> 12.7 us
  other arithmetic: 21.1 us -> 17.2 us
    ppermute x4, starting transfers between devices: 26 us -> 7.76 us  [swap_z(): return lax.ppermute(v, 'dp', [(i, i ^ 4 * bit) for i in range(n_dp)])]
    ppermute x8, waiting for transfers between devices: 50.9 us -> 39.2 us  [hop(): return lax.ppermute(v, both, pairs)]
    ppermute x9 -> x5, waiting for transfers between devices: 14 us -> 4.98 us  [from_worker(): lax.ppermute(v, 'worker', [((j + step) % n_worker, j) for j in range(n_wo...]
    ppermute x9 -> x5, starting transfers between devices: 11.9 us -> 3.68 us  [from_worker(): lax.ppermute(v, 'worker', [((j + step) % n_worker, j) for j in range(n_wo...]
    ppermute x4, waiting for transfers between devices: 3.11 us -> 6.94 us  [swap_z(): return lax.ppermute(v, 'dp', [(i, i ^ 4 * bit) for i in range(n_dp)])]
    ppermute x6 -> x10, waiting for transfers between devices: 1.87 us -> 5.62 us  [swap_core(): return lax.ppermute(v, 'dp', [(i, i ^ 1) for i in range(n_dp)])]
    slice x0 -> x4, local copies, waits for them, and re-layouts: none -> 3.26 us  [per_device(): arrivals[step, j, at] = swap_core(env['r', step, j, at][rows_dev:])]
    unnamed x38 -> x42, local copies, waits for them, and re-layouts: 4.6 us -> 7.63 us
  transfers between devices with their start and end apart: 34 -> 34, of which waited for: 15 -> 18; matrix products, arithmetic and copies ran while one was open for 7% -> 8% of each run, Pallas kernels for 28% -> 32%
where the time goes in v5:
time: 235 us; the launch traced here: 232 us
  Pallas kernels  83.1 us (35%)
  waiting for transfers between devices  73.6 us (31%)
  starting transfers between devices  42.7 us (18%)
  other arithmetic  17.2 us (7%)
  local copies, waits for them, and re-layouts  12.7 us (5%)
  between operations  2.79 us (1%)
    pallas_call x6, Pallas kernels, products(): pl.pallas_call(functools.partial(product_kernel, [len(half) for half in h...  44.6 us
    ppermute x8, waiting for transfers between devices, hop(): return lax.ppermute(v, both, pairs)  39.2 us
    ppermute x8, starting transfers between devices, hop(): return lax.ppermute(v, both, pairs)  23.2 us
    ppermute x6, waiting for transfers between devices, swap_x(): return lax.ppermute(v, 'dp', [(i, i ^ 2) for i in range(n_dp)])  14.5 us
    pallas_call x1, Pallas kernels, update_factors(): pl.pallas_call(factor_kernel, grid_spec=pltpu.PrefetchScalarGridSpec(num_...  11.6 us
    pallas_call x2, Pallas kernels, turned(): pl.pallas_call(turn_kernel, grid_spec=pltpu.PrefetchScalarGridSpec(num_sc...  10.5 us
    pallas_call x1, Pallas kernels, tail(): pl.pallas_call(functools.partial(tail_kernel, len(parts)), grid_spec=pltp...  7.92 us
    ppermute x4, starting transfers between devices, swap_z(): return lax.ppermute(v, 'dp', [(i, i ^ 4 * bit) for i in range(n_dp)])  7.76 us
  transfers between devices with their start and end apart: 34, of which 18 were waited for; matrix products, arithmetic and copies ran while one was open for 8% of the time, Pallas kernels for 32%

profile of v5, /device:TPU:12, one launch (start us, length us, event | category | flops | bytes accessed | tf_op | source)
XLA Modules:
  0.0 232.1 jit_solution(15229144568920502087)
XLA Ops:
  2.0 3.3 %shard_map.123 = (bf16[256,2048]{1,0:T(8,128)(2,1)}, bf16[256,2048]{1,0:T(8,128)(2,1)}) custom-call(s32[3]{0:T(128)} %pad_add_fusion.3.which_ref, bf16[1024,2048]{1,0:T(8,128)(2,1)} %refs_2_.5, bf16[1024,2048]{1,0:T(8,128)(2,1)} %block.2), custom_call_target="tpu_custom_call" | custom-call | flops 1 | bytes 1 | tf_op jit(solution)/shard_map/pallas_call | solution.py:35
  6.4 5.2 %shard_map.121 = (bf16[512,1024]{1,0:T(8,128)(2,1)}, bf16[512,1024]{1,0:T(8,128)(2,1)}, bf16[512,1024]{1,0:T(8,128)(2,1)}) custom-call(s32[4]{0:T(128)} %get-tuple-element.151.which_ref, bf16[1024,2048]{1,0:T(8,128)(2,1)} %block.2), custom_call_target="tpu_custom_call" | custom-call | flops 1 | bytes 1 | tf_op jit(solution)/shard_map/pallas_call | solution.py:225
  13.8 5.2 %shard_map.124 = (bf16[4,160,512]{2,1,0:T(8,128)(2,1)}, bf16[4,160,512]{2,1,0:T(8,128)(2,1)}) custom-call(s32[2]{0:T(128)} %pad_add_fusion.2.place_ref, bf16[256,2048]{1,0:T(8,128)(2,1)} %get-tuple-element.81.ours, bf16[256,2048]{1,0:T(8,128)(2,1)} %copy-done.4), custom_call_target="tpu_custom_call" | custom-call | flops 1 | bytes 1 | tf_op jit(solution)/shard_map/pallas_call | solution.py:73
  21.5 9.0 %shard_map.122 = (bf16[256,2048]{1,0:T(8,128)(2,1)}, bf16[256,2048]{1,0:T(8,128)(2,1)}) custom-call(bf16[512,1024]{1,0:T(8,128)(2,1)} %get-tuple-element.78.refs_0_, bf16[512,1024]{1,0:T(8,128)(2,1)} %get-tuple-element.95.refs_1_, bf16[512,1024]{1,0:T(8,128)(2,1)} %copy-done.13, bf16[1024,2048]{1,0:T(8,128)(2,1)} %refs_2_.5, ...), custom_call_target="tpu_custom_call" | custom-call | flops 8589934592 | bytes 8388608 | tf_op jit(solution)/shard_map/pallas_call | solution.py:277
  30.4 5.6 %collective-permute-done.4 = bf16[4,160,512]{2,1,0:T(8,128)(2,1)S(1)} collective-permute-done((bf16[4,160,512]{2,1,0:T(8,128)(2,1)}, bf16[4,160,512]{2,1,0:T(8,128)(2,1)S(1)}, u32[]{:S(2)}, u32[]{:S(2)}) %collective-permute-start.4) | collective-permute-done | bytes 655392 | tf_op jit(solution)/shard_map/ppermute | solution.py:317
  39.9 5.2 %shard_map.125 = (bf16[512,1024]{1,0:T(8,128)(2,1)}, bf16[512,1024]{1,0:T(8,128)(2,1)}, bf16[512,1024]{1,0:T(8,128)(2,1)}) custom-call(s32[4]{0:T(128)} %get-tuple-element.152.which_ref, bf16[1024,2048]{1,0:T(8,128)(2,1)} %block.2), custom_call_target="tpu_custom_call" | custom-call | flops 1 | bytes 1 | tf_op jit(solution)/shard_map/pallas_call | solution.py:225
  46.9 2.7 %collective-permute-start.10 = (bf16[160,512]{1,0:T(8,128)(2,1)S(1)}, bf16[160,512]{1,0:T(8,128)(2,1)S(1)}, u32[]{:S(2)}, u32[]{:S(2)}) collective-permute-start(bf16[160,512]{1,0:T(8,128)(2,1)S(1)} %dynamic-slice_bitcast_fusion.1), channel_id=1, source_target_pairs={{0,16},{2,18},{4,20},{6,22},{8,24},{10,26},{12,28},{14,30},{16,0},... | collective-permute-start | bytes 491528 | tf_op jit(solution)/shard_map/ppermute | solution.py:352
  49.6 6.4 %collective-permute-done.10 = bf16[160,512]{1,0:T(8,128)(2,1)S(1)} collective-permute-done((bf16[160,512]{1,0:T(8,128)(2,1)S(1)}, bf16[160,512]{1,0:T(8,128)(2,1)S(1)}, u32[]{:S(2)}, u32[]{:S(2)}) %collective-permute-start.10) | collective-permute-done | bytes 163872 | tf_op jit(solution)/shard_map/ppermute | solution.py:352
  56.0 3.4 %collective-permute-start.11 = (bf16[160,512]{1,0:T(8,128)(2,1)S(1)}, bf16[160,512]{1,0:T(8,128)(2,1)S(1)}, u32[]{:S(2)}, u32[]{:S(2)}) collective-permute-start(bf16[160,512]{1,0:T(8,128)(2,1)S(1)} %bitcast_add_fusion.1), channel_id=1, source_target_pairs={{0,16},{2,18},{4,20},{6,22},{8,24},{10,26},{12,28},{14,30},{16,0},... | collective-permute-start | bytes 491528 | tf_op jit(solution)/shard_map/ppermute | solution.py:352
  60.3 6.7 %shard_map.126 = bf16[256,2048]{1,0:T(8,128)(2,1)} custom-call(bf16[512,1024]{1,0:T(8,128)(2,1)} %copy-done.7, bf16[256,1024]{1,0:T(8,128)(2,1)} %copy-done.14, bf16[1024,2048]{1,0:T(8,128)(2,1)} %refs_2_.5, bf16[1024,2048]{1,0:T(8,128)(2,1)} %collective-permute-done.1.refs_4_.refs_3_), custom_call_target="tpu_custom_call" | custom-call | flops 4294967296 | bytes 8388608 | tf_op jit(solution)/shard_map/pallas_call | solution.py:277
  67.5 3.7 %collective-permute-done.8.refs_0_ = bf16[512,1024]{1,0:T(8,128)(2,1)} collective-permute-done((bf16[512,1024]{1,0:T(8,128)(2,1)}, bf16[512,1024]{1,0:T(8,128)(2,1)}, u32[]{:S(2)}, u32[]{:S(2)}) %collective-permute-start.8) | collective-permute-done | bytes 1048608 | tf_op jit(solution)/shard_map/ppermute | solution.py:320
  74.7 8.9 %shard_map.128 = (bf16[256,2048]{1,0:T(8,128)(2,1)}, bf16[256,2048]{1,0:T(8,128)(2,1)}) custom-call(bf16[512,1024]{1,0:T(8,128)(2,1)} %get-tuple-element.105.refs_0_, bf16[512,1024]{1,0:T(8,128)(2,1)} %get-tuple-element.117.refs_1_, bf16[512,1024]{1,0:T(8,128)(2,1)} %collective-permute-done.6.refs_2_, bf16[1024,2048]{1,0:T(8,128)(2,1)} %refs_2_.5, ...), custom_call_target="tpu_custom_call" | custom-call | flops 8589934592 | bytes 8388608 | tf_op jit(solution)/shard_map/pallas_call | solution.py:277
  84.8 6.7 %shard_map.127 = bf16[256,2048]{1,0:T(8,128)(2,1)} custom-call(bf16[512,1024]{1,0:T(8,128)(2,1)} %collective-permute-done.8.refs_0_, bf16[256,1024]{1,0:T(8,128)(2,1)} %copy-done.15, bf16[1024,2048]{1,0:T(8,128)(2,1)} %refs_2_.5, bf16[1024,2048]{1,0:T(8,128)(2,1)} %collective-permute-done.1.refs_4_.refs_3_), custom_call_target="tpu_custom_call" | custom-call | flops 4294967296 | bytes 8388608 | tf_op jit(solution)/shard_map/pallas_call | solution.py:277
  91.4 6.8 %collective-permute-done.13 = bf16[256,2048]{1,0:T(8,128)(2,1)S(1)} collective-permute-done((bf16[256,2048]{1,0:T(8,128)(2,1)}, bf16[256,2048]{1,0:T(8,128)(2,1)S(1)}, u32[]{:S(2)}, u32[]{:S(2)}) %collective-permute-start.13) | collective-permute-done | bytes 1048608 | tf_op jit(solution)/shard_map/ppermute | solution.py:317
  101.1 4.7 %collective-permute-start.18 = (bf16[256,2048]{1,0:T(8,128)(2,1)S(1)}, bf16[256,2048]{1,0:T(8,128)(2,1)S(1)}, u32[]{:S(2)}, u32[]{:S(2)}) collective-permute-start(bf16[256,2048]{1,0:T(8,128)(2,1)S(1)} %add.165), channel_id=1, source_target_pairs={{0,8},{2,10},{4,12},{6,14},{16,24},{18,26},{20,28},{22,30},{9,1},{... | collective-permute-start | bytes 3145736 | tf_op jit(solution)/shard_map/ppermute | solution.py:356
  107.6 1.9 collective-permute-done.19.refs_1_
  110.3 6.7 %shard_map.129 = bf16[256,2048]{1,0:T(8,128)(2,1)} custom-call(bf16[512,1024]{1,0:T(8,128)(2,1)} %copy-done.10, bf16[256,1024]{1,0:T(8,128)(2,1)} %copy-done.17, bf16[1024,2048]{1,0:T(8,128)(2,1)} %refs_2_.5, bf16[1024,2048]{1,0:T(8,128)(2,1)} %collective-permute-done.1.refs_4_.refs_3_), custom_call_target="tpu_custom_call" | custom-call | flops 4294967296 | bytes 8388608 | tf_op jit(solution)/shard_map/pallas_call | solution.py:277
  117.0 9.5 %collective-permute-done.16 = bf16[256,2048]{1,0:T(8,128)(2,1)S(1)} collective-permute-done((bf16[256,2048]{1,0:T(8,128)(2,1)S(1)}, bf16[256,2048]{1,0:T(8,128)(2,1)S(1)}, u32[]{:S(2)}, u32[]{:S(2)}) %collective-permute-start.16) | collective-permute-done | bytes 1048608 | tf_op jit(solution)/shard_map/ppermute | solution.py:356
  128.1 2.2 collective-permute-done.17
  130.7 5.5 %collective-permute-start.21 = (bf16[256,2048]{1,0:T(8,128)(2,1)S(1)}, bf16[256,2048]{1,0:T(8,128)(2,1)}, u32[]{:S(2)}, u32[]{:S(2)}) collective-permute-start(bf16[256,2048]{1,0:T(8,128)(2,1)S(1)} %add.166), channel_id=1, source_target_pairs={{16,0},{18,2},{20,4},{22,6},{9,25},{11,27},{13,29},{15,31}} | collective-permute-start | bytes 3145736 | tf_op jit(solution)/shard_map/ppermute | solution.py:356
  141.6 1.9 collective-permute-done.24.refs_1_
  144.3 6.7 %shard_map.130 = bf16[256,2048]{1,0:T(8,128)(2,1)} custom-call(bf16[512,1024]{1,0:T(8,128)(2,1)} %copy-done.9, bf16[256,1024]{1,0:T(8,128)(2,1)} %copy-done.16, bf16[1024,2048]{1,0:T(8,128)(2,1)} %refs_2_.5, bf16[1024,2048]{1,0:T(8,128)(2,1)} %collective-permute-done.1.refs_4_.refs_3_), custom_call_target="tpu_custom_call" | custom-call | flops 4294967296 | bytes 8388608 | tf_op jit(solution)/shard_map/pallas_call | solution.py:277
  151.0 5.0 %collective-permute-done.21 = bf16[256,2048]{1,0:T(8,128)(2,1)} collective-permute-done((bf16[256,2048]{1,0:T(8,128)(2,1)S(1)}, bf16[256,2048]{1,0:T(8,128)(2,1)}, u32[]{:S(2)}, u32[]{:S(2)}) %collective-permute-start.21) | collective-permute-done | bytes 1048608 | tf_op jit(solution)/shard_map/ppermute | solution.py:356
  157.5 3.5 %collective-permute-done.22 = bf16[256,2048]{1,0:T(8,128)(2,1)S(1)} collective-permute-done((bf16[256,2048]{1,0:T(8,128)(2,1)S(1)}, bf16[256,2048]{1,0:T(8,128)(2,1)S(1)}, u32[]{:S(2)}, u32[]{:S(2)}) %collective-permute-start.22) | collective-permute-done | bytes 1048608 | tf_op jit(solution)/shard_map/ppermute | solution.py:356
  163.4 6.3 %collective-permute-start.26 = (bf16[256,2048]{1,0:T(8,128)(2,1)S(1)}, bf16[256,2048]{1,0:T(8,128)(2,1)S(1)}, u32[]{:S(2)}, u32[]{:S(2)}) collective-permute-start(bf16[256,2048]{1,0:T(8,128)(2,1)S(1)} %add.170), channel_id=1, source_target_pairs={{16,8},{18,10},{20,12},{22,14},{9,17},{11,19},{13,21},{15,23}} | collective-permute-start | bytes 3145736 | tf_op jit(solution)/shard_map/ppermute | solution.py:356
  172.1 16.5 %collective-permute-done.26 = bf16[256,2048]{1,0:T(8,128)(2,1)S(1)} collective-permute-done((bf16[256,2048]{1,0:T(8,128)(2,1)S(1)}, bf16[256,2048]{1,0:T(8,128)(2,1)S(1)}, u32[]{:S(2)}, u32[]{:S(2)}) %collective-permute-start.26) | collective-permute-done | bytes 1048608 | tf_op jit(solution)/shard_map/ppermute | solution.py:356
  189.0 3.8 %collective-permute-done.27 = bf16[256,2048]{1,0:T(8,128)(2,1)S(1)} collective-permute-done((bf16[256,2048]{1,0:T(8,128)(2,1)S(1)}, bf16[256,2048]{1,0:T(8,128)(2,1)S(1)}, u32[]{:S(2)}, u32[]{:S(2)}) %collective-permute-start.27) | collective-permute-done | bytes 1048608 | tf_op jit(solution)/shard_map/ppermute | solution.py:356
  198.8 11.6 %shard_map.131 = (f32[4,512,512]{2,1,0:T(8,128)}, f32[4,512,512]{2,1,0:T(8,128)}, f32[4,1,512]{2,1,0:T(1,128)}, f32[4,1,512]{2,1,0:T(1,128)}) custom-call(s32[3]{0:T(128)} %pad_add_fusion.5.place_ref, bf16[4,160,512]{2,1,0:T(8,128)(2,1)} %bitcast.29, bf16[4,160,512]{2,1,0:T(8,128)(2,1)} %collective-permute-done.28.back, bf16[4,160,512]{2,1,0:T(8,128)(2,1)} %copy-done.5, ...), custom_call_target="tpu_custom_call" | custom-call | flops 1 | bytes 1 | tf_op jit(solution)/shard_map/pallas_call | solution.py:129
  210.4 2.2 collective-permute-start.31
  217.5 2.8 %select_select_fusion.refs_0_ = bf16[256,2048]{1,0:T(8,128)(2,1)} fusion(bf16[256,2048]{1,0:T(8,128)(2,1)S(1)} %add.173, bf16[256,2048]{1,0:T(8,128)(2,1)S(1)} %add.171, bf16[256,2048]{1,0:T(8,128)(2,1)S(1)} %add.169, bf16[256,2048]{1,0:T(8,128)(2,1)} %add.174, bf16[256,2048]{1,0:T(8,128)(2,1)} %collective-permute-done.32, pred[]{:T(512)S(6)} %eq.29, ...), kind=kLoop, calls=%fused_computation | loop fusion | flops 2097152 | bytes 6291459 | tf_op jit(solution)/shard_map/jit(_where)/select_n | solution.py:500
  220.8 2.3 collective-permute-done.33.refs_1_
  224.2 7.9 %shard_map.132 = bf16[256,2048]{1,0:T(8,128)(2,1)} custom-call(s32[3]{0:T(128)} %pad_add_fusion.place_ref, bf16[256,2048]{1,0:T(8,128)(2,1)} %select_select_fusion.refs_0_, bf16[256,2048]{1,0:T(8,128)(2,1)} %copy-done.12, bf16[4,512,512]{2,1,0:T(8,128)(2,1)} %refs_2_.7, bf16[8,512,512]{2,1,0:T(8,128)(2,1)} %refs_3_.6, ...), custom_call_target="tpu_custom_call" | custom-call | flops 3221225472 | bytes 4194304 | tf_op jit(solution)/shard_map/pallas_call | solution.py:183
  (122 shorter events, 49.9 us)
Async XLA Ops:
  0.6 19.9 %collective-permute-start.1 = (bf16[1024,2048]{1,0:T(8,128)(2,1)}, bf16[1024,2048]{1,0:T(8,128)(2,1)}, u32[]{:S(2)}, u32[]{:S(2)}) collective-permute-start(bf16[1024,2048]{1,0:T(8,128)(2,1)} %refs_2_.5), channel_id=1, source_target_pairs={{0,2},{2,0},{4,6},{6,4},{8,10},{10,8},{12,14},{14,12},{16,18},{18,... | collective-permute-start | bytes 12582920 | tf_op jit(solution)/shard_map/ppermute | solution.py:314
  5.3 7.5 %collective-permute-start.2 = (bf16[256,2048]{1,0:T(8,128)(2,1)}, bf16[256,2048]{1,0:T(8,128)(2,1)S(1)}, u32[]{:S(2)}, u32[]{:S(2)}) collective-permute-start(bf16[256,2048]{1,0:T(8,128)(2,1)} %get-tuple-element.82), channel_id=1, source_target_pairs={{0,2},{2,0},{4,6},{6,4},{8,10},{10,8},{12,14},{14,12},{16,18},{18,... | collective-permute-start | bytes 3145736 | tf_op jit(solution)/shard_map/ppermute | solution.py:314
  11.7 8.8 %collective-permute-start = (bf16[512,1024]{1,0:T(8,128)(2,1)}, bf16[512,1024]{1,0:T(8,128)(2,1)S(1)}, u32[]{:S(2)}, u32[]{:S(2)}) collective-permute-start(bf16[512,1024]{1,0:T(8,128)(2,1)} %get-tuple-element.77), channel_id=1, source_target_pairs={{0,2},{2,0},{4,6},{6,4},{8,10},{10,8},{12,14},{14,12},{16,18},{18,... | collective-permute-start | bytes 3145736 | tf_op jit(solution)/shard_map/ppermute | solution.py:314
  11.7 25.8 %collective-permute-start.3 = (bf16[512,1024]{1,0:T(8,128)(2,1)}, bf16[512,1024]{1,0:T(8,128)(2,1)S(1)}, u32[]{:S(2)}, u32[]{:S(2)}) collective-permute-start(bf16[512,1024]{1,0:T(8,128)(2,1)} %get-tuple-element.78.refs_0_), channel_id=1, source_target_pairs={{1,0},{0,1},{3,2},{2,3},{5,4},{4,5},{7,6},{6,7},{9,8},{8,9},{11,10... | collective-permute-start | bytes 3145736 | tf_op jit(solution)/shard_map/ppermute | solution.py:320
  19.0 17.0 %collective-permute-start.4 = (bf16[4,160,512]{2,1,0:T(8,128)(2,1)}, bf16[4,160,512]{2,1,0:T(8,128)(2,1)S(1)}, u32[]{:S(2)}, u32[]{:S(2)}) collective-permute-start(bf16[4,160,512]{2,1,0:T(8,128)(2,1)} %get-tuple-element.87), channel_id=1, source_target_pairs={{0,4},{2,6},{4,0},{6,2},{8,12},{10,14},{12,8},{14,10},{16,20},{18,... | collective-permute-start | bytes 1966088 | tf_op jit(solution)/shard_map/ppermute | solution.py:317
  37.5 9.4 %collective-permute-start.9 = (bf16[320,512]{1,0:T(8,128)(2,1)S(1)}, bf16[320,512]{1,0:T(8,128)(2,1)S(1)}, u32[]{:S(2)}, u32[]{:S(2)}) collective-permute-start(bf16[320,512]{1,0:T(8,128)(2,1)S(1)} %dynamic-slice_bitcast_fusion), channel_id=1, source_target_pairs={{0,8},{2,10},{4,12},{6,14},{8,0},{10,2},{12,4},{14,6},{16,24},{18,... | collective-permute-start | bytes 983048 | tf_op jit(solution)/shard_map/ppermute | solution.py:352
  38.4 28.7 %collective-permute-start.5 = (bf16[256,2048]{1,0:T(8,128)(2,1)}, bf16[256,2048]{1,0:T(8,128)(2,1)S(1)}, u32[]{:S(2)}, u32[]{:S(2)}) collective-permute-start(bf16[256,2048]{1,0:T(8,128)(2,1)} %get-tuple-element.89), channel_id=1, source_target_pairs={{0,4},{2,6},{4,0},{6,2},{8,12},{10,14},{12,8},{14,10},{16,20},{18,... | collective-permute-start | bytes 3145736 | tf_op jit(solution)/shard_map/ppermute | solution.py:317
  45.2 22.3 %collective-permute-start.6 = (bf16[512,1024]{1,0:T(8,128)(2,1)}, bf16[512,1024]{1,0:T(8,128)(2,1)}, u32[]{:S(2)}, u32[]{:S(2)}) collective-permute-start(bf16[512,1024]{1,0:T(8,128)(2,1)} %get-tuple-element.91), channel_id=1, source_target_pairs={{0,2},{2,0},{4,6},{6,4},{8,10},{10,8},{12,14},{14,12},{16,18},{18,... | collective-permute-start | bytes 3145736 | tf_op jit(solution)/shard_map/ppermute | solution.py:314
  45.2 14.2 %collective-permute-start.7 = (bf16[256,1024]{1,0:T(8,128)(2,1)S(1)}, bf16[256,1024]{1,0:T(8,128)(2,1)S(1)}, u32[]{:S(2)}, u32[]{:S(2)}) collective-permute-start(bf16[256,1024]{1,0:T(8,128)(2,1)S(1)} %slice.14), channel_id=1, source_target_pairs={{0,2},{2,0},{4,6},{6,4},{8,10},{10,8},{12,14},{14,12},{16,18},{18,... | collective-permute-start | bytes 1572872 | tf_op jit(solution)/shard_map/ppermute | solution.py:314
  45.8 25.5 %collective-permute-start.8 = (bf16[512,1024]{1,0:T(8,128)(2,1)}, bf16[512,1024]{1,0:T(8,128)(2,1)}, u32[]{:S(2)}, u32[]{:S(2)}) collective-permute-start(bf16[512,1024]{1,0:T(8,128)(2,1)} %get-tuple-element.95.refs_1_), channel_id=1, source_target_pairs={{1,0},{0,1},{3,2},{2,3},{5,4},{4,5},{7,6},{6,7},{9,8},{8,9},{11,10... | collective-permute-start | bytes 3145736 | tf_op jit(solution)/shard_map/ppermute | solution.py:320
  46.9 9.0 %collective-permute-start.10 = (bf16[160,512]{1,0:T(8,128)(2,1)S(1)}, bf16[160,512]{1,0:T(8,128)(2,1)S(1)}, u32[]{:S(2)}, u32[]{:S(2)}) collective-permute-start(bf16[160,512]{1,0:T(8,128)(2,1)S(1)} %dynamic-slice_bitcast_fusion.1), channel_id=1, source_target_pairs={{0,16},{2,18},{4,20},{6,22},{8,24},{10,26},{12,28},{14,30},{16,0},... | collective-permute-start | bytes 491528 | tf_op jit(solution)/shard_map/ppermute | solution.py:352
  56.0 11.0 %collective-permute-start.11 = (bf16[160,512]{1,0:T(8,128)(2,1)S(1)}, bf16[160,512]{1,0:T(8,128)(2,1)S(1)}, u32[]{:S(2)}, u32[]{:S(2)}) collective-permute-start(bf16[160,512]{1,0:T(8,128)(2,1)S(1)} %bitcast_add_fusion.1), channel_id=1, source_target_pairs={{0,16},{2,18},{4,20},{6,22},{8,24},{10,26},{12,28},{14,30},{16,0},... | collective-permute-start | bytes 491528 | tf_op jit(solution)/shard_map/ppermute | solution.py:352
  72.3 11.5 %collective-permute-start.12 = (bf16[256,1024]{1,0:T(8,128)(2,1)S(1)}, bf16[256,1024]{1,0:T(8,128)(2,1)S(1)}, u32[]{:S(2)}, u32[]{:S(2)}) collective-permute-start(bf16[256,1024]{1,0:T(8,128)(2,1)S(1)} %slice.15), channel_id=1, source_target_pairs={{0,2},{2,0},{4,6},{6,4},{8,10},{10,8},{12,14},{14,12},{16,18},{18,... | collective-permute-start | bytes 1572872 | tf_op jit(solution)/shard_map/ppermute | solution.py:314
  72.4 25.8 %collective-permute-start.13 = (bf16[256,2048]{1,0:T(8,128)(2,1)}, bf16[256,2048]{1,0:T(8,128)(2,1)S(1)}, u32[]{:S(2)}, u32[]{:S(2)}) collective-permute-start(bf16[256,2048]{1,0:T(8,128)(2,1)} %shard_map.126), channel_id=1, source_target_pairs={{0,4},{2,6},{4,0},{6,2},{8,12},{10,14},{12,8},{14,10},{16,20},{18,... | collective-permute-start | bytes 3145736 | tf_op jit(solution)/shard_map/ppermute | solution.py:317
  73.0 26.8 %collective-permute-start.14 = (bf16[512,1024]{1,0:T(8,128)(2,1)S(1)}, bf16[512,1024]{1,0:T(8,128)(2,1)S(1)}, u32[]{:S(2)}, u32[]{:S(2)}) collective-permute-start(bf16[512,1024]{1,0:T(8,128)(2,1)S(1)} %copy-done.11), channel_id=1, source_target_pairs={{1,0},{0,1},{3,2},{2,3},{5,4},{4,5},{7,6},{6,7},{9,8},{8,9},{11,10... | collective-permute-start | bytes 3145736 | tf_op jit(solution)/shard_map/ppermute | solution.py:320
  73.5 10.1 %collective-permute-start.15 = (bf16[320,512]{1,0:T(8,128)(2,1)S(1)}, bf16[320,512]{1,0:T(8,128)(2,1)S(1)}, u32[]{:S(2)}, u32[]{:S(2)}) collective-permute-start(bf16[320,512]{1,0:T(8,128)(2,1)S(1)} %maximum_select_fusion.1), channel_id=1, source_target_pairs={{0,8},{2,10},{4,12},{6,14},{8,0},{10,2},{12,4},{14,6},{16,24},{18,... | collective-permute-start | bytes 983048 | tf_op jit(solution)/shard_map/ppermute | solution.py:352
  99.8 26.6 %collective-permute-start.16 = (bf16[256,2048]{1,0:T(8,128)(2,1)S(1)}, bf16[256,2048]{1,0:T(8,128)(2,1)S(1)}, u32[]{:S(2)}, u32[]{:S(2)}) collective-permute-start(bf16[256,2048]{1,0:T(8,128)(2,1)S(1)} %add.150), channel_id=1, source_target_pairs={{8,0},{10,2},{12,4},{14,6},{24,16},{26,18},{28,20},{30,22},{1,9},{... | collective-permute-start | bytes 3145736 | tf_op jit(solution)/shard_map/ppermute | solution.py:356
  101.1 26.6 %collective-permute-start.18 = (bf16[256,2048]{1,0:T(8,128)(2,1)S(1)}, bf16[256,2048]{1,0:T(8,128)(2,1)S(1)}, u32[]{:S(2)}, u32[]{:S(2)}) collective-permute-start(bf16[256,2048]{1,0:T(8,128)(2,1)S(1)} %add.165), channel_id=1, source_target_pairs={{0,8},{2,10},{4,12},{6,14},{16,24},{18,26},{20,28},{22,30},{9,1},{... | collective-permute-start | bytes 3145736 | tf_op jit(solution)/shard_map/ppermute | solution.py:356
  105.8 24.4 %collective-permute-start.17 = (bf16[256,2048]{1,0:T(8,128)(2,1)}, bf16[256,2048]{1,0:T(8,128)(2,1)S(1)}, u32[]{:S(2)}, u32[]{:S(2)}) collective-permute-start(bf16[256,2048]{1,0:T(8,128)(2,1)} %get-tuple-element.112), channel_id=1, source_target_pairs={{0,4},{2,6},{4,0},{6,2},{8,12},{10,14},{12,8},{14,10},{16,20},{18,... | collective-permute-start | bytes 3145736 | tf_op jit(solution)/shard_map/ppermute | solution.py:317
  106.4 24.2 %collective-permute-start.20 = (bf16[512,1024]{1,0:T(8,128)(2,1)}, bf16[512,1024]{1,0:T(8,128)(2,1)S(1)}, u32[]{:S(2)}, u32[]{:S(2)}) collective-permute-start(bf16[512,1024]{1,0:T(8,128)(2,1)} %get-tuple-element.117.refs_1_), channel_id=1, source_target_pairs={{1,0},{0,1},{3,2},{2,3},{5,4},{4,5},{7,6},{6,7},{9,8},{8,9},{11,10... | collective-permute-start | bytes 3145736 | tf_op jit(solution)/shard_map/ppermute | solution.py:320
  130.7 25.2 %collective-permute-start.21 = (bf16[256,2048]{1,0:T(8,128)(2,1)S(1)}, bf16[256,2048]{1,0:T(8,128)(2,1)}, u32[]{:S(2)}, u32[]{:S(2)}) collective-permute-start(bf16[256,2048]{1,0:T(8,128)(2,1)S(1)} %add.166), channel_id=1, source_target_pairs={{16,0},{18,2},{20,4},{22,6},{9,25},{11,27},{13,29},{15,31}} | collective-permute-start | bytes 3145736 | tf_op jit(solution)/shard_map/ppermute | solution.py:356
  136.2 24.8 %collective-permute-start.22 = (bf16[256,2048]{1,0:T(8,128)(2,1)S(1)}, bf16[256,2048]{1,0:T(8,128)(2,1)S(1)}, u32[]{:S(2)}, u32[]{:S(2)}) collective-permute-start(bf16[256,2048]{1,0:T(8,128)(2,1)S(1)} %add.167), channel_id=1, source_target_pairs={{0,8},{2,10},{4,12},{6,14},{24,16},{26,18},{28,20},{30,22},{1,9},{... | collective-permute-start | bytes 3145736 | tf_op jit(solution)/shard_map/ppermute | solution.py:356
  137.5 23.9 %collective-permute-start.23 = (bf16[256,2048]{1,0:T(8,128)(2,1)S(1)}, bf16[256,2048]{1,0:T(8,128)(2,1)}, u32[]{:S(2)}, u32[]{:S(2)}) collective-permute-start(bf16[256,2048]{1,0:T(8,128)(2,1)S(1)} %add.168), channel_id=1, source_target_pairs={{8,24},{10,26},{12,28},{14,30},{17,1},{19,3},{21,5},{23,7}} | collective-permute-start | bytes 3145736 | tf_op jit(solution)/shard_map/ppermute | solution.py:356
  139.1 23.9 %collective-permute-start.25 = (bf16[256,2048]{1,0:T(8,128)(2,1)}, bf16[256,2048]{1,0:T(8,128)(2,1)S(1)}, u32[]{:S(2)}, u32[]{:S(2)}) collective-permute-start(bf16[256,2048]{1,0:T(8,128)(2,1)} %shard_map.129), channel_id=1, source_target_pairs={{0,4},{2,6},{4,0},{6,2},{8,12},{10,14},{12,8},{14,10},{16,20},{18,... | collective-permute-start | bytes 3145736 | tf_op jit(solution)/shard_map/ppermute | solution.py:317
  163.4 25.2 %collective-permute-start.26 = (bf16[256,2048]{1,0:T(8,128)(2,1)S(1)}, bf16[256,2048]{1,0:T(8,128)(2,1)S(1)}, u32[]{:S(2)}, u32[]{:S(2)}) collective-permute-start(bf16[256,2048]{1,0:T(8,128)(2,1)S(1)} %add.170), channel_id=1, source_target_pairs={{16,8},{18,10},{20,12},{22,14},{9,17},{11,19},{13,21},{15,23}} | collective-permute-start | bytes 3145736 | tf_op jit(solution)/shard_map/ppermute | solution.py:356
  169.7 23.1 %collective-permute-start.27 = (bf16[256,2048]{1,0:T(8,128)(2,1)S(1)}, bf16[256,2048]{1,0:T(8,128)(2,1)S(1)}, u32[]{:S(2)}, u32[]{:S(2)}) collective-permute-start(bf16[256,2048]{1,0:T(8,128)(2,1)S(1)} %add.172), channel_id=1, source_target_pairs={{0,8},{2,10},{4,12},{6,14},{24,16},{26,18},{28,20},{30,22},{1,9},{... | collective-permute-start | bytes 3145736 | tf_op jit(solution)/shard_map/ppermute | solution.py:356
  171.0 23.2 %collective-permute-start.28 = (bf16[4,160,512]{2,1,0:T(8,128)(2,1)S(1)}, bf16[4,160,512]{2,1,0:T(8,128)(2,1)}, u32[]{:S(2)}, u32[]{:S(2)}) collective-permute-start(bf16[4,160,512]{2,1,0:T(8,128)(2,1)S(1)} %bitcast.27), channel_id=1, source_target_pairs={{0,4},{2,6},{4,0},{6,2},{8,12},{10,14},{12,8},{14,10},{16,20},{18,... | collective-permute-start | bytes 1966088 | tf_op jit(solution)/shard_map/ppermute | solution.py:317
  172.1 22.1 %collective-permute-start.29 = (bf16[4,160,512]{2,1,0:T(8,128)(2,1)S(1)}, bf16[4,160,512]{2,1,0:T(8,128)(2,1)S(1)}, u32[]{:S(2)}, u32[]{:S(2)}) collective-permute-start(bf16[4,160,512]{2,1,0:T(8,128)(2,1)S(1)} %bitcast.28), channel_id=1, source_target_pairs={{0,2},{2,0},{4,6},{6,4},{8,10},{10,8},{12,14},{14,12},{16,18},{18,... | collective-permute-start | bytes 1966088 | tf_op jit(solution)/shard_map/ppermute | solution.py:314
  195.0 22.5 %collective-permute-start.32 = (bf16[256,2048]{1,0:T(8,128)(2,1)}, bf16[256,2048]{1,0:T(8,128)(2,1)}, u32[]{:S(2)}, u32[]{:S(2)}) collective-permute-start(bf16[256,2048]{1,0:T(8,128)(2,1)} %add.174), channel_id=1, source_target_pairs={{8,16},{10,18},{12,20},{14,22},{17,9},{19,11},{21,13},{23,15}} | collective-permute-start | bytes 3145736 | tf_op jit(solution)/shard_map/ppermute | solution.py:356
  196.3 2.5 %collective-permute-start.30 = (bf16[4,160,512]{2,1,0:T(8,128)(2,1)}, bf16[4,160,512]{2,1,0:T(8,128)(2,1)}, u32[]{:S(2)}, u32[]{:S(2)}) collective-permute-start(bf16[4,160,512]{2,1,0:T(8,128)(2,1)} %collective-permute-done.28.back), channel_id=1, source_target_pairs={{0,2},{2,0},{4,6},{6,4},{8,10},{10,8},{12,14},{14,12},{16,18},{18,... | collective-permute-start | bytes 1966088 | tf_op jit(solution)/shard_map/ppermute | solution.py:314
  210.4 5.6 %collective-permute-start.31 = (f32[4,1,512]{2,1,0:T(1,128)}, f32[4,1,512]{2,1,0:T(1,128)S(1)}, u32[]{:S(2)}, u32[]{:S(2)}) collective-permute-start(f32[4,1,512]{2,1,0:T(1,128)} %get-tuple-element.139), channel_id=1, source_target_pairs={{1,0},{0,1},{3,2},{2,3},{5,4},{4,5},{7,6},{6,7},{9,8},{8,9},{11,10... | collective-permute-start | bytes 24584 | tf_op jit(solution)/shard_map/ppermute | solution.py:320
  220.3 2.9 %collective-permute-start.33 = (bf16[256,2048]{1,0:T(8,128)(2,1)}, bf16[256,2048]{1,0:T(8,128)(2,1)S(1)}, u32[]{:S(2)}, u32[]{:S(2)}) collective-permute-start(bf16[256,2048]{1,0:T(8,128)(2,1)} %select_select_fusion.refs_0_), channel_id=1, source_target_pairs={{0,2},{2,0},{4,6},{6,4},{8,10},{10,8},{12,14},{14,12},{16,18},{18,... | collective-permute-start | bytes 3145736 | tf_op jit(solution)/shard_map/ppermute | solution.py:513
  (23 other events, 222.4 us)

commit v6 on v5

--- a/solution.py
+++ b/solution.py
@@ -149,9 +149,11 @@
     sharers = len(parts)
     rows = parts[0].shape[0]
     me = place_ref[1]
+    size = whole.shape[1]
+    columns = pl.ds(pl.multiple_of(pl.program_id(0) * size, size), size)
     for step, part in enumerate(parts):
         spot = lax.rem(me - step + sharers, sharers)
-        whole[pl.ds(pl.multiple_of(spot * rows, rows), rows), :] = part[...]
+        whole[pl.ds(pl.multiple_of(spot * rows, rows), rows), :] = part[:, columns]
     right = jnp.dot(whole[...], basis[0], preferred_element_type=F32).astype(BF16)
     inner = lax.dot_general(outer[0], right, (((0,), (0,)), ((), ())), preferred_element_type=F32)
     column = jnp.broadcast_to(eig_out[0], (QUARTER, eig_out.shape[2])).T[:, :1]
@@ -167,8 +169,7 @@
     blocks, size, _ = basis_in.shape
     rows, cols = parts[0].shape
     each = cols // size
-    strip = pl.BlockSpec((rows, size), lambda b, place: (0, b))
-    in_specs = [strip] * len(parts) + [
+    in_specs = [pl.BlockSpec(memory_space=pltpu.VMEM)] * len(parts) + [
         pl.BlockSpec((1, size, size), lambda b, place: (chunk * each + b, 0, 0)),
         pl.BlockSpec((1, size, size), lambda b, place: (place[0], 0, 0)),
         pl.BlockSpec((1, 1, size), lambda b, place: (chunk * each + b, 0, 0)),
@@ -414,18 +415,19 @@
             env = dict(zip(keys, lax.optimization_barrier(tuple(env[k] for k in keys))))
         joined = {}
         if stage == 0:
+            ours, theirs = pick(acts, cotan, block_ids, core)
             joined["acts_sib"] = swap_core(acts)
             env.update(turn(cotan, 0))
-            ours, theirs = pick(acts, cotan, block_ids, core)
             scales = (1.0 / samples, tokens / samples)
             keep, away = terms(flags[1:], ours, swap_core(theirs), block_size, scales)
             away = swap_x(away)
             joined["c", 0] = swap_core(env.pop(("p", 0)))
         if stage == 1:
             for j in range(1, z_per_worker):
-                found = turn(env["cotan"], j)
-                joined["c", j] = swap_core(found.pop(("p", j)))
-                joined.update(found)
+                joined.update(turn(env["cotan"], j))
+        if stage == 2:
+            for j in range(1, z_per_worker):
+                env["c", j] = swap_core(env.pop(("p", j)))
         arrivals = {}
         for (step, j, at), when in y_stage.items():
             if when == stage:
@@ -491,14 +493,11 @@
                 env[acc] = env.pop(mine) + env.pop(got)
             if ("hop", step, j, n) in env:
                 env[acc] = env[acc] + env.pop(("hop", step, j, n))
-        for n in chunks:
-            if stage == max(z_stage[step, j, n, len(z_bits) - 1] for step, j in shards):
-                total = None
-                for step, j in shards:
-                    ends = jnp.array([place((i + step) % n_worker, j) for i in range(n_worker)], jnp.int32)
-                    acc = env.pop(("acc", step, j, n))
-                    total = acc if total is None else jnp.where(ends[w] == z, acc, total)
-                done[n] = total
+        for step, j, n in x_stage:
+            if stage == z_stage[step, j, n, len(z_bits) - 1]:
+                ends = jnp.array([place((i + step) % n_worker, j) for i in range(n_worker)], jnp.int32)
+                acc = env.pop(("acc", step, j, n))
+                env["sum", n] = jnp.where(ends[w] == z, acc, env["sum", n]) if ("sum", n) in env else acc
 
     act_new, grad_new = done["factors"]
     held = (block // local_blocks - w) % n_worker * local_blocks + block % local_blocks
@@ -507,7 +506,7 @@
     spot = jnp.stack([block, d % sharers, held]).astype(jnp.int32)
     precond = None
     for n in range(len(starts)):
-        parts = [done[n]]
+        parts = [env["sum", n]]
         for step in range(1, sharers):
             pairs = [(i, i // sharers * sharers + (i + step) % sharers) for i in range(n_dp)]
             parts.append(lax.ppermute(parts[0], "dp", pairs))

time: 235 us -> 230 us (0.979)
  other arithmetic: 17.2 us -> 22.2 us
  starting transfers between devices: 42.7 us -> 38.3 us
  local copies, waits for them, and re-layouts: 12.7 us -> 9.8 us
  waiting for transfers between devices: 73.6 us -> 71 us
    ppermute x4, waiting for transfers between devices: 6.94 us -> 16.3 us  [swap_z(): return lax.ppermute(v, 'dp', [(i, i ^ 4 * bit) for i in range(n_dp)])]
    ppermute x8, waiting for transfers between devices: 39.2 us -> 34.7 us  [hop(): return lax.ppermute(v, both, pairs)]
    ppermute x6, waiting for transfers between devices: 14.5 us -> 10.8 us  [swap_x(): return lax.ppermute(v, 'dp', [(i, i ^ 2) for i in range(n_dp)])]
    select_n x1 -> x3, other arithmetic: 2.76 us -> 6.42 us  [per_device(): jnp.where(ends[w] == z, acc, env['sum', n])]
    ppermute x8, starting transfers between devices: 23.2 us -> 19.6 us  [hop(): return lax.ppermute(v, both, pairs)]
    unnamed x42 -> x32, local copies, waits for them, and re-layouts: 7.63 us -> 5.79 us
    add x7 -> x4, other arithmetic: 6.14 us -> 4.72 us  [per_device(): env[acc] = env[acc] + env.pop(('hop', step, j, n))]
  transfers between devices with their start and end apart: 34 -> 34, of which waited for: 18 -> 18; matrix products, arithmetic and copies ran while one was open for 8% -> 9% of each run, Pallas kernels for 32% -> 33%
where the time goes in v6:
time: 230 us; the launch traced here: 228 us
  Pallas kernels  83.5 us (36%)
  waiting for transfers between devices  71 us (31%)
  starting transfers between devices  38.3 us (17%)
  other arithmetic  22.2 us (10%)
  local copies, waits for them, and re-layouts  9.8 us (4%)
  between operations  3.02 us (1%)
    pallas_call x6, Pallas kernels, products(): pl.pallas_call(functools.partial(product_kernel, [len(half) for half in h...  44.7 us
    ppermute x8, waiting for transfers between devices, hop(): return lax.ppermute(v, both, pairs)  34.7 us
    ppermute x8, starting transfers between devices, hop(): return lax.ppermute(v, both, pairs)  19.6 us
    ppermute x4, waiting for transfers between devices, swap_z(): return lax.ppermute(v, 'dp', [(i, i ^ 4 * bit) for i in range(n_dp)])  16.3 us
    pallas_call x1, Pallas kernels, update_factors(): pl.pallas_call(factor_kernel, grid_spec=pltpu.PrefetchScalarGridSpec(num_...  11.5 us
    ppermute x6, waiting for transfers between devices, swap_x(): return lax.ppermute(v, 'dp', [(i, i ^ 2) for i in range(n_dp)])  10.8 us
    pallas_call x2, Pallas kernels, turned(): pl.pallas_call(turn_kernel, grid_spec=pltpu.PrefetchScalarGridSpec(num_sc...  10.5 us
    pallas_call x1, Pallas kernels, tail(): pl.pallas_call(functools.partial(tail_kernel, len(parts)), grid_spec=pltp...  8.25 us
  transfers between devices with their start and end apart: 34, of which 18 were waited for; matrix products, arithmetic and copies ran while one was open for 9% of the time, Pallas kernels for 33%

profile of v6, /device:TPU:12, one launch (start us, length us, event | category | flops | bytes accessed | tf_op | source)
XLA Modules:
  0.0 227.8 jit_solution(16905056287137303546)
XLA Ops:
  2.0 3.3 %shard_map.123 = (bf16[256,2048]{1,0:T(8,128)(2,1)}, bf16[256,2048]{1,0:T(8,128)(2,1)}) custom-call(s32[3]{0:T(128)} %pad_add_fusion.3.which_ref, bf16[1024,2048]{1,0:T(8,128)(2,1)} %refs_2_.5, bf16[1024,2048]{1,0:T(8,128)(2,1)} %block.2), custom_call_target="tpu_custom_call" | custom-call | flops 1 | bytes 1 | tf_op jit(solution)/shard_map/pallas_call | solution.py:35
  6.5 5.2 %shard_map.121 = (bf16[512,1024]{1,0:T(8,128)(2,1)}, bf16[512,1024]{1,0:T(8,128)(2,1)}, bf16[512,1024]{1,0:T(8,128)(2,1)}) custom-call(s32[4]{0:T(128)} %get-tuple-element.133.which_ref, bf16[1024,2048]{1,0:T(8,128)(2,1)} %block.2), custom_call_target="tpu_custom_call" | custom-call | flops 1 | bytes 1 | tf_op jit(solution)/shard_map/pallas_call | solution.py:226
  13.9 5.2 %shard_map.124 = (bf16[4,160,512]{2,1,0:T(8,128)(2,1)}, bf16[4,160,512]{2,1,0:T(8,128)(2,1)}) custom-call(s32[2]{0:T(128)} %pad_add_fusion.2.place_ref, bf16[256,2048]{1,0:T(8,128)(2,1)} %get-tuple-element.72.ours, bf16[256,2048]{1,0:T(8,128)(2,1)} %copy-done.3), custom_call_target="tpu_custom_call" | custom-call | flops 1 | bytes 1 | tf_op jit(solution)/shard_map/pallas_call | solution.py:73
  21.5 9.0 %shard_map.122 = (bf16[256,2048]{1,0:T(8,128)(2,1)}, bf16[256,2048]{1,0:T(8,128)(2,1)}) custom-call(bf16[512,1024]{1,0:T(8,128)(2,1)} %get-tuple-element.69.refs_0_, bf16[512,1024]{1,0:T(8,128)(2,1)} %get-tuple-element.84.refs_1_, bf16[512,1024]{1,0:T(8,128)(2,1)} %copy-done.10, bf16[1024,2048]{1,0:T(8,128)(2,1)} %refs_2_.5, ...), custom_call_target="tpu_custom_call" | custom-call | flops 8589934592 | bytes 8388608 | tf_op jit(solution)/shard_map/pallas_call | solution.py:278
  30.5 5.6 %collective-permute-done.4 = bf16[4,160,512]{2,1,0:T(8,128)(2,1)S(1)} collective-permute-done((bf16[4,160,512]{2,1,0:T(8,128)(2,1)}, bf16[4,160,512]{2,1,0:T(8,128)(2,1)S(1)}, u32[]{:S(2)}, u32[]{:S(2)}) %collective-permute-start.4) | collective-permute-done | bytes 655392 | tf_op jit(solution)/shard_map/ppermute | solution.py:318
  40.5 6.4 %collective-permute-done.8 = bf16[320,512]{1,0:T(8,128)(2,1)S(1)} collective-permute-done((bf16[320,512]{1,0:T(8,128)(2,1)S(1)}, bf16[320,512]{1,0:T(8,128)(2,1)S(1)}, u32[]{:S(2)}, u32[]{:S(2)}) %collective-permute-start.8) | collective-permute-done | bytes 327712 | tf_op jit(solution)/shard_map/ppermute | solution.py:353
  47.0 2.7 %collective-permute-start.9 = (bf16[160,512]{1,0:T(8,128)(2,1)S(1)}, bf16[160,512]{1,0:T(8,128)(2,1)S(1)}, u32[]{:S(2)}, u32[]{:S(2)}) collective-permute-start(bf16[160,512]{1,0:T(8,128)(2,1)S(1)} %dynamic-slice_bitcast_fusion.1), channel_id=1, source_target_pairs={{0,16},{2,18},{4,20},{6,22},{8,24},{10,26},{12,28},{14,30},{16,0},... | collective-permute-start | bytes 491528 | tf_op jit(solution)/shard_map/ppermute | solution.py:353
  49.6 5.2 %shard_map.126 = (bf16[512,1024]{1,0:T(8,128)(2,1)}, bf16[512,1024]{1,0:T(8,128)(2,1)}, bf16[512,1024]{1,0:T(8,128)(2,1)}) custom-call(s32[4]{0:T(128)} %get-tuple-element.134.which_ref, bf16[1024,2048]{1,0:T(8,128)(2,1)} %block.2), custom_call_target="tpu_custom_call" | custom-call | flops 1 | bytes 1 | tf_op jit(solution)/shard_map/pallas_call | solution.py:226
  55.6 3.4 %collective-permute-start.10 = (bf16[160,512]{1,0:T(8,128)(2,1)S(1)}, bf16[160,512]{1,0:T(8,128)(2,1)S(1)}, u32[]{:S(2)}, u32[]{:S(2)}) collective-permute-start(bf16[160,512]{1,0:T(8,128)(2,1)S(1)} %bitcast_add_fusion.1), channel_id=1, source_target_pairs={{0,16},{2,18},{4,20},{6,22},{8,24},{10,26},{12,28},{14,30},{16,0},... | collective-permute-start | bytes 491528 | tf_op jit(solution)/shard_map/ppermute | solution.py:353
  59.8 6.7 %shard_map.125 = bf16[256,2048]{1,0:T(8,128)(2,1)} custom-call(bf16[512,1024]{1,0:T(8,128)(2,1)} %copy-done.6, bf16[256,1024]{1,0:T(8,128)(2,1)} %copy-done.11, bf16[1024,2048]{1,0:T(8,128)(2,1)} %refs_2_.5, bf16[1024,2048]{1,0:T(8,128)(2,1)} %collective-permute-done.1.refs_4_.refs_3_), custom_call_target="tpu_custom_call" | custom-call | flops 4294967296 | bytes 8388608 | tf_op jit(solution)/shard_map/pallas_call | solution.py:278
  70.7 9.2 %collective-permute-done.15 = bf16[320,512]{1,0:T(8,128)(2,1)S(1)} collective-permute-done((bf16[320,512]{1,0:T(8,128)(2,1)S(1)}, bf16[320,512]{1,0:T(8,128)(2,1)S(1)}, u32[]{:S(2)}, u32[]{:S(2)}) %collective-permute-start.15) | collective-permute-done | bytes 327712 | tf_op jit(solution)/shard_map/ppermute | solution.py:353
  81.0 6.7 %shard_map.127 = bf16[256,2048]{1,0:T(8,128)(2,1)} custom-call(bf16[512,1024]{1,0:T(8,128)(2,1)} %collective-permute-done.7.refs_0_, bf16[256,1024]{1,0:T(8,128)(2,1)} %collective-permute-done.11.refs_1_, bf16[1024,2048]{1,0:T(8,128)(2,1)} %refs_2_.5, bf16[1024,2048]{1,0:T(8,128)(2,1)} %collective-permute-done.1.refs_4_.refs_3_), custom_call_target="tpu_custom_call" | custom-call | flops 4294967296 | bytes 8388608 | tf_op jit(solution)/shard_map/pallas_call | solution.py:278
  87.7 4.2 %collective-permute-done.12 = bf16[256,2048]{1,0:T(8,128)(2,1)S(1)} collective-permute-done((bf16[256,2048]{1,0:T(8,128)(2,1)}, bf16[256,2048]{1,0:T(8,128)(2,1)S(1)}, u32[]{:S(2)}, u32[]{:S(2)}) %collective-permute-start.12) | collective-permute-done | bytes 1048608 | tf_op jit(solution)/shard_map/ppermute | solution.py:318
  93.5 9.0 %shard_map.128 = (bf16[256,2048]{1,0:T(8,128)(2,1)}, bf16[256,2048]{1,0:T(8,128)(2,1)}) custom-call(bf16[512,1024]{1,0:T(8,128)(2,1)} %get-tuple-element.96.refs_0_, bf16[512,1024]{1,0:T(8,128)(2,1)} %get-tuple-element.108.refs_1_, bf16[512,1024]{1,0:T(8,128)(2,1)} %collective-permute-done.13.refs_2_, bf16[1024,2048]{1,0:T(8,128)(2,1)} %refs_2_.5, ...), custom_call_target="tpu_custom_call" | custom-call | flops 8589934592 | bytes 8388608 | tf_op jit(solution)/shard_map/pallas_call | solution.py:278
  103.8 4.7 %collective-permute-start.18 = (bf16[256,2048]{1,0:T(8,128)(2,1)S(1)}, bf16[256,2048]{1,0:T(8,128)(2,1)S(1)}, u32[]{:S(2)}, u32[]{:S(2)}) collective-permute-start(bf16[256,2048]{1,0:T(8,128)(2,1)S(1)} %add.165), channel_id=1, source_target_pairs={{0,8},{2,10},{4,12},{6,14},{16,24},{18,26},{20,28},{22,30},{9,1},{... | collective-permute-start | bytes 3145736 | tf_op jit(solution)/shard_map/ppermute | solution.py:357
  110.2 2.0 collective-permute-done.19.refs_1_
  112.2 6.7 %shard_map.129 = bf16[256,2048]{1,0:T(8,128)(2,1)} custom-call(bf16[512,1024]{1,0:T(8,128)(2,1)} %copy-done.7, bf16[256,1024]{1,0:T(8,128)(2,1)} %collective-permute-done.19.refs_1_, bf16[1024,2048]{1,0:T(8,128)(2,1)} %refs_2_.5, bf16[1024,2048]{1,0:T(8,128)(2,1)} %collective-permute-done.1.refs_4_.refs_3_), custom_call_target="tpu_custom_call" | custom-call | flops 4294967296 | bytes 8388608 | tf_op jit(solution)/shard_map/pallas_call | solution.py:278
  118.9 9.1 %collective-permute-done.16 = bf16[256,2048]{1,0:T(8,128)(2,1)S(1)} collective-permute-done((bf16[256,2048]{1,0:T(8,128)(2,1)S(1)}, bf16[256,2048]{1,0:T(8,128)(2,1)S(1)}, u32[]{:S(2)}, u32[]{:S(2)}) %collective-permute-start.16) | collective-permute-done | bytes 1048608 | tf_op jit(solution)/shard_map/ppermute | solution.py:357
  135.1 1.7 collective-permute-start.24
  136.9 5.7 %collective-permute-start.25 = (bf16[256,2048]{1,0:T(8,128)(2,1)}, bf16[256,2048]{1,0:T(8,128)(2,1)}, u32[]{:S(2)}, u32[]{:S(2)}) collective-permute-start(bf16[256,2048]{1,0:T(8,128)(2,1)} %add.166), channel_id=1, source_target_pairs={{16,0},{18,2},{20,4},{22,6},{9,25},{11,27},{13,29},{15,31}} | collective-permute-start | bytes 3145736 | tf_op jit(solution)/shard_map/ppermute | solution.py:357
  146.4 6.7 %shard_map.130 = bf16[256,2048]{1,0:T(8,128)(2,1)} custom-call(bf16[512,1024]{1,0:T(8,128)(2,1)} %collective-permute-done.20.refs_0_, bf16[256,1024]{1,0:T(8,128)(2,1)} %copy-done.12, bf16[1024,2048]{1,0:T(8,128)(2,1)} %refs_2_.5, bf16[1024,2048]{1,0:T(8,128)(2,1)} %collective-permute-done.1.refs_4_.refs_3_), custom_call_target="tpu_custom_call" | custom-call | flops 4294967296 | bytes 8388608 | tf_op jit(solution)/shard_map/pallas_call | solution.py:278
  153.1 3.7 %collective-permute-done.21 = bf16[256,2048]{1,0:T(8,128)(2,1)S(1)} collective-permute-done((bf16[256,2048]{1,0:T(8,128)(2,1)S(1)}, bf16[256,2048]{1,0:T(8,128)(2,1)S(1)}, u32[]{:S(2)}, u32[]{:S(2)}) %collective-permute-start.21) | collective-permute-done | bytes 1048608 | tf_op jit(solution)/shard_map/ppermute | solution.py:357
  157.2 1.9 add.170
  159.2 2.6 %collective-permute-done.25 = bf16[256,2048]{1,0:T(8,128)(2,1)} collective-permute-done((bf16[256,2048]{1,0:T(8,128)(2,1)}, bf16[256,2048]{1,0:T(8,128)(2,1)}, u32[]{:S(2)}, u32[]{:S(2)}) %collective-permute-start.25) | collective-permute-done | bytes 1048608 | tf_op jit(solution)/shard_map/ppermute | solution.py:357
  161.8 3.3 %add_select_fusion.2 = bf16[256,2048]{1,0:T(8,128)(2,1)} fusion(bf16[256,2048]{1,0:T(8,128)(2,1)} %add.166, bf16[256,2048]{1,0:T(8,128)(2,1)} %collective-permute-done.25, bf16[256,2048]{1,0:T(8,128)(2,1)} %add.168, bf16[256,2048]{1,0:T(8,128)(2,1)} %collective-permute-done.24, pred[]{:T(512)S(6)} %eq.28), kind=kLoop, calls=%fused_computation.2 | loop fusion | flops 1572864 | bytes 5242881 | tf_op jit(solution)/shard_map/jit(_where)/select_n | solution.py:500
  166.4 2.3 %collective-permute-start.27 = (bf16[256,2048]{1,0:T(8,128)(2,1)S(1)}, bf16[256,2048]{1,0:T(8,128)(2,1)}, u32[]{:S(2)}, u32[]{:S(2)}) collective-permute-start(bf16[256,2048]{1,0:T(8,128)(2,1)S(1)} %add.169), channel_id=1, source_target_pairs={{16,8},{18,10},{20,12},{22,14},{9,17},{11,19},{13,21},{15,23}} | collective-permute-start | bytes 3145736 | tf_op jit(solution)/shard_map/ppermute | solution.py:357
  170.5 18.1 %collective-permute-done.26 = bf16[256,2048]{1,0:T(8,128)(2,1)} collective-permute-done((bf16[256,2048]{1,0:T(8,128)(2,1)S(1)}, bf16[256,2048]{1,0:T(8,128)(2,1)}, u32[]{:S(2)}, u32[]{:S(2)}) %collective-permute-start.26) | collective-permute-done | bytes 1048608 | tf_op jit(solution)/shard_map/ppermute | solution.py:357
  190.2 1.7 add_select_fusion.1
  194.0 1.6 collective-permute-done.30.back_sib
  196.4 11.5 %shard_map.131 = (f32[4,512,512]{2,1,0:T(8,128)}, f32[4,512,512]{2,1,0:T(8,128)}, f32[4,1,512]{2,1,0:T(1,128)}, f32[4,1,512]{2,1,0:T(1,128)}) custom-call(s32[3]{0:T(128)} %pad_add_fusion.5.place_ref, bf16[4,160,512]{2,1,0:T(8,128)(2,1)} %bitcast.19.keep, bf16[4,160,512]{2,1,0:T(8,128)(2,1)} %collective-permute-done.28.back, ...), custom_call_target="tpu_custom_call" | custom-call | flops 1 | bytes 1 | tf_op jit(solution)/shard_map/pallas_call | solution.py:129
  216.8 1.8 collective-permute-done.33.refs_1_
  219.5 8.2 %shard_map.132 = bf16[256,2048]{1,0:T(8,128)(2,1)} custom-call(s32[3]{0:T(128)} %pad_add_fusion.place_ref, bf16[256,2048]{1,0:T(8,128)(2,1)} %copy-done.1, bf16[256,2048]{1,0:T(8,128)(2,1)} %copy-done.9, bf16[4,512,512]{2,1,0:T(8,128)(2,1)} %refs_2_.7, bf16[8,512,512]{2,1,0:T(8,128)(2,1)} %refs_3_.6, f32[4,1,512]{2,1,0:T(1,128)} %get-tuple-element.129.refs_4_, ...), custom_call_target="tpu_custom_call" | custom-call | flops 3221225472 | bytes 4194304 | tf_op jit(solution)/shard_map/pallas_call | solution.py:184
  (111 shorter events, 49.4 us)
Async XLA Ops:
  0.6 19.9 %collective-permute-start.1 = (bf16[1024,2048]{1,0:T(8,128)(2,1)}, bf16[1024,2048]{1,0:T(8,128)(2,1)}, u32[]{:S(2)}, u32[]{:S(2)}) collective-permute-start(bf16[1024,2048]{1,0:T(8,128)(2,1)} %refs_2_.5), channel_id=1, source_target_pairs={{0,2},{2,0},{4,6},{6,4},{8,10},{10,8},{12,14},{14,12},{16,18},{18,... | collective-permute-start | bytes 12582920 | tf_op jit(solution)/shard_map/ppermute | solution.py:315
  5.3 7.5 %collective-permute-start.2 = (bf16[256,2048]{1,0:T(8,128)(2,1)}, bf16[256,2048]{1,0:T(8,128)(2,1)S(1)}, u32[]{:S(2)}, u32[]{:S(2)}) collective-permute-start(bf16[256,2048]{1,0:T(8,128)(2,1)} %get-tuple-element.73), channel_id=1, source_target_pairs={{0,2},{2,0},{4,6},{6,4},{8,10},{10,8},{12,14},{14,12},{16,18},{18,... | collective-permute-start | bytes 3145736 | tf_op jit(solution)/shard_map/ppermute | solution.py:315
  11.7 8.8 %collective-permute-start = (bf16[512,1024]{1,0:T(8,128)(2,1)}, bf16[512,1024]{1,0:T(8,128)(2,1)S(1)}, u32[]{:S(2)}, u32[]{:S(2)}) collective-permute-start(bf16[512,1024]{1,0:T(8,128)(2,1)} %get-tuple-element.68), channel_id=1, source_target_pairs={{0,2},{2,0},{4,6},{6,4},{8,10},{10,8},{12,14},{14,12},{16,18},{18,... | collective-permute-start | bytes 3145736 | tf_op jit(solution)/shard_map/ppermute | solution.py:315
  11.7 25.8 %collective-permute-start.3 = (bf16[512,1024]{1,0:T(8,128)(2,1)}, bf16[512,1024]{1,0:T(8,128)(2,1)S(1)}, u32[]{:S(2)}, u32[]{:S(2)}) collective-permute-start(bf16[512,1024]{1,0:T(8,128)(2,1)} %get-tuple-element.69.refs_0_), channel_id=1, source_target_pairs={{1,0},{0,1},{3,2},{2,3},{5,4},{4,5},{7,6},{6,7},{9,8},{8,9},{11,10... | collective-permute-start | bytes 3145736 | tf_op jit(solution)/shard_map/ppermute | solution.py:321
  19.0 17.0 %collective-permute-start.4 = (bf16[4,160,512]{2,1,0:T(8,128)(2,1)}, bf16[4,160,512]{2,1,0:T(8,128)(2,1)S(1)}, u32[]{:S(2)}, u32[]{:S(2)}) collective-permute-start(bf16[4,160,512]{2,1,0:T(8,128)(2,1)} %get-tuple-element.78), channel_id=1, source_target_pairs={{0,4},{2,6},{4,0},{6,2},{8,12},{10,14},{12,8},{14,10},{16,20},{18,... | collective-permute-start | bytes 1966088 | tf_op jit(solution)/shard_map/ppermute | solution.py:318
  37.5 9.4 %collective-permute-start.8 = (bf16[320,512]{1,0:T(8,128)(2,1)S(1)}, bf16[320,512]{1,0:T(8,128)(2,1)S(1)}, u32[]{:S(2)}, u32[]{:S(2)}) collective-permute-start(bf16[320,512]{1,0:T(8,128)(2,1)S(1)} %dynamic-slice_bitcast_fusion), channel_id=1, source_target_pairs={{0,8},{2,10},{4,12},{6,14},{8,0},{10,2},{12,4},{14,6},{16,24},{18,... | collective-permute-start | bytes 983048 | tf_op jit(solution)/shard_map/ppermute | solution.py:353
  38.5 20.6 %collective-permute-start.6 = (bf16[256,1024]{1,0:T(8,128)(2,1)S(1)}, bf16[256,1024]{1,0:T(8,128)(2,1)S(1)}, u32[]{:S(2)}, u32[]{:S(2)}) collective-permute-start(bf16[256,1024]{1,0:T(8,128)(2,1)S(1)} %slice.14), channel_id=1, source_target_pairs={{0,2},{2,0},{4,6},{6,4},{8,10},{10,8},{12,14},{14,12},{16,18},{18,... | collective-permute-start | bytes 1572872 | tf_op jit(solution)/shard_map/ppermute | solution.py:315
  38.5 28.1 %collective-permute-start.5 = (bf16[256,2048]{1,0:T(8,128)(2,1)}, bf16[256,2048]{1,0:T(8,128)(2,1)S(1)}, u32[]{:S(2)}, u32[]{:S(2)}) collective-permute-start(bf16[256,2048]{1,0:T(8,128)(2,1)} %get-tuple-element.80), channel_id=1, source_target_pairs={{0,4},{2,6},{4,0},{6,2},{8,12},{10,14},{12,8},{14,10},{16,20},{18,... | collective-permute-start | bytes 3145736 | tf_op jit(solution)/shard_map/ppermute | solution.py:318
  40.0 27.0 %collective-permute-start.7 = (bf16[512,1024]{1,0:T(8,128)(2,1)}, bf16[512,1024]{1,0:T(8,128)(2,1)}, u32[]{:S(2)}, u32[]{:S(2)}) collective-permute-start(bf16[512,1024]{1,0:T(8,128)(2,1)} %get-tuple-element.84.refs_1_), channel_id=1, source_target_pairs={{1,0},{0,1},{3,2},{2,3},{5,4},{4,5},{7,6},{6,7},{9,8},{8,9},{11,10... | collective-permute-start | bytes 3145736 | tf_op jit(solution)/shard_map/ppermute | solution.py:321
  47.0 8.6 %collective-permute-start.9 = (bf16[160,512]{1,0:T(8,128)(2,1)S(1)}, bf16[160,512]{1,0:T(8,128)(2,1)S(1)}, u32[]{:S(2)}, u32[]{:S(2)}) collective-permute-start(bf16[160,512]{1,0:T(8,128)(2,1)S(1)} %dynamic-slice_bitcast_fusion.1), channel_id=1, source_target_pairs={{0,16},{2,18},{4,20},{6,22},{8,24},{10,26},{12,28},{14,30},{16,0},... | collective-permute-start | bytes 491528 | tf_op jit(solution)/shard_map/ppermute | solution.py:353
  55.6 10.9 %collective-permute-start.10 = (bf16[160,512]{1,0:T(8,128)(2,1)S(1)}, bf16[160,512]{1,0:T(8,128)(2,1)S(1)}, u32[]{:S(2)}, u32[]{:S(2)}) collective-permute-start(bf16[160,512]{1,0:T(8,128)(2,1)S(1)} %bitcast_add_fusion.1), channel_id=1, source_target_pairs={{0,16},{2,18},{4,20},{6,22},{8,24},{10,26},{12,28},{14,30},{16,0},... | collective-permute-start | bytes 491528 | tf_op jit(solution)/shard_map/ppermute | solution.py:353
  67.0 24.9 %collective-permute-start.12 = (bf16[256,2048]{1,0:T(8,128)(2,1)}, bf16[256,2048]{1,0:T(8,128)(2,1)S(1)}, u32[]{:S(2)}, u32[]{:S(2)}) collective-permute-start(bf16[256,2048]{1,0:T(8,128)(2,1)} %shard_map.125), channel_id=1, source_target_pairs={{0,4},{2,6},{4,0},{6,2},{8,12},{10,14},{12,8},{14,10},{16,20},{18,... | collective-permute-start | bytes 3145736 | tf_op jit(solution)/shard_map/ppermute | solution.py:318
  68.6 24.9 %collective-permute-start.13 = (bf16[512,1024]{1,0:T(8,128)(2,1)}, bf16[512,1024]{1,0:T(8,128)(2,1)}, u32[]{:S(2)}, u32[]{:S(2)}) collective-permute-start(bf16[512,1024]{1,0:T(8,128)(2,1)} %get-tuple-element.95), channel_id=1, source_target_pairs={{0,2},{2,0},{4,6},{6,4},{8,10},{10,8},{12,14},{14,12},{16,18},{18,... | collective-permute-start | bytes 3145736 | tf_op jit(solution)/shard_map/ppermute | solution.py:315
  69.6 11.4 %collective-permute-start.11 = (bf16[256,1024]{1,0:T(8,128)(2,1)S(1)}, bf16[256,1024]{1,0:T(8,128)(2,1)}, u32[]{:S(2)}, u32[]{:S(2)}) collective-permute-start(bf16[256,1024]{1,0:T(8,128)(2,1)S(1)} %slice.15), channel_id=1, source_target_pairs={{0,2},{2,0},{4,6},{6,4},{8,10},{10,8},{12,14},{14,12},{16,18},{18,... | collective-permute-start | bytes 1572872 | tf_op jit(solution)/shard_map/ppermute | solution.py:315
  70.2 9.7 %collective-permute-start.15 = (bf16[320,512]{1,0:T(8,128)(2,1)S(1)}, bf16[320,512]{1,0:T(8,128)(2,1)S(1)}, u32[]{:S(2)}, u32[]{:S(2)}) collective-permute-start(bf16[320,512]{1,0:T(8,128)(2,1)S(1)} %maximum_select_fusion.1), channel_id=1, source_target_pairs={{0,8},{2,10},{4,12},{6,14},{8,0},{10,2},{12,4},{14,6},{16,24},{18,... | collective-permute-start | bytes 983048 | tf_op jit(solution)/shard_map/ppermute | solution.py:353
  70.2 32.3 %collective-permute-start.14 = (bf16[512,1024]{1,0:T(8,128)(2,1)}, bf16[512,1024]{1,0:T(8,128)(2,1)S(1)}, u32[]{:S(2)}, u32[]{:S(2)}) collective-permute-start(bf16[512,1024]{1,0:T(8,128)(2,1)} %get-tuple-element.96.refs_0_), channel_id=1, source_target_pairs={{1,0},{0,1},{3,2},{2,3},{5,4},{4,5},{7,6},{6,7},{9,8},{8,9},{11,10... | collective-permute-start | bytes 3145736 | tf_op jit(solution)/shard_map/ppermute | solution.py:321
  102.5 25.6 %collective-permute-start.16 = (bf16[256,2048]{1,0:T(8,128)(2,1)S(1)}, bf16[256,2048]{1,0:T(8,128)(2,1)S(1)}, u32[]{:S(2)}, u32[]{:S(2)}) collective-permute-start(bf16[256,2048]{1,0:T(8,128)(2,1)S(1)} %add.150), channel_id=1, source_target_pairs={{8,0},{10,2},{12,4},{14,6},{24,16},{26,18},{28,20},{30,22},{1,9},{... | collective-permute-start | bytes 3145736 | tf_op jit(solution)/shard_map/ppermute | solution.py:357
  103.8 25.6 %collective-permute-start.18 = (bf16[256,2048]{1,0:T(8,128)(2,1)S(1)}, bf16[256,2048]{1,0:T(8,128)(2,1)S(1)}, u32[]{:S(2)}, u32[]{:S(2)}) collective-permute-start(bf16[256,2048]{1,0:T(8,128)(2,1)S(1)} %add.165), channel_id=1, source_target_pairs={{0,8},{2,10},{4,12},{6,14},{16,24},{18,26},{20,28},{22,30},{9,1},{... | collective-permute-start | bytes 3145736 | tf_op jit(solution)/shard_map/ppermute | solution.py:357
  108.5 23.4 %collective-permute-start.17 = (bf16[256,2048]{1,0:T(8,128)(2,1)}, bf16[256,2048]{1,0:T(8,128)(2,1)S(1)}, u32[]{:S(2)}, u32[]{:S(2)}) collective-permute-start(bf16[256,2048]{1,0:T(8,128)(2,1)} %get-tuple-element.103), channel_id=1, source_target_pairs={{0,4},{2,6},{4,0},{6,2},{8,12},{10,14},{12,8},{14,10},{16,20},{18,... | collective-permute-start | bytes 3145736 | tf_op jit(solution)/shard_map/ppermute | solution.py:318
  110.1 22.9 %collective-permute-start.20 = (bf16[512,1024]{1,0:T(8,128)(2,1)S(1)}, bf16[512,1024]{1,0:T(8,128)(2,1)}, u32[]{:S(2)}, u32[]{:S(2)}) collective-permute-start(bf16[512,1024]{1,0:T(8,128)(2,1)S(1)} %copy-done.8), channel_id=1, source_target_pairs={{1,0},{0,1},{3,2},{2,3},{5,4},{4,5},{7,6},{6,7},{9,8},{8,9},{11,10... | collective-permute-start | bytes 3145736 | tf_op jit(solution)/shard_map/ppermute | solution.py:321
  133.0 23.8 %collective-permute-start.21 = (bf16[256,2048]{1,0:T(8,128)(2,1)S(1)}, bf16[256,2048]{1,0:T(8,128)(2,1)S(1)}, u32[]{:S(2)}, u32[]{:S(2)}) collective-permute-start(bf16[256,2048]{1,0:T(8,128)(2,1)S(1)} %add.167), channel_id=1, source_target_pairs={{0,8},{2,10},{4,12},{6,14},{24,16},{26,18},{28,20},{30,22},{1,9},{... | collective-permute-start | bytes 3145736 | tf_op jit(solution)/shard_map/ppermute | solution.py:357
  134.3 22.9 %collective-permute-start.23 = (bf16[256,2048]{1,0:T(8,128)(2,1)}, bf16[256,2048]{1,0:T(8,128)(2,1)}, u32[]{:S(2)}, u32[]{:S(2)}) collective-permute-start(bf16[256,2048]{1,0:T(8,128)(2,1)} %shard_map.129), channel_id=1, source_target_pairs={{0,4},{2,6},{4,0},{6,2},{8,12},{10,14},{12,8},{14,10},{16,20},{18,... | collective-permute-start | bytes 3145736 | tf_op jit(solution)/shard_map/ppermute | solution.py:318
  135.1 24.0 %collective-permute-start.24 = (bf16[256,2048]{1,0:T(8,128)(2,1)}, bf16[256,2048]{1,0:T(8,128)(2,1)}, u32[]{:S(2)}, u32[]{:S(2)}) collective-permute-start(bf16[256,2048]{1,0:T(8,128)(2,1)} %add.168), channel_id=1, source_target_pairs={{8,24},{10,26},{12,28},{14,30},{17,1},{19,3},{21,5},{23,7}} | collective-permute-start | bytes 3145736 | tf_op jit(solution)/shard_map/ppermute | solution.py:357
  136.9 24.9 %collective-permute-start.25 = (bf16[256,2048]{1,0:T(8,128)(2,1)}, bf16[256,2048]{1,0:T(8,128)(2,1)}, u32[]{:S(2)}, u32[]{:S(2)}) collective-permute-start(bf16[256,2048]{1,0:T(8,128)(2,1)} %add.166), channel_id=1, source_target_pairs={{16,0},{18,2},{20,4},{22,6},{9,25},{11,27},{13,29},{15,31}} | collective-permute-start | bytes 3145736 | tf_op jit(solution)/shard_map/ppermute | solution.py:357
  165.1 23.4 %collective-permute-start.26 = (bf16[256,2048]{1,0:T(8,128)(2,1)S(1)}, bf16[256,2048]{1,0:T(8,128)(2,1)}, u32[]{:S(2)}, u32[]{:S(2)}) collective-permute-start(bf16[256,2048]{1,0:T(8,128)(2,1)S(1)} %add.170), channel_id=1, source_target_pairs={{0,8},{2,10},{4,12},{6,14},{24,16},{26,18},{28,20},{30,22},{1,9},{... | collective-permute-start | bytes 3145736 | tf_op jit(solution)/shard_map/ppermute | solution.py:357
  166.4 23.8 %collective-permute-start.27 = (bf16[256,2048]{1,0:T(8,128)(2,1)S(1)}, bf16[256,2048]{1,0:T(8,128)(2,1)}, u32[]{:S(2)}, u32[]{:S(2)}) collective-permute-start(bf16[256,2048]{1,0:T(8,128)(2,1)S(1)} %add.169), channel_id=1, source_target_pairs={{16,8},{18,10},{20,12},{22,14},{9,17},{11,19},{13,21},{15,23}} | collective-permute-start | bytes 3145736 | tf_op jit(solution)/shard_map/ppermute | solution.py:357
  168.7 23.2 %collective-permute-start.29 = (bf16[4,160,512]{2,1,0:T(8,128)(2,1)}, bf16[4,160,512]{2,1,0:T(8,128)(2,1)}, u32[]{:S(2)}, u32[]{:S(2)}) collective-permute-start(bf16[4,160,512]{2,1,0:T(8,128)(2,1)} %bitcast.19.keep), channel_id=1, source_target_pairs={{0,2},{2,0},{4,6},{6,4},{8,10},{10,8},{12,14},{14,12},{16,18},{18,... | collective-permute-start | bytes 1966088 | tf_op jit(solution)/shard_map/ppermute | solution.py:315
  168.7 23.2 %collective-permute-start.28 = (bf16[4,160,512]{2,1,0:T(8,128)(2,1)}, bf16[4,160,512]{2,1,0:T(8,128)(2,1)}, u32[]{:S(2)}, u32[]{:S(2)}) collective-permute-start(bf16[4,160,512]{2,1,0:T(8,128)(2,1)} %bitcast.19.keep), channel_id=1, source_target_pairs={{0,4},{2,6},{4,0},{6,2},{8,12},{10,14},{12,8},{14,10},{16,20},{18,... | collective-permute-start | bytes 1966088 | tf_op jit(solution)/shard_map/ppermute | solution.py:318
  191.9 22.5 %collective-permute-start.32 = (bf16[256,2048]{1,0:T(8,128)(2,1)S(1)}, bf16[256,2048]{1,0:T(8,128)(2,1)}, u32[]{:S(2)}, u32[]{:S(2)}) collective-permute-start(bf16[256,2048]{1,0:T(8,128)(2,1)S(1)} %add.173), channel_id=1, source_target_pairs={{8,16},{10,18},{12,20},{14,22},{17,9},{19,11},{21,13},{23,15}} | collective-permute-start | bytes 3145736 | tf_op jit(solution)/shard_map/ppermute | solution.py:357
  193.2 2.4 %collective-permute-start.30 = (bf16[4,160,512]{2,1,0:T(8,128)(2,1)}, bf16[4,160,512]{2,1,0:T(8,128)(2,1)S(1)}, u32[]{:S(2)}, u32[]{:S(2)}) collective-permute-start(bf16[4,160,512]{2,1,0:T(8,128)(2,1)} %collective-permute-done.28.back), channel_id=1, source_target_pairs={{0,2},{2,0},{4,6},{6,4},{8,10},{10,8},{12,14},{14,12},{16,18},{18,... | collective-permute-start | bytes 1966088 | tf_op jit(solution)/shard_map/ppermute | solution.py:315
  208.0 3.9 %collective-permute-start.31 = (f32[4,1,512]{2,1,0:T(1,128)}, f32[4,1,512]{2,1,0:T(1,128)S(1)}, u32[]{:S(2)}, u32[]{:S(2)}) collective-permute-start(f32[4,1,512]{2,1,0:T(1,128)} %get-tuple-element.126), channel_id=1, source_target_pairs={{1,0},{0,1},{3,2},{2,3},{5,4},{4,5},{7,6},{6,7},{9,8},{8,9},{11,10... | collective-permute-start | bytes 24584 | tf_op jit(solution)/shard_map/ppermute | solution.py:321
  215.8 2.7 %collective-permute-start.33 = (bf16[256,2048]{1,0:T(8,128)(2,1)S(1)}, bf16[256,2048]{1,0:T(8,128)(2,1)S(1)}, u32[]{:S(2)}, u32[]{:S(2)}) collective-permute-start(bf16[256,2048]{1,0:T(8,128)(2,1)S(1)} %add_select_fusion.refs_0_), channel_id=1, source_target_pairs={{0,2},{2,0},{4,6},{6,4},{8,10},{10,8},{12,14},{14,12},{16,18},{18,... | collective-permute-start | bytes 3145736 | tf_op jit(solution)/shard_map/ppermute | solution.py:512
  (18 other events, 120.0 us)

commit v7 on v6

--- a/solution.py
+++ b/solution.py
@@ -402,9 +402,9 @@
         other, own, across = turned(rows, which, rows_dev)
         return {("p", j, 0): other, ("p", j, 1): own, ("p", j): across}
 
-    def gathered(part, bits):
+    def gathered(part, bits, tie=lambda v: v):
         for far in bits:
-            other = swap_z(part, far)
+            other = tie(swap_z(part, far))
             mine_first = jnp.concatenate([part, other], axis=0)
             part = jnp.where(z // far % 2 == 0, mine_first, jnp.concatenate([other, part], axis=0))
         return part
@@ -449,9 +449,6 @@
                 there = lax.dynamic_index_in_dim(parts, 1 - bit, 0, keepdims=False)
                 part = lax.dynamic_index_in_dim(parts, bit, 0, keepdims=False) + swap_z(there, far)
             joined["keep"] = gathered(part, z_bits[-1:])
-        if stage == 2:
-            part = gathered(env["keep"], reversed(z_bits[:-1]))
-            joined["keep"] = part.reshape(local_blocks, -1, block_size)
         if stage == across:
             joined["back"] = swap_x(env["keep"])
             joined["keep_sib"] = swap_core(env["keep"])
@@ -483,6 +480,14 @@
                 for at, outs in zip(due, found):
                     for n in chunks:
                         joined["mine" if at else "out", step, j, n] = outs[n]
+        made = [value for key, value in joined.items() if key[0] in ("out", "mine")]
+
+        def behind(v, made=made):
+            return lax.optimization_barrier((v, *made))[0] if made else v
+
+        if stage == 2:
+            part = gathered(env["keep"], reversed(z_bits[:-1]), behind)
+            joined["keep"] = part.reshape(local_blocks, -1, block_size)
         if stage == 0:
             keep, joined["out", 0, 0, 0] = lax.optimization_barrier((keep, joined["out", 0, 0, 0]))
             joined["keep"] = keep + away
@@ -490,9 +495,9 @@
         for step, j, n in x_stage:
             mine, got, acc = ("mine", step, j, n), ("got", step, j, n), ("acc", step, j, n)
             if mine in env and got in env:
-                env[acc] = env.pop(mine) + env.pop(got)
+                env[acc] = behind(env.pop(mine)) + env.pop(got)
             if ("hop", step, j, n) in env:
-                env[acc] = env[acc] + env.pop(("hop", step, j, n))
+                env[acc] = behind(env[acc]) + env.pop(("hop", step, j, n))
         for step, j, n in x_stage:
             if stage == z_stage[step, j, n, len(z_bits) - 1]:
                 ends = jnp.array([place((i + step) % n_worker, j) for i in range(n_worker)], jnp.int32)

time: 230 us -> 223 us (0.970)
  waiting for transfers between devices: 71 us -> 60.4 us
  starting transfers between devices: 38.3 us -> 42.3 us
    ppermute x4, waiting for transfers between devices: 16.3 us -> 7.09 us  [swap_z(): return lax.ppermute(v, 'dp', [(i, i ^ 4 * bit) for i in range(n_dp)])]
    ppermute x8, waiting for transfers between devices: 34.7 us -> 27.5 us  [hop(): return lax.ppermute(v, both, pairs)]
    ppermute x6, waiting for transfers between devices: 10.8 us -> 17.8 us  [swap_x(): return lax.ppermute(v, 'dp', [(i, i ^ 2) for i in range(n_dp)])]
    ppermute x5, starting transfers between devices: 3.14 us -> 6.99 us  [from_worker(): lax.ppermute(v, 'worker', [((j + step) % n_worker, j) for j in range(n_wo...]
  transfers between devices with their start and end apart: 34 -> 34, of which waited for: 18 -> 16; matrix products, arithmetic and copies ran while one was open for 9% -> 9% of each run, Pallas kernels for 33% -> 34%
where the time goes in v7:
time: 223 us; the launch traced here: 220 us
  Pallas kernels  83.6 us (37%)
  waiting for transfers between devices  60.4 us (27%)
  starting transfers between devices  42.3 us (19%)
  other arithmetic  21 us (9%)
  local copies, waits for them, and re-layouts  9.81 us (4%)
  between operations  3 us (1%)
    pallas_call x6, Pallas kernels, products(): pl.pallas_call(functools.partial(product_kernel, [len(half) for half in h...  44.7 us
    ppermute x8, waiting for transfers between devices, hop(): return lax.ppermute(v, both, pairs)  27.5 us
    ppermute x8, starting transfers between devices, hop(): return lax.ppermute(v, both, pairs)  19.1 us
    ppermute x6, waiting for transfers between devices, swap_x(): return lax.ppermute(v, 'dp', [(i, i ^ 2) for i in range(n_dp)])  17.8 us
    pallas_call x1, Pallas kernels, update_factors(): pl.pallas_call(factor_kernel, grid_spec=pltpu.PrefetchScalarGridSpec(num_...  11.5 us
    pallas_call x2, Pallas kernels, turned(): pl.pallas_call(turn_kernel, grid_spec=pltpu.PrefetchScalarGridSpec(num_sc...  10.5 us
    pallas_call x1, Pallas kernels, tail(): pl.pallas_call(functools.partial(tail_kernel, len(parts)), grid_spec=pltp...  8.24 us
    ppermute x6, starting transfers between devices, swap_x(): return lax.ppermute(v, 'dp', [(i, i ^ 2) for i in range(n_dp)])  8.06 us
  transfers between devices with their start and end apart: 34, of which 16 were waited for; matrix products, arithmetic and copies ran while one was open for 9% of the time, Pallas kernels for 34%

profile of v7, /device:TPU:12, one launch (start us, length us, event | category | flops | bytes accessed | tf_op | source)
XLA Modules:
  0.0 220.1 jit_solution(3275042148675252322)
XLA Ops:
  2.0 3.3 %shard_map.123 = (bf16[256,2048]{1,0:T(8,128)(2,1)}, bf16[256,2048]{1,0:T(8,128)(2,1)}) custom-call(s32[3]{0:T(128)} %pad_add_fusion.3.which_ref, bf16[1024,2048]{1,0:T(8,128)(2,1)} %refs_2_.5, bf16[1024,2048]{1,0:T(8,128)(2,1)} %block.2), custom_call_target="tpu_custom_call" | custom-call | flops 1 | bytes 1 | tf_op jit(solution)/shard_map/pallas_call | solution.py:35
  6.5 5.2 %shard_map.121 = (bf16[512,1024]{1,0:T(8,128)(2,1)}, bf16[512,1024]{1,0:T(8,128)(2,1)}, bf16[512,1024]{1,0:T(8,128)(2,1)}) custom-call(s32[4]{0:T(128)} %get-tuple-element.153.which_ref, bf16[1024,2048]{1,0:T(8,128)(2,1)} %block.2), custom_call_target="tpu_custom_call" | custom-call | flops 1 | bytes 1 | tf_op jit(solution)/shard_map/pallas_call | solution.py:226
  13.9 5.2 %shard_map.124 = (bf16[4,160,512]{2,1,0:T(8,128)(2,1)}, bf16[4,160,512]{2,1,0:T(8,128)(2,1)}) custom-call(s32[2]{0:T(128)} %pad_add_fusion.2.place_ref, bf16[256,2048]{1,0:T(8,128)(2,1)} %get-tuple-element.82.ours, bf16[256,2048]{1,0:T(8,128)(2,1)} %copy-done.4), custom_call_target="tpu_custom_call" | custom-call | flops 1 | bytes 1 | tf_op jit(solution)/shard_map/pallas_call | solution.py:73
  21.5 9.0 %shard_map.122 = (bf16[256,2048]{1,0:T(8,128)(2,1)}, bf16[256,2048]{1,0:T(8,128)(2,1)}) custom-call(bf16[512,1024]{1,0:T(8,128)(2,1)} %get-tuple-element.79.refs_0_, bf16[512,1024]{1,0:T(8,128)(2,1)} %get-tuple-element.95.refs_1_, bf16[512,1024]{1,0:T(8,128)(2,1)} %copy-done.10, bf16[1024,2048]{1,0:T(8,128)(2,1)} %refs_2_.5, ...), custom_call_target="tpu_custom_call" | custom-call | flops 8589934592 | bytes 8388608 | tf_op jit(solution)/shard_map/pallas_call | solution.py:278
  30.6 5.6 %collective-permute-done.4 = bf16[4,160,512]{2,1,0:T(8,128)(2,1)S(1)} collective-permute-done((bf16[4,160,512]{2,1,0:T(8,128)(2,1)}, bf16[4,160,512]{2,1,0:T(8,128)(2,1)S(1)}, u32[]{:S(2)}, u32[]{:S(2)}) %collective-permute-start.4) | collective-permute-done | bytes 655392 | tf_op jit(solution)/shard_map/ppermute | solution.py:318
  40.5 6.4 %collective-permute-done.8 = bf16[320,512]{1,0:T(8,128)(2,1)S(1)} collective-permute-done((bf16[320,512]{1,0:T(8,128)(2,1)S(1)}, bf16[320,512]{1,0:T(8,128)(2,1)S(1)}, u32[]{:S(2)}, u32[]{:S(2)}) %collective-permute-start.8) | collective-permute-done | bytes 327712 | tf_op jit(solution)/shard_map/ppermute | solution.py:353
  47.0 2.7 %collective-permute-start.9 = (bf16[160,512]{1,0:T(8,128)(2,1)S(1)}, bf16[160,512]{1,0:T(8,128)(2,1)S(1)}, u32[]{:S(2)}, u32[]{:S(2)}) collective-permute-start(bf16[160,512]{1,0:T(8,128)(2,1)S(1)} %dynamic-slice_bitcast_fusion.1), channel_id=1, source_target_pairs={{0,16},{2,18},{4,20},{6,22},{8,24},{10,26},{12,28},{14,30},{16,0},... | collective-permute-start | bytes 491528 | tf_op jit(solution)/shard_map/ppermute | solution.py:353
  49.6 5.3 %shard_map.126 = (bf16[512,1024]{1,0:T(8,128)(2,1)}, bf16[512,1024]{1,0:T(8,128)(2,1)}, bf16[512,1024]{1,0:T(8,128)(2,1)}) custom-call(s32[4]{0:T(128)} %get-tuple-element.154.which_ref, bf16[1024,2048]{1,0:T(8,128)(2,1)} %block.2), custom_call_target="tpu_custom_call" | custom-call | flops 1 | bytes 1 | tf_op jit(solution)/shard_map/pallas_call | solution.py:226
  55.6 3.4 %collective-permute-start.10 = (bf16[160,512]{1,0:T(8,128)(2,1)S(1)}, bf16[160,512]{1,0:T(8,128)(2,1)S(1)}, u32[]{:S(2)}, u32[]{:S(2)}) collective-permute-start(bf16[160,512]{1,0:T(8,128)(2,1)S(1)} %bitcast_add_fusion.1), channel_id=1, source_target_pairs={{0,16},{2,18},{4,20},{6,22},{8,24},{10,26},{12,28},{14,30},{16,0},... | collective-permute-start | bytes 491528 | tf_op jit(solution)/shard_map/ppermute | solution.py:353
  59.8 6.7 %shard_map.125 = bf16[256,2048]{1,0:T(8,128)(2,1)} custom-call(bf16[512,1024]{1,0:T(8,128)(2,1)} %copy-done.7, bf16[256,1024]{1,0:T(8,128)(2,1)} %copy-done.11, bf16[1024,2048]{1,0:T(8,128)(2,1)} %refs_2_.5, bf16[1024,2048]{1,0:T(8,128)(2,1)} %collective-permute-done.1.refs_4_.refs_3_), custom_call_target="tpu_custom_call" | custom-call | flops 4294967296 | bytes 8388608 | tf_op jit(solution)/shard_map/pallas_call | solution.py:278
  70.7 6.7 %shard_map.127 = bf16[256,2048]{1,0:T(8,128)(2,1)} custom-call(bf16[512,1024]{1,0:T(8,128)(2,1)} %collective-permute-done.7.refs_0_, bf16[256,1024]{1,0:T(8,128)(2,1)} %collective-permute-done.11.refs_1_, bf16[1024,2048]{1,0:T(8,128)(2,1)} %refs_2_.5, bf16[1024,2048]{1,0:T(8,128)(2,1)} %collective-permute-done.1.refs_4_.refs_3_), custom_call_target="tpu_custom_call" | custom-call | flops 4294967296 | bytes 8388608 | tf_op jit(solution)/shard_map/pallas_call | solution.py:278
  77.4 9.1 %shard_map.128 = (bf16[256,2048]{1,0:T(8,128)(2,1)}, bf16[256,2048]{1,0:T(8,128)(2,1)}) custom-call(bf16[512,1024]{1,0:T(8,128)(2,1)} %get-tuple-element.105.refs_0_, bf16[512,1024]{1,0:T(8,128)(2,1)} %get-tuple-element.124.refs_1_, bf16[512,1024]{1,0:T(8,128)(2,1)} %collective-permute-done.12.refs_2_, bf16[1024,2048]{1,0:T(8,128)(2,1)} %refs_2_.5, ...), custom_call_target="tpu_custom_call" | custom-call | flops 8589934592 | bytes 8388608 | tf_op jit(solution)/shard_map/pallas_call | solution.py:278
  86.4 7.7 %collective-permute-done.13 = bf16[256,2048]{1,0:T(8,128)(2,1)S(1)} collective-permute-done((bf16[256,2048]{1,0:T(8,128)(2,1)}, bf16[256,2048]{1,0:T(8,128)(2,1)S(1)}, u32[]{:S(2)}, u32[]{:S(2)}) %collective-permute-start.13) | collective-permute-done | bytes 1048608 | tf_op jit(solution)/shard_map/ppermute | solution.py:318
  95.7 3.6 %collective-permute-start.19 = (bf16[256,2048]{1,0:T(8,128)(2,1)S(1)}, bf16[256,2048]{1,0:T(8,128)(2,1)S(1)}, u32[]{:S(2)}, u32[]{:S(2)}) collective-permute-start(bf16[256,2048]{1,0:T(8,128)(2,1)S(1)} %add.165), channel_id=1, source_target_pairs={{0,8},{2,10},{4,12},{6,14},{16,24},{18,26},{20,28},{22,30},{9,1},{... | collective-permute-start | bytes 3145736 | tf_op jit(solution)/shard_map/ppermute | solution.py:357
  103.9 2.0 collective-permute-done.16.refs_1_
  105.9 6.7 %shard_map.129 = bf16[256,2048]{1,0:T(8,128)(2,1)} custom-call(bf16[512,1024]{1,0:T(8,128)(2,1)} %copy-done.8, bf16[256,1024]{1,0:T(8,128)(2,1)} %collective-permute-done.16.refs_1_, bf16[1024,2048]{1,0:T(8,128)(2,1)} %refs_2_.5, bf16[1024,2048]{1,0:T(8,128)(2,1)} %collective-permute-done.1.refs_4_.refs_3_), custom_call_target="tpu_custom_call" | custom-call | flops 4294967296 | bytes 8388608 | tf_op jit(solution)/shard_map/pallas_call | solution.py:278
  112.6 8.1 %collective-permute-done.19 = bf16[256,2048]{1,0:T(8,128)(2,1)S(1)} collective-permute-done((bf16[256,2048]{1,0:T(8,128)(2,1)S(1)}, bf16[256,2048]{1,0:T(8,128)(2,1)S(1)}, u32[]{:S(2)}, u32[]{:S(2)}) %collective-permute-start.19) | collective-permute-done | bytes 1048608 | tf_op jit(solution)/shard_map/ppermute | solution.py:357
  123.7 2.5 %collective-permute-done.17 = bf16[256,2048]{1,0:T(8,128)(2,1)S(1)} collective-permute-done((bf16[256,2048]{1,0:T(8,128)(2,1)S(1)}, bf16[256,2048]{1,0:T(8,128)(2,1)S(1)}, u32[]{:S(2)}, u32[]{:S(2)}) %collective-permute-start.17) | collective-permute-done | bytes 1048608 | tf_op jit(solution)/shard_map/ppermute | solution.py:357
  129.4 1.7 collective-permute-start.24
  131.1 5.5 %collective-permute-start.25 = (bf16[256,2048]{1,0:T(8,128)(2,1)}, bf16[256,2048]{1,0:T(8,128)(2,1)}, u32[]{:S(2)}, u32[]{:S(2)}) collective-permute-start(bf16[256,2048]{1,0:T(8,128)(2,1)} %add.166), channel_id=1, source_target_pairs={{16,0},{18,2},{20,4},{22,6},{9,25},{11,27},{13,29},{15,31}} | collective-permute-start | bytes 3145736 | tf_op jit(solution)/shard_map/ppermute | solution.py:357
  140.4 6.7 %shard_map.130 = bf16[256,2048]{1,0:T(8,128)(2,1)} custom-call(bf16[512,1024]{1,0:T(8,128)(2,1)} %collective-permute-done.20.refs_0_, bf16[256,1024]{1,0:T(8,128)(2,1)} %copy-done.12, bf16[1024,2048]{1,0:T(8,128)(2,1)} %refs_2_.5, bf16[1024,2048]{1,0:T(8,128)(2,1)} %collective-permute-done.1.refs_4_.refs_3_), custom_call_target="tpu_custom_call" | custom-call | flops 4294967296 | bytes 8388608 | tf_op jit(solution)/shard_map/pallas_call | solution.py:278
  147.1 3.4 %collective-permute-done.23 = bf16[256,2048]{1,0:T(8,128)(2,1)} collective-permute-done((bf16[256,2048]{1,0:T(8,128)(2,1)}, bf16[256,2048]{1,0:T(8,128)(2,1)}, u32[]{:S(2)}, u32[]{:S(2)}) %collective-permute-start.23) | collective-permute-done | bytes 1048608 | tf_op jit(solution)/shard_map/ppermute | solution.py:318
  150.5 1.9 add.170
  155.1 3.3 %add_select_fusion.2 = bf16[256,2048]{1,0:T(8,128)(2,1)} fusion(bf16[256,2048]{1,0:T(8,128)(2,1)} %add.166, bf16[256,2048]{1,0:T(8,128)(2,1)} %collective-permute-done.25, bf16[256,2048]{1,0:T(8,128)(2,1)} %add.168, bf16[256,2048]{1,0:T(8,128)(2,1)} %collective-permute-done.24, pred[]{:T(512)S(6)} %eq.28), kind=kLoop, calls=%fused_computation.2 | loop fusion | flops 1572864 | bytes 5242881 | tf_op jit(solution)/shard_map/jit(_where)/select_n | solution.py:505
  159.7 3.2 %collective-permute-start.27 = (bf16[256,2048]{1,0:T(8,128)(2,1)}, bf16[256,2048]{1,0:T(8,128)(2,1)}, u32[]{:S(2)}, u32[]{:S(2)}) collective-permute-start(bf16[256,2048]{1,0:T(8,128)(2,1)} %add.169), channel_id=1, source_target_pairs={{16,8},{18,10},{20,12},{22,14},{9,17},{11,19},{13,21},{15,23}} | collective-permute-start | bytes 3145736 | tf_op jit(solution)/shard_map/ppermute | solution.py:357
  165.6 15.6 %collective-permute-done.26 = bf16[256,2048]{1,0:T(8,128)(2,1)S(1)} collective-permute-done((bf16[256,2048]{1,0:T(8,128)(2,1)S(1)}, bf16[256,2048]{1,0:T(8,128)(2,1)S(1)}, u32[]{:S(2)}, u32[]{:S(2)}) %collective-permute-start.26) | collective-permute-done | bytes 1048608 | tf_op jit(solution)/shard_map/ppermute | solution.py:357
  181.6 2.0 add_select_fusion.1
  185.7 1.6 collective-permute-done.30.back_sib
  188.2 11.5 %shard_map.131 = (f32[4,512,512]{2,1,0:T(8,128)}, f32[4,512,512]{2,1,0:T(8,128)}, f32[4,1,512]{2,1,0:T(1,128)}, f32[4,1,512]{2,1,0:T(1,128)}) custom-call(s32[3]{0:T(128)} %pad_add_fusion.5.place_ref, bf16[4,160,512]{2,1,0:T(8,128)(2,1)} %bitcast.19.keep, bf16[4,160,512]{2,1,0:T(8,128)(2,1)} %collective-permute-done.28.back, ...), custom_call_target="tpu_custom_call" | custom-call | flops 1 | bytes 1 | tf_op jit(solution)/shard_map/pallas_call | solution.py:129
  199.7 3.9 %collective-permute-start.31 = (f32[4,1,512]{2,1,0:T(1,128)}, f32[4,1,512]{2,1,0:T(1,128)S(1)}, u32[]{:S(2)}, u32[]{:S(2)}) collective-permute-start(f32[4,1,512]{2,1,0:T(1,128)} %get-tuple-element.146), channel_id=1, source_target_pairs={{1,0},{0,1},{3,2},{2,3},{5,4},{4,5},{7,6},{6,7},{9,8},{8,9},{11,10... | collective-permute-start | bytes 24584 | tf_op jit(solution)/shard_map/ppermute | solution.py:321
  209.1 1.8 collective-permute-done.33.refs_1_
  211.9 8.2 %shard_map.132 = bf16[256,2048]{1,0:T(8,128)(2,1)} custom-call(s32[3]{0:T(128)} %pad_add_fusion.place_ref, bf16[256,2048]{1,0:T(8,128)(2,1)} %copy-done.1, bf16[256,2048]{1,0:T(8,128)(2,1)} %copy-done.9, bf16[4,512,512]{2,1,0:T(8,128)(2,1)} %refs_2_.7, bf16[8,512,512]{2,1,0:T(8,128)(2,1)} %refs_3_.6, f32[4,1,512]{2,1,0:T(1,128)} %get-tuple-element.149.refs_4_, ...), custom_call_target="tpu_custom_call" | custom-call | flops 3221225472 | bytes 4194304 | tf_op jit(solution)/shard_map/pallas_call | solution.py:184
  (111 shorter events, 47.5 us)
Async XLA Ops:
  0.6 19.9 %collective-permute-start.1 = (bf16[1024,2048]{1,0:T(8,128)(2,1)}, bf16[1024,2048]{1,0:T(8,128)(2,1)}, u32[]{:S(2)}, u32[]{:S(2)}) collective-permute-start(bf16[1024,2048]{1,0:T(8,128)(2,1)} %refs_2_.5), channel_id=1, source_target_pairs={{0,2},{2,0},{4,6},{6,4},{8,10},{10,8},{12,14},{14,12},{16,18},{18,... | collective-permute-start | bytes 12582920 | tf_op jit(solution)/shard_map/ppermute | solution.py:315
  5.3 7.6 %collective-permute-start.2 = (bf16[256,2048]{1,0:T(8,128)(2,1)}, bf16[256,2048]{1,0:T(8,128)(2,1)S(1)}, u32[]{:S(2)}, u32[]{:S(2)}) collective-permute-start(bf16[256,2048]{1,0:T(8,128)(2,1)} %get-tuple-element.83), channel_id=1, source_target_pairs={{0,2},{2,0},{4,6},{6,4},{8,10},{10,8},{12,14},{14,12},{16,18},{18,... | collective-permute-start | bytes 3145736 | tf_op jit(solution)/shard_map/ppermute | solution.py:315
  11.7 8.9 %collective-permute-start = (bf16[512,1024]{1,0:T(8,128)(2,1)}, bf16[512,1024]{1,0:T(8,128)(2,1)S(1)}, u32[]{:S(2)}, u32[]{:S(2)}) collective-permute-start(bf16[512,1024]{1,0:T(8,128)(2,1)} %get-tuple-element.78), channel_id=1, source_target_pairs={{0,2},{2,0},{4,6},{6,4},{8,10},{10,8},{12,14},{14,12},{16,18},{18,... | collective-permute-start | bytes 3145736 | tf_op jit(solution)/shard_map/ppermute | solution.py:315
  11.7 25.8 %collective-permute-start.3 = (bf16[512,1024]{1,0:T(8,128)(2,1)}, bf16[512,1024]{1,0:T(8,128)(2,1)S(1)}, u32[]{:S(2)}, u32[]{:S(2)}) collective-permute-start(bf16[512,1024]{1,0:T(8,128)(2,1)} %get-tuple-element.79.refs_0_), channel_id=1, source_target_pairs={{1,0},{0,1},{3,2},{2,3},{5,4},{4,5},{7,6},{6,7},{9,8},{8,9},{11,10... | collective-permute-start | bytes 3145736 | tf_op jit(solution)/shard_map/ppermute | solution.py:321
  19.1 17.0 %collective-permute-start.4 = (bf16[4,160,512]{2,1,0:T(8,128)(2,1)}, bf16[4,160,512]{2,1,0:T(8,128)(2,1)S(1)}, u32[]{:S(2)}, u32[]{:S(2)}) collective-permute-start(bf16[4,160,512]{2,1,0:T(8,128)(2,1)} %get-tuple-element.88), channel_id=1, source_target_pairs={{0,4},{2,6},{4,0},{6,2},{8,12},{10,14},{12,8},{14,10},{16,20},{18,... | collective-permute-start | bytes 1966088 | tf_op jit(solution)/shard_map/ppermute | solution.py:318
  37.5 9.4 %collective-permute-start.8 = (bf16[320,512]{1,0:T(8,128)(2,1)S(1)}, bf16[320,512]{1,0:T(8,128)(2,1)S(1)}, u32[]{:S(2)}, u32[]{:S(2)}) collective-permute-start(bf16[320,512]{1,0:T(8,128)(2,1)S(1)} %dynamic-slice_bitcast_fusion), channel_id=1, source_target_pairs={{0,8},{2,10},{4,12},{6,14},{8,0},{10,2},{12,4},{14,6},{16,24},{18,... | collective-permute-start | bytes 983048 | tf_op jit(solution)/shard_map/ppermute | solution.py:353
  38.5 20.6 %collective-permute-start.5 = (bf16[256,1024]{1,0:T(8,128)(2,1)S(1)}, bf16[256,1024]{1,0:T(8,128)(2,1)S(1)}, u32[]{:S(2)}, u32[]{:S(2)}) collective-permute-start(bf16[256,1024]{1,0:T(8,128)(2,1)S(1)} %slice.14), channel_id=1, source_target_pairs={{0,2},{2,0},{4,6},{6,4},{8,10},{10,8},{12,14},{14,12},{16,18},{18,... | collective-permute-start | bytes 1572872 | tf_op jit(solution)/shard_map/ppermute | solution.py:315
  38.5 28.1 %collective-permute-start.6 = (bf16[256,2048]{1,0:T(8,128)(2,1)}, bf16[256,2048]{1,0:T(8,128)(2,1)S(1)}, u32[]{:S(2)}, u32[]{:S(2)}) collective-permute-start(bf16[256,2048]{1,0:T(8,128)(2,1)} %get-tuple-element.94), channel_id=1, source_target_pairs={{0,4},{2,6},{4,0},{6,2},{8,12},{10,14},{12,8},{14,10},{16,20},{18,... | collective-permute-start | bytes 3145736 | tf_op jit(solution)/shard_map/ppermute | solution.py:318
  40.0 27.0 %collective-permute-start.7 = (bf16[512,1024]{1,0:T(8,128)(2,1)}, bf16[512,1024]{1,0:T(8,128)(2,1)}, u32[]{:S(2)}, u32[]{:S(2)}) collective-permute-start(bf16[512,1024]{1,0:T(8,128)(2,1)} %get-tuple-element.95.refs_1_), channel_id=1, source_target_pairs={{1,0},{0,1},{3,2},{2,3},{5,4},{4,5},{7,6},{6,7},{9,8},{8,9},{11,10... | collective-permute-start | bytes 3145736 | tf_op jit(solution)/shard_map/ppermute | solution.py:321
  47.0 8.6 %collective-permute-start.9 = (bf16[160,512]{1,0:T(8,128)(2,1)S(1)}, bf16[160,512]{1,0:T(8,128)(2,1)S(1)}, u32[]{:S(2)}, u32[]{:S(2)}) collective-permute-start(bf16[160,512]{1,0:T(8,128)(2,1)S(1)} %dynamic-slice_bitcast_fusion.1), channel_id=1, source_target_pairs={{0,16},{2,18},{4,20},{6,22},{8,24},{10,26},{12,28},{14,30},{16,0},... | collective-permute-start | bytes 491528 | tf_op jit(solution)/shard_map/ppermute | solution.py:353
  55.6 10.9 %collective-permute-start.10 = (bf16[160,512]{1,0:T(8,128)(2,1)S(1)}, bf16[160,512]{1,0:T(8,128)(2,1)S(1)}, u32[]{:S(2)}, u32[]{:S(2)}) collective-permute-start(bf16[160,512]{1,0:T(8,128)(2,1)S(1)} %bitcast_add_fusion.1), channel_id=1, source_target_pairs={{0,16},{2,18},{4,20},{6,22},{8,24},{10,26},{12,28},{14,30},{16,0},... | collective-permute-start | bytes 491528 | tf_op jit(solution)/shard_map/ppermute | solution.py:353
  67.0 10.4 %collective-permute-start.12 = (bf16[512,1024]{1,0:T(8,128)(2,1)}, bf16[512,1024]{1,0:T(8,128)(2,1)}, u32[]{:S(2)}, u32[]{:S(2)}) collective-permute-start(bf16[512,1024]{1,0:T(8,128)(2,1)} %get-tuple-element.107), channel_id=1, source_target_pairs={{0,2},{2,0},{4,6},{6,4},{8,10},{10,8},{12,14},{14,12},{16,18},{18,... | collective-permute-start | bytes 3145736 | tf_op jit(solution)/shard_map/ppermute | solution.py:315
  68.2 2.6 %collective-permute-start.11 = (bf16[256,1024]{1,0:T(8,128)(2,1)S(1)}, bf16[256,1024]{1,0:T(8,128)(2,1)}, u32[]{:S(2)}, u32[]{:S(2)}) collective-permute-start(bf16[256,1024]{1,0:T(8,128)(2,1)S(1)} %slice.15), channel_id=1, source_target_pairs={{0,2},{2,0},{4,6},{6,4},{8,10},{10,8},{12,14},{14,12},{16,18},{18,... | collective-permute-start | bytes 1572872 | tf_op jit(solution)/shard_map/ppermute | solution.py:315
  68.7 17.7 %collective-permute-start.15 = (bf16[320,512]{1,0:T(8,128)(2,1)S(1)}, bf16[320,512]{1,0:T(8,128)(2,1)S(1)}, u32[]{:S(2)}, u32[]{:S(2)}) collective-permute-start(bf16[320,512]{1,0:T(8,128)(2,1)S(1)} %maximum_select_fusion.1), channel_id=1, source_target_pairs={{0,8},{2,10},{4,12},{6,14},{8,0},{10,2},{12,4},{14,6},{16,24},{18,... | collective-permute-start | bytes 983048 | tf_op jit(solution)/shard_map/ppermute | solution.py:353
  68.7 25.4 %collective-permute-start.13 = (bf16[256,2048]{1,0:T(8,128)(2,1)}, bf16[256,2048]{1,0:T(8,128)(2,1)S(1)}, u32[]{:S(2)}, u32[]{:S(2)}) collective-permute-start(bf16[256,2048]{1,0:T(8,128)(2,1)} %shard_map.125), channel_id=1, source_target_pairs={{0,4},{2,6},{4,0},{6,2},{8,12},{10,14},{12,8},{14,10},{16,20},{18,... | collective-permute-start | bytes 3145736 | tf_op jit(solution)/shard_map/ppermute | solution.py:318
  70.2 25.5 %collective-permute-start.14 = (bf16[512,1024]{1,0:T(8,128)(2,1)}, bf16[512,1024]{1,0:T(8,128)(2,1)S(1)}, u32[]{:S(2)}, u32[]{:S(2)}) collective-permute-start(bf16[512,1024]{1,0:T(8,128)(2,1)} %get-tuple-element.105.refs_0_), channel_id=1, source_target_pairs={{1,0},{0,1},{3,2},{2,3},{5,4},{4,5},{7,6},{6,7},{9,8},{8,9},{11,10... | collective-permute-start | bytes 3145736 | tf_op jit(solution)/shard_map/ppermute | solution.py:321
  95.7 25.1 %collective-permute-start.19 = (bf16[256,2048]{1,0:T(8,128)(2,1)S(1)}, bf16[256,2048]{1,0:T(8,128)(2,1)S(1)}, u32[]{:S(2)}, u32[]{:S(2)}) collective-permute-start(bf16[256,2048]{1,0:T(8,128)(2,1)S(1)} %add.165), channel_id=1, source_target_pairs={{0,8},{2,10},{4,12},{6,14},{16,24},{18,26},{20,28},{22,30},{9,1},{... | collective-permute-start | bytes 3145736 | tf_op jit(solution)/shard_map/ppermute | solution.py:357
  99.3 24.0 %collective-permute-start.18 = (bf16[256,2048]{1,0:T(8,128)(2,1)}, bf16[256,2048]{1,0:T(8,128)(2,1)S(1)}, u32[]{:S(2)}, u32[]{:S(2)}) collective-permute-start(bf16[256,2048]{1,0:T(8,128)(2,1)} %get-tuple-element.121), channel_id=1, source_target_pairs={{0,4},{2,6},{4,0},{6,2},{8,12},{10,14},{12,8},{14,10},{16,20},{18,... | collective-permute-start | bytes 3145736 | tf_op jit(solution)/shard_map/ppermute | solution.py:318
  100.9 25.3 %collective-permute-start.17 = (bf16[256,2048]{1,0:T(8,128)(2,1)S(1)}, bf16[256,2048]{1,0:T(8,128)(2,1)S(1)}, u32[]{:S(2)}, u32[]{:S(2)}) collective-permute-start(bf16[256,2048]{1,0:T(8,128)(2,1)S(1)} %add.150), channel_id=1, source_target_pairs={{8,0},{10,2},{12,4},{14,6},{24,16},{26,18},{28,20},{30,22},{1,9},{... | collective-permute-start | bytes 3145736 | tf_op jit(solution)/shard_map/ppermute | solution.py:357
  102.2 25.4 %collective-permute-start.20 = (bf16[512,1024]{1,0:T(8,128)(2,1)}, bf16[512,1024]{1,0:T(8,128)(2,1)}, u32[]{:S(2)}, u32[]{:S(2)}) collective-permute-start(bf16[512,1024]{1,0:T(8,128)(2,1)} %get-tuple-element.124.refs_1_), channel_id=1, source_target_pairs={{1,0},{0,1},{3,2},{2,3},{5,4},{4,5},{7,6},{6,7},{9,8},{8,9},{11,10... | collective-permute-start | bytes 3145736 | tf_op jit(solution)/shard_map/ppermute | solution.py:321
  127.5 22.9 %collective-permute-start.23 = (bf16[256,2048]{1,0:T(8,128)(2,1)}, bf16[256,2048]{1,0:T(8,128)(2,1)}, u32[]{:S(2)}, u32[]{:S(2)}) collective-permute-start(bf16[256,2048]{1,0:T(8,128)(2,1)} %shard_map.129), channel_id=1, source_target_pairs={{0,4},{2,6},{4,0},{6,2},{8,12},{10,14},{12,8},{14,10},{16,20},{18,... | collective-permute-start | bytes 3145736 | tf_op jit(solution)/shard_map/ppermute | solution.py:318
  128.1 24.3 %collective-permute-start.22 = (bf16[256,2048]{1,0:T(8,128)(2,1)S(1)}, bf16[256,2048]{1,0:T(8,128)(2,1)S(1)}, u32[]{:S(2)}, u32[]{:S(2)}) collective-permute-start(bf16[256,2048]{1,0:T(8,128)(2,1)S(1)} %add.167), channel_id=1, source_target_pairs={{0,8},{2,10},{4,12},{6,14},{24,16},{26,18},{28,20},{30,22},{1,9},{... | collective-permute-start | bytes 3145736 | tf_op jit(solution)/shard_map/ppermute | solution.py:357
  129.4 24.4 %collective-permute-start.24 = (bf16[256,2048]{1,0:T(8,128)(2,1)}, bf16[256,2048]{1,0:T(8,128)(2,1)}, u32[]{:S(2)}, u32[]{:S(2)}) collective-permute-start(bf16[256,2048]{1,0:T(8,128)(2,1)} %add.168), channel_id=1, source_target_pairs={{8,24},{10,26},{12,28},{14,30},{17,1},{19,3},{21,5},{23,7}} | collective-permute-start | bytes 3145736 | tf_op jit(solution)/shard_map/ppermute | solution.py:357
  131.1 24.0 %collective-permute-start.25 = (bf16[256,2048]{1,0:T(8,128)(2,1)}, bf16[256,2048]{1,0:T(8,128)(2,1)}, u32[]{:S(2)}, u32[]{:S(2)}) collective-permute-start(bf16[256,2048]{1,0:T(8,128)(2,1)} %add.166), channel_id=1, source_target_pairs={{16,0},{18,2},{20,4},{22,6},{9,25},{11,27},{13,29},{15,31}} | collective-permute-start | bytes 3145736 | tf_op jit(solution)/shard_map/ppermute | solution.py:357
  158.4 22.8 %collective-permute-start.26 = (bf16[256,2048]{1,0:T(8,128)(2,1)S(1)}, bf16[256,2048]{1,0:T(8,128)(2,1)S(1)}, u32[]{:S(2)}, u32[]{:S(2)}) collective-permute-start(bf16[256,2048]{1,0:T(8,128)(2,1)S(1)} %add.170), channel_id=1, source_target_pairs={{0,8},{2,10},{4,12},{6,14},{24,16},{26,18},{28,20},{30,22},{1,9},{... | collective-permute-start | bytes 3145736 | tf_op jit(solution)/shard_map/ppermute | solution.py:357
  159.7 21.9 %collective-permute-start.27 = (bf16[256,2048]{1,0:T(8,128)(2,1)}, bf16[256,2048]{1,0:T(8,128)(2,1)}, u32[]{:S(2)}, u32[]{:S(2)}) collective-permute-start(bf16[256,2048]{1,0:T(8,128)(2,1)} %add.169), channel_id=1, source_target_pairs={{16,8},{18,10},{20,12},{22,14},{9,17},{11,19},{13,21},{15,23}} | collective-permute-start | bytes 3145736 | tf_op jit(solution)/shard_map/ppermute | solution.py:357
  162.9 20.8 %collective-permute-start.28 = (bf16[4,160,512]{2,1,0:T(8,128)(2,1)}, bf16[4,160,512]{2,1,0:T(8,128)(2,1)}, u32[]{:S(2)}, u32[]{:S(2)}) collective-permute-start(bf16[4,160,512]{2,1,0:T(8,128)(2,1)} %bitcast.19.keep), channel_id=1, source_target_pairs={{0,4},{2,6},{4,0},{6,2},{8,12},{10,14},{12,8},{14,10},{16,20},{18,... | collective-permute-start | bytes 1966088 | tf_op jit(solution)/shard_map/ppermute | solution.py:318
  164.4 19.3 %collective-permute-start.29 = (bf16[4,160,512]{2,1,0:T(8,128)(2,1)}, bf16[4,160,512]{2,1,0:T(8,128)(2,1)}, u32[]{:S(2)}, u32[]{:S(2)}) collective-permute-start(bf16[4,160,512]{2,1,0:T(8,128)(2,1)} %bitcast.19.keep), channel_id=1, source_target_pairs={{0,2},{2,0},{4,6},{6,4},{8,10},{10,8},{12,14},{14,12},{16,18},{18,... | collective-permute-start | bytes 1966088 | tf_op jit(solution)/shard_map/ppermute | solution.py:315
  183.7 23.1 %collective-permute-start.32 = (bf16[256,2048]{1,0:T(8,128)(2,1)S(1)}, bf16[256,2048]{1,0:T(8,128)(2,1)}, u32[]{:S(2)}, u32[]{:S(2)}) collective-permute-start(bf16[256,2048]{1,0:T(8,128)(2,1)S(1)} %add.173), channel_id=1, source_target_pairs={{8,16},{10,18},{12,20},{14,22},{17,9},{19,11},{21,13},{23,15}} | collective-permute-start | bytes 3145736 | tf_op jit(solution)/shard_map/ppermute | solution.py:357
  185.0 2.4 %collective-permute-start.30 = (bf16[4,160,512]{2,1,0:T(8,128)(2,1)}, bf16[4,160,512]{2,1,0:T(8,128)(2,1)S(1)}, u32[]{:S(2)}, u32[]{:S(2)}) collective-permute-start(bf16[4,160,512]{2,1,0:T(8,128)(2,1)} %collective-permute-done.28.back), channel_id=1, source_target_pairs={{0,2},{2,0},{4,6},{6,4},{8,10},{10,8},{12,14},{14,12},{16,18},{18,... | collective-permute-start | bytes 1966088 | tf_op jit(solution)/shard_map/ppermute | solution.py:315
  199.7 5.7 %collective-permute-start.31 = (f32[4,1,512]{2,1,0:T(1,128)}, f32[4,1,512]{2,1,0:T(1,128)S(1)}, u32[]{:S(2)}, u32[]{:S(2)}) collective-permute-start(f32[4,1,512]{2,1,0:T(1,128)} %get-tuple-element.146), channel_id=1, source_target_pairs={{1,0},{0,1},{3,2},{2,3},{5,4},{4,5},{7,6},{6,7},{9,8},{8,9},{11,10... | collective-permute-start | bytes 24584 | tf_op jit(solution)/shard_map/ppermute | solution.py:321
  208.2 2.7 %collective-permute-start.33 = (bf16[256,2048]{1,0:T(8,128)(2,1)S(1)}, bf16[256,2048]{1,0:T(8,128)(2,1)S(1)}, u32[]{:S(2)}, u32[]{:S(2)}) collective-permute-start(bf16[256,2048]{1,0:T(8,128)(2,1)S(1)} %add_select_fusion.refs_0_), channel_id=1, source_target_pairs={{0,2},{2,0},{4,6},{6,4},{8,10},{10,8},{12,14},{14,12},{16,18},{18,... | collective-permute-start | bytes 3145736 | tf_op jit(solution)/shard_map/ppermute | solution.py:517
  (18 other events, 130.8 us)

commit v8 on v7

--- a/solution.py
+++ b/solution.py
@@ -22,25 +22,26 @@
 SMALL = pl.CostEstimate(flops=1, bytes_accessed=1, transcendentals=0)
 
 
-def pick_kernel(n_picks, which_ref, acts, cotan, ours, theirs):
-    is_act = which_ref[n_picks] == 0
+def pick_kernel(ids_ref, place_ref, acts, cotan, ours, theirs):
+    del ids_ref
+    is_act = place_ref[1] == 0
     ours[...] = jnp.where(is_act, acts[...], cotan[...])
     theirs[...] = jnp.where(is_act, cotan[...], acts[...])
 
 
-def pick(acts, cotan, block_ids, core):
+def pick(acts, cotan, block_ids, place):
     n_picks, width = block_ids.shape[0], acts.shape[1]
-    chosen = pl.BlockSpec((BLK, width), lambda i, which: (which[i], 0))
-    out = pl.BlockSpec((BLK, width), lambda i, which: (i, 0))
+    chosen = pl.BlockSpec((BLK, width), lambda i, ids, place: (ids[i], 0))
+    out = pl.BlockSpec((BLK, width), lambda i, ids, place: (i, 0))
     return pl.pallas_call(
-        functools.partial(pick_kernel, n_picks),
+        pick_kernel,
         grid_spec=pltpu.PrefetchScalarGridSpec(
-            num_scalar_prefetch=1, grid=(n_picks,), in_specs=[chosen] * 2, out_specs=[out] * 2
+            num_scalar_prefetch=2, grid=(n_picks,), in_specs=[chosen] * 2, out_specs=[out] * 2
         ),
         out_shape=[jax.ShapeDtypeStruct((n_picks * BLK, width), BF16)] * 2,
         compiler_params=pltpu.CompilerParams(vmem_limit_bytes=VMEM),
         cost_estimate=SMALL,
-    )(jnp.concatenate([block_ids, jnp.reshape(core, (1,))]).astype(jnp.int32), acts, cotan)
+    )(block_ids, place, acts, cotan)
 
 
 def pack_upper(full):
@@ -57,10 +58,10 @@
         total = total + lax.dot_general(
             rows, rows, (((0,), (0,)), ((), ())), preferred_element_type=F32
         )
-    scale = jnp.where(place_ref[0] == 0, scales[0], scales[1]).astype(F32)
+    scale = jnp.where(place_ref[1] == 0, scales[0], scales[1]).astype(F32)
     packed = pack_upper(total * scale)
     half = packed.shape[0] // 2
-    low = place_ref[1] == 0
+    low = place_ref[2] == 0
     keep[0] = jnp.where(low, packed[:half], packed[half:]).astype(BF16)
     away[0] = jnp.where(low, packed[half:], packed[:half]).astype(BF16)
 
@@ -145,17 +146,22 @@
 
 def tail_kernel(n_parts, place_ref, *refs):
     parts, (basis, outer, eig_in, eig_out) = refs[:n_parts], refs[n_parts : n_parts + 4]
-    out, whole = refs[-2:]
+    out, whole, flipped = refs[-3:]
     sharers = len(parts)
     rows = parts[0].shape[0]
-    me = place_ref[1]
+    me = place_ref[4]
     size = whole.shape[1]
     columns = pl.ds(pl.multiple_of(pl.program_id(0) * size, size), size)
     for step, part in enumerate(parts):
         spot = lax.rem(me - step + sharers, sharers)
         whole[pl.ds(pl.multiple_of(spot * rows, rows), rows), :] = part[:, columns]
     right = jnp.dot(whole[...], basis[0], preferred_element_type=F32).astype(BF16)
-    inner = lax.dot_general(outer[0], right, (((0,), (0,)), ((), ())), preferred_element_type=F32)
+
+    @pl.when(pl.program_id(0) == 0)
+    def _():
+        flipped[...] = outer[0].T
+
+    inner = jnp.dot(flipped[...], right, preferred_element_type=F32)
     column = jnp.broadcast_to(eig_out[0], (QUARTER, eig_out.shape[2])).T[:, :1]
     scaled = (inner / (column * eig_in[0] + DAMPING)).astype(BF16)
     mine = outer[0, pl.ds(pl.multiple_of(me * rows, rows), rows), :]
@@ -171,9 +177,9 @@
     each = cols // size
     in_specs = [pl.BlockSpec(memory_space=pltpu.VMEM)] * len(parts) + [
         pl.BlockSpec((1, size, size), lambda b, place: (chunk * each + b, 0, 0)),
-        pl.BlockSpec((1, size, size), lambda b, place: (place[0], 0, 0)),
+        pl.BlockSpec((1, size, size), lambda b, place: (place[3], 0, 0)),
         pl.BlockSpec((1, 1, size), lambda b, place: (chunk * each + b, 0, 0)),
-        pl.BlockSpec((1, 1, size), lambda b, place: (place[2], 0, 0)),
+        pl.BlockSpec((1, 1, size), lambda b, place: (place[5], 0, 0)),
     ]
     args = [place, *parts, basis_in, basis_out, eig_in, eig_out]
     aliases = {}
@@ -188,7 +194,7 @@
             grid=(each,),
             in_specs=in_specs,
             out_specs=pl.BlockSpec((rows, size), lambda b, place: (0, chunk * each + b)),
-            scratch_shapes=[pltpu.VMEM((size, size), BF16)],
+            scratch_shapes=[pltpu.VMEM((size, size), BF16)] * 2,
         ),
         out_shape=jax.ShapeDtypeStruct((rows, blocks * size), BF16),
         input_output_aliases=aliases,
@@ -217,18 +223,18 @@
         across[...] = flipped
 
 
-def turned(rows, which, n_rows):
+def turned(rows, place, first_piece, n_rows):
     tokens, _ = rows.shape
 
-    def out(place):
-        return pl.BlockSpec((n_rows, tokens), lambda i, which: (place(i), 0))
+    def out(spot):
+        return pl.BlockSpec((n_rows, tokens), lambda i, place: (spot(i), 0))
 
     return pl.pallas_call(
         turn_kernel,
         grid_spec=pltpu.PrefetchScalarGridSpec(
             num_scalar_prefetch=1,
             grid=(4,),
-            in_specs=[pl.BlockSpec((tokens, n_rows), lambda i, which: (0, which[i]))],
+            in_specs=[pl.BlockSpec((tokens, n_rows), lambda i, place: (0, place[first_piece + i]))],
             out_specs=[
                 out(lambda i: jnp.minimum(i, 1)),
                 out(lambda i: jnp.maximum(i - 2, 0)),
@@ -238,7 +244,7 @@
         out_shape=[jax.ShapeDtypeStruct((2 * n_rows, tokens), BF16)] * 3,
         compiler_params=pltpu.CompilerParams(vmem_limit_bytes=VMEM),
         cost_estimate=SMALL,
-    )(jnp.stack(which).astype(jnp.int32), rows)
+    )(place, rows)
 
 
 def product_kernel(counts, n_outs, *refs):
@@ -393,13 +399,17 @@
 
     my_start = d * rows_dev
     block = my_start // block_size
-    flags = jnp.stack([w * local_blocks, core, x]).astype(jnp.int32)
+    sharers = block_size // rows_dev
+    held = (block // local_blocks - w) % n_worker * local_blocks + block % local_blocks
+    scalars = [w * local_blocks, core, x, block, d % sharers, held]
+    first_piece = len(scalars)
+    scalars += [piece(j, at, flip) for j in range(z_per_worker) for at in range(2) for flip in range(2)]
+    flags = jnp.stack(scalars).astype(jnp.int32)
     env = {"acts": acts, "cotan": cotan}
     done = {}
 
     def turn(rows, j):
-        which = [piece(j, at, flip) for at in range(2) for flip in range(2)]
-        other, own, across = turned(rows, which, rows_dev)
+        other, own, across = turned(rows, flags, first_piece + 4 * j, rows_dev)
         return {("p", j, 0): other, ("p", j, 1): own, ("p", j): across}
 
     def gathered(part, bits, tie=lambda v: v):
@@ -415,11 +425,11 @@
             env = dict(zip(keys, lax.optimization_barrier(tuple(env[k] for k in keys))))
         joined = {}
         if stage == 0:
-            ours, theirs = pick(acts, cotan, block_ids, core)
+            ours, theirs = pick(acts, cotan, block_ids, flags)
             joined["acts_sib"] = swap_core(acts)
             env.update(turn(cotan, 0))
             scales = (1.0 / samples, tokens / samples)
-            keep, away = terms(flags[1:], ours, swap_core(theirs), block_size, scales)
+            keep, away = terms(flags, ours, swap_core(theirs), block_size, scales)
             away = swap_x(away)
             joined["c", 0] = swap_core(env.pop(("p", 0)))
         if stage == 1:
@@ -505,17 +515,14 @@
                 env["sum", n] = jnp.where(ends[w] == z, acc, env["sum", n]) if ("sum", n) in env else acc
 
     act_new, grad_new = done["factors"]
-    held = (block // local_blocks - w) % n_worker * local_blocks + block % local_blocks
-
-    sharers = block_size // rows_dev
-    spot = jnp.stack([block, d % sharers, held]).astype(jnp.int32)
+
     precond = None
     for n in range(len(starts)):
         parts = [env["sum", n]]
         for step in range(1, sharers):
             pairs = [(i, i // sharers * sharers + (i + step) % sharers) for i in range(n_dp)]
             parts.append(lax.ppermute(parts[0], "dp", pairs))
-        precond = tail(spot, parts, basis_in, basis_out, eig_in, eig_out, n, precond)
+        precond = tail(flags, parts, basis_in, basis_out, eig_in, eig_out, n, precond)
     return precond, act_new, grad_new
 
 

time: 223 us -> 220 us (0.987)
  other arithmetic: 21 us -> 15.8 us
  waiting for transfers between devices: 60.4 us -> 62.9 us
    another operation x4 -> x0, other arithmetic: 2.75 us -> none  [the longest x2 1.3 us: per_device(): flags = jnp.stack([w * local_blocks, core, x]).astype(jnp.int32)]
  transfers between devices with their start and end apart: 34 -> 34, of which waited for: 16 -> 17; matrix products, arithmetic and copies ran while one was open for 9% -> 8% of each run, Pallas kernels for 34% -> 35%
where the time goes in v8:
time: 220 us; the launch traced here: 218 us
  Pallas kernels  84.1 us (38%)
  waiting for transfers between devices  62.9 us (29%)
  starting transfers between devices  41.3 us (19%)
  other arithmetic  15.8 us (7%)
  local copies, waits for them, and re-layouts  10.4 us (5%)
  between operations  3.04 us (1%)
    pallas_call x6, Pallas kernels, products(): pl.pallas_call(functools.partial(product_kernel, [len(half) for half in h...  44.7 us
    ppermute x8, waiting for transfers between devices, hop(): return lax.ppermute(v, both, pairs)  28.5 us
    ppermute x8, starting transfers between devices, hop(): return lax.ppermute(v, both, pairs)  19.1 us
    ppermute x6, waiting for transfers between devices, swap_x(): return lax.ppermute(v, 'dp', [(i, i ^ 2) for i in range(n_dp)])  17.5 us
    pallas_call x1, Pallas kernels, update_factors(): pl.pallas_call(factor_kernel, grid_spec=pltpu.PrefetchScalarGridSpec(num_...  11.5 us
    pallas_call x2, Pallas kernels, turned(): pl.pallas_call(turn_kernel, grid_spec=pltpu.PrefetchScalarGridSpec(num_sc...  10.5 us
    pallas_call x1, Pallas kernels, tail(): pl.pallas_call(functools.partial(tail_kernel, len(parts)), grid_spec=pltp...  8.8 us
    ppermute x6, starting transfers between devices, swap_x(): return lax.ppermute(v, 'dp', [(i, i ^ 2) for i in range(n_dp)])  7.99 us
  transfers between devices with their start and end apart: 34, of which 17 were waited for; matrix products, arithmetic and copies ran while one was open for 8% of the time, Pallas kernels for 35%

profile of v8, /device:TPU:12, one launch (start us, length us, event | category | flops | bytes accessed | tf_op | source)
XLA Modules:
  0.0 217.6 jit_solution(5067694133491093068)
XLA Ops:
  1.4 3.4 %shard_map.123 = (bf16[256,2048]{1,0:T(8,128)(2,1)}, bf16[256,2048]{1,0:T(8,128)(2,1)}) custom-call(s32[2]{0:T(128)} %ids_ref.1, s32[14]{0:T(128)} %stack.56.which_ref.place_ref, bf16[1024,2048]{1,0:T(8,128)(2,1)} %refs_2_.5, bf16[1024,2048]{1,0:T(8,128)(2,1)} %block.2), custom_call_target="tpu_custom_call" | custom-call | flops 1 | bytes 1 | tf_op jit(solution)/shard_map/pallas_call | solution.py:36
  5.1 5.2 %shard_map.121 = (bf16[512,1024]{1,0:T(8,128)(2,1)}, bf16[512,1024]{1,0:T(8,128)(2,1)}, bf16[512,1024]{1,0:T(8,128)(2,1)}) custom-call(s32[14]{0:T(128)} %stack.56.which_ref.place_ref, bf16[1024,2048]{1,0:T(8,128)(2,1)} %block.2), custom_call_target="tpu_custom_call" | custom-call | flops 1 | bytes 1 | tf_op jit(solution)/shard_map/pallas_call | solution.py:232
  12.0 5.2 %shard_map.124 = (bf16[4,160,512]{2,1,0:T(8,128)(2,1)}, bf16[4,160,512]{2,1,0:T(8,128)(2,1)}) custom-call(s32[14]{0:T(128)} %stack.56.which_ref.place_ref, bf16[256,2048]{1,0:T(8,128)(2,1)} %get-tuple-element.82.ours, bf16[256,2048]{1,0:T(8,128)(2,1)} %copy-done.4), custom_call_target="tpu_custom_call" | custom-call | flops 1 | bytes 1 | tf_op jit(solution)/shard_map/pallas_call | solution.py:74
  19.7 9.0 %shard_map.122 = (bf16[256,2048]{1,0:T(8,128)(2,1)}, bf16[256,2048]{1,0:T(8,128)(2,1)}) custom-call(bf16[512,1024]{1,0:T(8,128)(2,1)} %get-tuple-element.79.refs_0_, bf16[512,1024]{1,0:T(8,128)(2,1)} %get-tuple-element.95.refs_1_, bf16[512,1024]{1,0:T(8,128)(2,1)} %copy-done.9, bf16[1024,2048]{1,0:T(8,128)(2,1)} %refs_2_.5, ...), custom_call_target="tpu_custom_call" | custom-call | flops 8589934592 | bytes 8388608 | tf_op jit(solution)/shard_map/pallas_call | solution.py:284
  28.7 5.5 %collective-permute-done.4 = bf16[4,160,512]{2,1,0:T(8,128)(2,1)S(1)} collective-permute-done((bf16[4,160,512]{2,1,0:T(8,128)(2,1)}, bf16[4,160,512]{2,1,0:T(8,128)(2,1)S(1)}, u32[]{:S(2)}, u32[]{:S(2)}) %collective-permute-start.4) | collective-permute-done | bytes 655392 | tf_op jit(solution)/shard_map/ppermute | solution.py:324
  34.3 1.9 collective-permute-done.3.refs_0_
  39.2 6.3 %collective-permute-done.8 = bf16[320,512]{1,0:T(8,128)(2,1)S(1)} collective-permute-done((bf16[320,512]{1,0:T(8,128)(2,1)S(1)}, bf16[320,512]{1,0:T(8,128)(2,1)S(1)}, u32[]{:S(2)}, u32[]{:S(2)}) %collective-permute-start.8) | collective-permute-done | bytes 327712 | tf_op jit(solution)/shard_map/ppermute | solution.py:359
  45.5 2.7 %collective-permute-start.9 = (bf16[160,512]{1,0:T(8,128)(2,1)S(1)}, bf16[160,512]{1,0:T(8,128)(2,1)S(1)}, u32[]{:S(2)}, u32[]{:S(2)}) collective-permute-start(bf16[160,512]{1,0:T(8,128)(2,1)S(1)} %dynamic-slice_bitcast_fusion.1), channel_id=1, source_target_pairs={{0,16},{2,18},{4,20},{6,22},{8,24},{10,26},{12,28},{14,30},{16,0},... | collective-permute-start | bytes 491528 | tf_op jit(solution)/shard_map/ppermute | solution.py:359
  48.2 5.3 %shard_map.126 = (bf16[512,1024]{1,0:T(8,128)(2,1)}, bf16[512,1024]{1,0:T(8,128)(2,1)}, bf16[512,1024]{1,0:T(8,128)(2,1)}) custom-call(s32[14]{0:T(128)} %stack.56.which_ref.place_ref, bf16[1024,2048]{1,0:T(8,128)(2,1)} %block.2), custom_call_target="tpu_custom_call" | custom-call | flops 1 | bytes 1 | tf_op jit(solution)/shard_map/pallas_call | solution.py:232
  54.0 3.4 %collective-permute-start.10 = (bf16[160,512]{1,0:T(8,128)(2,1)S(1)}, bf16[160,512]{1,0:T(8,128)(2,1)S(1)}, u32[]{:S(2)}, u32[]{:S(2)}) collective-permute-start(bf16[160,512]{1,0:T(8,128)(2,1)S(1)} %bitcast_add_fusion.1), channel_id=1, source_target_pairs={{0,16},{2,18},{4,20},{6,22},{8,24},{10,26},{12,28},{14,30},{16,0},... | collective-permute-start | bytes 491528 | tf_op jit(solution)/shard_map/ppermute | solution.py:359
  58.2 6.7 %shard_map.125 = bf16[256,2048]{1,0:T(8,128)(2,1)} custom-call(bf16[512,1024]{1,0:T(8,128)(2,1)} %copy-done.7, bf16[256,1024]{1,0:T(8,128)(2,1)} %copy-done.11, bf16[1024,2048]{1,0:T(8,128)(2,1)} %refs_2_.5, bf16[1024,2048]{1,0:T(8,128)(2,1)} %collective-permute-done.1.refs_4_.refs_3_), custom_call_target="tpu_custom_call" | custom-call | flops 4294967296 | bytes 8388608 | tf_op jit(solution)/shard_map/pallas_call | solution.py:284
  69.1 6.7 %shard_map.127 = bf16[256,2048]{1,0:T(8,128)(2,1)} custom-call(bf16[512,1024]{1,0:T(8,128)(2,1)} %collective-permute-done.7.refs_0_, bf16[256,1024]{1,0:T(8,128)(2,1)} %collective-permute-done.11.refs_1_, bf16[1024,2048]{1,0:T(8,128)(2,1)} %refs_2_.5, bf16[1024,2048]{1,0:T(8,128)(2,1)} %collective-permute-done.1.refs_4_.refs_3_), custom_call_target="tpu_custom_call" | custom-call | flops 4294967296 | bytes 8388608 | tf_op jit(solution)/shard_map/pallas_call | solution.py:284
  75.8 9.0 %shard_map.128 = (bf16[256,2048]{1,0:T(8,128)(2,1)}, bf16[256,2048]{1,0:T(8,128)(2,1)}) custom-call(bf16[512,1024]{1,0:T(8,128)(2,1)} %get-tuple-element.105.refs_0_, bf16[512,1024]{1,0:T(8,128)(2,1)} %get-tuple-element.124.refs_1_, bf16[512,1024]{1,0:T(8,128)(2,1)} %collective-permute-done.12.refs_2_, bf16[1024,2048]{1,0:T(8,128)(2,1)} %refs_2_.5, ...), custom_call_target="tpu_custom_call" | custom-call | flops 8589934592 | bytes 8388608 | tf_op jit(solution)/shard_map/pallas_call | solution.py:284
  84.8 7.7 %collective-permute-done.13 = bf16[256,2048]{1,0:T(8,128)(2,1)S(1)} collective-permute-done((bf16[256,2048]{1,0:T(8,128)(2,1)}, bf16[256,2048]{1,0:T(8,128)(2,1)S(1)}, u32[]{:S(2)}, u32[]{:S(2)}) %collective-permute-start.13) | collective-permute-done | bytes 1048608 | tf_op jit(solution)/shard_map/ppermute | solution.py:324
  94.1 3.6 %collective-permute-start.19 = (bf16[256,2048]{1,0:T(8,128)(2,1)S(1)}, bf16[256,2048]{1,0:T(8,128)(2,1)S(1)}, u32[]{:S(2)}, u32[]{:S(2)}) collective-permute-start(bf16[256,2048]{1,0:T(8,128)(2,1)S(1)} %add.165), channel_id=1, source_target_pairs={{0,8},{2,10},{4,12},{6,14},{16,24},{18,26},{20,28},{22,30},{9,1},{... | collective-permute-start | bytes 3145736 | tf_op jit(solution)/shard_map/ppermute | solution.py:363
  102.3 2.0 collective-permute-done.16.refs_1_
  104.3 6.7 %shard_map.129 = bf16[256,2048]{1,0:T(8,128)(2,1)} custom-call(bf16[512,1024]{1,0:T(8,128)(2,1)} %copy-done.8, bf16[256,1024]{1,0:T(8,128)(2,1)} %collective-permute-done.16.refs_1_, bf16[1024,2048]{1,0:T(8,128)(2,1)} %refs_2_.5, bf16[1024,2048]{1,0:T(8,128)(2,1)} %collective-permute-done.1.refs_4_.refs_3_), custom_call_target="tpu_custom_call" | custom-call | flops 4294967296 | bytes 8388608 | tf_op jit(solution)/shard_map/pallas_call | solution.py:284
  111.1 8.1 %collective-permute-done.19 = bf16[256,2048]{1,0:T(8,128)(2,1)S(1)} collective-permute-done((bf16[256,2048]{1,0:T(8,128)(2,1)S(1)}, bf16[256,2048]{1,0:T(8,128)(2,1)S(1)}, u32[]{:S(2)}, u32[]{:S(2)}) %collective-permute-start.19) | collective-permute-done | bytes 1048608 | tf_op jit(solution)/shard_map/ppermute | solution.py:363
  122.1 2.5 %collective-permute-done.17 = bf16[256,2048]{1,0:T(8,128)(2,1)S(1)} collective-permute-done((bf16[256,2048]{1,0:T(8,128)(2,1)S(1)}, bf16[256,2048]{1,0:T(8,128)(2,1)S(1)}, u32[]{:S(2)}, u32[]{:S(2)}) %collective-permute-start.17) | collective-permute-done | bytes 1048608 | tf_op jit(solution)/shard_map/ppermute | solution.py:363
  129.5 5.8 %collective-permute-start.25 = (bf16[256,2048]{1,0:T(8,128)(2,1)}, bf16[256,2048]{1,0:T(8,128)(2,1)}, u32[]{:S(2)}, u32[]{:S(2)}) collective-permute-start(bf16[256,2048]{1,0:T(8,128)(2,1)} %add.166), channel_id=1, source_target_pairs={{16,0},{18,2},{20,4},{22,6},{9,25},{11,27},{13,29},{15,31}} | collective-permute-start | bytes 3145736 | tf_op jit(solution)/shard_map/ppermute | solution.py:363
  139.2 6.7 %shard_map.130 = bf16[256,2048]{1,0:T(8,128)(2,1)} custom-call(bf16[512,1024]{1,0:T(8,128)(2,1)} %collective-permute-done.20.refs_0_, bf16[256,1024]{1,0:T(8,128)(2,1)} %copy-done.12, bf16[1024,2048]{1,0:T(8,128)(2,1)} %refs_2_.5, bf16[1024,2048]{1,0:T(8,128)(2,1)} %collective-permute-done.1.refs_4_.refs_3_), custom_call_target="tpu_custom_call" | custom-call | flops 4294967296 | bytes 8388608 | tf_op jit(solution)/shard_map/pallas_call | solution.py:284
  145.8 3.1 %collective-permute-done.23 = bf16[256,2048]{1,0:T(8,128)(2,1)} collective-permute-done((bf16[256,2048]{1,0:T(8,128)(2,1)}, bf16[256,2048]{1,0:T(8,128)(2,1)}, u32[]{:S(2)}, u32[]{:S(2)}) %collective-permute-start.23) | collective-permute-done | bytes 1048608 | tf_op jit(solution)/shard_map/ppermute | solution.py:324
  148.9 1.9 add.170
  153.8 3.3 %add_select_fusion.2 = bf16[256,2048]{1,0:T(8,128)(2,1)} fusion(bf16[256,2048]{1,0:T(8,128)(2,1)} %add.166, bf16[256,2048]{1,0:T(8,128)(2,1)} %collective-permute-done.25, bf16[256,2048]{1,0:T(8,128)(2,1)} %add.168, bf16[256,2048]{1,0:T(8,128)(2,1)} %collective-permute-done.24, pred[]{:T(512)S(6)} %eq.28), kind=kLoop, calls=%fused_computation.2 | loop fusion | flops 1572864 | bytes 5242881 | tf_op jit(solution)/shard_map/jit(_where)/select_n | solution.py:515
  158.4 2.9 %collective-permute-start.27 = (bf16[256,2048]{1,0:T(8,128)(2,1)}, bf16[256,2048]{1,0:T(8,128)(2,1)}, u32[]{:S(2)}, u32[]{:S(2)}) collective-permute-start(bf16[256,2048]{1,0:T(8,128)(2,1)} %add.169), channel_id=1, source_target_pairs={{16,8},{18,10},{20,12},{22,14},{9,17},{11,19},{13,21},{15,23}} | collective-permute-start | bytes 3145736 | tf_op jit(solution)/shard_map/ppermute | solution.py:363
  164.0 15.7 %collective-permute-done.26 = bf16[256,2048]{1,0:T(8,128)(2,1)S(1)} collective-permute-done((bf16[256,2048]{1,0:T(8,128)(2,1)S(1)}, bf16[256,2048]{1,0:T(8,128)(2,1)S(1)}, u32[]{:S(2)}, u32[]{:S(2)}) %collective-permute-start.26) | collective-permute-done | bytes 1048608 | tf_op jit(solution)/shard_map/ppermute | solution.py:363
  180.2 2.0 add_select_fusion.1
  183.6 2.3 %collective-permute-done.30.back_sib = bf16[4,160,512]{2,1,0:T(8,128)(2,1)S(1)} collective-permute-done((bf16[4,160,512]{2,1,0:T(8,128)(2,1)}, bf16[4,160,512]{2,1,0:T(8,128)(2,1)S(1)}, u32[]{:S(2)}, u32[]{:S(2)}) %collective-permute-start.30) | collective-permute-done | bytes 655392 | tf_op jit(solution)/shard_map/ppermute | solution.py:321
  186.7 11.5 %shard_map.131 = (f32[4,512,512]{2,1,0:T(8,128)}, f32[4,512,512]{2,1,0:T(8,128)}, f32[4,1,512]{2,1,0:T(1,128)}, f32[4,1,512]{2,1,0:T(1,128)}) custom-call(s32[14]{0:T(128)} %stack.56.which_ref.place_ref, bf16[4,160,512]{2,1,0:T(8,128)(2,1)} %bitcast.20.keep, bf16[4,160,512]{2,1,0:T(8,128)(2,1)} %collective-permute-done.28.back, ...), custom_call_target="tpu_custom_call" | custom-call | flops 1 | bytes 1 | tf_op jit(solution)/shard_map/pallas_call | solution.py:130
  198.3 2.9 %collective-permute-start.31 = (f32[4,1,512]{2,1,0:T(1,128)}, f32[4,1,512]{2,1,0:T(1,128)S(1)}, u32[]{:S(2)}, u32[]{:S(2)}) collective-permute-start(f32[4,1,512]{2,1,0:T(1,128)} %get-tuple-element.146), channel_id=1, source_target_pairs={{1,0},{0,1},{3,2},{2,3},{5,4},{4,5},{7,6},{6,7},{9,8},{8,9},{11,10... | collective-permute-start | bytes 24584 | tf_op jit(solution)/shard_map/ppermute | solution.py:327
  205.1 2.6 %collective-permute-done.33.refs_1_ = bf16[256,2048]{1,0:T(8,128)(2,1)S(1)} collective-permute-done((bf16[256,2048]{1,0:T(8,128)(2,1)S(1)}, bf16[256,2048]{1,0:T(8,128)(2,1)S(1)}, u32[]{:S(2)}, u32[]{:S(2)}) %collective-permute-start.33) | collective-permute-done | bytes 1048608 | tf_op jit(solution)/shard_map/ppermute | solution.py:524
  208.8 8.8 %shard_map.132 = bf16[256,2048]{1,0:T(8,128)(2,1)} custom-call(s32[14]{0:T(128)} %stack.56.which_ref.place_ref, bf16[256,2048]{1,0:T(8,128)(2,1)} %copy-done.3, bf16[256,2048]{1,0:T(8,128)(2,1)} %copy-done.10, bf16[4,512,512]{2,1,0:T(8,128)(2,1)} %refs_2_.7, bf16[8,512,512]{2,1,0:T(8,128)(2,1)} %refs_3_.6, f32[4,1,512]{2,1,0:T(1,128)} %get-tuple-element.149.refs_4_, ...), custom_call_target="tpu_custom_call" | custom-call | flops 3221225472 | bytes 4194304 | tf_op jit(solution)/shard_map/pallas_call | solution.py:190
  (107 shorter events, 44.2 us)
Async XLA Ops:
  0.6 18.1 %collective-permute-start.1 = (bf16[1024,2048]{1,0:T(8,128)(2,1)}, bf16[1024,2048]{1,0:T(8,128)(2,1)}, u32[]{:S(2)}, u32[]{:S(2)}) collective-permute-start(bf16[1024,2048]{1,0:T(8,128)(2,1)} %refs_2_.5), channel_id=1, source_target_pairs={{0,2},{2,0},{4,6},{6,4},{8,10},{10,8},{12,14},{14,12},{16,18},{18,... | collective-permute-start | bytes 12582920 | tf_op jit(solution)/shard_map/ppermute | solution.py:321
  4.8 6.3 %collective-permute-start.2 = (bf16[256,2048]{1,0:T(8,128)(2,1)}, bf16[256,2048]{1,0:T(8,128)(2,1)S(1)}, u32[]{:S(2)}, u32[]{:S(2)}) collective-permute-start(bf16[256,2048]{1,0:T(8,128)(2,1)} %get-tuple-element.83), channel_id=1, source_target_pairs={{0,2},{2,0},{4,6},{6,4},{8,10},{10,8},{12,14},{14,12},{16,18},{18,... | collective-permute-start | bytes 3145736 | tf_op jit(solution)/shard_map/ppermute | solution.py:321
  10.4 8.3 %collective-permute-start = (bf16[512,1024]{1,0:T(8,128)(2,1)}, bf16[512,1024]{1,0:T(8,128)(2,1)S(1)}, u32[]{:S(2)}, u32[]{:S(2)}) collective-permute-start(bf16[512,1024]{1,0:T(8,128)(2,1)} %get-tuple-element.78), channel_id=1, source_target_pairs={{0,2},{2,0},{4,6},{6,4},{8,10},{10,8},{12,14},{14,12},{16,18},{18,... | collective-permute-start | bytes 3145736 | tf_op jit(solution)/shard_map/ppermute | solution.py:321
  10.5 25.7 %collective-permute-start.3 = (bf16[512,1024]{1,0:T(8,128)(2,1)}, bf16[512,1024]{1,0:T(8,128)(2,1)S(1)}, u32[]{:S(2)}, u32[]{:S(2)}) collective-permute-start(bf16[512,1024]{1,0:T(8,128)(2,1)} %get-tuple-element.79.refs_0_), channel_id=1, source_target_pairs={{1,0},{0,1},{3,2},{2,3},{5,4},{4,5},{7,6},{6,7},{9,8},{8,9},{11,10... | collective-permute-start | bytes 3145736 | tf_op jit(solution)/shard_map/ppermute | solution.py:327
  17.2 16.9 %collective-permute-start.4 = (bf16[4,160,512]{2,1,0:T(8,128)(2,1)}, bf16[4,160,512]{2,1,0:T(8,128)(2,1)S(1)}, u32[]{:S(2)}, u32[]{:S(2)}) collective-permute-start(bf16[4,160,512]{2,1,0:T(8,128)(2,1)} %get-tuple-element.88), channel_id=1, source_target_pairs={{0,4},{2,6},{4,0},{6,2},{8,12},{10,14},{12,8},{14,10},{16,20},{18,... | collective-permute-start | bytes 1966088 | tf_op jit(solution)/shard_map/ppermute | solution.py:324
  36.2 9.2 %collective-permute-start.8 = (bf16[320,512]{1,0:T(8,128)(2,1)S(1)}, bf16[320,512]{1,0:T(8,128)(2,1)S(1)}, u32[]{:S(2)}, u32[]{:S(2)}) collective-permute-start(bf16[320,512]{1,0:T(8,128)(2,1)S(1)} %dynamic-slice_bitcast_fusion), channel_id=1, source_target_pairs={{0,8},{2,10},{4,12},{6,14},{8,0},{10,2},{12,4},{14,6},{16,24},{18,... | collective-permute-start | bytes 983048 | tf_op jit(solution)/shard_map/ppermute | solution.py:359
  37.1 20.3 %collective-permute-start.5 = (bf16[256,1024]{1,0:T(8,128)(2,1)S(1)}, bf16[256,1024]{1,0:T(8,128)(2,1)S(1)}, u32[]{:S(2)}, u32[]{:S(2)}) collective-permute-start(bf16[256,1024]{1,0:T(8,128)(2,1)S(1)} %slice.12), channel_id=1, source_target_pairs={{0,2},{2,0},{4,6},{6,4},{8,10},{10,8},{12,14},{14,12},{16,18},{18,... | collective-permute-start | bytes 1572872 | tf_op jit(solution)/shard_map/ppermute | solution.py:321
  37.2 27.8 %collective-permute-start.6 = (bf16[256,2048]{1,0:T(8,128)(2,1)}, bf16[256,2048]{1,0:T(8,128)(2,1)S(1)}, u32[]{:S(2)}, u32[]{:S(2)}) collective-permute-start(bf16[256,2048]{1,0:T(8,128)(2,1)} %get-tuple-element.94), channel_id=1, source_target_pairs={{0,4},{2,6},{4,0},{6,2},{8,12},{10,14},{12,8},{14,10},{16,20},{18,... | collective-permute-start | bytes 3145736 | tf_op jit(solution)/shard_map/ppermute | solution.py:324
  38.6 26.8 %collective-permute-start.7 = (bf16[512,1024]{1,0:T(8,128)(2,1)}, bf16[512,1024]{1,0:T(8,128)(2,1)}, u32[]{:S(2)}, u32[]{:S(2)}) collective-permute-start(bf16[512,1024]{1,0:T(8,128)(2,1)} %get-tuple-element.95.refs_1_), channel_id=1, source_target_pairs={{1,0},{0,1},{3,2},{2,3},{5,4},{4,5},{7,6},{6,7},{9,8},{8,9},{11,10... | collective-permute-start | bytes 3145736 | tf_op jit(solution)/shard_map/ppermute | solution.py:327
  45.5 8.4 %collective-permute-start.9 = (bf16[160,512]{1,0:T(8,128)(2,1)S(1)}, bf16[160,512]{1,0:T(8,128)(2,1)S(1)}, u32[]{:S(2)}, u32[]{:S(2)}) collective-permute-start(bf16[160,512]{1,0:T(8,128)(2,1)S(1)} %dynamic-slice_bitcast_fusion.1), channel_id=1, source_target_pairs={{0,16},{2,18},{4,20},{6,22},{8,24},{10,26},{12,28},{14,30},{16,0},... | collective-permute-start | bytes 491528 | tf_op jit(solution)/shard_map/ppermute | solution.py:359
  54.0 10.9 %collective-permute-start.10 = (bf16[160,512]{1,0:T(8,128)(2,1)S(1)}, bf16[160,512]{1,0:T(8,128)(2,1)S(1)}, u32[]{:S(2)}, u32[]{:S(2)}) collective-permute-start(bf16[160,512]{1,0:T(8,128)(2,1)S(1)} %bitcast_add_fusion.1), channel_id=1, source_target_pairs={{0,16},{2,18},{4,20},{6,22},{8,24},{10,26},{12,28},{14,30},{16,0},... | collective-permute-start | bytes 491528 | tf_op jit(solution)/shard_map/ppermute | solution.py:359
  65.4 10.4 %collective-permute-start.12 = (bf16[512,1024]{1,0:T(8,128)(2,1)}, bf16[512,1024]{1,0:T(8,128)(2,1)}, u32[]{:S(2)}, u32[]{:S(2)}) collective-permute-start(bf16[512,1024]{1,0:T(8,128)(2,1)} %get-tuple-element.107), channel_id=1, source_target_pairs={{0,2},{2,0},{4,6},{6,4},{8,10},{10,8},{12,14},{14,12},{16,18},{18,... | collective-permute-start | bytes 3145736 | tf_op jit(solution)/shard_map/ppermute | solution.py:321
  66.6 2.6 %collective-permute-start.11 = (bf16[256,1024]{1,0:T(8,128)(2,1)S(1)}, bf16[256,1024]{1,0:T(8,128)(2,1)}, u32[]{:S(2)}, u32[]{:S(2)}) collective-permute-start(bf16[256,1024]{1,0:T(8,128)(2,1)S(1)} %slice.13), channel_id=1, source_target_pairs={{0,2},{2,0},{4,6},{6,4},{8,10},{10,8},{12,14},{14,12},{16,18},{18,... | collective-permute-start | bytes 1572872 | tf_op jit(solution)/shard_map/ppermute | solution.py:321
  67.1 17.7 %collective-permute-start.15 = (bf16[320,512]{1,0:T(8,128)(2,1)S(1)}, bf16[320,512]{1,0:T(8,128)(2,1)S(1)}, u32[]{:S(2)}, u32[]{:S(2)}) collective-permute-start(bf16[320,512]{1,0:T(8,128)(2,1)S(1)} %maximum_select_fusion.1), channel_id=1, source_target_pairs={{0,8},{2,10},{4,12},{6,14},{8,0},{10,2},{12,4},{14,6},{16,24},{18,... | collective-permute-start | bytes 983048 | tf_op jit(solution)/shard_map/ppermute | solution.py:359
  67.2 25.4 %collective-permute-start.13 = (bf16[256,2048]{1,0:T(8,128)(2,1)}, bf16[256,2048]{1,0:T(8,128)(2,1)S(1)}, u32[]{:S(2)}, u32[]{:S(2)}) collective-permute-start(bf16[256,2048]{1,0:T(8,128)(2,1)} %shard_map.125), channel_id=1, source_target_pairs={{0,4},{2,6},{4,0},{6,2},{8,12},{10,14},{12,8},{14,10},{16,20},{18,... | collective-permute-start | bytes 3145736 | tf_op jit(solution)/shard_map/ppermute | solution.py:324
  68.6 25.5 %collective-permute-start.14 = (bf16[512,1024]{1,0:T(8,128)(2,1)}, bf16[512,1024]{1,0:T(8,128)(2,1)S(1)}, u32[]{:S(2)}, u32[]{:S(2)}) collective-permute-start(bf16[512,1024]{1,0:T(8,128)(2,1)} %get-tuple-element.105.refs_0_), channel_id=1, source_target_pairs={{1,0},{0,1},{3,2},{2,3},{5,4},{4,5},{7,6},{6,7},{9,8},{8,9},{11,10... | collective-permute-start | bytes 3145736 | tf_op jit(solution)/shard_map/ppermute | solution.py:327
  94.1 25.1 %collective-permute-start.19 = (bf16[256,2048]{1,0:T(8,128)(2,1)S(1)}, bf16[256,2048]{1,0:T(8,128)(2,1)S(1)}, u32[]{:S(2)}, u32[]{:S(2)}) collective-permute-start(bf16[256,2048]{1,0:T(8,128)(2,1)S(1)} %add.165), channel_id=1, source_target_pairs={{0,8},{2,10},{4,12},{6,14},{16,24},{18,26},{20,28},{22,30},{9,1},{... | collective-permute-start | bytes 3145736 | tf_op jit(solution)/shard_map/ppermute | solution.py:363
  97.7 24.0 %collective-permute-start.18 = (bf16[256,2048]{1,0:T(8,128)(2,1)}, bf16[256,2048]{1,0:T(8,128)(2,1)S(1)}, u32[]{:S(2)}, u32[]{:S(2)}) collective-permute-start(bf16[256,2048]{1,0:T(8,128)(2,1)} %get-tuple-element.121), channel_id=1, source_target_pairs={{0,4},{2,6},{4,0},{6,2},{8,12},{10,14},{12,8},{14,10},{16,20},{18,... | collective-permute-start | bytes 3145736 | tf_op jit(solution)/shard_map/ppermute | solution.py:324
  99.3 25.3 %collective-permute-start.17 = (bf16[256,2048]{1,0:T(8,128)(2,1)S(1)}, bf16[256,2048]{1,0:T(8,128)(2,1)S(1)}, u32[]{:S(2)}, u32[]{:S(2)}) collective-permute-start(bf16[256,2048]{1,0:T(8,128)(2,1)S(1)} %add.156), channel_id=1, source_target_pairs={{8,0},{10,2},{12,4},{14,6},{24,16},{26,18},{28,20},{30,22},{1,9},{... | collective-permute-start | bytes 3145736 | tf_op jit(solution)/shard_map/ppermute | solution.py:363
  100.6 25.4 %collective-permute-start.20 = (bf16[512,1024]{1,0:T(8,128)(2,1)}, bf16[512,1024]{1,0:T(8,128)(2,1)}, u32[]{:S(2)}, u32[]{:S(2)}) collective-permute-start(bf16[512,1024]{1,0:T(8,128)(2,1)} %get-tuple-element.124.refs_1_), channel_id=1, source_target_pairs={{1,0},{0,1},{3,2},{2,3},{5,4},{4,5},{7,6},{6,7},{9,8},{8,9},{11,10... | collective-permute-start | bytes 3145736 | tf_op jit(solution)/shard_map/ppermute | solution.py:327
  126.0 22.9 %collective-permute-start.23 = (bf16[256,2048]{1,0:T(8,128)(2,1)}, bf16[256,2048]{1,0:T(8,128)(2,1)}, u32[]{:S(2)}, u32[]{:S(2)}) collective-permute-start(bf16[256,2048]{1,0:T(8,128)(2,1)} %shard_map.129), channel_id=1, source_target_pairs={{0,4},{2,6},{4,0},{6,2},{8,12},{10,14},{12,8},{14,10},{16,20},{18,... | collective-permute-start | bytes 3145736 | tf_op jit(solution)/shard_map/ppermute | solution.py:324
  126.5 24.3 %collective-permute-start.22 = (bf16[256,2048]{1,0:T(8,128)(2,1)S(1)}, bf16[256,2048]{1,0:T(8,128)(2,1)S(1)}, u32[]{:S(2)}, u32[]{:S(2)}) collective-permute-start(bf16[256,2048]{1,0:T(8,128)(2,1)S(1)} %add.167), channel_id=1, source_target_pairs={{0,8},{2,10},{4,12},{6,14},{24,16},{26,18},{28,20},{30,22},{1,9},{... | collective-permute-start | bytes 3145736 | tf_op jit(solution)/shard_map/ppermute | solution.py:363
  127.8 24.4 %collective-permute-start.24 = (bf16[256,2048]{1,0:T(8,128)(2,1)}, bf16[256,2048]{1,0:T(8,128)(2,1)}, u32[]{:S(2)}, u32[]{:S(2)}) collective-permute-start(bf16[256,2048]{1,0:T(8,128)(2,1)} %add.168), channel_id=1, source_target_pairs={{8,24},{10,26},{12,28},{14,30},{17,1},{19,3},{21,5},{23,7}} | collective-permute-start | bytes 3145736 | tf_op jit(solution)/shard_map/ppermute | solution.py:363
  129.5 24.3 %collective-permute-start.25 = (bf16[256,2048]{1,0:T(8,128)(2,1)}, bf16[256,2048]{1,0:T(8,128)(2,1)}, u32[]{:S(2)}, u32[]{:S(2)}) collective-permute-start(bf16[256,2048]{1,0:T(8,128)(2,1)} %add.166), channel_id=1, source_target_pairs={{16,0},{18,2},{20,4},{22,6},{9,25},{11,27},{13,29},{15,31}} | collective-permute-start | bytes 3145736 | tf_op jit(solution)/shard_map/ppermute | solution.py:363
  157.1 22.6 %collective-permute-start.26 = (bf16[256,2048]{1,0:T(8,128)(2,1)S(1)}, bf16[256,2048]{1,0:T(8,128)(2,1)S(1)}, u32[]{:S(2)}, u32[]{:S(2)}) collective-permute-start(bf16[256,2048]{1,0:T(8,128)(2,1)S(1)} %add.170), channel_id=1, source_target_pairs={{0,8},{2,10},{4,12},{6,14},{24,16},{26,18},{28,20},{30,22},{1,9},{... | collective-permute-start | bytes 3145736 | tf_op jit(solution)/shard_map/ppermute | solution.py:363
  158.4 21.7 %collective-permute-start.27 = (bf16[256,2048]{1,0:T(8,128)(2,1)}, bf16[256,2048]{1,0:T(8,128)(2,1)}, u32[]{:S(2)}, u32[]{:S(2)}) collective-permute-start(bf16[256,2048]{1,0:T(8,128)(2,1)} %add.169), channel_id=1, source_target_pairs={{16,8},{18,10},{20,12},{22,14},{9,17},{11,19},{13,21},{15,23}} | collective-permute-start | bytes 3145736 | tf_op jit(solution)/shard_map/ppermute | solution.py:363
  161.3 20.9 %collective-permute-start.28 = (bf16[4,160,512]{2,1,0:T(8,128)(2,1)}, bf16[4,160,512]{2,1,0:T(8,128)(2,1)}, u32[]{:S(2)}, u32[]{:S(2)}) collective-permute-start(bf16[4,160,512]{2,1,0:T(8,128)(2,1)} %bitcast.20.keep), channel_id=1, source_target_pairs={{0,4},{2,6},{4,0},{6,2},{8,12},{10,14},{12,8},{14,10},{16,20},{18,... | collective-permute-start | bytes 1966088 | tf_op jit(solution)/shard_map/ppermute | solution.py:324
  162.8 19.4 %collective-permute-start.29 = (bf16[4,160,512]{2,1,0:T(8,128)(2,1)}, bf16[4,160,512]{2,1,0:T(8,128)(2,1)}, u32[]{:S(2)}, u32[]{:S(2)}) collective-permute-start(bf16[4,160,512]{2,1,0:T(8,128)(2,1)} %bitcast.20.keep), channel_id=1, source_target_pairs={{0,2},{2,0},{4,6},{6,4},{8,10},{10,8},{12,14},{14,12},{16,18},{18,... | collective-permute-start | bytes 1966088 | tf_op jit(solution)/shard_map/ppermute | solution.py:321
  182.2 22.7 %collective-permute-start.32 = (bf16[256,2048]{1,0:T(8,128)(2,1)S(1)}, bf16[256,2048]{1,0:T(8,128)(2,1)S(1)}, u32[]{:S(2)}, u32[]{:S(2)}) collective-permute-start(bf16[256,2048]{1,0:T(8,128)(2,1)S(1)} %add.173), channel_id=1, source_target_pairs={{8,16},{10,18},{12,20},{14,22},{17,9},{19,11},{21,13},{23,15}} | collective-permute-start | bytes 3145736 | tf_op jit(solution)/shard_map/ppermute | solution.py:363
  183.5 2.4 %collective-permute-start.30 = (bf16[4,160,512]{2,1,0:T(8,128)(2,1)}, bf16[4,160,512]{2,1,0:T(8,128)(2,1)S(1)}, u32[]{:S(2)}, u32[]{:S(2)}) collective-permute-start(bf16[4,160,512]{2,1,0:T(8,128)(2,1)} %collective-permute-done.28.back), channel_id=1, source_target_pairs={{0,2},{2,0},{4,6},{6,4},{8,10},{10,8},{12,14},{14,12},{16,18},{18,... | collective-permute-start | bytes 1966088 | tf_op jit(solution)/shard_map/ppermute | solution.py:321
  198.3 4.7 %collective-permute-start.31 = (f32[4,1,512]{2,1,0:T(1,128)}, f32[4,1,512]{2,1,0:T(1,128)S(1)}, u32[]{:S(2)}, u32[]{:S(2)}) collective-permute-start(f32[4,1,512]{2,1,0:T(1,128)} %get-tuple-element.146), channel_id=1, source_target_pairs={{1,0},{0,1},{3,2},{2,3},{5,4},{4,5},{7,6},{6,7},{9,8},{8,9},{11,10... | collective-permute-start | bytes 24584 | tf_op jit(solution)/shard_map/ppermute | solution.py:327
  205.1 2.7 %collective-permute-start.33 = (bf16[256,2048]{1,0:T(8,128)(2,1)S(1)}, bf16[256,2048]{1,0:T(8,128)(2,1)S(1)}, u32[]{:S(2)}, u32[]{:S(2)}) collective-permute-start(bf16[256,2048]{1,0:T(8,128)(2,1)S(1)} %add_select_fusion.refs_0_), channel_id=1, source_target_pairs={{0,2},{2,0},{4,6},{6,4},{8,10},{10,8},{12,14},{14,12},{16,18},{18,... | collective-permute-start | bytes 3145736 | tf_op jit(solution)/shard_map/ppermute | solution.py:524
  (18 other events, 132.0 us)
